TPU v7x, 32 devices: a whole 2x2x4 slice. The times are simulated.
32 devices in a mesh: row: 4 (over y, core), col: 8 (over z, x).
Axes of the slice: x: 2, y: 2, z: 4, core: 2. Of those that a mesh axis runs over, the one named last changes fastest.
Arguments:
- a_vals: bfloat16 [2, 8, 16, 5, 128, 128], P(None, 'row', 'col'), may hold values from -0.5 to 0.5
- a_off: int32 [2, 8, 16, 5], P(None, 'row', 'col'), may hold values from 0 to 8, as said below
- a_count: int32 [2, 8, 16], P(None, 'row', 'col'), may hold values from 1 to 5
- p_vals: bfloat16 [8, 16, 4, 128, 128], P('row', 'col'), may hold values from -1.1953125 to 1.1953125
Outputs:
- coarse: bfloat16 [2, 4, 8, 25, 128, 128], P(None, 'row', 'col')
Inputs may be any that keep to these rules, and one draw needn't show every extreme that they name: Each row of a_off lists 5 different stencil positions of 0 to 8.
All inputs are finite; a program needn't handle non-finite values.
Results may differ from a plain program's by a relative error of at most 0.0049.
Values may be sent and summed in bfloat16 or wider, within the bound.
No kernel may reach another device: no remote copies, remote signals or barrier semaphores. Data moves between devices by JAX's collectives and lax.ppermute only.
A program may use at most 64 MiB of HBM per device.

v0:
```python
import jax
import jax.numpy as jnp
from jax import lax
from jax.sharding import PartitionSpec as P


def padded(block, sides, width):
    for axis, dim in sides:
        count = lax.axis_size(axis)
        forward = [(i, i + 1) for i in range(count - 1)]
        forward.append((count - 1, 0))
        backward = [(target, source) for source, target in forward]
        low = lax.ppermute(
            lax.slice_in_dim(block, block.shape[dim] - width, None, axis=dim), axis, forward
        )
        high = lax.ppermute(lax.slice_in_dim(block, 0, width, axis=dim), axis, backward)
        block = jnp.concatenate([low, block, high], axis=dim)
    return block


def corner_of(lag):
    return 1 if lag in (-1, 2) else 0


def shift_groups():
    lags = [(lag_x, lag_y) for lag_x in range(-1, 3) for lag_y in range(-1, 3)]
    result = []
    for place_x in range(3):
        for place_y in range(3):
            members = [
                (lag_x, lag_y, 2 * corner_of(lag_x) + corner_of(lag_y))
                for lag_x, lag_y in lags
                if lag_x // 2 + 1 == place_x and lag_y // 2 + 1 == place_y
            ]
            result = result + [((place_x, place_y), members)]
    return result


def band_index(near, anchor, corner):
    return (
        jnp.floor_divide(near, 2)
        + corner * (2 * jnp.remainder(near, 2) - 1)
        - jnp.floor_divide(anchor, 2)
        + 1
    )


def products_of_rows(blocks, slot_offsets, p_window, margin):
    rows_x, rows_y = (blocks.shape[0], blocks.shape[1])
    window_y = p_window.shape[1]
    p_flat = p_window.reshape((p_window.shape[0] * window_y,) + p_window.shape[2:])
    anchor_x = jnp.arange(rows_x, dtype=jnp.int32)[:, None, None]
    anchor_y = jnp.arange(rows_y, dtype=jnp.int32)[None, :, None]
    near_x = anchor_x + slot_offsets // 3 - 1
    near_y = anchor_y + slot_offsets % 3 - 1
    position = (near_x + margin) * window_y + (near_y + margin)
    picked = p_flat[position]
    quadrants = jnp.arange(4, dtype=jnp.int32)
    band = band_index(near_x[..., None], anchor_x[..., None], quadrants // 2) * 3 + band_index(
        near_y[..., None], anchor_y[..., None], quadrants % 2
    )
    onehot = (band[..., None] == jnp.arange(9, dtype=jnp.int32)).astype(jnp.bfloat16)
    selected = jnp.einsum(
        "xykqj,xykqbc->xykjbc", onehot, picked, preferred_element_type=jnp.bfloat16
    )
    summed = jnp.einsum("xykab,xykjbc->xyjac", blocks, selected, preferred_element_type=jnp.float32)
    return summed.astype(jnp.bfloat16)


def assemble(w_window, p_window, w_margin, p_margin):
    operators = w_window.shape[0]
    block = p_window.shape[-1]
    total = jnp.zeros((operators, 5, 5, block, block), jnp.float32)
    for place, members in shift_groups():
        p_rows = jnp.stack(
            [
                p_window[lag_x + p_margin, lag_y + p_margin, quadrant]
                for lag_x, lag_y, quadrant in members
            ]
        )
        w_rows = jnp.stack(
            [w_window[:, lag_x + w_margin, lag_y + w_margin] for lag_x, lag_y, quadrant in members],
            axis=1,
        )
        partial_terms = jnp.einsum(
            "uab,sujac->sjbc", p_rows, w_rows, preferred_element_type=jnp.float32
        )
        partial_terms = partial_terms.reshape((operators, 3, 3, block, block))
        total = total.at[:, place[0] : place[0] + 3, place[1] : place[1] + 3].add(partial_terms)
    return total.reshape((operators, 25, block, block)).astype(jnp.bfloat16)[:, None, None]


def per_device(a_vals, a_off, a_count, p_vals):
    slot_total = a_vals.shape[3]
    operators = a_vals.shape[0]
    alive = (jnp.arange(slot_total, dtype=jnp.int32) < a_count[..., None]).astype(jnp.bfloat16)
    a_live = a_vals * alive[..., None, None]
    p_window = padded(p_vals, (("row", 0), ("col", 1)), 1)
    w_own = jnp.stack(
        [
            products_of_rows(a_live[operator], a_off[operator], p_window, 1)
            for operator in range(operators)
        ]
    )
    w_window = padded(w_own, (("row", 1), ("col", 2)), 1)
    return assemble(w_window, p_window, 1, 1)


def solution(mesh):
    placed = (
        P(None, "row", "col", None, None, None),
        P(None, "row", "col", None),
        P(None, "row", "col"),
        P("row", "col", None, None, None),
    )
    return jax.shard_map(
        per_device,
        mesh=mesh,
        in_specs=placed,
        out_specs=P(None, "row", "col", None, None, None),
        check_vma=False,
    )
```

profile of v0, /device:TPU:0, one launch (start us, length us, event | category | flops | bytes accessed | tf_op | source)
XLA Modules:
  0.0 208.9 jit_solution(3883494703580026884)
XLA Ops:
  0.0 1.1 fusion.107
  1.1 0.5 collective-permute-start
  1.6 2.0 collective-permute-start.1
  3.6 0.7 compare_select_fusion
  4.3 0.7 and_select_fusion.5
  5.1 0.8 compare_convert_fusion
  6.1 1.7 collective-permute-done
  7.8 1.2 constant_dynamic-update-slice_fusion.1
  9.0 1.2 collective-permute-done.1
  10.3 4.9 %collective-permute-start.3 = (bf16[4,1,4,128,128]{4,3,2,1,0:T(8,128)(2,1)S(1)}, bf16[4,1,4,128,128]{4,3,2,1,0:T(8,128)(2,1)S(1)}, u32[]{:S(2)}, u32[]{:S(2)}) collective-permute-start(bf16[4,1,4,128,128]{4,3,2,1,0:T(8,128)(2,1)S(1)} %get-tuple-element.138), channel_id=1, source_target_pairs={{1,0},{2,1},{3,2},{4,3},{5,4},{6,5},{7,6},{0,7},{9,8},{10,9},{11,1... | collective-permute-start | bytes 1572872 | tf_op jit(solution)/shard_map/ppermute | solution.py:16
  15.6 20.5 %collective-permute-done.3 = bf16[4,1,4,128,128]{4,3,2,1,0:T(8,128)(2,1)S(1)} collective-permute-done((bf16[4,1,4,128,128]{4,3,2,1,0:T(8,128)(2,1)S(1)}, bf16[4,1,4,128,128]{4,3,2,1,0:T(8,128)(2,1)S(1)}, u32[]{:S(2)}, u32[]{:S(2)}) %collective-permute-start.3) | collective-permute-done | bytes 524320 | tf_op jit(solution)/shard_map/ppermute | solution.py:16
  36.4 0.5 copy-done.2
  37.1 2.5 %gather_fusion = bf16[20,4,128,128]{3,2,1,0:T(8,128)(2,1)} fusion(bf16[16,4,128,128]{3,2,1,0:T(8,128)(2,1)S(1)} %bitcast.302, s32[1024]{0:T(1024)S(1)} %get-tuple-element.174), kind=kCustom, calls=%fused_computation | custom fusion | bytes 5242960 | tf_op jit(solution)/shard_map/gather | solution.py:57
  39.6 2.6 %gather_fusion.1 = bf16[20,4,128,128]{3,2,1,0:T(8,128)(2,1)} fusion(bf16[16,4,128,128]{3,2,1,0:T(8,128)(2,1)S(1)} %bitcast.303, s32[1024]{0:T(1024)S(1)} %get-tuple-element.173), kind=kCustom, calls=%fused_computation.1 | custom fusion | bytes 5242960 | tf_op jit(solution)/shard_map/gather | solution.py:57
  42.2 6.3 %fusion.6 = bf16[2,2,5,9,128,128]{5,3,4,2,1,0:T(8,128)(2,1)S(1)} fusion(bf16[2,2,5,4,128,128]{5,4,3,2,1,0:T(8,128)(2,1)} %bitcast.305, s32[2,2,5,4]{3,2,1,0:T(8,128)S(1)} %get-tuple-element.162), kind=kOutput, calls=%fused_computation.19 | convolution fusion | flops 23593680 | bytes 8520000 | tf_op jit(solution)/shard_map/xykqj,xykqbc->xykjbc/dot_general | solution.py:63
  48.4 2.3 %fusion.14 = bf16[1,2,2,9,128,128]{4,5,3,2,1,0:T(8,128)(2,1)S(1)} fusion(bf16[2,2,5,9,128,128]{5,3,4,2,1,0:T(8,128)(2,1)S(1)} %fusion.6, bf16[2,2,2,5,128,128]{5,4,3,2,1,0:T(8,128)(2,1)S(1)} %broadcast_multiply_fusion), kind=kOutput, calls=%fused_computation.28 | convolution fusion | flops 755564544 | bytes 12320768 | tf_op jit(solution)/shard_map/xykab,xykjbc->xyjac/dot_general | solution.py:66
  50.8 5.2 %fusion.4 = bf16[2,2,5,9,128,128]{5,3,4,2,1,0:T(8,128)(2,1)S(1)} fusion(bf16[2,2,5,4,128,128]{5,4,3,2,1,0:T(8,128)(2,1)S(1)} %bitcast.304, s32[2,2,5,4]{3,2,1,0:T(8,128)S(1)} %get-tuple-element.161), kind=kOutput, calls=%fused_computation.17 | convolution fusion | flops 23593680 | bytes 8520000 | tf_op jit(solution)/shard_map/xykqj,xykqbc->xykjbc/dot_general | solution.py:63
  56.0 2.3 %fusion.17 = bf16[1,2,2,9,128,128]{4,5,3,2,1,0:T(8,128)(2,1)S(1)} fusion(bf16[2,2,5,9,128,128]{5,3,4,2,1,0:T(8,128)(2,1)S(1)} %fusion.4, bf16[2,2,2,5,128,128]{5,4,3,2,1,0:T(8,128)(2,1)S(1)} %broadcast_multiply_fusion), kind=kOutput, calls=%fused_computation.29 | convolution fusion | flops 755564544 | bytes 12320768 | tf_op jit(solution)/shard_map/xykab,xykjbc->xyjac/dot_general | solution.py:66
  58.6 1.1 collective-permute-start.5
  59.7 0.6 fusion.109
  60.2 0.6 fusion.108
  60.9 0.7 and_reduce_fusion
  61.6 23.9 %collective-permute-done.5 = bf16[2,1,2,9,128,128]{4,5,3,2,1,0:T(8,128)(2,1)S(1)} collective-permute-done((bf16[2,1,2,9,128,128]{4,5,3,2,1,0:T(8,128)(2,1)S(1)}, bf16[2,1,2,9,128,128]{4,5,3,2,1,0:T(8,128)(2,1)S(1)}, u32[]{:S(2)}, u32[]{:S(2)}) %collective-permute-start.5) | collective-permute-done | bytes 1179680 | tf_op jit(solution)/shard_map/ppermute | solution.py:16
  85.5 1.8 collective-permute-done.4
  87.3 0.6 pad_maximum_fusion
  87.9 1.8 fusion.105
  89.8 2.2 %collective-permute-start.6 = (bf16[2,4,1,9,128,128]{4,5,3,2,1,0:T(8,128)(2,1)S(1)}, bf16[2,4,1,9,128,128]{4,5,3,2,1,0:T(8,128)(2,1)S(1)}, u32[]{:S(2)}, u32[]{:S(2)}) collective-permute-start(bf16[2,4,1,9,128,128]{4,5,3,2,1,0:T(8,128)(2,1)S(1)} %get-tuple-element.122), channel_id=1, source_target_pairs={{0,1},{1,2},{2,3},{3,4},{4,5},{5,6},{6,7},{7,0},{8,9},{9,10},{10,1... | collective-permute-start | bytes 7077896 | tf_op jit(solution)/shard_map/ppermute | solution.py:13
  92.0 0.8 slice_bitcast_fusion.39
  92.8 2.6 %collective-permute-start.7 = (bf16[2,4,1,9,128,128]{4,5,3,2,1,0:T(8,128)(2,1)S(1)}, bf16[2,4,1,9,128,128]{4,5,3,2,1,0:T(8,128)(2,1)S(1)}, u32[]{:S(2)}, u32[]{:S(2)}) collective-permute-start(bf16[2,4,1,9,128,128]{4,5,3,2,1,0:T(8,128)(2,1)S(1)} %get-tuple-element.121), channel_id=1, source_target_pairs={{1,0},{2,1},{3,2},{4,3},{5,4},{6,5},{7,6},{0,7},{9,8},{10,9},{11,1... | collective-permute-start | bytes 7077896 | tf_op jit(solution)/shard_map/ppermute | solution.py:16
  95.4 0.8 slice_bitcast_fusion.33
  96.2 0.8 slice_bitcast_fusion.23
  97.2 0.8 fusion.8
  98.1 0.8 slice_bitcast_fusion.29
  98.9 0.8 slice_bitcast_fusion.27
  99.7 0.5 fusion.35
  100.4 0.5 fusion.29
  101.0 91.5 %collective-permute-done.6 = bf16[2,4,1,9,128,128]{4,5,3,2,1,0:T(8,128)(2,1)S(1)} collective-permute-done((bf16[2,4,1,9,128,128]{4,5,3,2,1,0:T(8,128)(2,1)S(1)}, bf16[2,4,1,9,128,128]{4,5,3,2,1,0:T(8,128)(2,1)S(1)}, u32[]{:S(2)}, u32[]{:S(2)}) %collective-permute-start.6) | collective-permute-done | bytes 2359328 | tf_op jit(solution)/shard_map/ppermute | solution.py:13
  192.6 0.5 fusion.33
  193.2 2.4 %collective-permute-done.7 = bf16[2,4,1,9,128,128]{4,5,3,2,1,0:T(8,128)(2,1)S(1)} collective-permute-done((bf16[2,4,1,9,128,128]{4,5,3,2,1,0:T(8,128)(2,1)S(1)}, bf16[2,4,1,9,128,128]{4,5,3,2,1,0:T(8,128)(2,1)S(1)}, u32[]{:S(2)}, u32[]{:S(2)}) %collective-permute-start.7) | collective-permute-done | bytes 2359328 | tf_op jit(solution)/shard_map/ppermute | solution.py:16
  195.6 0.5 fusion.31
  196.2 1.1 fusion.47
  197.3 0.4 scatter-add.30
  197.6 1.4 add_dynamic-update-slice_fusion
  199.1 1.1 fusion.46
  200.1 2.1 %fusion.20 = f32[2,5,5,128,128]{3,4,2,1,0:T(8,128)S(1)} fusion(f32[2,5,5,128,128]{3,4,2,1,0:T(8,128)S(1)} %add_dynamic-update-slice_fusion, s32[]{:T(128)} %bitcast.50, s32[]{:T(128)} %bitcast.51, f32[2,3,3,128,128]{3,4,2,1,0:T(8,128)S(1)} %bitcast.314, pred[]{:T(512)} %and_reduce_fusion), kind=kLoop, calls=%fused_computation.30 | loop fusion | flops 589824 | bytes 3538953 | tf_op jit(solution)/shard_map/scatter-add | solution.py:89
  203.2 1.1 fusion.44
  204.9 1.1 fusion.43
  206.5 2.4 %copy.17 = bf16[2,5,5,128,128]{4,3,2,1,0:T(8,128)(2,1)} copy(bf16[2,5,5,128,128]{3,4,2,1,0:T(8,128)(2,1)S(1)} %convert_element_type.39) | data formatting | bytes 3276800 | tf_op jit(solution)/shard_map/convert_element_type | solution.py:90
  (49 shorter events, 4.5 us)
Async XLA Ops:
  1.1 6.7 %collective-permute-start = (bf16[1,2,4,128,128]{4,3,2,1,0:T(8,128)(2,1)S(1)}, bf16[1,2,4,128,128]{4,3,2,1,0:T(8,128)(2,1)S(1)}, u32[]{:S(2)}, u32[]{:S(2)}) collective-permute-start(bf16[1,2,4,128,128]{4,3,2,1,0:T(8,128)(2,1)S(1)} %get-tuple-element.148), channel_id=1, source_target_pairs={{0,8},{8,16},{16,24},{24,0},{1,9},{9,17},{17,25},{25,1},{2,10},{10... | collective-permute-start | bytes 786440 | tf_op jit(solution)/shard_map/ppermute | solution.py:13
  1.6 8.6 %collective-permute-start.1 = (bf16[1,2,4,128,128]{4,3,2,1,0:T(8,128)(2,1)S(1)}, bf16[1,2,4,128,128]{4,3,2,1,0:T(8,128)(2,1)S(1)}, u32[]{:S(2)}, u32[]{:S(2)}) collective-permute-start(bf16[1,2,4,128,128]{4,3,2,1,0:T(8,128)(2,1)S(1)} %get-tuple-element.147), channel_id=1, source_target_pairs={{8,0},{16,8},{24,16},{0,24},{9,1},{17,9},{25,17},{1,25},{10,2},{18... | collective-permute-start | bytes 786440 | tf_op jit(solution)/shard_map/ppermute | solution.py:16
  6.0 9.4 %copy-start.1 = (bf16[2,2,2,5,128,128]{5,4,3,2,1,0:T(8,128)(2,1)S(1)}, bf16[2,2,2,5,128,128]{5,4,3,2,1,0:T(8,128)(2,1)}, u32[]{:S(2)}) copy-start(bf16[2,2,2,5,128,128]{5,4,3,2,1,0:T(8,128)(2,1)} %param.22) | copy-start | bytes 3932164
  7.7 2.6 %copy-start.4 = (bf16[1,2,4,128,128]{4,3,2,1,0:T(8,128)(2,1)}, bf16[1,2,4,128,128]{4,3,2,1,0:T(8,128)(2,1)S(1)}, u32[]{:S(2)}) copy-start(bf16[1,2,4,128,128]{4,3,2,1,0:T(8,128)(2,1)S(1)} %collective-permute-done) | copy-start | bytes 786436
  10.2 5.3 %copy-start.5 = (bf16[1,2,4,128,128]{4,3,2,1,0:T(8,128)(2,1)}, bf16[1,2,4,128,128]{4,3,2,1,0:T(8,128)(2,1)S(1)}, u32[]{:S(2)}) copy-start(bf16[1,2,4,128,128]{4,3,2,1,0:T(8,128)(2,1)S(1)} %collective-permute-done.1) | copy-start | bytes 786436
  10.3 25.8 %collective-permute-start.3 = (bf16[4,1,4,128,128]{4,3,2,1,0:T(8,128)(2,1)S(1)}, bf16[4,1,4,128,128]{4,3,2,1,0:T(8,128)(2,1)S(1)}, u32[]{:S(2)}, u32[]{:S(2)}) collective-permute-start(bf16[4,1,4,128,128]{4,3,2,1,0:T(8,128)(2,1)S(1)} %get-tuple-element.138), channel_id=1, source_target_pairs={{1,0},{2,1},{3,2},{4,3},{5,4},{6,5},{7,6},{0,7},{9,8},{10,9},{11,1... | collective-permute-start | bytes 1572872 | tf_op jit(solution)/shard_map/ppermute | solution.py:16
  15.3 20.9 %collective-permute-start.2 = (bf16[4,1,4,128,128]{4,3,2,1,0:T(8,128)(2,1)S(1)}, bf16[4,1,4,128,128]{4,3,2,1,0:T(8,128)(2,1)S(1)}, u32[]{:S(2)}, u32[]{:S(2)}) collective-permute-start(bf16[4,1,4,128,128]{4,3,2,1,0:T(8,128)(2,1)S(1)} %get-tuple-element.137), channel_id=1, source_target_pairs={{0,1},{1,2},{2,3},{3,4},{4,5},{5,6},{6,7},{7,0},{8,9},{9,10},{10,1... | collective-permute-start | bytes 1572872 | tf_op jit(solution)/shard_map/ppermute | solution.py:13
  36.1 0.8 copy-start.2
  36.2 0.9 copy-start.3
  48.4 2.3 %copy-start = (bf16[20,4,128,128]{3,2,1,0:T(8,128)(2,1)S(1)}, bf16[20,4,128,128]{3,2,1,0:T(8,128)(2,1)}, u32[]{:S(2)}) copy-start(bf16[20,4,128,128]{3,2,1,0:T(8,128)(2,1)} %gather_fusion.1) | copy-start | bytes 7864324
  58.3 2.5 %copy-start.6 = (s32[5]{0:T(128)S(1)}, s32[5]{0:T(128)}, u32[]{:S(2)}) copy-start(s32[5]{0:T(128)} %constant.421.clone.1) | copy-start | bytes 64
  58.6 27.0 %collective-permute-start.5 = (bf16[2,1,2,9,128,128]{4,5,3,2,1,0:T(8,128)(2,1)S(1)}, bf16[2,1,2,9,128,128]{4,5,3,2,1,0:T(8,128)(2,1)S(1)}, u32[]{:S(2)}, u32[]{:S(2)}) collective-permute-start(bf16[2,1,2,9,128,128]{4,5,3,2,1,0:T(8,128)(2,1)S(1)} %get-tuple-element.132), channel_id=1, source_target_pairs={{8,0},{16,8},{24,16},{0,24},{9,1},{17,9},{25,17},{1,25},{10,2},{18... | collective-permute-start | bytes 3538952 | tf_op jit(solution)/shard_map/ppermute | solution.py:16
  59.6 27.7 %collective-permute-start.4 = (bf16[2,1,2,9,128,128]{4,5,3,2,1,0:T(8,128)(2,1)S(1)}, bf16[2,1,2,9,128,128]{4,5,3,2,1,0:T(8,128)(2,1)S(1)}, u32[]{:S(2)}, u32[]{:S(2)}) collective-permute-start(bf16[2,1,2,9,128,128]{4,5,3,2,1,0:T(8,128)(2,1)S(1)} %get-tuple-element.131), channel_id=1, source_target_pairs={{0,8},{8,16},{16,24},{24,0},{1,9},{9,17},{17,25},{25,1},{2,10},{10... | collective-permute-start | bytes 3538952 | tf_op jit(solution)/shard_map/ppermute | solution.py:13
  89.8 102.7 %collective-permute-start.6 = (bf16[2,4,1,9,128,128]{4,5,3,2,1,0:T(8,128)(2,1)S(1)}, bf16[2,4,1,9,128,128]{4,5,3,2,1,0:T(8,128)(2,1)S(1)}, u32[]{:S(2)}, u32[]{:S(2)}) collective-permute-start(bf16[2,4,1,9,128,128]{4,5,3,2,1,0:T(8,128)(2,1)S(1)} %get-tuple-element.122), channel_id=1, source_target_pairs={{0,1},{1,2},{2,3},{3,4},{4,5},{5,6},{6,7},{7,0},{8,9},{9,10},{10,1... | collective-permute-start | bytes 7077896 | tf_op jit(solution)/shard_map/ppermute | solution.py:13
  92.8 102.7 %collective-permute-start.7 = (bf16[2,4,1,9,128,128]{4,5,3,2,1,0:T(8,128)(2,1)S(1)}, bf16[2,4,1,9,128,128]{4,5,3,2,1,0:T(8,128)(2,1)S(1)}, u32[]{:S(2)}, u32[]{:S(2)}) collective-permute-start(bf16[2,4,1,9,128,128]{4,5,3,2,1,0:T(8,128)(2,1)S(1)} %get-tuple-element.121), channel_id=1, source_target_pairs={{1,0},{2,1},{3,2},{4,3},{5,4},{6,5},{7,6},{0,7},{9,8},{10,9},{11,1... | collective-permute-start | bytes 7077896 | tf_op jit(solution)/shard_map/ppermute | solution.py:16
where the time goes:
time: 210 us; the launch traced here: 209 us
  waiting for transfers between devices  143 us (68%)
  matrix products  22.9 us (11%)
  local copies, waits for them, and re-layouts  18.9 us (9%)
  starting transfers between devices  13.4 us (6%)
  other arithmetic  10.2 us (5%)
    ppermute x4, waiting for transfers between devices, padded(): lax.ppermute(lax.slice_in_dim(block, block.shape[dim] - width, None, axis...  95 us
    ppermute x4, waiting for transfers between devices, padded(): lax.ppermute(lax.slice_in_dim(block, 0, width, axis=dim), axis, backward)  48.1 us
    dot_general x2, matrix products, products_of_rows(): jnp.einsum('xykqj,xykqbc->xykjbc', onehot, picked, preferred_element_type...  11.5 us
    ppermute x4, starting transfers between devices, padded(): lax.ppermute(lax.slice_in_dim(block, 0, width, axis=dim), axis, backward)  10.6 us
    dot_general x9, matrix products, assemble(): jnp.einsum('uab,sujac->sjbc', p_rows, w_rows, preferred_element_type=jnp....  6.82 us
    scatter-add x8, other arithmetic, assemble(): total.at[:, place[0]:place[0] + 3, place[1]:place[1] + 3].add(partial_terms)  5.38 us
    gather x2, local copies, waits for them, and re-layouts, products_of_rows(): picked = p_flat[position]  5.11 us
    dot_general x2, matrix products, products_of_rows(): jnp.einsum('xykab,xykjbc->xyjac', blocks, selected, preferred_element_typ...  4.65 us
  transfers between devices with their start and end apart: 8, of which 8 were waited for; matrix products, arithmetic and copies ran while one was open for 6% of the time, Pallas kernels for 0%

commit v1 on v0

v1 whole, which is shorter than its diff:
```python
import functools

import jax
import jax.numpy as jnp
from jax import lax
from jax.experimental import pallas as pl
from jax.experimental.pallas import tpu as pltpu
from jax.sharding import PartitionSpec as P

P_ROWS, P_COLS = 4, 6
A_COLS = 4
VMEM_LIMIT = 48 * 1024 * 1024


def ring(count, step):
    return [(i, (i + step) % count) for i in range(count)]


def pair(count):
    return [(i, i ^ 1) for i in range(count)]


def outward(count, width):
    return [(i, (i + (width if i % 2 else -width)) % count) for i in range(count)]


def onward(count):
    return [(i, (i + (-2 if i % 2 else 2)) % count) for i in range(count)]


def product_table(offsets, counts, zero_at):
    slots = offsets.shape[-1]
    shape = offsets.shape + (3, 3)
    dims = len(shape)
    fine_x = lax.broadcasted_iota(jnp.int32, shape, dims - 5)
    fine_y = lax.broadcasted_iota(jnp.int32, shape, dims - 4) - 1
    slot = lax.broadcasted_iota(jnp.int32, shape, dims - 3)
    band_y = lax.broadcasted_iota(jnp.int32, shape, dims - 2)
    band_x = lax.broadcasted_iota(jnp.int32, shape, dims - 1)
    off = offsets[..., None, None]
    near_x = fine_x + off // 3 - 1
    near_y = fine_y + off % 3 - 1
    first_x = ((near_x - 1) >> 1) - (fine_x >> 1) + 1
    first_y = ((near_y - 1) >> 1) - (fine_y >> 1) + 1
    place_x = band_x - first_x
    place_y = band_y - first_y
    corner_x = jnp.where(near_x & 1, place_x, 1 - place_x)
    corner_y = jnp.where(near_y & 1, place_y, 1 - place_y)
    good = (place_x >= 0) & (place_x < 2) & (place_y >= 0) & (place_y < 2)
    good = good & (slot < counts[..., None, None, None])
    index = ((near_x + 1) * P_COLS + near_y + 2) * 4 + 2 * corner_x + corner_y
    index = jnp.where(good, index, zero_at)
    return index.reshape(offsets.shape[:-3] + (2 * A_COLS * slots * 9,))


def load_window(odd, pieces, window, sems, number):
    copies = []
    for place, (rows, first) in enumerate(((2, 1), (1, 0), (1, 3))):
        own, near, far = pieces[3 * place : 3 * place + 3]
        for piece, col in ((own, 2), (near, jnp.where(odd, 0, 4)), (far, jnp.where(odd, 4, 0))):
            copies.append(
                pltpu.make_async_copy(
                    piece, window.at[pl.ds(first, rows), pl.ds(col, 2)], sems.at[number + len(copies)]
                )
            )
    return copies


def edge_kernel(operator, slots, table, odd_ref, a_own, a_near, a_far, *refs):
    pieces = refs[:9]
    low_ref, high_ref, w_ref, p_ref = refs[9:13]
    window, zero, blocks, sems = refs[13:]
    odd = odd_ref[0] == 1
    copies = load_window(odd, pieces, window, sems, 0)
    for src, col, width in ((a_own.at[operator], 1, 2), (a_near, jnp.where(odd, 0, 3), 1), (a_far, jnp.where(odd, 3, 0), 1)):
        copies.append(
            pltpu.make_async_copy(src, blocks.at[:, pl.ds(col, width)], sems.at[len(copies)])
        )
    for copy in copies:
        copy.start()
    block = zero.shape[-1]
    zero[...] = jnp.zeros(zero.shape, zero.dtype)
    for copy in copies:
        copy.wait()
    flat = p_ref
    for x in range(P_ROWS):
        for y in range(P_COLS):
            for q in range(4):
                flat[(x * P_COLS + y) * 4 + q] = window[x, y, q]
    flat[P_ROWS * P_COLS * 4] = zero[...]

    def one_row(row, carry):
        fine_x = row // A_COLS
        fine_y = row % A_COLS
        left = jnp.concatenate([blocks[fine_x, fine_y, k] for k in range(slots)], axis=1)
        for band_y in range(3):
            right = jnp.concatenate(
                [
                    jnp.concatenate(
                        [flat[table[((row * slots + k) * 3 + band_y) * 3 + band_x]] for band_x in range(3)],
                        axis=1,
                    )
                    for k in range(slots)
                ],
                axis=0,
            )
            w_ref[row, band_y] = jnp.dot(left, right, preferred_element_type=jnp.float32).astype(w_ref.dtype)
        return carry

    lax.fori_loop(0, 2 * A_COLS, one_row, 0)
    for out, fine_x in ((low_ref, 0), (high_ref, 1)):
        for lag_y in range(5):
            total = coarse_column(flat, w_ref, (fine_x,), lag_y, 2)
            for lag_x in range(3):
                out[lag_x, lag_y] = total[:, lag_x * block : (lag_x + 1) * block].astype(out.dtype)


def coarse_column(flat, w_ref, fine_rows, lag_y, corner_x):
    lefts, rights = [], []
    for fine_x in fine_rows:
        for col in range(A_COLS):
            fine_y = col - 1
            band_y = lag_y - (fine_y // 2 + 1)
            if 0 <= band_y < 3:
                corner_y = 1 if fine_y in (-1, 2) else 0
                lefts.append(flat[((fine_x + 1) * P_COLS + fine_y + 2) * 4 + corner_x + corner_y])
                rights.append(w_ref[fine_x * A_COLS + col, band_y])
    left = jnp.concatenate(lefts, axis=0)
    right = jnp.concatenate(rights, axis=0)
    return lax.dot_general(left, right, (((0,), (0,)), ((), ())), preferred_element_type=jnp.float32)


def own_kernel(flat, w_ref, out):
    block = out.shape[-1]
    for lag_y in range(5):
        total = coarse_column(flat, w_ref, (0, 1), lag_y, 0)
        for lag_x in range(3):
            out[lag_x, lag_y] = total[:, lag_x * block : (lag_x + 1) * block]


def final_kernel(*refs):
    out = refs[-1]
    for operator in range(out.shape[0]):
        own, low, high = refs[3 * operator : 3 * operator + 3]
        for lag_x in range(5):
            for lag_y in range(5):
                total = None
                for part, first in ((low, 0), (own, 1), (high, 2)):
                    if 0 <= lag_x - first < 3:
                        term = part[lag_x - first, lag_y].astype(jnp.float32)
                        total = term if total is None else total + term
                out[operator, 0, 0, 5 * lag_x + lag_y] = total.astype(out.dtype)


def per_device(a_vals, a_off, a_count, p_vals):
    operators, _, _, slots, block, _ = a_vals.shape
    cols = lax.axis_size("col")
    rows = lax.axis_size("row")
    odd = lax.axis_index("col") % 2
    up, down = ring(rows, 1), ring(rows, -1)
    near_way, far_way, on_way = pair(cols), outward(cols, 1), onward(cols)

    def both_rows(piece):
        low = lax.ppermute(piece[1:2], "row", up)
        high = lax.ppermute(piece[0:1], "row", down)
        return low, high

    def facing(array, dim, index):
        return lax.dynamic_slice_in_dim(array, index, 1, axis=dim)

    info = jnp.concatenate([a_off, a_count[..., None]], axis=-1)
    p_near = lax.ppermute(p_vals, "col", near_way)
    info_near = lax.ppermute(facing(info, 2, 1 - odd), "col", near_way)
    info_far = lax.ppermute(facing(info, 2, odd), "col", far_way)
    own_low, own_high = both_rows(p_vals)
    a_near, a_far = [], []
    for operator in range(operators):
        a_near.append(lax.ppermute(facing(a_vals[operator], 1, 1 - odd), "col", near_way))
        a_far.append(lax.ppermute(facing(a_vals[operator], 1, odd), "col", far_way))
    p_far = lax.ppermute(p_near, "col", on_way)
    near_low, near_high = both_rows(p_near)
    far_low, far_high = both_rows(p_far)
    pieces = (p_vals, p_near, p_far, own_low, near_low, far_low, own_high, near_high, far_high)

    left = jnp.where(odd == 1, info_near, info_far)
    right = jnp.where(odd == 1, info_far, info_near)
    info_all = jnp.concatenate([left, info, right], axis=2)
    zero_at = P_ROWS * P_COLS * 4
    table = product_table(info_all[..., :slots], info_all[..., slots], zero_at)
    odd_arg = odd.astype(jnp.int32)[None]

    any_spec = pl.BlockSpec(memory_space=pl.ANY)
    smem = pl.BlockSpec(memory_space=pltpu.SMEM)
    vmem = pl.BlockSpec(memory_space=pltpu.VMEM)
    bf16, f32 = jnp.bfloat16, jnp.float32
    params = pltpu.CompilerParams(vmem_limit_bytes=VMEM_LIMIT)
    partial_shape = jax.ShapeDtypeStruct((3, 5, block, block), bf16)
    finals = []
    for operator in range(operators):
        low, high, w_all, flat = pl.pallas_call(
            functools.partial(edge_kernel, operator, slots),
            in_specs=[smem, smem] + [any_spec] * 12,
            out_specs=[vmem] * 4,
            out_shape=[
                partial_shape,
                partial_shape,
                jax.ShapeDtypeStruct((2 * A_COLS, 3, block, 3 * block), bf16),
                jax.ShapeDtypeStruct((zero_at + 1, block, block), bf16),
            ],
            scratch_shapes=[
                pltpu.VMEM((P_ROWS, P_COLS, 4, block, block), bf16),
                pltpu.VMEM((block, block), bf16),
                pltpu.VMEM((2, A_COLS, slots, block, block), bf16),
                pltpu.SemaphoreType.DMA((12,)),
            ],
            compiler_params=params,
            cost_estimate=pl.CostEstimate(flops=500 * 2 * block**3, bytes_accessed=8 << 20, transcendentals=0),
            name="edge",
        )(table[operator], odd_arg, a_vals, a_near[operator], a_far[operator], *pieces)
        from_low = lax.ppermute(high, "row", up)
        from_high = lax.ppermute(low, "row", down)
        own = pl.pallas_call(
            own_kernel,
            in_specs=[vmem] * 2,
            out_specs=vmem,
            out_shape=jax.ShapeDtypeStruct((3, 5, block, block), f32),
            compiler_params=params,
            cost_estimate=pl.CostEstimate(flops=100 * 2 * block**3, bytes_accessed=6 << 20, transcendentals=0),
            name="own",
        )(flat, w_all)
        finals += [own, from_low, from_high]
    return pl.pallas_call(
        final_kernel,
        in_specs=[vmem] * len(finals),
        out_specs=vmem,
        out_shape=jax.ShapeDtypeStruct((operators, 1, 1, 25, block, block), bf16),
        compiler_params=params,
        cost_estimate=pl.CostEstimate(flops=1 << 20, bytes_accessed=8 << 20, transcendentals=0),
        name="final",
    )(*finals)


def solution(mesh):
    placed = (
        P(None, "row", "col", None, None, None),
        P(None, "row", "col", None),
        P(None, "row", "col"),
        P("row", "col", None, None, None),
    )
    return jax.shard_map(
        per_device,
        mesh=mesh,
        in_specs=placed,
        out_specs=P(None, "row", "col", None, None, None),
        check_vma=False,
    )
```

time: 210 us -> 90.3 us (0.43)
  waiting for transfers between devices: 143 us -> 36.7 us
  Pallas kernels: 0 us -> 23.5 us
  matrix products: 22.9 us -> 0 us
  other arithmetic: 10.2 us -> 1.48 us
  local copies, waits for them, and re-layouts: 18.9 us -> 11.6 us
  starting transfers between devices: 13.4 us -> 16.4 us
    ppermute x8 -> x18, waiting for transfers between devices: 143 us -> 36.7 us  [the longest x1 13.8 us: per_device(): p_near = lax.ppermute(p_vals, 'col', near_way)]
    pallas_call x0 -> x5, Pallas kernels: none -> 23.5 us  [the longest x2 16.9 us: per_device(): pl.pallas_call(functools.partial(edge_kernel, operator, slots), in_specs=...]
    dot_general x13 -> x0, matrix products: 22.9 us -> none  [the longest x2 11.5 us: products_of_rows(): jnp.einsum('xykqj,xykqbc->xykjbc', onehot, picked, preferred_element_type...]
    another operation x12 -> x0, local copies, waits for them, and re-layouts: 5.55 us -> none  [the longest x5 3.94 us: assemble(): jnp.stack([p_window[lag_x + p_margin, lag_y + p_margin, quadrant] for lag...]
    scatter-add x8 -> x0, other arithmetic: 5.38 us -> none  [assemble(): total.at[:, place[0]:place[0] + 3, place[1]:place[1] + 3].add(partial_terms)]
    gather x2 -> x0, local copies, waits for them, and re-layouts: 5.11 us -> none  [products_of_rows(): picked = p_flat[position]]
    ppermute x8 -> x18, starting transfers between devices: 13.4 us -> 16.4 us  [the longest x1 3.57 us: per_device(): info_far = lax.ppermute(facing(info, 2, odd), 'col', far_way)]
    slice x3 -> x6, local copies, waits for them, and re-layouts: 2.96 us -> 5.83 us  [the longest x3 3.45 us: both_rows(): high = lax.ppermute(piece[0:1], 'row', down)]
  transfers between devices with their start and end apart: 8 -> 18, of which waited for: 8 -> 6; matrix products, arithmetic and copies ran while one was open for 6% -> 12% of each run, Pallas kernels for 0% -> 25%
where the time goes in v1:
time: 90.3 us; the launch traced here: 89.8 us
  waiting for transfers between devices  36.7 us (41%)
  Pallas kernels  23.5 us (26%)
  starting transfers between devices  16.4 us (18%)
  local copies, waits for them, and re-layouts  11.6 us (13%)
  other arithmetic  1.48 us (2%)
    pallas_call x2, Pallas kernels, per_device(): pl.pallas_call(functools.partial(edge_kernel, operator, slots), in_specs=...  16.9 us
    ppermute x1, waiting for transfers between devices, per_device(): p_near = lax.ppermute(p_vals, 'col', near_way)  13.8 us
    ppermute x1, waiting for transfers between devices, per_device(): p_far = lax.ppermute(p_near, 'col', on_way)  9.99 us
    ppermute x3, waiting for transfers between devices, both_rows(): low = lax.ppermute(piece[1:2], 'row', up)  6.22 us
    ppermute x2, waiting for transfers between devices, per_device(): from_low = lax.ppermute(high, 'row', up)  6.05 us
    pallas_call x2, Pallas kernels, per_device(): pl.pallas_call(own_kernel, in_specs=[vmem] * 2, out_specs=vmem, out_shape...  5.17 us
    ppermute x1, starting transfers between devices, per_device(): info_far = lax.ppermute(facing(info, 2, odd), 'col', far_way)  3.57 us
    ppermute x2, starting transfers between devices, per_device(): from_high = lax.ppermute(low, 'row', down)  3.46 us
  transfers between devices with their start and end apart: 18, of which 6 were waited for; matrix products, arithmetic and copies ran while one was open for 12% of the time, Pallas kernels for 25%

profile of v1, /device:TPU:0, one launch (start us, length us, event | category | flops | bytes accessed | tf_op | source)
XLA Modules:
  0.0 89.8 jit_solution(17960499003524673746)
XLA Ops:
  0.0 0.8 copy.6
  0.8 0.8 fusion.17
  1.6 2.9 %collective-permute-start = (s32[2,2,1,6]{3,2,1,0:T(1,128)S(1)}, s32[2,2,1,6]{3,2,1,0:T(1,128)S(1)}, u32[]{:S(2)}, u32[]{:S(2)}) collective-permute-start(s32[2,2,1,6]{3,2,1,0:T(1,128)S(1)} %get-tuple-element.37), channel_id=1, source_target_pairs={{0,1},{1,0},{2,3},{3,2},{4,5},{5,4},{6,7},{7,6},{8,9},{9,8},{10,11... | collective-permute-start | bytes 296 | tf_op jit(solution)/shard_map/ppermute | solution.py:173
  4.6 3.6 %collective-permute-start.1 = (s32[2,2,1,6]{3,2,1,0:T(1,128)S(1)}, s32[2,2,1,6]{3,2,1,0:T(1,128)S(1)}, u32[]{:S(2)}, u32[]{:S(2)}) collective-permute-start(s32[2,2,1,6]{3,2,1,0:T(1,128)S(1)} %get-tuple-element.38), channel_id=1, source_target_pairs={{0,7},{1,2},{2,1},{3,4},{4,3},{5,6},{6,5},{7,0},{8,15},{9,10},{10,... | collective-permute-start | bytes 296 | tf_op jit(solution)/shard_map/ppermute | solution.py:174
  8.2 1.9 %fusion.22 = (bf16[1,2,4,128,128]{4,3,2,1,0:T(8,128)(2,1)}, bf16[1,2,4,128,128]{4,3,2,1,0:T(8,128)(2,1)}) fusion(bf16[2,2,4,128,128]{4,3,2,1,0:T(8,128)(2,1)} %refs_0_.3), kind=kLoop, calls=%fused_computation.48 | loop fusion | bytes 1048576 | tf_op jit(solution)/shard_map/slice | solution.py:165
  10.0 0.4 collective-permute-start.9
  10.4 0.1 collective-permute-start.6
  10.5 1.4 %fusion.19 = (bf16[1,2,2,5,128,128]{5,4,3,2,1,0:T(8,128)(2,1)S(1)}, bf16[1,2,2,5,128,128]{5,4,3,2,1,0:T(8,128)(2,1)S(1)}) fusion(bf16[2,2,2,5,128,128]{5,4,3,2,1,0:T(8,128)(2,1)} %a_own.3), kind=kLoop, calls=%fused_computation.45 | loop fusion | bytes 2621440 | tf_op jit(solution)/shard_map/slice | solution.py:178
  12.0 0.9 %dynamic-slice_bitcast_fusion = (bf16[2,1,5,128,128]{4,3,2,1,0:T(8,128)(2,1)}, bf16[2,1,5,128,128]{4,3,2,1,0:T(8,128)(2,1)}) fusion(bf16[1,2,2,5,128,128]{5,4,3,2,1,0:T(8,128)(2,1)S(1)} %get-tuple-element.23, s32[]{:T(128)S(6)} %select_n.56, s32[]{:T(128)S(6)} %select_n.55), kind=kLoop, calls=%fused_computation | loop fusion | bytes 1310728 | tf_op jit(solution)/shard_map/dynamic_slice | solution.py:169
  12.9 0.9 %dynamic-slice_bitcast_fusion.2 = (bf16[2,1,5,128,128]{4,3,2,1,0:T(8,128)(2,1)}, bf16[2,1,5,128,128]{4,3,2,1,0:T(8,128)(2,1)}) fusion(bf16[1,2,2,5,128,128]{5,4,3,2,1,0:T(8,128)(2,1)S(1)} %get-tuple-element.24, s32[]{:T(128)S(6)} %select_n.56, s32[]{:T(128)S(6)} %select_n.55), kind=kLoop, calls=%fused_computation.2 | loop fusion | bytes 1310728 | tf_op jit(solution)/shard_map/dynamic_slice | solution.py:169
  13.8 0.0 collective-permute-done
  13.8 1.9 %collective-permute-start.3 = (bf16[2,1,5,128,128]{4,3,2,1,0:T(8,128)(2,1)}, bf16[2,1,5,128,128]{4,3,2,1,0:T(8,128)(2,1)S(1)}, u32[]{:S(2)}, u32[]{:S(2)}) collective-permute-start(bf16[2,1,5,128,128]{4,3,2,1,0:T(8,128)(2,1)} %get-tuple-element.27), channel_id=1, source_target_pairs={{0,7},{1,2},{2,1},{3,4},{4,3},{5,6},{6,5},{7,0},{8,15},{9,10},{10,... | collective-permute-start | bytes 983048 | tf_op jit(solution)/shard_map/ppermute | solution.py:179
  15.7 0.6 collective-permute-start.2
  16.3 0.1 pad_add_fusion
  16.4 13.8 %collective-permute-done.4.refs_1_ = bf16[2,2,4,128,128]{4,3,2,1,0:T(8,128)(2,1)S(1)} collective-permute-done((bf16[2,2,4,128,128]{4,3,2,1,0:T(8,128)(2,1)}, bf16[2,2,4,128,128]{4,3,2,1,0:T(8,128)(2,1)S(1)}, u32[]{:S(2)}, u32[]{:S(2)}) %collective-permute-start.4) | collective-permute-done | bytes 524320 | tf_op jit(solution)/shard_map/ppermute | solution.py:172
  30.2 0.2 slice_reduce_fusion
  30.5 0.7 fusion.21
  31.2 10.0 %collective-permute-done.5.refs_2_ = bf16[2,2,4,128,128]{4,3,2,1,0:T(8,128)(2,1)S(1)} collective-permute-done((bf16[2,2,4,128,128]{4,3,2,1,0:T(8,128)(2,1)S(1)}, bf16[2,2,4,128,128]{4,3,2,1,0:T(8,128)(2,1)S(1)}, u32[]{:S(2)}, u32[]{:S(2)}) %collective-permute-start.5) | collective-permute-done | bytes 524320 | tf_op jit(solution)/shard_map/ppermute | solution.py:180
  41.2 0.0 collective-permute-start.10
  41.2 0.8 fusion.20
  42.1 0.0 collective-permute-done.9.refs_6_
  42.1 0.5 collective-permute-start.7
  42.6 0.0 collective-permute-done.6.refs_3_
  42.6 1.2 %collective-permute-start.11 = (bf16[1,2,4,128,128]{4,3,2,1,0:T(8,128)(2,1)}, bf16[1,2,4,128,128]{4,3,2,1,0:T(8,128)(2,1)}, u32[]{:S(2)}, u32[]{:S(2)}) collective-permute-start(bf16[1,2,4,128,128]{4,3,2,1,0:T(8,128)(2,1)} %get-tuple-element.29), channel_id=1, source_target_pairs={{0,24},{8,0},{16,8},{24,16},{1,25},{9,1},{17,9},{25,17},{2,26},{10... | collective-permute-start | bytes 786440 | tf_op jit(solution)/shard_map/ppermute | solution.py:165
  43.8 0.0 collective-permute-done.3.a_far
  43.8 0.0 collective-permute-start.8
  43.8 0.5 fusion.6
  44.3 0.0 collective-permute-done.2.a_near
  44.4 1.5 %collective-permute-start.15 = (bf16[2,1,5,128,128]{4,3,2,1,0:T(8,128)(2,1)}, bf16[2,1,5,128,128]{4,3,2,1,0:T(8,128)(2,1)}, u32[]{:S(2)}, u32[]{:S(2)}) collective-permute-start(bf16[2,1,5,128,128]{4,3,2,1,0:T(8,128)(2,1)} %get-tuple-element.25), channel_id=1, source_target_pairs={{0,7},{1,2},{2,1},{3,4},{4,3},{5,6},{6,5},{7,0},{8,15},{9,10},{10,... | collective-permute-start | bytes 983048 | tf_op jit(solution)/shard_map/ppermute | solution.py:179
  45.9 0.0 collective-permute-done.10.refs_7_
  45.9 0.0 collective-permute-start.14
  45.9 0.7 fusion.23
  46.6 1.1 %squeeze.5.table = s32[360]{0:T(512)S(1)} reshape(s32[1,2,4,5,3,3]{5,4,3,2,1,0:T(4,128)} %get-tuple-element.35) | data formatting | bytes 2880 | tf_op jit(solution)/shard_map/squeeze | solution.py:219
  47.7 1.1 %squeeze.4.table = s32[360]{0:T(512)S(1)} reshape(s32[1,2,4,5,3,3]{5,4,3,2,1,0:T(4,128)} %get-tuple-element.36) | data formatting | bytes 2880 | tf_op jit(solution)/shard_map/squeeze | solution.py:219
  48.8 2.2 %collective-permute-done.7.refs_4_ = bf16[1,2,4,128,128]{4,3,2,1,0:T(8,128)(2,1)} collective-permute-done((bf16[1,2,4,128,128]{4,3,2,1,0:T(8,128)(2,1)}, bf16[1,2,4,128,128]{4,3,2,1,0:T(8,128)(2,1)}, u32[]{:S(2)}, u32[]{:S(2)}) %collective-permute-start.7) | collective-permute-done | bytes 262176 | tf_op jit(solution)/shard_map/ppermute | solution.py:164
  51.0 0.6 collective-permute-done.11.refs_8_
  51.6 4.0 %collective-permute-done.8.refs_5_ = bf16[1,2,4,128,128]{4,3,2,1,0:T(8,128)(2,1)} collective-permute-done((bf16[1,2,4,128,128]{4,3,2,1,0:T(8,128)(2,1)}, bf16[1,2,4,128,128]{4,3,2,1,0:T(8,128)(2,1)}, u32[]{:S(2)}, u32[]{:S(2)}) %collective-permute-start.8) | collective-permute-done | bytes 262176 | tf_op jit(solution)/shard_map/ppermute | solution.py:164
  55.6 0.9 %copy-done.5 = bf16[1,2,4,128,128]{4,3,2,1,0:T(8,128)(2,1)S(1)} copy-done((bf16[1,2,4,128,128]{4,3,2,1,0:T(8,128)(2,1)S(1)}, bf16[1,2,4,128,128]{4,3,2,1,0:T(8,128)(2,1)}, u32[]{:S(2)}) %copy-start.5) | copy-done | bytes 262168
  56.6 8.3 %edge.2 = (bf16[3,5,128,128]{3,2,1,0:T(8,128)(2,1)S(1)}, bf16[3,5,128,128]{3,2,1,0:T(8,128)(2,1)S(1)}, bf16[8,3,128,384]{3,2,1,0:T(8,128)(2,1)}, bf16[97,128,128]{2,1,0:T(8,128)(2,1)}) custom-call(s32[360]{0:T(512)S(1)} %squeeze.4.table, s32[1]{0:T(128)} %bitcast.1.odd_ref, bf16[2,2,2,5,128,128]{5,4,3,2,1,0:T(8,128)(2,1)S(1)} %copy-done.2, ...), custom_call_target="tpu_custom_call" | custom-call | flops 2097152000 | bytes 8388608 | tf_op jit(solution)/shard_map/edge/pallas_call | solution.py:200
  64.9 0.1 collective-permute-start.12
  65.0 1.7 %collective-permute-start.13 = (bf16[3,5,128,128]{3,2,1,0:T(8,128)(2,1)S(1)}, bf16[3,5,128,128]{3,2,1,0:T(8,128)(2,1)S(1)}, u32[]{:S(2)}, u32[]{:S(2)}) collective-permute-start(bf16[3,5,128,128]{3,2,1,0:T(8,128)(2,1)S(1)} %get-tuple-element.16), channel_id=1, source_target_pairs={{0,24},{8,0},{16,8},{24,16},{1,25},{9,1},{17,9},{25,17},{2,26},{10... | collective-permute-start | bytes 1474568 | tf_op jit(solution)/shard_map/ppermute | solution.py:221
  66.7 8.6 %edge.3 = (bf16[3,5,128,128]{3,2,1,0:T(8,128)(2,1)S(1)}, bf16[3,5,128,128]{3,2,1,0:T(8,128)(2,1)S(1)}, bf16[8,3,128,384]{3,2,1,0:T(8,128)(2,1)}, bf16[97,128,128]{2,1,0:T(8,128)(2,1)}) custom-call(s32[360]{0:T(512)S(1)} %squeeze.5.table, s32[1]{0:T(128)} %bitcast.1.odd_ref, bf16[2,2,2,5,128,128]{5,4,3,2,1,0:T(8,128)(2,1)S(1)} %copy-done.2, ...), custom_call_target="tpu_custom_call" | custom-call | flops 2097152000 | bytes 8388608 | tf_op jit(solution)/shard_map/edge/pallas_call | solution.py:200
  75.3 0.1 collective-permute-start.16
  75.4 1.7 %collective-permute-start.17 = (bf16[3,5,128,128]{3,2,1,0:T(8,128)(2,1)S(1)}, bf16[3,5,128,128]{3,2,1,0:T(8,128)(2,1)S(1)}, u32[]{:S(2)}, u32[]{:S(2)}) collective-permute-start(bf16[3,5,128,128]{3,2,1,0:T(8,128)(2,1)S(1)} %get-tuple-element.20), channel_id=1, source_target_pairs={{0,24},{8,0},{16,8},{24,16},{1,25},{9,1},{17,9},{25,17},{2,26},{10... | collective-permute-start | bytes 1474568 | tf_op jit(solution)/shard_map/ppermute | solution.py:221
  77.1 2.7 %own.2.refs_0_ = f32[3,5,128,128]{3,2,1,0:T(8,128)S(1)} custom-call(bf16[97,128,128]{2,1,0:T(8,128)(2,1)} %get-tuple-element.13.flat, bf16[8,3,128,384]{3,2,1,0:T(8,128)(2,1)S(1)} %copy-done), custom_call_target="tpu_custom_call" | custom-call | flops 419430400 | bytes 6291456 | tf_op jit(solution)/shard_map/own/pallas_call | solution.py:222
  79.8 2.5 %own.3.refs_3_ = f32[3,5,128,128]{3,2,1,0:T(8,128)S(1)} custom-call(bf16[97,128,128]{2,1,0:T(8,128)(2,1)} %get-tuple-element.17.flat, bf16[8,3,128,384]{3,2,1,0:T(8,128)(2,1)S(1)} %copy-done.1), custom_call_target="tpu_custom_call" | custom-call | flops 419430400 | bytes 6291456 | tf_op jit(solution)/shard_map/own/pallas_call | solution.py:222
  82.3 6.0 %collective-permute-done.16.refs_4_ = bf16[3,5,128,128]{3,2,1,0:T(8,128)(2,1)S(1)} collective-permute-done((bf16[3,5,128,128]{3,2,1,0:T(8,128)(2,1)S(1)}, bf16[3,5,128,128]{3,2,1,0:T(8,128)(2,1)S(1)}, u32[]{:S(2)}, u32[]{:S(2)}) %collective-permute-start.16) | collective-permute-done | bytes 491552 | tf_op jit(solution)/shard_map/ppermute | solution.py:220
  88.4 1.4 %final.1 = bf16[2,1,1,25,128,128]{5,4,3,2,1,0:T(8,128)(2,1)} custom-call(f32[3,5,128,128]{3,2,1,0:T(8,128)S(1)} %own.2.refs_0_, bf16[3,5,128,128]{3,2,1,0:T(8,128)(2,1)S(1)} %collective-permute-done.12.refs_1_, bf16[3,5,128,128]{3,2,1,0:T(8,128)(2,1)S(1)} %collective-permute-done.13.refs_2_, f32[3,5,128,128]{3,2,1,0:T(8,128)S(1)} %own.3.refs_3_, ...), custom_call_target="tpu_custom_call" | custom-call | flops 1048576 | bytes 8388608 | tf_op jit(solution)/shard_map/final/pallas_call | solution.py:232
  (28 shorter events, 0.1 us)
Async XLA Ops:
  1.6 12.2 %collective-permute-start = (s32[2,2,1,6]{3,2,1,0:T(1,128)S(1)}, s32[2,2,1,6]{3,2,1,0:T(1,128)S(1)}, u32[]{:S(2)}, u32[]{:S(2)}) collective-permute-start(s32[2,2,1,6]{3,2,1,0:T(1,128)S(1)} %get-tuple-element.37), channel_id=1, source_target_pairs={{0,1},{1,0},{2,3},{3,2},{4,5},{5,4},{6,7},{7,6},{8,9},{9,8},{10,11... | collective-permute-start | bytes 296 | tf_op jit(solution)/shard_map/ppermute | solution.py:173
  4.6 11.1 %collective-permute-start.1 = (s32[2,2,1,6]{3,2,1,0:T(1,128)S(1)}, s32[2,2,1,6]{3,2,1,0:T(1,128)S(1)}, u32[]{:S(2)}, u32[]{:S(2)}) collective-permute-start(s32[2,2,1,6]{3,2,1,0:T(1,128)S(1)} %get-tuple-element.38), channel_id=1, source_target_pairs={{0,7},{1,2},{2,1},{3,4},{4,3},{5,6},{6,5},{7,0},{8,15},{9,10},{10,... | collective-permute-start | bytes 296 | tf_op jit(solution)/shard_map/ppermute | solution.py:174
  8.1 22.1 %collective-permute-start.4 = (bf16[2,2,4,128,128]{4,3,2,1,0:T(8,128)(2,1)}, bf16[2,2,4,128,128]{4,3,2,1,0:T(8,128)(2,1)S(1)}, u32[]{:S(2)}, u32[]{:S(2)}) collective-permute-start(bf16[2,2,4,128,128]{4,3,2,1,0:T(8,128)(2,1)} %refs_0_.3), channel_id=1, source_target_pairs={{0,1},{1,0},{2,3},{3,2},{4,5},{5,4},{6,7},{7,6},{8,9},{9,8},{10,11... | collective-permute-start | bytes 1572872 | tf_op jit(solution)/shard_map/ppermute | solution.py:172
  10.0 32.1 %collective-permute-start.9 = (bf16[1,2,4,128,128]{4,3,2,1,0:T(8,128)(2,1)}, bf16[1,2,4,128,128]{4,3,2,1,0:T(8,128)(2,1)}, u32[]{:S(2)}, u32[]{:S(2)}) collective-permute-start(bf16[1,2,4,128,128]{4,3,2,1,0:T(8,128)(2,1)} %get-tuple-element.33), channel_id=1, source_target_pairs={{0,24},{8,0},{16,8},{24,16},{1,25},{9,1},{17,9},{25,17},{2,26},{10... | collective-permute-start | bytes 786440 | tf_op jit(solution)/shard_map/ppermute | solution.py:165
  10.4 32.2 %collective-permute-start.6 = (bf16[1,2,4,128,128]{4,3,2,1,0:T(8,128)(2,1)}, bf16[1,2,4,128,128]{4,3,2,1,0:T(8,128)(2,1)}, u32[]{:S(2)}, u32[]{:S(2)}) collective-permute-start(bf16[1,2,4,128,128]{4,3,2,1,0:T(8,128)(2,1)} %get-tuple-element.34), channel_id=1, source_target_pairs={{0,8},{8,16},{16,24},{24,0},{1,9},{9,17},{17,25},{25,1},{2,10},{10... | collective-permute-start | bytes 786440 | tf_op jit(solution)/shard_map/ppermute | solution.py:164
  10.5 5.8 %copy-start.7 = (s32[2,2,2,5]{3,2,1,0:T(2,128)S(1)}, s32[2,2,2,5]{3,2,1,0:T(2,128)}, u32[]{:S(2)}) copy-start(s32[2,2,2,5]{3,2,1,0:T(2,128)} %param.5) | copy-start | bytes 484
  12.9 42.7 %copy-start.2 = (bf16[2,2,2,5,128,128]{5,4,3,2,1,0:T(8,128)(2,1)S(1)}, bf16[2,2,2,5,128,128]{5,4,3,2,1,0:T(8,128)(2,1)}, u32[]{:S(2)}) copy-start(bf16[2,2,2,5,128,128]{5,4,3,2,1,0:T(8,128)(2,1)} %a_own.3) | copy-start | bytes 3932164
  12.9 42.7 %copy-start.3 = (bf16[2,2,4,128,128]{4,3,2,1,0:T(8,128)(2,1)S(1)}, bf16[2,2,4,128,128]{4,3,2,1,0:T(8,128)(2,1)}, u32[]{:S(2)}) copy-start(bf16[2,2,4,128,128]{4,3,2,1,0:T(8,128)(2,1)} %refs_0_.3) | copy-start | bytes 1572868
  13.8 30.0 %collective-permute-start.3 = (bf16[2,1,5,128,128]{4,3,2,1,0:T(8,128)(2,1)}, bf16[2,1,5,128,128]{4,3,2,1,0:T(8,128)(2,1)S(1)}, u32[]{:S(2)}, u32[]{:S(2)}) collective-permute-start(bf16[2,1,5,128,128]{4,3,2,1,0:T(8,128)(2,1)} %get-tuple-element.27), channel_id=1, source_target_pairs={{0,7},{1,2},{2,1},{3,4},{4,3},{5,6},{6,5},{7,0},{8,15},{9,10},{10,... | collective-permute-start | bytes 983048 | tf_op jit(solution)/shard_map/ppermute | solution.py:179
  15.7 28.6 %collective-permute-start.2 = (bf16[2,1,5,128,128]{4,3,2,1,0:T(8,128)(2,1)}, bf16[2,1,5,128,128]{4,3,2,1,0:T(8,128)(2,1)S(1)}, u32[]{:S(2)}, u32[]{:S(2)}) collective-permute-start(bf16[2,1,5,128,128]{4,3,2,1,0:T(8,128)(2,1)} %get-tuple-element.28), channel_id=1, source_target_pairs={{0,1},{1,0},{2,3},{3,2},{4,5},{5,4},{6,7},{7,6},{8,9},{9,8},{10,11... | collective-permute-start | bytes 983048 | tf_op jit(solution)/shard_map/ppermute | solution.py:178
  30.2 11.0 %collective-permute-start.5 = (bf16[2,2,4,128,128]{4,3,2,1,0:T(8,128)(2,1)S(1)}, bf16[2,2,4,128,128]{4,3,2,1,0:T(8,128)(2,1)S(1)}, u32[]{:S(2)}, u32[]{:S(2)}) collective-permute-start(bf16[2,2,4,128,128]{4,3,2,1,0:T(8,128)(2,1)S(1)} %collective-permute-done.4.refs_1_), channel_id=1, source_target_pairs={{0,2},{1,7},{2,4},{3,1},{4,6},{5,3},{6,0},{7,5},{8,10},{9,15},{10,... | collective-permute-start | bytes 1572872 | tf_op jit(solution)/shard_map/ppermute | solution.py:180
  41.2 4.7 %collective-permute-start.10 = (bf16[1,2,4,128,128]{4,3,2,1,0:T(8,128)(2,1)S(1)}, bf16[1,2,4,128,128]{4,3,2,1,0:T(8,128)(2,1)S(1)}, u32[]{:S(2)}, u32[]{:S(2)}) collective-permute-start(bf16[1,2,4,128,128]{4,3,2,1,0:T(8,128)(2,1)S(1)} %get-tuple-element.31), channel_id=1, source_target_pairs={{0,24},{8,0},{16,8},{24,16},{1,25},{9,1},{17,9},{25,17},{2,26},{10... | collective-permute-start | bytes 786440 | tf_op jit(solution)/shard_map/ppermute | solution.py:165
  42.1 8.9 %collective-permute-start.7 = (bf16[1,2,4,128,128]{4,3,2,1,0:T(8,128)(2,1)}, bf16[1,2,4,128,128]{4,3,2,1,0:T(8,128)(2,1)}, u32[]{:S(2)}, u32[]{:S(2)}) collective-permute-start(bf16[1,2,4,128,128]{4,3,2,1,0:T(8,128)(2,1)} %get-tuple-element.32), channel_id=1, source_target_pairs={{0,8},{8,16},{16,24},{24,0},{1,9},{9,17},{17,25},{25,1},{2,10},{10... | collective-permute-start | bytes 786440 | tf_op jit(solution)/shard_map/ppermute | solution.py:164
  42.6 9.0 %collective-permute-start.11 = (bf16[1,2,4,128,128]{4,3,2,1,0:T(8,128)(2,1)}, bf16[1,2,4,128,128]{4,3,2,1,0:T(8,128)(2,1)}, u32[]{:S(2)}, u32[]{:S(2)}) collective-permute-start(bf16[1,2,4,128,128]{4,3,2,1,0:T(8,128)(2,1)} %get-tuple-element.29), channel_id=1, source_target_pairs={{0,24},{8,0},{16,8},{24,16},{1,25},{9,1},{17,9},{25,17},{2,26},{10... | collective-permute-start | bytes 786440 | tf_op jit(solution)/shard_map/ppermute | solution.py:165
  43.8 11.8 %collective-permute-start.8 = (bf16[1,2,4,128,128]{4,3,2,1,0:T(8,128)(2,1)}, bf16[1,2,4,128,128]{4,3,2,1,0:T(8,128)(2,1)}, u32[]{:S(2)}, u32[]{:S(2)}) collective-permute-start(bf16[1,2,4,128,128]{4,3,2,1,0:T(8,128)(2,1)} %get-tuple-element.30), channel_id=1, source_target_pairs={{0,8},{8,16},{16,24},{24,0},{1,9},{9,17},{17,25},{25,1},{2,10},{10... | collective-permute-start | bytes 786440 | tf_op jit(solution)/shard_map/ppermute | solution.py:164
  44.4 22.4 %collective-permute-start.15 = (bf16[2,1,5,128,128]{4,3,2,1,0:T(8,128)(2,1)}, bf16[2,1,5,128,128]{4,3,2,1,0:T(8,128)(2,1)}, u32[]{:S(2)}, u32[]{:S(2)}) collective-permute-start(bf16[2,1,5,128,128]{4,3,2,1,0:T(8,128)(2,1)} %get-tuple-element.25), channel_id=1, source_target_pairs={{0,7},{1,2},{2,1},{3,4},{4,3},{5,6},{6,5},{7,0},{8,15},{9,10},{10,... | collective-permute-start | bytes 983048 | tf_op jit(solution)/shard_map/ppermute | solution.py:179
  45.9 0.7 copy-start.4
  45.9 20.8 %collective-permute-start.14 = (bf16[2,1,5,128,128]{4,3,2,1,0:T(8,128)(2,1)}, bf16[2,1,5,128,128]{4,3,2,1,0:T(8,128)(2,1)}, u32[]{:S(2)}, u32[]{:S(2)}) collective-permute-start(bf16[2,1,5,128,128]{4,3,2,1,0:T(8,128)(2,1)} %get-tuple-element.26), channel_id=1, source_target_pairs={{0,1},{1,0},{2,3},{3,2},{4,5},{5,4},{6,7},{7,6},{8,9},{9,8},{10,11... | collective-permute-start | bytes 983048 | tf_op jit(solution)/shard_map/ppermute | solution.py:178
  55.6 1.0 %copy-start.5 = (bf16[1,2,4,128,128]{4,3,2,1,0:T(8,128)(2,1)S(1)}, bf16[1,2,4,128,128]{4,3,2,1,0:T(8,128)(2,1)}, u32[]{:S(2)}) copy-start(bf16[1,2,4,128,128]{4,3,2,1,0:T(8,128)(2,1)} %copy-done.4) | copy-start | bytes 786436
  56.6 10.1 %copy-start.6 = (bf16[1,2,4,128,128]{4,3,2,1,0:T(8,128)(2,1)S(1)}, bf16[1,2,4,128,128]{4,3,2,1,0:T(8,128)(2,1)}, u32[]{:S(2)}) copy-start(bf16[1,2,4,128,128]{4,3,2,1,0:T(8,128)(2,1)} %copy-done.4) | copy-start | bytes 786436
  64.9 17.4 %collective-permute-start.12 = (bf16[3,5,128,128]{3,2,1,0:T(8,128)(2,1)S(1)}, bf16[3,5,128,128]{3,2,1,0:T(8,128)(2,1)S(1)}, u32[]{:S(2)}, u32[]{:S(2)}) collective-permute-start(bf16[3,5,128,128]{3,2,1,0:T(8,128)(2,1)S(1)} %get-tuple-element.15), channel_id=1, source_target_pairs={{0,8},{8,16},{16,24},{24,0},{1,9},{9,17},{17,25},{25,1},{2,10},{10... | collective-permute-start | bytes 1474568 | tf_op jit(solution)/shard_map/ppermute | solution.py:220
  65.0 12.1 %copy-start = (bf16[8,3,128,384]{3,2,1,0:T(8,128)(2,1)S(1)}, bf16[8,3,128,384]{3,2,1,0:T(8,128)(2,1)}, u32[]{:S(2)}) copy-start(bf16[8,3,128,384]{3,2,1,0:T(8,128)(2,1)} %get-tuple-element.14.w_ref) | copy-start | bytes 7077892
  65.0 17.3 %collective-permute-start.13 = (bf16[3,5,128,128]{3,2,1,0:T(8,128)(2,1)S(1)}, bf16[3,5,128,128]{3,2,1,0:T(8,128)(2,1)S(1)}, u32[]{:S(2)}, u32[]{:S(2)}) collective-permute-start(bf16[3,5,128,128]{3,2,1,0:T(8,128)(2,1)S(1)} %get-tuple-element.16), channel_id=1, source_target_pairs={{0,24},{8,0},{16,8},{24,16},{1,25},{9,1},{17,9},{25,17},{2,26},{10... | collective-permute-start | bytes 1474568 | tf_op jit(solution)/shard_map/ppermute | solution.py:221
  75.3 13.1 %collective-permute-start.16 = (bf16[3,5,128,128]{3,2,1,0:T(8,128)(2,1)S(1)}, bf16[3,5,128,128]{3,2,1,0:T(8,128)(2,1)S(1)}, u32[]{:S(2)}, u32[]{:S(2)}) collective-permute-start(bf16[3,5,128,128]{3,2,1,0:T(8,128)(2,1)S(1)} %get-tuple-element.19), channel_id=1, source_target_pairs={{0,8},{8,16},{16,24},{24,0},{1,9},{9,17},{17,25},{25,1},{2,10},{10... | collective-permute-start | bytes 1474568 | tf_op jit(solution)/shard_map/ppermute | solution.py:220
  75.4 13.0 %collective-permute-start.17 = (bf16[3,5,128,128]{3,2,1,0:T(8,128)(2,1)S(1)}, bf16[3,5,128,128]{3,2,1,0:T(8,128)(2,1)S(1)}, u32[]{:S(2)}, u32[]{:S(2)}) collective-permute-start(bf16[3,5,128,128]{3,2,1,0:T(8,128)(2,1)S(1)} %get-tuple-element.20), channel_id=1, source_target_pairs={{0,24},{8,0},{16,8},{24,16},{1,25},{9,1},{17,9},{25,17},{2,26},{10... | collective-permute-start | bytes 1474568 | tf_op jit(solution)/shard_map/ppermute | solution.py:221
  77.1 2.7 %copy-start.1 = (bf16[8,3,128,384]{3,2,1,0:T(8,128)(2,1)S(1)}, bf16[8,3,128,384]{3,2,1,0:T(8,128)(2,1)}, u32[]{:S(2)}) copy-start(bf16[8,3,128,384]{3,2,1,0:T(8,128)(2,1)} %get-tuple-element.18.w_ref) | copy-start | bytes 7077892

commit v2 on v0

v2 whole, which is shorter than its diff:
```python
import functools

import jax
import jax.numpy as jnp
from jax import lax
from jax.experimental import pallas as pl
from jax.experimental.pallas import tpu as pltpu
from jax.sharding import PartitionSpec as P

FAR, OWN_0, OWN_1, NEAR = range(4)
HALF = 32
ZERO = 2 * HALF
VMEM_LIMIT = 24 * 1024 * 1024


def ring(count, step):
    return [(i, (i + step) % count) for i in range(count)]


def pair(count):
    return [(i, i ^ 1) for i in range(count)]


def outward(count):
    return [(i, (i + (1 if i % 2 else -1)) % count) for i in range(count)]


def onward(count):
    return [(i, (i + (-2 if i % 2 else 2)) % count) for i in range(count)]


def product_table(info, odd):
    slots = info.shape[1] - 1
    shape = (info.shape[0], slots * 9)
    row = lax.broadcasted_iota(jnp.int32, shape, 0)
    place = lax.broadcasted_iota(jnp.int32, shape, 1)
    slot = place // 9
    band = place - 9 * slot
    band_y = band // 3
    band_x = band - 3 * band_y
    fine_x = (row >> 2) & 1
    fine_y = (row & 3) - 1
    off = jnp.zeros(shape, jnp.int32)
    for k in range(slots):
        off = off + jnp.where(slot == k, info[:, k : k + 1], 0)
    off_x = off // 3
    near_x = fine_x + off_x - 1
    near_y = fine_y + (off - 3 * off_x - 1) * (1 - 2 * odd)
    place_x = band_x - (((near_x - 1) >> 1) - (fine_x >> 1) + 1)
    place_y = band_y - (((near_y - 1) >> 1) - (fine_y >> 1) + 1)
    corner_x = jnp.where((near_x & 1) == 1, place_x, 1 - place_x)
    corner_y = jnp.where((near_y & 1) == 1, place_y, 1 - place_y)
    good = (place_x >= 0) & (place_x < 2) & (place_y >= 0) & (place_y < 2)
    good = good & (slot < info[:, slots:])
    side = jnp.where((near_y >> 1) == 0, 0, HALF)
    index = side + (near_x + 1) * 8 + ((near_y & 1) ^ odd) * 4 + 2 * corner_x + corner_y
    return jnp.where(good, index, ZERO)


def fill(flat, sems, first, low, mid, high):
    block = flat.shape[-1]
    copies = []
    for piece, start, rows in ((low, 0, 1), (mid, 8, 2), (high, 24, 1)):
        for x in range(rows):
            for y in range(2):
                copies.append((piece.at[x, y], flat.at[pl.ds(first + start + 8 * x + 4 * y, 4)]))
    return [pltpu.make_async_copy(src, dst, sems.at[first // 4 + i]) for i, (src, dst) in enumerate(copies)]


def fine_row(table, number, flat, blocks, w_ref):
    slots = blocks.shape[0]
    left = jnp.concatenate([blocks[k] for k in range(slots)], axis=1)
    for band_y in range(3):
        right = jnp.concatenate(
            [
                jnp.concatenate(
                    [flat[table[number, k * 9 + band_y * 3 + band_x]] for band_x in range(3)], axis=1
                )
                for k in range(slots)
            ],
            axis=0,
        )
        w_ref[band_y] = jnp.dot(left, right, preferred_element_type=jnp.float32).astype(w_ref.dtype)


def coarse_column(odd, pieces, w_refs, fine_rows, lag_y, corner_x):
    lefts, rights = [], []
    for fine_x in fine_rows:
        for role in range(4):
            fine_y = role - 1
            band_y = lag_y - (fine_y // 2 + 1)
            if 0 <= band_y < 3:
                corner_y = 1 if role in (FAR, NEAR) else 0
                lefts.append(pieces[role][fine_x, (fine_y & 1) ^ odd, corner_x + corner_y])
                rights.append(w_refs[role][fine_x, band_y])
    left = jnp.concatenate(lefts, axis=0)
    right = jnp.concatenate(rights, axis=0)
    return lax.dot_general(left, right, (((0,), (0,)), ((), ())), preferred_element_type=jnp.float32)


def edges(odd, pieces, w_refs, outs):
    block = outs[0].shape[-1]
    for fine_x, out in enumerate(outs):
        for lag_y in range(5):
            total = coarse_column(odd, pieces, w_refs, (fine_x,), lag_y, 2)
            for lag_x in range(3):
                out[lag_x, lag_y] = total[:, lag_x * block : (lag_x + 1) * block].astype(out.dtype)


def near_own_kernel(table, odd_ref, a_own, *refs):
    own, near = refs[:3], refs[3:6]
    flat, w_ref = refs[6:8]
    blocks, sems = refs[8:]
    odd = odd_ref[0]
    operators = a_own.shape[0]
    copies = fill(flat, sems, 0, *own) + fill(flat, sems, HALF, *near)
    copies.append(pltpu.make_async_copy(a_own.at[:, :, 1 - odd], blocks, sems.at[16]))
    for copy in copies:
        copy.start()
    flat[ZERO] = jnp.zeros(flat.shape[1:], flat.dtype)
    for copy in copies:
        copy.wait()

    def one(i, carry):
        s, x = i >> 1, i & 1
        fine_row(table, s * 8 + x * 4 + OWN_1, flat, blocks.at[s, x], w_ref.at[s, x])
        return carry

    lax.fori_loop(0, 2 * operators, one, 0)


def near_kernel(operator, table, flat, a_near, w_ref):
    def one(x, carry):
        fine_row(table, operator * 8 + x * 4 + NEAR, flat, a_near.at[x, 0], w_ref.at[x])
        return carry

    lax.fori_loop(0, 2, one, 0)


def far_first_kernel(table, odd_ref, a_own, a_far, w_own, w_near, p_own, p_near, p_far, *refs):
    own, far = refs[:3], refs[3:6]
    low, high, flat, w_own_0, w_far = refs[6:11]
    blocks, sems = refs[11:]
    odd = odd_ref[0]
    copies = fill(flat, sems, 0, *own) + fill(flat, sems, HALF, *far)
    copies.append(pltpu.make_async_copy(a_own.at[0, :, odd], blocks, sems.at[16]))
    for copy in copies:
        copy.start()
    flat[ZERO] = jnp.zeros(flat.shape[1:], flat.dtype)
    for copy in copies:
        copy.wait()

    def one(x, carry):
        fine_row(table, x * 4 + FAR, flat, a_far.at[x, 0], w_far.at[x])
        fine_row(table, x * 4 + OWN_0, flat, blocks.at[x], w_own_0.at[x])
        return carry

    lax.fori_loop(0, 2, one, 0)
    edges(odd, (p_far, p_own, p_own, p_near), (w_far, w_own_0, w_own.at[0], w_near), (low, high))


def own_0_kernel(operator, table, odd_ref, a_own, flat, w_ref, blocks, sem):
    odd = odd_ref[0]
    copy = pltpu.make_async_copy(a_own.at[operator, :, odd], blocks, sem)
    copy.start()
    copy.wait()

    def one(x, carry):
        fine_row(table, operator * 8 + x * 4 + OWN_0, flat, blocks.at[x], w_ref.at[x])
        return carry

    lax.fori_loop(0, 2, one, 0)


def far_kernel(operator, table, odd_ref, a_far, flat, w_own, w_near, w_own_0, p_own, p_near, p_far, low, high, w_far):
    odd = odd_ref[0]

    def one(x, carry):
        fine_row(table, operator * 8 + x * 4 + FAR, flat, a_far.at[x, 0], w_far.at[x])
        return carry

    lax.fori_loop(0, 2, one, 0)
    edges(odd, (p_far, p_own, p_own, p_near), (w_far, w_own_0, w_own.at[operator], w_near), (low, high))


def centre_kernel(operator, odd_ref, p_own, p_near, p_far, w_far, w_own_0, w_own, w_near, out):
    block = out.shape[-1]
    odd = odd_ref[0]
    for lag_y in range(5):
        total = coarse_column(
            odd, (p_far, p_own, p_own, p_near), (w_far, w_own_0, w_own.at[operator], w_near), (0, 1), lag_y, 0
        )
        for lag_x in range(3):
            out[lag_x, lag_y] = total[:, lag_x * block : (lag_x + 1) * block]


def final_kernel(odd_ref, *refs):
    out = refs[-1]
    odd = odd_ref[0]
    for operator in range(out.shape[0]):
        own, low, high = refs[3 * operator : 3 * operator + 3]
        for lag_x in range(5):
            for lag_y in range(5):
                total = None
                for part, first in ((low, 0), (own, 1), (high, 2)):
                    if 0 <= lag_x - first < 3:
                        term = part[lag_x - first, lag_y].astype(jnp.float32)
                        total = term if total is None else total + term
                place = 5 * lag_x + lag_y + odd * (4 - 2 * lag_y)
                out[operator, 0, 0, place] = total.astype(out.dtype)


def per_device(a_vals, a_off, a_count, p_vals):
    operators, _, _, slots, block, _ = a_vals.shape
    cols = lax.axis_size("col")
    rows = lax.axis_size("row")
    odd = (lax.axis_index("col") & 1).astype(jnp.int32)
    up, down = ring(rows, 1), ring(rows, -1)
    near_way, far_way, on_way = pair(cols), outward(cols), onward(cols)

    def both_rows(piece):
        return lax.ppermute(piece[1:2], "row", up), lax.ppermute(piece[0:1], "row", down)

    def column(array, operator, index):
        zero = jnp.int32(0)
        start = (jnp.int32(operator), zero, index) + (zero,) * (array.ndim - 3)
        return lax.dynamic_slice(array, start, (1, 2, 1) + array.shape[3:])[0]

    p_near = lax.ppermute(p_vals, "col", near_way)
    own_low, own_high = both_rows(p_vals)

    info = jnp.concatenate([a_off, a_count[..., None]], axis=-1)
    info_near = lax.ppermute(lax.dynamic_slice_in_dim(info, 1 - odd, 1, axis=2), "col", near_way)
    info_far = lax.ppermute(lax.dynamic_slice_in_dim(info, odd, 1, axis=2), "col", far_way)
    mirrored = jnp.where(odd == 1, info[:, :, ::-1], info)
    table = product_table(
        jnp.concatenate([info_far, mirrored, info_near], axis=2).reshape(operators * 8, slots + 1), odd
    )

    near_sends = [column(a_vals, s, 1 - odd) for s in range(operators)]
    far_sends = [column(a_vals, s, odd) for s in range(operators)]
    p_near, near_sends, far_sends = lax.optimization_barrier((p_near, near_sends, far_sends))
    p_far = lax.ppermute(p_near, "col", on_way)
    near_low, near_high = both_rows(p_near)
    a_near, a_far = [None] * operators, [None] * operators
    a_near[0] = lax.ppermute(near_sends[0], "col", near_way)
    a_far[0] = lax.ppermute(far_sends[0], "col", far_way)
    p_far, later_near, later_far = lax.optimization_barrier((p_far, near_sends[1:], far_sends[1:]))
    far_low, far_high = both_rows(p_far)
    for s in range(1, operators):
        a_near[s] = lax.ppermute(later_near[s - 1], "col", near_way)
        a_far[s] = lax.ppermute(later_far[s - 1], "col", far_way)

    any_spec = pl.BlockSpec(memory_space=pl.ANY)
    smem = pl.BlockSpec(memory_space=pltpu.SMEM)
    vmem = pl.BlockSpec(memory_space=pltpu.VMEM)
    bf16, f32 = jnp.bfloat16, jnp.float32
    odd_arg = odd[None]
    flat_shape = jax.ShapeDtypeStruct((ZERO + 1, block, block), bf16)
    w_shape = jax.ShapeDtypeStruct((2, 3, block, 3 * block), bf16)
    part_shape = jax.ShapeDtypeStruct((3, 5, block, block), bf16)
    own_pieces = (own_low, p_vals, own_high)

    def call(kernel, in_specs, out_shape, products, scratch=(), name=None):
        single = not isinstance(out_shape, list)
        return pl.pallas_call(
            kernel,
            in_specs=in_specs,
            out_specs=vmem if single else [vmem] * len(out_shape),
            out_shape=out_shape,
            scratch_shapes=list(scratch),
            compiler_params=pltpu.CompilerParams(vmem_limit_bytes=VMEM_LIMIT),
            cost_estimate=pl.CostEstimate(flops=products * 2 * block**3, bytes_accessed=4 << 20, transcendentals=0),
            name=name,
        )

    flat_near, w_own = call(
        near_own_kernel,
        [smem, smem] + [any_spec] * 7,
        [flat_shape, jax.ShapeDtypeStruct((operators,) + w_shape.shape, bf16)],
        360,
        [pltpu.VMEM((operators, 2, slots, block, block), bf16), pltpu.SemaphoreType.DMA((17,))],
        "near_own",
    )(table, odd_arg, a_vals, *own_pieces, near_low, p_near, near_high)

    finals = []
    for s in range(operators):
        w_near = call(functools.partial(near_kernel, s), [smem, vmem, vmem], w_shape, 90, (), "near")(
            table, flat_near, a_near[s]
        )
        if s == 0:
            low, high, flat_far, w_own_0, w_far = call(
                far_first_kernel,
                [smem, smem, any_spec, vmem, vmem, vmem, vmem, vmem, vmem] + [any_spec] * 6,
                [part_shape, part_shape, flat_shape, w_shape, w_shape],
                300,
                [pltpu.VMEM((2, slots, block, block), bf16), pltpu.SemaphoreType.DMA((17,))],
                "far_first",
            )(
                table, odd_arg, a_vals, a_far[s], w_own, w_near, p_vals, p_near, p_far,
                *own_pieces, far_low, p_far, far_high,
            )
        else:
            w_own_0 = call(
                functools.partial(own_0_kernel, s),
                [smem, smem, any_spec, vmem],
                w_shape,
                90,
                [pltpu.VMEM((2, slots, block, block), bf16), pltpu.SemaphoreType.DMA],
                "own_0",
            )(table, odd_arg, a_vals, flat_far)
            low, high, w_far = call(
                functools.partial(far_kernel, s),
                [smem, smem] + [vmem] * 8,
                [part_shape, part_shape, w_shape],
                200,
                (),
                "far",
            )(table, odd_arg, a_far[s], flat_far, w_own, w_near, w_own_0, p_vals, p_near, p_far)
        from_low = lax.ppermute(high, "row", up)
        from_high = lax.ppermute(low, "row", down)
        centre = call(
            functools.partial(centre_kernel, s),
            [smem] + [vmem] * 7,
            jax.ShapeDtypeStruct((3, 5, block, block), f32),
            144,
            (),
            "centre",
        )(odd_arg, p_vals, p_near, p_far, w_far, w_own_0, w_own, w_near)
        finals += [centre, from_low, from_high]
    return call(
        final_kernel,
        [smem] + [vmem] * len(finals),
        jax.ShapeDtypeStruct((operators, 1, 1, 25, block, block), bf16),
        1,
        (),
        "final",
    )(odd_arg, *finals)


def solution(mesh):
    placed = (
        P(None, "row", "col", None, None, None),
        P(None, "row", "col", None),
        P(None, "row", "col"),
        P("row", "col", None, None, None),
    )
    return jax.shard_map(
        per_device,
        mesh=mesh,
        in_specs=placed,
        out_specs=P(None, "row", "col", None, None, None),
        check_vma=False,
    )
```

time: 210 us -> 81.8 us (0.39)
  waiting for transfers between devices: 143 us -> 33.6 us
  matrix products: 22.9 us -> 0 us
  Pallas kernels: 0 us -> 21.2 us
  local copies, waits for them, and re-layouts: 18.9 us -> 5.42 us
  other arithmetic: 10.2 us -> 1.82 us
  starting transfers between devices: 13.4 us -> 18.6 us
    ppermute x8 -> x18, waiting for transfers between devices: 143 us -> 33.6 us  [the longest x1 11.6 us: per_device(): p_far = lax.ppermute(p_near, 'col', on_way)]
    dot_general x13 -> x0, matrix products: 22.9 us -> none  [the longest x2 11.5 us: products_of_rows(): jnp.einsum('xykqj,xykqbc->xykjbc', onehot, picked, preferred_element_type...]
    pallas_call x0 -> x9, Pallas kernels: none -> 21.2 us  [the longest x1 5.84 us: per_device(): call(far_first_kernel, [smem, smem, any_spec, vmem, vmem, vmem, vmem, vme...]
    another operation x12 -> x0, local copies, waits for them, and re-layouts: 5.55 us -> none  [the longest x5 3.94 us: assemble(): jnp.stack([p_window[lag_x + p_margin, lag_y + p_margin, quadrant] for lag...]
    scatter-add x8 -> x0, other arithmetic: 5.38 us -> none  [assemble(): total.at[:, place[0]:place[0] + 3, place[1]:place[1] + 3].add(partial_terms)]
    ppermute x8 -> x18, starting transfers between devices: 13.4 us -> 18.6 us  [the longest x1 5.98 us: per_device(): lax.ppermute(lax.dynamic_slice_in_dim(info, odd, 1, axis=2), 'col', far_way)]
    gather x2 -> x0, local copies, waits for them, and re-layouts: 5.11 us -> none  [products_of_rows(): picked = p_flat[position]]
    squeeze x0 -> x1, local copies, waits for them, and re-layouts: none -> 2.37 us  [column(): return lax.dynamic_slice(array, start, (1, 2, 1) + array.shape[3:])[0]]
  transfers between devices with their start and end apart: 8 -> 18, of which waited for: 8 -> 6; matrix products, arithmetic and copies ran while one was open for 6% -> 7% of each run, Pallas kernels for 0% -> 24%
where the time goes in v2:
time: 81.8 us; the launch traced here: 80.9 us
  waiting for transfers between devices  33.6 us (41%)
  Pallas kernels  21.2 us (26%)
  starting transfers between devices  18.6 us (23%)
  local copies, waits for them, and re-layouts  5.42 us (7%)
  other arithmetic  1.82 us (2%)
    ppermute x1, waiting for transfers between devices, per_device(): p_far = lax.ppermute(p_near, 'col', on_way)  11.6 us
    ppermute x2, waiting for transfers between devices, per_device(): from_low = lax.ppermute(high, 'row', up)  8.96 us
    ppermute x1, starting transfers between devices, per_device(): lax.ppermute(lax.dynamic_slice_in_dim(info, odd, 1, axis=2), 'col', far_way)  5.98 us
    ppermute x1, waiting for transfers between devices, per_device(): p_near = lax.ppermute(p_vals, 'col', near_way)  5.95 us
    pallas_call x1, Pallas kernels, per_device(): call(far_first_kernel, [smem, smem, any_spec, vmem, vmem, vmem, vmem, vme...  5.84 us
    pallas_call x1, Pallas kernels, per_device(): call(near_own_kernel, [smem, smem] + [any_spec] * 7, [flat_shape, jax.Sha...  5.49 us
    ppermute x1, waiting for transfers between devices, per_device(): a_near[s] = lax.ppermute(later_near[s - 1], 'col', near_way)  4.05 us
    pallas_call x2, Pallas kernels, per_device(): call(functools.partial(near_kernel, s), [smem, vmem, vmem], w_shape, 90,...  3.18 us
  transfers between devices with their start and end apart: 18, of which 6 were waited for; matrix products, arithmetic and copies ran while one was open for 7% of the time, Pallas kernels for 24%

profile of v2, /device:TPU:0, one launch (start us, length us, event | category | flops | bytes accessed | tf_op | source)
XLA Modules:
  0.0 80.9 jit_solution(5948133974829813158)
XLA Ops:
  0.0 0.8 copy.6
  0.8 0.8 %fusion.8 = (s32[2,2,1,6]{3,2,1,0:T(1,128)S(1)}, s32[2,2,1,6]{3,2,1,0:T(1,128)S(1)}) fusion(s32[]{:T(128)S(6)} %select_n.76, s32[2,2,2,5]{3,2,1,0:T(2,128)} %param.5, s32[2,2,2,1]{3,2,1,0:T(2,128)S(1)} %copy.6, s32[]{:T(128)S(6)} %select_n.75), kind=kLoop, calls=%fused_computation.46 | loop fusion | flops 48 | bytes 392 | tf_op jit(solution)/shard_map/concatenate | solution.py:232
  1.6 6.0 %collective-permute-start.2 = (s32[2,2,1,6]{3,2,1,0:T(1,128)S(1)}, s32[2,2,1,6]{3,2,1,0:T(1,128)S(1)}, u32[]{:S(2)}, u32[]{:S(2)}) collective-permute-start(s32[2,2,1,6]{3,2,1,0:T(1,128)S(1)} %get-tuple-element.57), channel_id=1, source_target_pairs={{0,7},{1,2},{2,1},{3,4},{4,3},{5,6},{6,5},{7,0},{8,15},{9,10},{10,... | collective-permute-start | bytes 296 | tf_op jit(solution)/shard_map/ppermute | solution.py:234
  7.6 0.0 collective-permute-start.3
  7.6 2.0 %collective-permute-start = (bf16[2,2,4,128,128]{4,3,2,1,0:T(8,128)(2,1)}, bf16[2,2,4,128,128]{4,3,2,1,0:T(8,128)(2,1)S(1)}, u32[]{:S(2)}, u32[]{:S(2)}) collective-permute-start(bf16[2,2,4,128,128]{4,3,2,1,0:T(8,128)(2,1)} %p_own.7), channel_id=1, source_target_pairs={{0,1},{1,0},{2,3},{3,2},{4,5},{5,4},{6,7},{7,6},{8,9},{9,8},{10,11... | collective-permute-start | bytes 1572872 | tf_op jit(solution)/shard_map/ppermute | solution.py:229
  9.6 1.9 %fusion.12 = (bf16[1,2,4,128,128]{4,3,2,1,0:T(8,128)(2,1)}, bf16[1,2,4,128,128]{4,3,2,1,0:T(8,128)(2,1)}) fusion(bf16[2,2,4,128,128]{4,3,2,1,0:T(8,128)(2,1)} %p_own.7), kind=kLoop, calls=%fused_computation.59 | loop fusion | bytes 1048576 | tf_op jit(solution)/shard_map/slice | solution.py:222
  11.5 0.1 collective-permute-start.6
  11.7 0.4 collective-permute-start.5
  12.1 0.8 pad_add_fusion.1
  12.9 2.4 %dynamic-slice_bitcast_fusion = (bf16[2,1,5,128,128]{4,3,2,1,0:T(8,128)(2,1)}, bf16[2,1,5,128,128]{4,3,2,1,0:T(8,128)(2,1)}, bf16[2,1,5,128,128]{4,3,2,1,0:T(8,128)(2,1)}, bf16[2,1,5,128,128]{4,3,2,1,0:T(8,128)(2,1)}) fusion(bf16[2,2,2,5,128,128]{5,4,3,2,1,0:T(8,128)(2,1)} %a_own.5, s32[]{:T(128)S(6)} %select_n.76, s32[]{:T(128)S(6)} %select_n.75), kind=kLoop, calls=%fused_computation | loop fusion | bytes 2621448 | tf_op jit(solution)/shard_map/squeeze | solution.py:227
  15.2 0.1 broadcast_select_fusion
  15.3 5.9 %collective-permute-done.refs_4_.p_near = bf16[2,2,4,128,128]{4,3,2,1,0:T(8,128)(2,1)S(1)} collective-permute-done((bf16[2,2,4,128,128]{4,3,2,1,0:T(8,128)(2,1)}, bf16[2,2,4,128,128]{4,3,2,1,0:T(8,128)(2,1)S(1)}, u32[]{:S(2)}, u32[]{:S(2)}) %collective-permute-start) | collective-permute-done | bytes 524320 | tf_op jit(solution)/shard_map/ppermute | solution.py:229
  21.3 0.0 copy-start.2
  21.3 0.0 collective-permute-done.2
  21.3 0.0 collective-permute-done.3
  21.4 0.1 collective-permute-start.8
  21.4 0.3 slice_reduce_fusion.5
  21.7 2.2 %collective-permute-start.9 = (bf16[2,1,5,128,128]{4,3,2,1,0:T(8,128)(2,1)}, bf16[2,1,5,128,128]{4,3,2,1,0:T(8,128)(2,1)S(1)}, u32[]{:S(2)}, u32[]{:S(2)}) collective-permute-start(bf16[2,1,5,128,128]{4,3,2,1,0:T(8,128)(2,1)} %get-tuple-element.30), channel_id=1, source_target_pairs={{0,1},{1,0},{2,3},{3,2},{4,5},{5,4},{6,7},{7,6},{8,9},{9,8},{10,11... | collective-permute-start | bytes 983048 | tf_op jit(solution)/shard_map/ppermute | solution.py:246
  23.9 11.6 %collective-permute-done.1.p_far.refs_4_ = bf16[2,2,4,128,128]{4,3,2,1,0:T(8,128)(2,1)S(1)} collective-permute-done((bf16[2,2,4,128,128]{4,3,2,1,0:T(8,128)(2,1)S(1)}, bf16[2,2,4,128,128]{4,3,2,1,0:T(8,128)(2,1)S(1)}, u32[]{:S(2)}, u32[]{:S(2)}) %collective-permute-start.1) | collective-permute-done | bytes 524320 | tf_op jit(solution)/shard_map/ppermute | solution.py:243
  35.6 0.0 collective-permute-done.6.refs_2_
  35.6 1.4 %collective-permute-start.4 = (bf16[2,1,5,128,128]{4,3,2,1,0:T(8,128)(2,1)}, bf16[2,1,5,128,128]{4,3,2,1,0:T(8,128)(2,1)S(1)}, u32[]{:S(2)}, u32[]{:S(2)}) collective-permute-start(bf16[2,1,5,128,128]{4,3,2,1,0:T(8,128)(2,1)} %get-tuple-element.27), channel_id=1, source_target_pairs={{0,7},{1,2},{2,1},{3,4},{4,3},{5,6},{6,5},{7,0},{8,15},{9,10},{10,... | collective-permute-start | bytes 983048 | tf_op jit(solution)/shard_map/ppermute | solution.py:247
  37.0 0.0 collective-permute-done.5.refs_0_
  37.0 1.5 %collective-permute-start.11 = (bf16[1,2,4,128,128]{4,3,2,1,0:T(8,128)(2,1)S(1)}, bf16[1,2,4,128,128]{4,3,2,1,0:T(8,128)(2,1)S(1)}, u32[]{:S(2)}, u32[]{:S(2)}) collective-permute-start(bf16[1,2,4,128,128]{4,3,2,1,0:T(8,128)(2,1)S(1)} %get-tuple-element.51), channel_id=1, source_target_pairs={{0,24},{8,0},{16,8},{24,16},{1,25},{9,1},{17,9},{25,17},{2,26},{10... | collective-permute-start | bytes 786440 | tf_op jit(solution)/shard_map/ppermute | solution.py:222
  38.5 0.0 collective-permute-done.8.refs_5_
  38.5 0.0 collective-permute-start.10
  38.5 0.1 fusion.3.table
  38.6 2.8 %collective-permute-done.7.refs_3_ = bf16[1,2,4,128,128]{4,3,2,1,0:T(8,128)(2,1)S(1)} collective-permute-done((bf16[1,2,4,128,128]{4,3,2,1,0:T(8,128)(2,1)S(1)}, bf16[1,2,4,128,128]{4,3,2,1,0:T(8,128)(2,1)S(1)}, u32[]{:S(2)}, u32[]{:S(2)}) %collective-permute-start.7) | collective-permute-done | bytes 262176 | tf_op jit(solution)/shard_map/ppermute | solution.py:222
  41.4 1.3 %collective-permute-start.14 = (bf16[2,1,5,128,128]{4,3,2,1,0:T(8,128)(2,1)S(1)}, bf16[2,1,5,128,128]{4,3,2,1,0:T(8,128)(2,1)S(1)}, u32[]{:S(2)}, u32[]{:S(2)}) collective-permute-start(bf16[2,1,5,128,128]{4,3,2,1,0:T(8,128)(2,1)S(1)} %copy-done.2), channel_id=1, source_target_pairs={{0,7},{1,2},{2,1},{3,4},{4,3},{5,6},{6,5},{7,0},{8,15},{9,10},{10,... | collective-permute-start | bytes 983048 | tf_op jit(solution)/shard_map/ppermute | solution.py:252
  42.7 5.5 %near_own.1 = (bf16[65,128,128]{2,1,0:T(8,128)(2,1)S(1)}, bf16[2,2,3,128,384]{4,3,2,1,0:T(8,128)(2,1)S(1)}) custom-call(s32[16,45]{1,0:T(8,128)S(1)} %fusion.3.table, s32[1]{0:T(128)} %bitcast.odd_ref, bf16[2,2,2,5,128,128]{5,4,3,2,1,0:T(8,128)(2,1)S(1)} %copy-done.1, bf16[1,2,4,128,128]{4,3,2,1,0:T(8,128)(2,1)S(1)} %collective-permute-done.5.refs_0_, ...), custom_call_target="tpu_custom_call" | custom-call | flops 1509949440 | bytes 4194304 | tf_op jit(solution)/shard_map/near_own/pallas_call | solution.py:277
  48.2 1.6 %near.2.w_near = bf16[2,3,128,384]{3,2,1,0:T(8,128)(2,1)S(1)} custom-call(s32[16,45]{1,0:T(8,128)S(1)} %fusion.3.table, bf16[65,128,128]{2,1,0:T(8,128)(2,1)S(1)} %get-tuple-element.29.flat, bf16[2,1,5,128,128]{4,3,2,1,0:T(8,128)(2,1)S(1)} %collective-permute-done.9.a_near), custom_call_target="tpu_custom_call" | custom-call | flops 377487360 | bytes 4194304 | tf_op jit(solution)/shard_map/near/pallas_call | solution.py:288
  49.8 0.0 collective-permute-done.11.refs_5_
  49.8 0.0 collective-permute-done.10.refs_3_
  49.8 5.8 %far_first.1 = (bf16[3,5,128,128]{3,2,1,0:T(8,128)(2,1)S(1)}, bf16[3,5,128,128]{3,2,1,0:T(8,128)(2,1)S(1)}, bf16[65,128,128]{2,1,0:T(8,128)(2,1)S(1)}, bf16[2,3,...) custom-call(s32[16,45]{1,0:T(8,128)S(1)} %fusion.3.table, s32[1]{0:T(128)} %bitcast.odd_ref, ...), custom_call_target="tpu_custom_call" | custom-call | flops 1258291200 | bytes 4194304 | tf_op jit(solution)/shard_map/far_first/pallas_call | solution.py:292
  55.7 0.8 collective-permute-start.12
  56.5 1.0 %collective-permute-start.13 = (bf16[3,5,128,128]{3,2,1,0:T(8,128)(2,1)S(1)}, bf16[3,5,128,128]{3,2,1,0:T(8,128)(2,1)S(1)}, u32[]{:S(2)}, u32[]{:S(2)}) collective-permute-start(bf16[3,5,128,128]{3,2,1,0:T(8,128)(2,1)S(1)} %get-tuple-element.34), channel_id=1, source_target_pairs={{0,24},{8,0},{16,8},{24,16},{1,25},{9,1},{17,9},{25,17},{2,26},{10... | collective-permute-start | bytes 1474568 | tf_op jit(solution)/shard_map/ppermute | solution.py:321
  57.5 1.7 %own_0.1.w_own_0 = bf16[2,3,128,384]{3,2,1,0:T(8,128)(2,1)S(1)} custom-call(s32[16,45]{1,0:T(8,128)S(1)} %fusion.3.table, s32[1]{0:T(128)} %bitcast.odd_ref, bf16[2,2,2,5,128,128]{5,4,3,2,1,0:T(8,128)(2,1)S(1)} %copy-done.1, bf16[65,128,128]{2,1,0:T(8,128)(2,1)S(1)} %get-tuple-element.36.flat), custom_call_target="tpu_custom_call" | custom-call | flops 377487360 | bytes 4194304 | tf_op jit(solution)/shard_map/own_0/pallas_call | solution.py:304
  59.2 4.1 %collective-permute-done.15.a_near = bf16[2,1,5,128,128]{4,3,2,1,0:T(8,128)(2,1)S(1)} collective-permute-done((bf16[2,1,5,128,128]{4,3,2,1,0:T(8,128)(2,1)}, bf16[2,1,5,128,128]{4,3,2,1,0:T(8,128)(2,1)S(1)}, u32[]{:S(2)}, u32[]{:S(2)}) %collective-permute-start.15) | collective-permute-done | bytes 327712 | tf_op jit(solution)/shard_map/ppermute | solution.py:251
  63.2 1.6 %near.3.w_near = bf16[2,3,128,384]{3,2,1,0:T(8,128)(2,1)S(1)} custom-call(s32[16,45]{1,0:T(8,128)S(1)} %fusion.3.table, bf16[65,128,128]{2,1,0:T(8,128)(2,1)S(1)} %get-tuple-element.29.flat, bf16[2,1,5,128,128]{4,3,2,1,0:T(8,128)(2,1)S(1)} %collective-permute-done.15.a_near), custom_call_target="tpu_custom_call" | custom-call | flops 377487360 | bytes 4194304 | tf_op jit(solution)/shard_map/near/pallas_call | solution.py:288
  64.8 0.0 collective-permute-done.14.a_far
  64.8 2.3 %far.1 = (bf16[3,5,128,128]{3,2,1,0:T(8,128)(2,1)S(1)}, bf16[3,5,128,128]{3,2,1,0:T(8,128)(2,1)S(1)}, bf16[2,3,128,384]{3,2,1,0:T(8,128)(2,1)S(1)}) custom-call(s32[16,45]{1,0:T(8,128)S(1)} %fusion.3.table, s32[1]{0:T(128)} %bitcast.odd_ref, bf16[2,1,5,128,128]{4,3,2,1,0:T(8,128)(2,1)S(1)} %collective-permute-done.14.a_far, ...), custom_call_target="tpu_custom_call" | custom-call | flops 838860800 | bytes 4194304 | tf_op jit(solution)/shard_map/far/pallas_call | solution.py:312
  67.1 0.1 collective-permute-start.16
  67.2 1.7 %collective-permute-start.17 = (bf16[3,5,128,128]{3,2,1,0:T(8,128)(2,1)S(1)}, bf16[3,5,128,128]{3,2,1,0:T(8,128)(2,1)S(1)}, u32[]{:S(2)}, u32[]{:S(2)}) collective-permute-start(bf16[3,5,128,128]{3,2,1,0:T(8,128)(2,1)S(1)} %get-tuple-element.40), channel_id=1, source_target_pairs={{0,24},{8,0},{16,8},{24,16},{1,25},{9,1},{17,9},{25,17},{2,26},{10... | collective-permute-start | bytes 1474568 | tf_op jit(solution)/shard_map/ppermute | solution.py:321
  68.9 0.6 centre.2.refs_0_
  69.5 0.6 centre.3.refs_3_
  70.2 0.0 collective-permute-done.13.refs_2_
  70.2 9.0 %collective-permute-done.16.refs_4_ = bf16[3,5,128,128]{3,2,1,0:T(8,128)(2,1)S(1)} collective-permute-done((bf16[3,5,128,128]{3,2,1,0:T(8,128)(2,1)S(1)}, bf16[3,5,128,128]{3,2,1,0:T(8,128)(2,1)S(1)}, u32[]{:S(2)}, u32[]{:S(2)}) %collective-permute-start.16) | collective-permute-done | bytes 491552 | tf_op jit(solution)/shard_map/ppermute | solution.py:320
  79.1 0.2 collective-permute-done.17.refs_5_
  79.4 1.5 %final.1 = bf16[2,1,1,25,128,128]{5,4,3,2,1,0:T(8,128)(2,1)} custom-call(s32[1]{0:T(128)} %bitcast.odd_ref, f32[3,5,128,128]{3,2,1,0:T(8,128)S(1)} %centre.2.refs_0_, bf16[3,5,128,128]{3,2,1,0:T(8,128)(2,1)S(1)} %collective-permute-done.12.refs_1_, bf16[3,5,128,128]{3,2,1,0:T(8,128)(2,1)S(1)} %collective-permute-done.13.refs_2_, ...), custom_call_target="tpu_custom_call" | custom-call | flops 4194304 | bytes 4194304 | tf_op jit(solution)/shard_map/final/pallas_call | solution.py:331
  (21 shorter events, 0.2 us)
Async XLA Ops:
  1.6 19.7 %collective-permute-start.2 = (s32[2,2,1,6]{3,2,1,0:T(1,128)S(1)}, s32[2,2,1,6]{3,2,1,0:T(1,128)S(1)}, u32[]{:S(2)}, u32[]{:S(2)}) collective-permute-start(s32[2,2,1,6]{3,2,1,0:T(1,128)S(1)} %get-tuple-element.57), channel_id=1, source_target_pairs={{0,7},{1,2},{2,1},{3,4},{4,3},{5,6},{6,5},{7,0},{8,15},{9,10},{10,... | collective-permute-start | bytes 296 | tf_op jit(solution)/shard_map/ppermute | solution.py:234
  7.6 7.6 %copy-start.3 = (s32[2,2,2,5]{3,2,1,0:T(2,128)S(1)}, s32[2,2,2,5]{3,2,1,0:T(2,128)}, u32[]{:S(2)}) copy-start(s32[2,2,2,5]{3,2,1,0:T(2,128)} %param.5) | copy-start | bytes 484
  7.6 13.7 %collective-permute-start.3 = (s32[2,2,1,6]{3,2,1,0:T(1,128)S(1)}, s32[2,2,1,6]{3,2,1,0:T(1,128)S(1)}, u32[]{:S(2)}, u32[]{:S(2)}) collective-permute-start(s32[2,2,1,6]{3,2,1,0:T(1,128)S(1)} %get-tuple-element.58), channel_id=1, source_target_pairs={{0,1},{1,0},{2,3},{3,2},{4,5},{5,4},{6,7},{7,6},{8,9},{9,8},{10,11... | collective-permute-start | bytes 296 | tf_op jit(solution)/shard_map/ppermute | solution.py:233
  7.6 13.6 %collective-permute-start = (bf16[2,2,4,128,128]{4,3,2,1,0:T(8,128)(2,1)}, bf16[2,2,4,128,128]{4,3,2,1,0:T(8,128)(2,1)S(1)}, u32[]{:S(2)}, u32[]{:S(2)}) collective-permute-start(bf16[2,2,4,128,128]{4,3,2,1,0:T(8,128)(2,1)} %p_own.7), channel_id=1, source_target_pairs={{0,1},{1,0},{2,3},{3,2},{4,5},{5,4},{6,7},{7,6},{8,9},{9,8},{10,11... | collective-permute-start | bytes 1572872 | tf_op jit(solution)/shard_map/ppermute | solution.py:229
  11.5 24.1 %collective-permute-start.6 = (bf16[1,2,4,128,128]{4,3,2,1,0:T(8,128)(2,1)}, bf16[1,2,4,128,128]{4,3,2,1,0:T(8,128)(2,1)S(1)}, u32[]{:S(2)}, u32[]{:S(2)}) collective-permute-start(bf16[1,2,4,128,128]{4,3,2,1,0:T(8,128)(2,1)} %get-tuple-element.55), channel_id=1, source_target_pairs={{0,24},{8,0},{16,8},{24,16},{1,25},{9,1},{17,9},{25,17},{2,26},{10... | collective-permute-start | bytes 786440 | tf_op jit(solution)/shard_map/ppermute | solution.py:222
  11.7 25.4 %collective-permute-start.5 = (bf16[1,2,4,128,128]{4,3,2,1,0:T(8,128)(2,1)}, bf16[1,2,4,128,128]{4,3,2,1,0:T(8,128)(2,1)S(1)}, u32[]{:S(2)}, u32[]{:S(2)}) collective-permute-start(bf16[1,2,4,128,128]{4,3,2,1,0:T(8,128)(2,1)} %get-tuple-element.56), channel_id=1, source_target_pairs={{0,8},{8,16},{16,24},{24,0},{1,9},{9,17},{17,25},{25,1},{2,10},{10... | collective-permute-start | bytes 786440 | tf_op jit(solution)/shard_map/ppermute | solution.py:222
  15.2 27.5 %copy-start = (bf16[2,2,4,128,128]{4,3,2,1,0:T(8,128)(2,1)S(1)}, bf16[2,2,4,128,128]{4,3,2,1,0:T(8,128)(2,1)}, u32[]{:S(2)}) copy-start(bf16[2,2,4,128,128]{4,3,2,1,0:T(8,128)(2,1)} %p_own.7) | copy-start | bytes 1572868
  15.2 27.5 %copy-start.1 = (bf16[2,2,2,5,128,128]{5,4,3,2,1,0:T(8,128)(2,1)S(1)}, bf16[2,2,2,5,128,128]{5,4,3,2,1,0:T(8,128)(2,1)}, u32[]{:S(2)}) copy-start(bf16[2,2,2,5,128,128]{5,4,3,2,1,0:T(8,128)(2,1)} %a_own.5) | copy-start | bytes 3932164
  21.3 14.3 %collective-permute-start.1 = (bf16[2,2,4,128,128]{4,3,2,1,0:T(8,128)(2,1)S(1)}, bf16[2,2,4,128,128]{4,3,2,1,0:T(8,128)(2,1)S(1)}, u32[]{:S(2)}, u32[]{:S(2)}) collective-permute-start(bf16[2,2,4,128,128]{4,3,2,1,0:T(8,128)(2,1)S(1)} %collective-permute-done.refs_4_.p_near), channel_id=1, source_target_pairs={{0,2},{1,7},{2,4},{3,1},{4,6},{5,3},{6,0},{7,5},{8,10},{9,15},{10,... | collective-permute-start | bytes 1572872 | tf_op jit(solution)/shard_map/ppermute | solution.py:243
  21.3 20.1 %copy-start.2 = (bf16[2,1,5,128,128]{4,3,2,1,0:T(8,128)(2,1)S(1)}, bf16[2,1,5,128,128]{4,3,2,1,0:T(8,128)(2,1)}, u32[]{:S(2)}) copy-start(bf16[2,1,5,128,128]{4,3,2,1,0:T(8,128)(2,1)} %get-tuple-element.35) | copy-start | bytes 983044
  21.4 17.1 %collective-permute-start.8 = (bf16[1,2,4,128,128]{4,3,2,1,0:T(8,128)(2,1)S(1)}, bf16[1,2,4,128,128]{4,3,2,1,0:T(8,128)(2,1)S(1)}, u32[]{:S(2)}, u32[]{:S(2)}) collective-permute-start(bf16[1,2,4,128,128]{4,3,2,1,0:T(8,128)(2,1)S(1)} %get-tuple-element.53), channel_id=1, source_target_pairs={{0,24},{8,0},{16,8},{24,16},{1,25},{9,1},{17,9},{25,17},{2,26},{10... | collective-permute-start | bytes 786440 | tf_op jit(solution)/shard_map/ppermute | solution.py:222
  21.7 21.0 %collective-permute-start.9 = (bf16[2,1,5,128,128]{4,3,2,1,0:T(8,128)(2,1)}, bf16[2,1,5,128,128]{4,3,2,1,0:T(8,128)(2,1)S(1)}, u32[]{:S(2)}, u32[]{:S(2)}) collective-permute-start(bf16[2,1,5,128,128]{4,3,2,1,0:T(8,128)(2,1)} %get-tuple-element.30), channel_id=1, source_target_pairs={{0,1},{1,0},{2,3},{3,2},{4,5},{5,4},{6,7},{7,6},{8,9},{9,8},{10,11... | collective-permute-start | bytes 983048 | tf_op jit(solution)/shard_map/ppermute | solution.py:246
  35.6 5.8 %collective-permute-start.7 = (bf16[1,2,4,128,128]{4,3,2,1,0:T(8,128)(2,1)S(1)}, bf16[1,2,4,128,128]{4,3,2,1,0:T(8,128)(2,1)S(1)}, u32[]{:S(2)}, u32[]{:S(2)}) collective-permute-start(bf16[1,2,4,128,128]{4,3,2,1,0:T(8,128)(2,1)S(1)} %get-tuple-element.54), channel_id=1, source_target_pairs={{0,8},{8,16},{16,24},{24,0},{1,9},{9,17},{17,25},{25,1},{2,10},{10... | collective-permute-start | bytes 786440 | tf_op jit(solution)/shard_map/ppermute | solution.py:222
  35.6 14.2 %collective-permute-start.4 = (bf16[2,1,5,128,128]{4,3,2,1,0:T(8,128)(2,1)}, bf16[2,1,5,128,128]{4,3,2,1,0:T(8,128)(2,1)S(1)}, u32[]{:S(2)}, u32[]{:S(2)}) collective-permute-start(bf16[2,1,5,128,128]{4,3,2,1,0:T(8,128)(2,1)} %get-tuple-element.27), channel_id=1, source_target_pairs={{0,7},{1,2},{2,1},{3,4},{4,3},{5,6},{6,5},{7,0},{8,15},{9,10},{10,... | collective-permute-start | bytes 983048 | tf_op jit(solution)/shard_map/ppermute | solution.py:247
  37.0 12.8 %collective-permute-start.11 = (bf16[1,2,4,128,128]{4,3,2,1,0:T(8,128)(2,1)S(1)}, bf16[1,2,4,128,128]{4,3,2,1,0:T(8,128)(2,1)S(1)}, u32[]{:S(2)}, u32[]{:S(2)}) collective-permute-start(bf16[1,2,4,128,128]{4,3,2,1,0:T(8,128)(2,1)S(1)} %get-tuple-element.51), channel_id=1, source_target_pairs={{0,24},{8,0},{16,8},{24,16},{1,25},{9,1},{17,9},{25,17},{2,26},{10... | collective-permute-start | bytes 786440 | tf_op jit(solution)/shard_map/ppermute | solution.py:222
  38.5 11.4 %collective-permute-start.10 = (bf16[1,2,4,128,128]{4,3,2,1,0:T(8,128)(2,1)S(1)}, bf16[1,2,4,128,128]{4,3,2,1,0:T(8,128)(2,1)S(1)}, u32[]{:S(2)}, u32[]{:S(2)}) collective-permute-start(bf16[1,2,4,128,128]{4,3,2,1,0:T(8,128)(2,1)S(1)} %get-tuple-element.52), channel_id=1, source_target_pairs={{0,8},{8,16},{16,24},{24,0},{1,9},{9,17},{17,25},{25,1},{2,10},{10... | collective-permute-start | bytes 786440 | tf_op jit(solution)/shard_map/ppermute | solution.py:222
  41.4 23.4 %collective-permute-start.14 = (bf16[2,1,5,128,128]{4,3,2,1,0:T(8,128)(2,1)S(1)}, bf16[2,1,5,128,128]{4,3,2,1,0:T(8,128)(2,1)S(1)}, u32[]{:S(2)}, u32[]{:S(2)}) collective-permute-start(bf16[2,1,5,128,128]{4,3,2,1,0:T(8,128)(2,1)S(1)} %copy-done.2), channel_id=1, source_target_pairs={{0,7},{1,2},{2,1},{3,4},{4,3},{5,6},{6,5},{7,0},{8,15},{9,10},{10,... | collective-permute-start | bytes 983048 | tf_op jit(solution)/shard_map/ppermute | solution.py:252
  42.7 20.5 %collective-permute-start.15 = (bf16[2,1,5,128,128]{4,3,2,1,0:T(8,128)(2,1)}, bf16[2,1,5,128,128]{4,3,2,1,0:T(8,128)(2,1)S(1)}, u32[]{:S(2)}, u32[]{:S(2)}) collective-permute-start(bf16[2,1,5,128,128]{4,3,2,1,0:T(8,128)(2,1)} %get-tuple-element.37), channel_id=1, source_target_pairs={{0,1},{1,0},{2,3},{3,2},{4,5},{5,4},{6,7},{7,6},{8,9},{9,8},{10,11... | collective-permute-start | bytes 983048 | tf_op jit(solution)/shard_map/ppermute | solution.py:251
  55.7 14.5 %collective-permute-start.12 = (bf16[3,5,128,128]{3,2,1,0:T(8,128)(2,1)S(1)}, bf16[3,5,128,128]{3,2,1,0:T(8,128)(2,1)S(1)}, u32[]{:S(2)}, u32[]{:S(2)}) collective-permute-start(bf16[3,5,128,128]{3,2,1,0:T(8,128)(2,1)S(1)} %get-tuple-element.33), channel_id=1, source_target_pairs={{0,8},{8,16},{16,24},{24,0},{1,9},{9,17},{17,25},{25,1},{2,10},{10... | collective-permute-start | bytes 1474568 | tf_op jit(solution)/shard_map/ppermute | solution.py:320
  56.5 13.7 %collective-permute-start.13 = (bf16[3,5,128,128]{3,2,1,0:T(8,128)(2,1)S(1)}, bf16[3,5,128,128]{3,2,1,0:T(8,128)(2,1)S(1)}, u32[]{:S(2)}, u32[]{:S(2)}) collective-permute-start(bf16[3,5,128,128]{3,2,1,0:T(8,128)(2,1)S(1)} %get-tuple-element.34), channel_id=1, source_target_pairs={{0,24},{8,0},{16,8},{24,16},{1,25},{9,1},{17,9},{25,17},{2,26},{10... | collective-permute-start | bytes 1474568 | tf_op jit(solution)/shard_map/ppermute | solution.py:321
  67.1 12.0 %collective-permute-start.16 = (bf16[3,5,128,128]{3,2,1,0:T(8,128)(2,1)S(1)}, bf16[3,5,128,128]{3,2,1,0:T(8,128)(2,1)S(1)}, u32[]{:S(2)}, u32[]{:S(2)}) collective-permute-start(bf16[3,5,128,128]{3,2,1,0:T(8,128)(2,1)S(1)} %get-tuple-element.39), channel_id=1, source_target_pairs={{0,8},{8,16},{16,24},{24,0},{1,9},{9,17},{17,25},{25,1},{2,10},{10... | collective-permute-start | bytes 1474568 | tf_op jit(solution)/shard_map/ppermute | solution.py:320
  67.2 12.1 %collective-permute-start.17 = (bf16[3,5,128,128]{3,2,1,0:T(8,128)(2,1)S(1)}, bf16[3,5,128,128]{3,2,1,0:T(8,128)(2,1)S(1)}, u32[]{:S(2)}, u32[]{:S(2)}) collective-permute-start(bf16[3,5,128,128]{3,2,1,0:T(8,128)(2,1)S(1)} %get-tuple-element.40), channel_id=1, source_target_pairs={{0,24},{8,0},{16,8},{24,16},{1,25},{9,1},{17,9},{25,17},{2,26},{10... | collective-permute-start | bytes 1474568 | tf_op jit(solution)/shard_map/ppermute | solution.py:321

commit v3 on v2

v3 whole, which is shorter than its diff:
```python
import functools

import jax
import jax.numpy as jnp
from jax import lax
from jax.experimental import pallas as pl
from jax.experimental.pallas import tpu as pltpu
from jax.sharding import PartitionSpec as P

FAR, OWN_0, OWN_1, NEAR = range(4)
HALF = 32
ZERO = 3 * HALF
VMEM_LIMIT = 24 * 1024 * 1024


def ring(count, step):
    return [(i, (i + step) % count) for i in range(count)]


def pair(count):
    return [(i, i ^ 1) for i in range(count)]


def outward(count):
    return [(i, (i + (1 if i % 2 else -1)) % count) for i in range(count)]


def onward(count):
    return [(i, (i + (-2 if i % 2 else 2)) % count) for i in range(count)]


def product_table(info, odd):
    slots = info.shape[1] - 1
    shape = (info.shape[0], slots * 9)
    row = lax.broadcasted_iota(jnp.int32, shape, 0)
    place = lax.broadcasted_iota(jnp.int32, shape, 1)
    slot = place // 9
    band = place - 9 * slot
    band_y = band // 3
    band_x = band - 3 * band_y
    fine_x = (row >> 2) & 1
    fine_y = (row & 3) - 1
    off = jnp.zeros(shape, jnp.int32)
    for k in range(slots):
        off = off + jnp.where(slot == k, info[:, k : k + 1], 0)
    off_x = off // 3
    near_x = fine_x + off_x - 1
    near_y = fine_y + (off - 3 * off_x - 1) * (1 - 2 * odd)
    place_x = band_x - (((near_x - 1) >> 1) - (fine_x >> 1) + 1)
    place_y = band_y - (((near_y - 1) >> 1) - (fine_y >> 1) + 1)
    corner_x = jnp.where((near_x & 1) == 1, place_x, 1 - place_x)
    corner_y = jnp.where((near_y & 1) == 1, place_y, 1 - place_y)
    good = (place_x >= 0) & (place_x < 2) & (place_y >= 0) & (place_y < 2)
    good = good & (slot < info[:, slots:])
    side = jnp.where(near_y < 0, 2 * HALF, jnp.where(near_y < 2, 0, HALF))
    index = side + (near_x + 1) * 8 + ((near_y & 1) ^ odd) * 4 + 2 * corner_x + corner_y
    return jnp.where(good, index, ZERO)


def fill(flat, first, low, mid, high):
    for piece, start in ((low, 0), (mid, 8), (high, 24)):
        for x in range(piece.shape[0]):
            for y in range(2):
                flat[pl.ds(first + start + 8 * x + 4 * y, 4)] = piece[x, y]


def pack_kernel(odd_ref, a_own, info, *refs):
    sems = refs[-1]
    operators = a_own.shape[0]
    odd = odd_ref[0]
    info_near, info_far = refs[2 * operators : 2 * operators + 2]
    copies = []
    for s in range(operators):
        copies.append((a_own.at[s, :, pl.ds(1 - odd, 1)], refs[s]))
        copies.append((a_own.at[s, :, pl.ds(odd, 1)], refs[operators + s]))
    copies = [pltpu.make_async_copy(src, dst, sems.at[i]) for i, (src, dst) in enumerate(copies)]
    for copy in copies:
        copy.start()
    info_near[...] = info[:, :, pl.ds(1 - odd, 1)]
    info_far[...] = info[:, :, pl.ds(odd, 1)]
    for copy in copies:
        copy.wait()


def rows_kernel(own, near, low, high):
    for out, x in ((low, 0), (high, 1)):
        out[0, 0:2] = own[x]
        out[0, 2:4] = near[x]


def fine_row(table, number, flat, blocks, w_ref):
    slots = blocks.shape[0]
    left = jnp.concatenate([blocks[k] for k in range(slots)], axis=1)
    for band_y in range(3):
        right = jnp.concatenate(
            [
                jnp.concatenate(
                    [flat[table[number, k * 9 + band_y * 3 + band_x]] for band_x in range(3)], axis=1
                )
                for k in range(slots)
            ],
            axis=0,
        )
        w_ref[band_y] = jnp.dot(left, right, preferred_element_type=jnp.float32).astype(w_ref.dtype)


def coarse_column(odd, pieces, w_refs, fine_rows, lag_y, corner_x):
    lefts, rights = [], []
    for fine_x in fine_rows:
        for role in range(4):
            fine_y = role - 1
            band_y = lag_y - (fine_y // 2 + 1)
            if 0 <= band_y < 3:
                corner_y = 1 if role in (FAR, NEAR) else 0
                lefts.append(pieces[role][fine_x, (fine_y & 1) ^ odd, corner_x + corner_y])
                rights.append(w_refs[role][fine_x, band_y])
    left = jnp.concatenate(lefts, axis=0)
    right = jnp.concatenate(rights, axis=0)
    return lax.dot_general(left, right, (((0,), (0,)), ((), ())), preferred_element_type=jnp.float32)


def edges(odd, pieces, w_refs, outs):
    block = outs[0].shape[-1]
    for fine_x, out in enumerate(outs):
        for lag_y in range(5):
            total = coarse_column(odd, pieces, w_refs, (fine_x,), lag_y, 2)
            for lag_x in range(3):
                out[lag_x, lag_y] = total[:, lag_x * block : (lag_x + 1) * block].astype(out.dtype)


def near_own_kernel(table, odd_ref, a_own, p_own, p_near, low, high, flat, w_ref):
    odd = odd_ref[0]
    fill(flat, 0, low.at[:, 0:2], p_own, high.at[:, 0:2])
    fill(flat, HALF, low.at[:, 2:4], p_near, high.at[:, 2:4])
    flat[ZERO] = jnp.zeros(flat.shape[1:], flat.dtype)
    for s in range(a_own.shape[0]):
        for x in range(2):
            fine_row(table, s * 8 + x * 4 + OWN_1, flat, a_own.at[s, x, 1 - odd], w_ref.at[s, x])


def near_kernel(operator, table, flat, a_near, w_ref):
    for x in range(2):
        fine_row(table, operator * 8 + x * 4 + NEAR, flat, a_near.at[x, 0], w_ref.at[x])


def far_first_kernel(
    table, odd_ref, a_own, a_far, w_own, w_near, p_own, p_near, p_far, far_low, far_high, held, low, high, flat, w_own_0, w_far
):
    odd = odd_ref[0]
    fill(flat, 2 * HALF, far_low, p_far, far_high)
    for x in range(2):
        fine_row(table, x * 4 + FAR, flat, a_far.at[x, 0], w_far.at[x])
        fine_row(table, x * 4 + OWN_0, flat, a_own.at[0, x, odd], w_own_0.at[x])
    edges(odd, (p_far, p_own, p_own, p_near), (w_far, w_own_0, w_own.at[0], w_near), (low, high))


def own_0_kernel(operator, table, odd_ref, a_own, flat, w_ref):
    odd = odd_ref[0]
    for x in range(2):
        fine_row(table, operator * 8 + x * 4 + OWN_0, flat, a_own.at[operator, x, odd], w_ref.at[x])


def far_kernel(operator, table, odd_ref, a_far, flat, w_own, w_near, w_own_0, p_own, p_near, p_far, low, high, w_far):
    odd = odd_ref[0]
    for x in range(2):
        fine_row(table, operator * 8 + x * 4 + FAR, flat, a_far.at[x, 0], w_far.at[x])
    edges(odd, (p_far, p_own, p_own, p_near), (w_far, w_own_0, w_own.at[operator], w_near), (low, high))


def centre_kernel(operator, odd_ref, p_own, p_near, p_far, w_far, w_own_0, w_own, w_near, out):
    block = out.shape[-1]
    odd = odd_ref[0]
    for lag_y in range(5):
        total = coarse_column(
            odd, (p_far, p_own, p_own, p_near), (w_far, w_own_0, w_own.at[operator], w_near), (0, 1), lag_y, 0
        )
        for lag_x in range(3):
            out[lag_x, lag_y] = total[:, lag_x * block : (lag_x + 1) * block]


def final_kernel(odd_ref, *refs):
    out = refs[-1]
    odd = odd_ref[0]
    for operator in range(out.shape[0]):
        own, low, high = refs[3 * operator : 3 * operator + 3]
        for lag_x in range(5):
            for lag_y in range(5):
                total = None
                for part, first in ((low, 0), (own, 1), (high, 2)):
                    if 0 <= lag_x - first < 3:
                        term = part[lag_x - first, lag_y].astype(jnp.float32)
                        total = term if total is None else total + term
                place = 5 * lag_x + lag_y + odd * (4 - 2 * lag_y)
                out[operator, 0, 0, place] = total.astype(out.dtype)


def per_device(a_vals, a_off, a_count, p_vals):
    operators, _, _, slots, block, _ = a_vals.shape
    cols = lax.axis_size("col")
    rows = lax.axis_size("row")
    odd = (lax.axis_index("col") & 1).astype(jnp.int32)
    up, down = ring(rows, 1), ring(rows, -1)
    near_way, far_way, on_way = pair(cols), outward(cols), onward(cols)

    any_spec = pl.BlockSpec(memory_space=pl.ANY)
    smem = pl.BlockSpec(memory_space=pltpu.SMEM)
    vmem = pl.BlockSpec(memory_space=pltpu.VMEM)
    bf16, f32 = jnp.bfloat16, jnp.float32
    odd_arg = odd[None]
    flat_shape = jax.ShapeDtypeStruct((ZERO + 1, block, block), bf16)
    w_shape = jax.ShapeDtypeStruct((2, 3, block, 3 * block), bf16)
    part_shape = jax.ShapeDtypeStruct((3, 5, block, block), bf16)

    def call(kernel, in_specs, out_shape, products, name, scratch=(), aliases=None):
        single = not isinstance(out_shape, list)
        return pl.pallas_call(
            kernel,
            in_specs=in_specs,
            out_specs=vmem if single else [vmem] * len(out_shape),
            out_shape=out_shape,
            scratch_shapes=list(scratch),
            input_output_aliases=aliases or {},
            compiler_params=pltpu.CompilerParams(vmem_limit_bytes=VMEM_LIMIT),
            cost_estimate=pl.CostEstimate(flops=products * 2 * block**3, bytes_accessed=4 << 20, transcendentals=0),
            name=name,
        )

    p_near = lax.ppermute(p_vals, "col", near_way)
    info = jnp.concatenate([a_off, a_count[..., None]], axis=-1)
    column = jax.ShapeDtypeStruct((2, 1, slots, block, block), bf16)
    info_column = jax.ShapeDtypeStruct((operators, 2, 1, slots + 1), jnp.int32)
    *sends, info_near, info_far = call(
        pack_kernel,
        [smem, any_spec, vmem],
        [column] * (2 * operators) + [info_column] * 2,
        1,
        "pack",
        [pltpu.SemaphoreType.DMA((2 * operators,))],
    )(odd_arg, a_vals, info)
    info_near = lax.ppermute(info_near, "col", near_way)
    info_far = lax.ppermute(info_far, "col", far_way)
    mirrored = jnp.where(odd == 1, info[:, :, ::-1], info)
    table = product_table(
        jnp.concatenate([info_far, mirrored, info_near], axis=2).reshape(operators * 8, slots + 1), odd
    )

    p_near, sends = lax.optimization_barrier((p_near, sends))
    near_sends, far_sends = sends[:operators], sends[operators:]
    p_far = lax.ppermute(p_near, "col", on_way)
    row_shape = jax.ShapeDtypeStruct((1, 4, 4, block, block), bf16)
    low, high = call(rows_kernel, [vmem, vmem], [row_shape, row_shape], 1, "rows")(p_vals, p_near)
    from_low = lax.ppermute(high, "row", up)
    from_high = lax.ppermute(low, "row", down)
    a_near, a_far = [None] * operators, [None] * operators
    a_near[0] = lax.ppermute(near_sends[0], "col", near_way)
    a_far[0] = lax.ppermute(far_sends[0], "col", far_way)
    p_far, later_near, later_far = lax.optimization_barrier((p_far, near_sends[1:], far_sends[1:]))
    far_low = lax.ppermute(p_far[1:2], "row", up)
    far_high = lax.ppermute(p_far[0:1], "row", down)
    for s in range(1, operators):
        a_near[s] = lax.ppermute(later_near[s - 1], "col", near_way)
        a_far[s] = lax.ppermute(later_far[s - 1], "col", far_way)

    flat, w_own = call(
        near_own_kernel,
        [smem, smem] + [vmem] * 5,
        [flat_shape, jax.ShapeDtypeStruct((operators,) + w_shape.shape, bf16)],
        360,
        "near_own",
    )(table, odd_arg, a_vals, p_vals, p_near, from_low, from_high)

    finals = []
    for s in range(operators):
        w_near = call(functools.partial(near_kernel, s), [smem, vmem, vmem], w_shape, 90, "near")(
            table, flat, a_near[s]
        )
        if s == 0:
            low, high, flat, w_own_0, w_far = call(
                far_first_kernel,
                [smem, smem] + [vmem] * 10,
                [part_shape, part_shape, flat_shape, w_shape, w_shape],
                300,
                "far_first",
                aliases={11: 2},
            )(table, odd_arg, a_vals, a_far[s], w_own, w_near, p_vals, p_near, p_far, far_low, far_high, flat)
        else:
            w_own_0 = call(functools.partial(own_0_kernel, s), [smem, smem, vmem, vmem], w_shape, 90, "own_0")(
                table, odd_arg, a_vals, flat
            )
            low, high, w_far = call(
                functools.partial(far_kernel, s),
                [smem, smem] + [vmem] * 8,
                [part_shape, part_shape, w_shape],
                200,
                "far",
            )(table, odd_arg, a_far[s], flat, w_own, w_near, w_own_0, p_vals, p_near, p_far)
        from_low = lax.ppermute(high, "row", up)
        from_high = lax.ppermute(low, "row", down)
        centre = call(
            functools.partial(centre_kernel, s),
            [smem] + [vmem] * 7,
            jax.ShapeDtypeStruct((3, 5, block, block), f32),
            144,
            "centre",
        )(odd_arg, p_vals, p_near, p_far, w_far, w_own_0, w_own, w_near)
        finals += [centre, from_low, from_high]
    return call(
        final_kernel,
        [smem] + [vmem] * len(finals),
        jax.ShapeDtypeStruct((operators, 1, 1, 25, block, block), bf16),
        1,
        "final",
    )(odd_arg, *finals)


def solution(mesh):
    placed = (
        P(None, "row", "col", None, None, None),
        P(None, "row", "col", None),
        P(None, "row", "col"),
        P("row", "col", None, None, None),
    )
    return jax.shard_map(
        per_device,
        mesh=mesh,
        in_specs=placed,
        out_specs=P(None, "row", "col", None, None, None),
        check_vma=False,
    )
```

time: 81.8 us -> 72.9 us (0.89)
  Pallas kernels: 21.2 us -> 14.2 us
  waiting for transfers between devices: 33.6 us -> 27.5 us
  other arithmetic: 1.82 us -> 5.21 us
  starting transfers between devices: 18.6 us -> 21.2 us
  local copies, waits for them, and re-layouts: 5.42 us -> 3.91 us
    pallas_call x3 -> x5, Pallas kernels: 13 us -> 6.61 us  [the longest x1 2.65 us: per_device(): call(far_first_kernel, [smem, smem] + [vmem] * 10, [part_shape, part_shap...]
    ppermute x1, waiting for transfers between devices: 11.6 us -> 6.42 us  [per_device(): p_far = lax.ppermute(p_near, 'col', on_way)]
    ppermute x8 -> x4, starting transfers between devices: 8.02 us -> 4.12 us  [the longest x1 3.57 us: per_device(): info_far = lax.ppermute(info_far, 'col', far_way)]
    ppermute x2 -> x3, waiting for transfers between devices: 8.96 us -> 12.6 us  [per_device(): from_low = lax.ppermute(high, 'row', up)]
    ppermute x1, waiting for transfers between devices: 5.95 us -> 2.34 us  [per_device(): p_near = lax.ppermute(p_vals, 'col', near_way)]
    unnamed x8 -> x24, local copies, waits for them, and re-layouts: 0.02 us -> 2.8 us
    ppermute x8 -> x4, waiting for transfers between devices: 2.79 us -> 0.01 us  [the longest x1 0.01 us: per_device(): info_far = lax.ppermute(info_far, 'col', far_way)]
    squeeze x1 -> x0, local copies, waits for them, and re-layouts: 2.37 us -> none  [column(): return lax.dynamic_slice(array, start, (1, 2, 1) + array.shape[3:])[0]]
  transfers between devices with their start and end apart: 18 -> 16, of which waited for: 6 -> 5; matrix products, arithmetic and copies ran while one was open for 7% -> 9% of each run, Pallas kernels for 24% -> 18%
where the time goes in v3:
time: 72.9 us; the launch traced here: 72.3 us
  waiting for transfers between devices  27.5 us (38%)
  starting transfers between devices  21.2 us (29%)
  Pallas kernels  14.2 us (19%)
  other arithmetic  5.21 us (7%)
  local copies, waits for them, and re-layouts  3.91 us (5%)
    ppermute x3, waiting for transfers between devices, per_device(): from_low = lax.ppermute(high, 'row', up)  12.6 us
    ppermute x1, waiting for transfers between devices, per_device(): p_far = lax.ppermute(p_near, 'col', on_way)  6.42 us
    ppermute x1, waiting for transfers between devices, per_device(): a_near[s] = lax.ppermute(later_near[s - 1], 'col', near_way)  6.08 us
    ppermute x1, starting transfers between devices, per_device(): a_near[0] = lax.ppermute(near_sends[0], 'col', near_way)  3.58 us
    ppermute x1, starting transfers between devices, per_device(): info_far = lax.ppermute(info_far, 'col', far_way)  3.57 us
    ppermute x3, starting transfers between devices, per_device(): from_high = lax.ppermute(low, 'row', down)  3.45 us
    ppermute x1, starting transfers between devices, per_device(): p_near = lax.ppermute(p_vals, 'col', near_way)  2.94 us
    pallas_call x2, Pallas kernels, per_device(): call(functools.partial(near_kernel, s), [smem, vmem, vmem], w_shape, 90,...  2.87 us
  transfers between devices with their start and end apart: 16, of which 5 were waited for; matrix products, arithmetic and copies ran while one was open for 9% of the time, Pallas kernels for 18%

profile of v3, /device:TPU:0, one launch (start us, length us, event | category | flops | bytes accessed | tf_op | source)
XLA Modules:
  0.0 72.3 jit_solution(2251011803638833366)
XLA Ops:
  0.0 2.9 %collective-permute-start = (bf16[2,2,4,128,128]{4,3,2,1,0:T(8,128)(2,1)}, bf16[2,2,4,128,128]{4,3,2,1,0:T(8,128)(2,1)S(1)}, u32[]{:S(2)}, u32[]{:S(2)}) collective-permute-start(bf16[2,2,4,128,128]{4,3,2,1,0:T(8,128)(2,1)} %p_own.9), channel_id=1, source_target_pairs={{0,1},{1,0},{2,3},{3,2},{4,5},{5,4},{6,7},{7,6},{8,9},{9,8},{10,11... | collective-permute-start | bytes 1572872 | tf_op jit(solution)/shard_map/ppermute | solution.py:228
  2.9 0.8 %copy.7 = s32[2,2,2,1]{3,2,1,0:T(2,128)S(1)} copy(s32[2,2,2,1]{2,1,0,3:T(2,128)} %bitcast.4) | data formatting | bytes 64 | tf_op jit(solution)/shard_map/broadcast_in_dim | solution.py:229
  3.7 0.8 %pad_add_fusion.1.info = s32[2,2,2,6]{3,2,1,0:T(2,128)S(1)} fusion(s32[2,2,2,1]{3,2,1,0:T(2,128)S(1)} %copy.7, s32[2,2,2,5]{3,2,1,0:T(2,128)} %param.5), kind=kLoop, calls=%fused_computation.35 | loop fusion | flops 48 | bytes 384 | tf_op jit(solution)/shard_map/concatenate | solution.py:229
  4.5 1.3 %copy-done.1 = bf16[2,2,2,5,128,128]{5,4,3,2,1,0:T(8,128)(2,1)S(1)} copy-done((bf16[2,2,2,5,128,128]{5,4,3,2,1,0:T(8,128)(2,1)S(1)}, bf16[2,2,2,5,128,128]{5,4,3,2,1,0:T(8,128)(2,1)}, u32[]{:S(2)}) %copy-start.1) | copy-done | bytes 1310744
  5.8 0.3 pack.1
  6.1 0.0 copy-start.3
  6.1 0.7 copy-done.3
  6.8 0.7 %copy-done.4 = bf16[2,1,5,128,128]{4,3,2,1,0:T(8,128)(2,1)} copy-done((bf16[2,1,5,128,128]{4,3,2,1,0:T(8,128)(2,1)}, bf16[2,1,5,128,128]{4,3,2,1,0:T(8,128)(2,1)S(1)}, u32[]{:S(2)}) %copy-start.4) | copy-done | bytes 327704
  7.6 3.6 %collective-permute-start.2 = (s32[2,2,1,6]{3,2,1,0:T(1,128)S(1)}, s32[2,2,1,6]{3,2,1,0:T(1,128)}, u32[]{:S(2)}, u32[]{:S(2)}) collective-permute-start(s32[2,2,1,6]{3,2,1,0:T(1,128)S(1)} %get-tuple-element.39), channel_id=1, source_target_pairs={{0,7},{1,2},{2,1},{3,4},{4,3},{5,6},{6,5},{7,0},{8,15},{9,10},{10,... | collective-permute-start | bytes 296 | tf_op jit(solution)/shard_map/ppermute | solution.py:241
  11.2 0.6 broadcast_shift-right-arithmetic_fusion
  11.7 0.6 and_add_fusion
  12.3 0.5 iota_divide_fusion
  12.9 2.3 %collective-permute-done.near.p_near = bf16[2,2,4,128,128]{4,3,2,1,0:T(8,128)(2,1)S(1)} collective-permute-done((bf16[2,2,4,128,128]{4,3,2,1,0:T(8,128)(2,1)}, bf16[2,2,4,128,128]{4,3,2,1,0:T(8,128)(2,1)S(1)}, u32[]{:S(2)}, u32[]{:S(2)}) %collective-permute-start) | collective-permute-done | bytes 524320 | tf_op jit(solution)/shard_map/ppermute | solution.py:228
  15.2 1.8 %collective-permute-start.1 = (bf16[2,2,4,128,128]{4,3,2,1,0:T(8,128)(2,1)S(1)}, bf16[2,2,4,128,128]{4,3,2,1,0:T(8,128)(2,1)S(1)}, u32[]{:S(2)}, u32[]{:S(2)}) collective-permute-start(bf16[2,2,4,128,128]{4,3,2,1,0:T(8,128)(2,1)S(1)} %collective-permute-done.near.p_near), channel_id=1, source_target_pairs={{0,2},{1,7},{2,4},{3,1},{4,6},{5,3},{6,0},{7,5},{8,10},{9,15},{10,... | collective-permute-start | bytes 1572872 | tf_op jit(solution)/shard_map/ppermute | solution.py:249
  17.0 0.6 compare_and_fusion
  17.6 1.4 %broadcast_select_fusion = s32[2,2,2,6]{3,2,1,0:T(2,128)} fusion(s32[2,2,2,6]{3,2,1,0:T(2,128)S(1)} %rev.3, pred[]{:T(512)S(6)} %eq.25, s32[2,2,2,1]{3,2,1,0:T(2,128)S(1)} %copy.7, s32[2,2,2,5]{3,2,1,0:T(2,128)} %param.5), kind=kLoop, calls=%fused_computation.36 | loop fusion | flops 96 | bytes 577 | tf_op jit(solution)/shard_map/jit(_where)/select_n | solution.py:242
  18.9 0.0 collective-permute-done.2
  19.0 0.0 collective-permute-done.3
  19.0 0.7 pad_add_fusion
  19.7 3.6 %collective-permute-start.7 = (bf16[2,1,5,128,128]{4,3,2,1,0:T(8,128)(2,1)}, bf16[2,1,5,128,128]{4,3,2,1,0:T(8,128)(2,1)S(1)}, u32[]{:S(2)}, u32[]{:S(2)}) collective-permute-start(bf16[2,1,5,128,128]{4,3,2,1,0:T(8,128)(2,1)} %copy-done.4), channel_id=1, source_target_pairs={{0,1},{1,0},{2,3},{3,2},{4,5},{5,4},{6,7},{7,6},{8,9},{9,8},{10,11... | collective-permute-start | bytes 983048 | tf_op jit(solution)/shard_map/ppermute | solution.py:255
  23.3 0.1 rows.1
  23.3 0.1 collective-permute-start.5
  23.4 1.7 %collective-permute-start.6 = (bf16[1,4,4,128,128]{4,3,2,1,0:T(8,128)(2,1)S(1)}, bf16[1,4,4,128,128]{4,3,2,1,0:T(8,128)(2,1)S(1)}, u32[]{:S(2)}, u32[]{:S(2)}) collective-permute-start(bf16[1,4,4,128,128]{4,3,2,1,0:T(8,128)(2,1)S(1)} %get-tuple-element.43), channel_id=1, source_target_pairs={{0,24},{8,0},{16,8},{24,16},{1,25},{9,1},{17,9},{25,17},{2,26},{10... | collective-permute-start | bytes 1572872 | tf_op jit(solution)/shard_map/ppermute | solution.py:253
  25.1 0.3 slice_reduce_fusion.5
  25.4 0.1 collective-permute-start.4
  25.5 6.4 %collective-permute-done.1.p_far = bf16[2,2,4,128,128]{4,3,2,1,0:T(8,128)(2,1)S(1)} collective-permute-done((bf16[2,2,4,128,128]{4,3,2,1,0:T(8,128)(2,1)S(1)}, bf16[2,2,4,128,128]{4,3,2,1,0:T(8,128)(2,1)S(1)}, u32[]{:S(2)}, u32[]{:S(2)}) %collective-permute-start.1) | collective-permute-done | bytes 524320 | tf_op jit(solution)/shard_map/ppermute | solution.py:249
  31.9 0.1 collective-permute-start.9
  32.0 0.5 collective-permute-start.8
  32.5 0.1 fusion.3.table
  32.6 3.1 %collective-permute-done.5.low = bf16[1,4,4,128,128]{4,3,2,1,0:T(8,128)(2,1)S(1)} collective-permute-done((bf16[1,4,4,128,128]{4,3,2,1,0:T(8,128)(2,1)S(1)}, bf16[1,4,4,128,128]{4,3,2,1,0:T(8,128)(2,1)S(1)}, u32[]{:S(2)}, u32[]{:S(2)}) %collective-permute-start.5) | collective-permute-done | bytes 524320 | tf_op jit(solution)/shard_map/ppermute | solution.py:252
  35.7 1.8 %collective-permute-start.12 = (bf16[2,1,5,128,128]{4,3,2,1,0:T(8,128)(2,1)S(1)}, bf16[2,1,5,128,128]{4,3,2,1,0:T(8,128)(2,1)S(1)}, u32[]{:S(2)}, u32[]{:S(2)}) collective-permute-start(bf16[2,1,5,128,128]{4,3,2,1,0:T(8,128)(2,1)S(1)} %get-tuple-element.51), channel_id=1, source_target_pairs={{0,7},{1,2},{2,1},{3,4},{4,3},{5,6},{6,5},{7,0},{8,15},{9,10},{10,... | collective-permute-start | bytes 983048 | tf_op jit(solution)/shard_map/ppermute | solution.py:262
  37.5 1.6 %collective-permute-start.13 = (bf16[2,1,5,128,128]{4,3,2,1,0:T(8,128)(2,1)S(1)}, bf16[2,1,5,128,128]{4,3,2,1,0:T(8,128)(2,1)S(1)}, u32[]{:S(2)}, u32[]{:S(2)}) collective-permute-start(bf16[2,1,5,128,128]{4,3,2,1,0:T(8,128)(2,1)S(1)} %get-tuple-element.53), channel_id=1, source_target_pairs={{0,1},{1,0},{2,3},{3,2},{4,5},{5,4},{6,7},{7,6},{8,9},{9,8},{10,11... | collective-permute-start | bytes 983048 | tf_op jit(solution)/shard_map/ppermute | solution.py:261
  39.1 2.2 %near_own.1 = (bf16[97,128,128]{2,1,0:T(8,128)(2,1)S(1)}, bf16[2,2,3,128,384]{4,3,2,1,0:T(8,128)(2,1)S(1)}) custom-call(s32[16,45]{1,0:T(8,128)S(1)} %fusion.3.table, s32[1]{0:T(128)} %bitcast.odd_ref, bf16[2,2,2,5,128,128]{5,4,3,2,1,0:T(8,128)(2,1)S(1)} %copy-done.2, bf16[2,2,4,128,128]{4,3,2,1,0:T(8,128)(2,1)S(1)} %copy-done, ...), custom_call_target="tpu_custom_call" | custom-call | flops 1509949440 | bytes 4194304 | tf_op jit(solution)/shard_map/near_own/pallas_call | solution.py:264
  41.3 1.4 %near.2.w_near = bf16[2,3,128,384]{3,2,1,0:T(8,128)(2,1)S(1)} custom-call(s32[16,45]{1,0:T(8,128)S(1)} %fusion.3.table, bf16[97,128,128]{2,1,0:T(8,128)(2,1)S(1)} %get-tuple-element.45.flat.held, bf16[2,1,5,128,128]{4,3,2,1,0:T(8,128)(2,1)S(1)} %collective-permute-done.7.a_near), custom_call_target="tpu_custom_call" | custom-call | flops 377487360 | bytes 4194304 | tf_op jit(solution)/shard_map/near/pallas_call | solution.py:274
  42.7 0.0 collective-permute-done.4.a_far
  42.8 2.6 %far_first.1 = (bf16[3,5,128,128]{3,2,1,0:T(8,128)(2,1)S(1)}, bf16[3,5,128,128]{3,2,1,0:T(8,128)(2,1)S(1)}, bf16[97,128,128]{2,1,0:T(8,128)(2,1)S(1)}, bf16[2,3,...) custom-call(s32[16,45]{1,0:T(8,128)S(1)} %fusion.3.table, ...), custom_call_target="tpu_custom_call", output_to_operand_aliasing={{2}: (11, {})} | custom-call | flops 1258291200 | bytes 4194304 | tf_op jit(solution)/shard_map/far_first/pallas_call | solution.py:278
  45.4 1.4 %collective-permute-start.10 = (bf16[3,5,128,128]{3,2,1,0:T(8,128)(2,1)S(1)}, bf16[3,5,128,128]{3,2,1,0:T(8,128)(2,1)S(1)}, u32[]{:S(2)}, u32[]{:S(2)}) collective-permute-start(bf16[3,5,128,128]{3,2,1,0:T(8,128)(2,1)S(1)} %get-tuple-element.49), channel_id=1, source_target_pairs={{0,8},{8,16},{16,24},{24,0},{1,9},{9,17},{17,25},{25,1},{2,10},{10... | collective-permute-start | bytes 1474568 | tf_op jit(solution)/shard_map/ppermute | solution.py:297
  46.8 0.4 collective-permute-start.11
  47.2 1.4 %own_0.1.w_own_0 = bf16[2,3,128,384]{3,2,1,0:T(8,128)(2,1)S(1)} custom-call(s32[16,45]{1,0:T(8,128)S(1)} %fusion.3.table, s32[1]{0:T(128)} %bitcast.odd_ref, bf16[2,2,2,5,128,128]{5,4,3,2,1,0:T(8,128)(2,1)S(1)} %copy-done.2, bf16[97,128,128]{2,1,0:T(8,128)(2,1)S(1)} %get-tuple-element.52.flat), custom_call_target="tpu_custom_call" | custom-call | flops 377487360 | bytes 4194304 | tf_op jit(solution)/shard_map/own_0/pallas_call | solution.py:287
  48.7 6.1 %collective-permute-done.13.a_near = bf16[2,1,5,128,128]{4,3,2,1,0:T(8,128)(2,1)S(1)} collective-permute-done((bf16[2,1,5,128,128]{4,3,2,1,0:T(8,128)(2,1)S(1)}, bf16[2,1,5,128,128]{4,3,2,1,0:T(8,128)(2,1)S(1)}, u32[]{:S(2)}, u32[]{:S(2)}) %collective-permute-start.13) | collective-permute-done | bytes 327712 | tf_op jit(solution)/shard_map/ppermute | solution.py:261
  54.8 1.4 %near.3.w_near = bf16[2,3,128,384]{3,2,1,0:T(8,128)(2,1)S(1)} custom-call(s32[16,45]{1,0:T(8,128)S(1)} %fusion.3.table, bf16[97,128,128]{2,1,0:T(8,128)(2,1)S(1)} %get-tuple-element.52.flat, bf16[2,1,5,128,128]{4,3,2,1,0:T(8,128)(2,1)S(1)} %collective-permute-done.13.a_near), custom_call_target="tpu_custom_call" | custom-call | flops 377487360 | bytes 4194304 | tf_op jit(solution)/shard_map/near/pallas_call | solution.py:274
  56.2 2.0 %far.1 = (bf16[3,5,128,128]{3,2,1,0:T(8,128)(2,1)S(1)}, bf16[3,5,128,128]{3,2,1,0:T(8,128)(2,1)S(1)}, bf16[2,3,128,384]{3,2,1,0:T(8,128)(2,1)S(1)}) custom-call(s32[16,45]{1,0:T(8,128)S(1)} %fusion.3.table, s32[1]{0:T(128)} %bitcast.odd_ref, bf16[2,1,5,128,128]{4,3,2,1,0:T(8,128)(2,1)S(1)} %collective-permute-done.12.a_far, ...), custom_call_target="tpu_custom_call" | custom-call | flops 838860800 | bytes 4194304 | tf_op jit(solution)/shard_map/far/pallas_call | solution.py:290
  58.2 0.5 collective-permute-start.14
  58.7 1.3 %collective-permute-start.15 = (bf16[3,5,128,128]{3,2,1,0:T(8,128)(2,1)S(1)}, bf16[3,5,128,128]{3,2,1,0:T(8,128)(2,1)S(1)}, u32[]{:S(2)}, u32[]{:S(2)}) collective-permute-start(bf16[3,5,128,128]{3,2,1,0:T(8,128)(2,1)S(1)} %get-tuple-element.56), channel_id=1, source_target_pairs={{0,24},{8,0},{16,8},{24,16},{1,25},{9,1},{17,9},{25,17},{2,26},{10... | collective-permute-start | bytes 1474568 | tf_op jit(solution)/shard_map/ppermute | solution.py:298
  60.0 0.6 centre.2.refs_0_
  60.6 0.6 centre.3.refs_3_
  61.3 9.5 %collective-permute-done.14.refs_4_ = bf16[3,5,128,128]{3,2,1,0:T(8,128)(2,1)S(1)} collective-permute-done((bf16[3,5,128,128]{3,2,1,0:T(8,128)(2,1)S(1)}, bf16[3,5,128,128]{3,2,1,0:T(8,128)(2,1)S(1)}, u32[]{:S(2)}, u32[]{:S(2)}) %collective-permute-start.14) | collective-permute-done | bytes 491552 | tf_op jit(solution)/shard_map/ppermute | solution.py:297
  70.8 1.5 %final.1 = bf16[2,1,1,25,128,128]{5,4,3,2,1,0:T(8,128)(2,1)} custom-call(s32[1]{0:T(128)} %bitcast.odd_ref, f32[3,5,128,128]{3,2,1,0:T(8,128)S(1)} %centre.2.refs_0_, bf16[3,5,128,128]{3,2,1,0:T(8,128)(2,1)S(1)} %collective-permute-done.10.refs_1_, bf16[3,5,128,128]{3,2,1,0:T(8,128)(2,1)S(1)} %collective-permute-done.11.refs_2_, ...), custom_call_target="tpu_custom_call" | custom-call | flops 4194304 | bytes 4194304 | tf_op jit(solution)/shard_map/final/pallas_call | solution.py:307
  (31 shorter events, 0.1 us)
Async XLA Ops:
  0.0 23.3 %copy-start = (bf16[2,2,4,128,128]{4,3,2,1,0:T(8,128)(2,1)S(1)}, bf16[2,2,4,128,128]{4,3,2,1,0:T(8,128)(2,1)}, u32[]{:S(2)}) copy-start(bf16[2,2,4,128,128]{4,3,2,1,0:T(8,128)(2,1)} %p_own.9) | copy-start | bytes 1572868
  0.0 15.2 %collective-permute-start = (bf16[2,2,4,128,128]{4,3,2,1,0:T(8,128)(2,1)}, bf16[2,2,4,128,128]{4,3,2,1,0:T(8,128)(2,1)S(1)}, u32[]{:S(2)}, u32[]{:S(2)}) collective-permute-start(bf16[2,2,4,128,128]{4,3,2,1,0:T(8,128)(2,1)} %p_own.9), channel_id=1, source_target_pairs={{0,1},{1,0},{2,3},{3,2},{4,5},{5,4},{6,7},{7,6},{8,9},{9,8},{10,11... | collective-permute-start | bytes 1572872 | tf_op jit(solution)/shard_map/ppermute | solution.py:228
  4.5 1.3 %copy-start.1 = (bf16[2,2,2,5,128,128]{5,4,3,2,1,0:T(8,128)(2,1)S(1)}, bf16[2,2,2,5,128,128]{5,4,3,2,1,0:T(8,128)(2,1)}, u32[]{:S(2)}) copy-start(bf16[2,2,2,5,128,128]{5,4,3,2,1,0:T(8,128)(2,1)} %a_own.7) | copy-start | bytes 3932164
  5.8 33.3 %copy-start.2 = (bf16[2,2,2,5,128,128]{5,4,3,2,1,0:T(8,128)(2,1)S(1)}, bf16[2,2,2,5,128,128]{5,4,3,2,1,0:T(8,128)(2,1)}, u32[]{:S(2)}) copy-start(bf16[2,2,2,5,128,128]{5,4,3,2,1,0:T(8,128)(2,1)} %a_own.7) | copy-start | bytes 3932164
  6.1 0.7 %copy-start.3 = (bf16[2,1,5,128,128]{4,3,2,1,0:T(8,128)(2,1)}, bf16[2,1,5,128,128]{4,3,2,1,0:T(8,128)(2,1)S(1)}, u32[]{:S(2)}) copy-start(bf16[2,1,5,128,128]{4,3,2,1,0:T(8,128)(2,1)S(1)} %get-tuple-element.41) | copy-start | bytes 983044
  6.8 0.7 %copy-start.4 = (bf16[2,1,5,128,128]{4,3,2,1,0:T(8,128)(2,1)}, bf16[2,1,5,128,128]{4,3,2,1,0:T(8,128)(2,1)S(1)}, u32[]{:S(2)}) copy-start(bf16[2,1,5,128,128]{4,3,2,1,0:T(8,128)(2,1)S(1)} %get-tuple-element.46) | copy-start | bytes 983044
  7.6 11.4 %collective-permute-start.2 = (s32[2,2,1,6]{3,2,1,0:T(1,128)S(1)}, s32[2,2,1,6]{3,2,1,0:T(1,128)}, u32[]{:S(2)}, u32[]{:S(2)}) collective-permute-start(s32[2,2,1,6]{3,2,1,0:T(1,128)S(1)} %get-tuple-element.39), channel_id=1, source_target_pairs={{0,7},{1,2},{2,1},{3,4},{4,3},{5,6},{6,5},{7,0},{8,15},{9,10},{10,... | collective-permute-start | bytes 296 | tf_op jit(solution)/shard_map/ppermute | solution.py:241
  11.1 7.8 %collective-permute-start.3 = (s32[2,2,1,6]{3,2,1,0:T(1,128)S(1)}, s32[2,2,1,6]{3,2,1,0:T(1,128)}, u32[]{:S(2)}, u32[]{:S(2)}) collective-permute-start(s32[2,2,1,6]{3,2,1,0:T(1,128)S(1)} %get-tuple-element.40), channel_id=1, source_target_pairs={{0,1},{1,0},{2,3},{3,2},{4,5},{5,4},{6,7},{7,6},{8,9},{9,8},{10,11... | collective-permute-start | bytes 296 | tf_op jit(solution)/shard_map/ppermute | solution.py:240
  15.2 16.7 %collective-permute-start.1 = (bf16[2,2,4,128,128]{4,3,2,1,0:T(8,128)(2,1)S(1)}, bf16[2,2,4,128,128]{4,3,2,1,0:T(8,128)(2,1)S(1)}, u32[]{:S(2)}, u32[]{:S(2)}) collective-permute-start(bf16[2,2,4,128,128]{4,3,2,1,0:T(8,128)(2,1)S(1)} %collective-permute-done.near.p_near), channel_id=1, source_target_pairs={{0,2},{1,7},{2,4},{3,1},{4,6},{5,3},{6,0},{7,5},{8,10},{9,15},{10,... | collective-permute-start | bytes 1572872 | tf_op jit(solution)/shard_map/ppermute | solution.py:249
  18.9 13.6 %copy-start.5 = (s32[16]{0:T(128)S(1)}, s32[16]{0:T(128)}, u32[]{:S(2)}) copy-start(s32[16]{0:T(128)} %get-tuple-element.69) | copy-start | bytes 196
  18.9 13.6 %copy-start.6 = (s32[16]{0:T(128)S(1)}, s32[16]{0:T(128)}, u32[]{:S(2)}) copy-start(s32[16]{0:T(128)} %get-tuple-element.70) | copy-start | bytes 196
  18.9 13.6 %copy-start.7 = (s32[16]{0:T(128)S(1)}, s32[16]{0:T(128)}, u32[]{:S(2)}) copy-start(s32[16]{0:T(128)} %get-tuple-element.67) | copy-start | bytes 196
  18.9 13.6 %copy-start.8 = (s32[16]{0:T(128)S(1)}, s32[16]{0:T(128)}, u32[]{:S(2)}) copy-start(s32[16]{0:T(128)} %get-tuple-element.68) | copy-start | bytes 196
  18.9 13.6 %copy-start.9 = (s32[45]{0:T(128)S(1)}, s32[45]{0:T(128)}, u32[]{:S(2)}) copy-start(s32[45]{0:T(128)} %get-tuple-element.65) | copy-start | bytes 544
  18.9 13.6 %copy-start.10 = (s32[45]{0:T(128)S(1)}, s32[45]{0:T(128)}, u32[]{:S(2)}) copy-start(s32[45]{0:T(128)} %get-tuple-element.66) | copy-start | bytes 544
  18.9 13.6 %copy-start.11 = (pred[45]{0:T(512)(128)(4,1)S(1)}, pred[45]{0:T(512)(128)(4,1)}, u32[]{:S(2)}) copy-start(pred[45]{0:T(512)(128)(4,1)} %compare_and_fusion) | copy-start | bytes 139
  19.7 12.3 %collective-permute-start.7 = (bf16[2,1,5,128,128]{4,3,2,1,0:T(8,128)(2,1)}, bf16[2,1,5,128,128]{4,3,2,1,0:T(8,128)(2,1)S(1)}, u32[]{:S(2)}, u32[]{:S(2)}) collective-permute-start(bf16[2,1,5,128,128]{4,3,2,1,0:T(8,128)(2,1)} %copy-done.4), channel_id=1, source_target_pairs={{0,1},{1,0},{2,3},{3,2},{4,5},{5,4},{6,7},{7,6},{8,9},{9,8},{10,11... | collective-permute-start | bytes 983048 | tf_op jit(solution)/shard_map/ppermute | solution.py:255
  23.3 12.4 %collective-permute-start.5 = (bf16[1,4,4,128,128]{4,3,2,1,0:T(8,128)(2,1)S(1)}, bf16[1,4,4,128,128]{4,3,2,1,0:T(8,128)(2,1)S(1)}, u32[]{:S(2)}, u32[]{:S(2)}) collective-permute-start(bf16[1,4,4,128,128]{4,3,2,1,0:T(8,128)(2,1)S(1)} %get-tuple-element.42), channel_id=1, source_target_pairs={{0,8},{8,16},{16,24},{24,0},{1,9},{9,17},{17,25},{25,1},{2,10},{10... | collective-permute-start | bytes 1572872 | tf_op jit(solution)/shard_map/ppermute | solution.py:252
  23.4 14.1 %collective-permute-start.6 = (bf16[1,4,4,128,128]{4,3,2,1,0:T(8,128)(2,1)S(1)}, bf16[1,4,4,128,128]{4,3,2,1,0:T(8,128)(2,1)S(1)}, u32[]{:S(2)}, u32[]{:S(2)}) collective-permute-start(bf16[1,4,4,128,128]{4,3,2,1,0:T(8,128)(2,1)S(1)} %get-tuple-element.43), channel_id=1, source_target_pairs={{0,24},{8,0},{16,8},{24,16},{1,25},{9,1},{17,9},{25,17},{2,26},{10... | collective-permute-start | bytes 1572872 | tf_op jit(solution)/shard_map/ppermute | solution.py:253
  25.4 17.4 %collective-permute-start.4 = (bf16[2,1,5,128,128]{4,3,2,1,0:T(8,128)(2,1)}, bf16[2,1,5,128,128]{4,3,2,1,0:T(8,128)(2,1)S(1)}, u32[]{:S(2)}, u32[]{:S(2)}) collective-permute-start(bf16[2,1,5,128,128]{4,3,2,1,0:T(8,128)(2,1)} %copy-done.3), channel_id=1, source_target_pairs={{0,7},{1,2},{2,1},{3,4},{4,3},{5,6},{6,5},{7,0},{8,15},{9,10},{10,... | collective-permute-start | bytes 983048 | tf_op jit(solution)/shard_map/ppermute | solution.py:256
  31.9 10.8 %collective-permute-start.9 = (bf16[1,2,4,128,128]{4,3,2,1,0:T(8,128)(2,1)S(1)}, bf16[1,2,4,128,128]{4,3,2,1,0:T(8,128)(2,1)S(1)}, u32[]{:S(2)}, u32[]{:S(2)}) collective-permute-start(bf16[1,2,4,128,128]{4,3,2,1,0:T(8,128)(2,1)S(1)} %get-tuple-element.63), channel_id=1, source_target_pairs={{0,24},{8,0},{16,8},{24,16},{1,25},{9,1},{17,9},{25,17},{2,26},{10... | collective-permute-start | bytes 786440 | tf_op jit(solution)/shard_map/ppermute | solution.py:259
  32.0 10.8 %collective-permute-start.8 = (bf16[1,2,4,128,128]{4,3,2,1,0:T(8,128)(2,1)S(1)}, bf16[1,2,4,128,128]{4,3,2,1,0:T(8,128)(2,1)S(1)}, u32[]{:S(2)}, u32[]{:S(2)}) collective-permute-start(bf16[1,2,4,128,128]{4,3,2,1,0:T(8,128)(2,1)S(1)} %get-tuple-element.64), channel_id=1, source_target_pairs={{0,8},{8,16},{16,24},{24,0},{1,9},{9,17},{17,25},{25,1},{2,10},{10... | collective-permute-start | bytes 786440 | tf_op jit(solution)/shard_map/ppermute | solution.py:258
  35.7 20.5 %collective-permute-start.12 = (bf16[2,1,5,128,128]{4,3,2,1,0:T(8,128)(2,1)S(1)}, bf16[2,1,5,128,128]{4,3,2,1,0:T(8,128)(2,1)S(1)}, u32[]{:S(2)}, u32[]{:S(2)}) collective-permute-start(bf16[2,1,5,128,128]{4,3,2,1,0:T(8,128)(2,1)S(1)} %get-tuple-element.51), channel_id=1, source_target_pairs={{0,7},{1,2},{2,1},{3,4},{4,3},{5,6},{6,5},{7,0},{8,15},{9,10},{10,... | collective-permute-start | bytes 983048 | tf_op jit(solution)/shard_map/ppermute | solution.py:262
  37.5 17.3 %collective-permute-start.13 = (bf16[2,1,5,128,128]{4,3,2,1,0:T(8,128)(2,1)S(1)}, bf16[2,1,5,128,128]{4,3,2,1,0:T(8,128)(2,1)S(1)}, u32[]{:S(2)}, u32[]{:S(2)}) collective-permute-start(bf16[2,1,5,128,128]{4,3,2,1,0:T(8,128)(2,1)S(1)} %get-tuple-element.53), channel_id=1, source_target_pairs={{0,1},{1,0},{2,3},{3,2},{4,5},{5,4},{6,7},{7,6},{8,9},{9,8},{10,11... | collective-permute-start | bytes 983048 | tf_op jit(solution)/shard_map/ppermute | solution.py:261
  45.4 15.8 %collective-permute-start.10 = (bf16[3,5,128,128]{3,2,1,0:T(8,128)(2,1)S(1)}, bf16[3,5,128,128]{3,2,1,0:T(8,128)(2,1)S(1)}, u32[]{:S(2)}, u32[]{:S(2)}) collective-permute-start(bf16[3,5,128,128]{3,2,1,0:T(8,128)(2,1)S(1)} %get-tuple-element.49), channel_id=1, source_target_pairs={{0,8},{8,16},{16,24},{24,0},{1,9},{9,17},{17,25},{25,1},{2,10},{10... | collective-permute-start | bytes 1474568 | tf_op jit(solution)/shard_map/ppermute | solution.py:297
  46.8 14.5 %collective-permute-start.11 = (bf16[3,5,128,128]{3,2,1,0:T(8,128)(2,1)S(1)}, bf16[3,5,128,128]{3,2,1,0:T(8,128)(2,1)S(1)}, u32[]{:S(2)}, u32[]{:S(2)}) collective-permute-start(bf16[3,5,128,128]{3,2,1,0:T(8,128)(2,1)S(1)} %get-tuple-element.50), channel_id=1, source_target_pairs={{0,24},{8,0},{16,8},{24,16},{1,25},{9,1},{17,9},{25,17},{2,26},{10... | collective-permute-start | bytes 1474568 | tf_op jit(solution)/shard_map/ppermute | solution.py:298
  58.2 12.6 %collective-permute-start.14 = (bf16[3,5,128,128]{3,2,1,0:T(8,128)(2,1)S(1)}, bf16[3,5,128,128]{3,2,1,0:T(8,128)(2,1)S(1)}, u32[]{:S(2)}, u32[]{:S(2)}) collective-permute-start(bf16[3,5,128,128]{3,2,1,0:T(8,128)(2,1)S(1)} %get-tuple-element.55), channel_id=1, source_target_pairs={{0,8},{8,16},{16,24},{24,0},{1,9},{9,17},{17,25},{25,1},{2,10},{10... | collective-permute-start | bytes 1474568 | tf_op jit(solution)/shard_map/ppermute | solution.py:297
  58.7 12.2 %collective-permute-start.15 = (bf16[3,5,128,128]{3,2,1,0:T(8,128)(2,1)S(1)}, bf16[3,5,128,128]{3,2,1,0:T(8,128)(2,1)S(1)}, u32[]{:S(2)}, u32[]{:S(2)}) collective-permute-start(bf16[3,5,128,128]{3,2,1,0:T(8,128)(2,1)S(1)} %get-tuple-element.56), channel_id=1, source_target_pairs={{0,24},{8,0},{16,8},{24,16},{1,25},{9,1},{17,9},{25,17},{2,26},{10... | collective-permute-start | bytes 1474568 | tf_op jit(solution)/shard_map/ppermute | solution.py:298

commit v4 on v3

v4 whole, which is shorter than its diff:
```python
import functools

import jax
import jax.numpy as jnp
from jax import lax
from jax.experimental import pallas as pl
from jax.experimental.pallas import tpu as pltpu
from jax.sharding import PartitionSpec as P

FAR, OWN_0, OWN_1, NEAR = range(4)
HALF = 32
ZERO = 3 * HALF
INFO = 16
VMEM_LIMIT = 24 * 1024 * 1024


def ring(count, step):
    return [(i, (i + step) % count) for i in range(count)]


def pair(count):
    return [(i, i ^ 1) for i in range(count)]


def outward(count):
    return [(i, (i + (1 if i % 2 else -1)) % count) for i in range(count)]


def aside(count):
    return [(i, (i + (2 if i % 2 else -2)) % count) for i in range(count)]


def onward(count):
    return [(i, (i + (-2 if i % 2 else 2)) % count) for i in range(count)]


def table_kernel(operators, odd_ref, own_1, own_0, joined, table):
    odd = odd_ref[0]
    each = 2 * operators
    wide = table.shape[1] // 9 + 1
    last = joined.shape[0]
    parts = (
        joined[last - INFO :, :],
        own_0[own_0.shape[0] - INFO :, :],
        own_1[own_1.shape[0] - INFO :, :],
        joined[last - 2 * INFO : last - INFO, :],
    )
    info = jnp.concatenate([part.astype(jnp.float32)[:each, :wide] for part in parts], axis=0).astype(jnp.int32)
    slots = info.shape[1] - 1
    shape = table.shape
    row = lax.broadcasted_iota(jnp.int32, shape, 0)
    place = lax.broadcasted_iota(jnp.int32, shape, 1)
    slot = place // 9
    band = place - 9 * slot
    band_y = band // 3
    band_x = band - 3 * band_y
    fine_x = row & 1
    fine_y = row // each - 1
    off = jnp.zeros(shape, jnp.int32)
    for k in range(slots):
        off = off + jnp.where(slot == k, info[:, k : k + 1], 0)
    off_x = jnp.where(off >= 6, 2, jnp.where(off >= 3, 1, 0))
    near_x = fine_x + off_x - 1
    near_y = fine_y + (off - 3 * off_x - 1) * (1 - 2 * odd)
    place_x = band_x - (((near_x - 1) >> 1) - (fine_x >> 1) + 1)
    place_y = band_y - (((near_y - 1) >> 1) - (fine_y >> 1) + 1)
    corner_x = jnp.where((near_x & 1) == 1, place_x, 1 - place_x)
    corner_y = jnp.where((near_y & 1) == 1, place_y, 1 - place_y)
    good = (place_x >= 0) & (place_x < 2) & (place_y >= 0) & (place_y < 2)
    good = good & (slot < info[:, slots:])
    side = jnp.where(near_y < 0, 2 * HALF, jnp.where(near_y < 2, 0, HALF))
    index = side + (near_x + 1) * 8 + ((near_y & 1) ^ odd) * 4 + 2 * corner_x + corner_y
    table[...] = jnp.where(good, index, ZERO)


def table_row(operators, role, operator, x):
    return (role * operators + operator) * 2 + x


def fill(flat, first, low, mid, high):
    for piece, start in ((low, 0), (mid, 8), (high, 24)):
        for x in range(piece.shape[0]):
            for y in range(2):
                flat[pl.ds(first + start + 8 * x + 4 * y, 4)] = piece[x, y]


def pack_kernel(odd_ref, off, count, a_own, *outs):
    operators, _, _, slots = off.shape
    block = a_own.shape[-1]
    odd = odd_ref[0]
    row = lax.broadcasted_iota(jnp.int32, (INFO, block), 0)
    lane = lax.broadcasted_iota(jnp.int32, (INFO, block), 1)
    for out, y in zip(outs, (1 - odd, odd)):
        for x in range(2):
            for k in range(slots):
                out[pl.ds((x * slots + k) * block, block), :] = a_own[0, x, y, k]
        line = jnp.zeros((INFO, block), jnp.int32)
        for s in range(operators):
            for x in range(2):
                here = row == 2 * s + x
                line = jnp.where(here & (lane == slots), count[s, x, y], line)
                for k in range(slots):
                    line = jnp.where(here & (lane == k), off[s, x, y, k], line)
        out[pl.ds(2 * slots * block, INFO), :] = line.astype(jnp.float32).astype(out.dtype)
    for s in range(1, operators):
        for out, y in zip(outs[2 * s : 2 * s + 2], (1 - odd, odd)):
            for x in range(2):
                out[x, 0] = a_own[s, x, y]


def rows_kernel(own, near, low, high):
    for out, x in ((low, 0), (high, 1)):
        out[0, 0:2] = own[x]
        out[0, 2:4] = near[x]


def join_kernel(near, far, out):
    count = near.shape[0] - INFO
    out[pl.ds(0, count), :] = near[pl.ds(0, count), :]
    out[pl.ds(count, count), :] = far[pl.ds(0, count), :]
    out[pl.ds(2 * count, INFO), :] = near[pl.ds(count, INFO), :]
    out[pl.ds(2 * count + INFO, INFO), :] = far[pl.ds(count, INFO), :]


def joined_row(joined, side, x):
    block = joined.shape[1]
    slots = joined.shape[0] // (4 * block)
    first = (side * 2 + x) * slots
    return [joined.at[pl.ds((first + k) * block, block), :] for k in range(slots)]


def row_of(array):
    return [array.at[k] for k in range(array.shape[0])]


def fine_row(table, number, flat, blocks, w_ref):
    slots = len(blocks)
    left = jnp.concatenate([ref[...] for ref in blocks], axis=1)
    for band_y in range(3):
        right = jnp.concatenate(
            [
                jnp.concatenate(
                    [flat[table[number, k * 9 + band_y * 3 + band_x]] for band_x in range(3)], axis=1
                )
                for k in range(slots)
            ],
            axis=0,
        )
        w_ref[band_y] = jnp.dot(left, right, preferred_element_type=jnp.float32).astype(w_ref.dtype)


def coarse_column(odd, pieces, w_refs, fine_rows, lag_y, corner_x):
    lefts, rights = [], []
    for fine_x in fine_rows:
        for role in range(4):
            fine_y = role - 1
            band_y = lag_y - (fine_y // 2 + 1)
            if 0 <= band_y < 3:
                corner_y = 1 if role in (FAR, NEAR) else 0
                lefts.append(pieces[role][fine_x, (fine_y & 1) ^ odd, corner_x + corner_y])
                rights.append(w_refs[role][fine_x, band_y])
    left = jnp.concatenate(lefts, axis=0)
    right = jnp.concatenate(rights, axis=0)
    return lax.dot_general(left, right, (((0,), (0,)), ((), ())), preferred_element_type=jnp.float32)


def edges(odd, pieces, w_refs, outs):
    block = outs[0].shape[-1]
    for fine_x, out in enumerate(outs):
        for lag_y in range(5):
            total = coarse_column(odd, pieces, w_refs, (fine_x,), lag_y, 2)
            for lag_x in range(3):
                out[lag_x, lag_y] = total[:, lag_x * block : (lag_x + 1) * block].astype(out.dtype)


def near_own_kernel(operators, table, odd_ref, a_own, p_own, p_near, low, high, flat, w_ref):
    odd = odd_ref[0]
    fill(flat, 0, low.at[:, 0:2], p_own, high.at[:, 0:2])
    fill(flat, HALF, low.at[:, 2:4], p_near, high.at[:, 2:4])
    flat[ZERO] = jnp.zeros(flat.shape[1:], flat.dtype)
    for s in range(operators):
        for x in range(2):
            fine_row(table, table_row(operators, OWN_1, s, x), flat, row_of(a_own.at[s, x, 1 - odd]), w_ref.at[s, x])


def near_kernel(operators, operator, table, flat, a_pair, w_ref):
    for x in range(2):
        fine_row(table, table_row(operators, NEAR, operator, x), flat, joined_row(a_pair, 0, x), w_ref.at[x])


def far_first_kernel(
    operators, table, odd_ref, a_own, a_pair, w_own, w_near, p_own, p_near, p_far, far_low, far_high, held, low, high, flat, w_own_0, w_far
):
    odd = odd_ref[0]
    fill(flat, 2 * HALF, far_low, p_far, far_high)
    for x in range(2):
        fine_row(table, table_row(operators, FAR, 0, x), flat, joined_row(a_pair, 1, x), w_far.at[x])
        fine_row(table, table_row(operators, OWN_0, 0, x), flat, row_of(a_own.at[0, x, odd]), w_own_0.at[x])
    edges(odd, (p_far, p_own, p_own, p_near), (w_far, w_own_0, w_own.at[0], w_near), (low, high))


def own_0_kernel(operators, operator, table, odd_ref, a_own, flat, w_ref):
    odd = odd_ref[0]
    for x in range(2):
        fine_row(table, table_row(operators, OWN_0, operator, x), flat, row_of(a_own.at[operator, x, odd]), w_ref.at[x])


def sides_kernel(
    operators, operator, table, odd_ref, a_near, a_far, flat, w_own, w_own_0, p_own, p_near, p_far, low, high, w_near, w_far
):
    odd = odd_ref[0]
    for x in range(2):
        fine_row(table, table_row(operators, NEAR, operator, x), flat, row_of(a_near.at[x, 0]), w_near.at[x])
        fine_row(table, table_row(operators, FAR, operator, x), flat, row_of(a_far.at[x, 0]), w_far.at[x])
    edges(odd, (p_far, p_own, p_own, p_near), (w_far, w_own_0, w_own.at[operator], w_near), (low, high))


def centre_kernel(operator, odd_ref, p_own, p_near, p_far, w_far, w_own_0, w_own, w_near, out):
    block = out.shape[-1]
    odd = odd_ref[0]
    for lag_y in range(5):
        total = coarse_column(
            odd, (p_far, p_own, p_own, p_near), (w_far, w_own_0, w_own.at[operator], w_near), (0, 1), lag_y, 0
        )
        for lag_x in range(3):
            out[lag_x, lag_y] = total[:, lag_x * block : (lag_x + 1) * block]


def final_kernel(odd_ref, *refs):
    out = refs[-1]
    odd = odd_ref[0]
    for operator in range(out.shape[0]):
        own, low, high = refs[3 * operator : 3 * operator + 3]
        for lag_x in range(5):
            for lag_y in range(5):
                total = None
                for part, first in ((low, 0), (own, 1), (high, 2)):
                    if 0 <= lag_x - first < 3:
                        term = part[lag_x - first, lag_y].astype(jnp.float32)
                        total = term if total is None else total + term
                place = 5 * lag_x + lag_y + odd * (4 - 2 * lag_y)
                out[operator, 0, 0, place] = total.astype(out.dtype)


def per_device(a_vals, a_off, a_count, p_vals):
    operators, _, _, slots, block, _ = a_vals.shape
    cols = lax.axis_size("col")
    rows = lax.axis_size("row")
    odd = (lax.axis_index("col") & 1).astype(jnp.int32)
    up, down = ring(rows, 1), ring(rows, -1)
    near_way, far_way, on_way, aside_way = pair(cols), outward(cols), onward(cols), aside(cols)

    smem = pl.BlockSpec(memory_space=pltpu.SMEM)
    vmem = pl.BlockSpec(memory_space=pltpu.VMEM)
    bf16, f32 = jnp.bfloat16, jnp.float32
    odd_arg = odd[None]
    flat_shape = jax.ShapeDtypeStruct((ZERO + 1, block, block), bf16)
    w_shape = jax.ShapeDtypeStruct((2, 3, block, 3 * block), bf16)
    part_shape = jax.ShapeDtypeStruct((3, 5, block, block), bf16)

    def call(kernel, in_specs, out_shape, products, name, scratch=(), aliases=None, limit=VMEM_LIMIT):
        single = not isinstance(out_shape, list)
        return pl.pallas_call(
            kernel,
            in_specs=in_specs,
            out_specs=vmem if single else [vmem] * len(out_shape),
            out_shape=out_shape,
            scratch_shapes=list(scratch),
            input_output_aliases=aliases or {},
            compiler_params=pltpu.CompilerParams(vmem_limit_bytes=limit),
            cost_estimate=pl.CostEstimate(flops=products, bytes_accessed=1024, transcendentals=0),
            name=name,
        )

    p_near = lax.ppermute(p_vals, "col", near_way)
    column = jax.ShapeDtypeStruct((2 * slots * block + INFO, block), bf16)
    later = jax.ShapeDtypeStruct((2, 1, slots, block, block), bf16)
    own_1, own_0, *later = call(
        pack_kernel, [smem] * 3 + [vmem], [column] * 2 + [later] * (2 * operators - 2), 1, "pack"
    )(odd_arg, a_off, a_count, a_vals)
    moved = lax.ppermute(own_0, "col", aside_way)
    joined = jax.ShapeDtypeStruct((4 * slots * block + 2 * INFO, block), bf16)
    joined = call(join_kernel, [vmem, vmem], joined, 1, "join")(own_1, moved)
    p_near, joined = lax.optimization_barrier((p_near, joined))
    p_far = lax.ppermute(p_near, "col", on_way)
    from_pair = lax.ppermute(joined, "col", near_way)
    a_near, a_far = [None], [None]
    row_shape = jax.ShapeDtypeStruct((1, 4, 4, block, block), bf16)
    low, high = call(rows_kernel, [vmem, vmem], [row_shape, row_shape], 1, "rows")(p_vals, p_near)
    from_low = lax.ppermute(high, "row", up)
    from_high = lax.ppermute(low, "row", down)
    table = call(
        functools.partial(table_kernel, operators),
        [smem] + [vmem] * 3,
        jax.ShapeDtypeStruct((operators * 8, slots * 9), jnp.int32),
        1,
        "table",
    )(odd_arg, own_1, own_0, from_pair)
    from_pair, later = lax.optimization_barrier((from_pair, later))
    far_low = lax.ppermute(p_far[1:2], "row", up)
    far_high = lax.ppermute(p_far[0:1], "row", down)
    a_near += [lax.ppermute(send, "col", near_way) for send in later[0::2]]
    a_far += [lax.ppermute(send, "col", far_way) for send in later[1::2]]

    flat, w_own = call(
        functools.partial(near_own_kernel, operators),
        [smem, smem] + [vmem] * 5,
        [flat_shape, jax.ShapeDtypeStruct((operators,) + w_shape.shape, bf16)],
        360,
        "near_own",
    )(table, odd_arg, a_vals, p_vals, p_near, from_low, from_high)

    finals = []
    for s in range(operators):
        if s == 0:
            w_near = call(functools.partial(near_kernel, operators, s), [smem, vmem, vmem], w_shape, 90, "near")(
                table, flat, from_pair
            )
            low, high, flat, w_own_0, w_far = call(
                functools.partial(far_first_kernel, operators),
                [smem, smem] + [vmem] * 10,
                [part_shape, part_shape, flat_shape, w_shape, w_shape],
                300,
                "far_first",
                aliases={11: 2},
            )(table, odd_arg, a_vals, from_pair, w_own, w_near, p_vals, p_near, p_far, far_low, far_high, flat)
        else:
            w_own_0 = call(functools.partial(own_0_kernel, operators, s), [smem, smem, vmem, vmem], w_shape, 90, "own_0")(
                table, odd_arg, a_vals, flat
            )
            low, high, w_near, w_far = call(
                functools.partial(sides_kernel, operators, s),
                [smem, smem] + [vmem] * 8,
                [part_shape, part_shape, w_shape, w_shape],
                200,
                "sides",
            )(table, odd_arg, a_near[s], a_far[s], flat, w_own, w_own_0, p_vals, p_near, p_far)
        from_low = lax.ppermute(high, "row", up)
        from_high = lax.ppermute(low, "row", down)
        centre = call(
            functools.partial(centre_kernel, s),
            [smem] + [vmem] * 7,
            jax.ShapeDtypeStruct((3, 5, block, block), f32),
            144,
            "centre",
        )(odd_arg, p_vals, p_near, p_far, w_far, w_own_0, w_own, w_near)
        finals += [centre, from_low, from_high]
    return call(
        final_kernel,
        [smem] + [vmem] * len(finals),
        jax.ShapeDtypeStruct((operators, 1, 1, 25, block, block), bf16),
        1,
        "final",
    )(odd_arg, *finals)


def solution(mesh):
    placed = (
        P(None, "row", "col", None, None, None),
        P(None, "row", "col", None),
        P(None, "row", "col"),
        P("row", "col", None, None, None),
    )
    return jax.shard_map(
        per_device,
        mesh=mesh,
        in_specs=placed,
        out_specs=P(None, "row", "col", None, None, None),
        check_vma=False,
    )
```

time: 72.9 us -> 74.7 us (1.025)
  waiting for transfers between devices: 27.5 us -> 37.8 us
  other arithmetic: 5.21 us -> 0 us
  starting transfers between devices: 21.2 us -> 19.8 us
  local copies, waits for them, and re-layouts: 3.91 us -> 2.73 us
    ppermute x6 -> x4, waiting for transfers between devices: 6.09 us -> 18.9 us  [the longest x1 12.1 us: per_device(): from_pair = lax.ppermute(joined, 'col', near_way)]
    ppermute x1, waiting for transfers between devices: 6.42 us -> 0.01 us  [per_device(): p_far = lax.ppermute(p_near, 'col', on_way)]
    ppermute x1, waiting for transfers between devices: 0.01 us -> 2.99 us  [per_device(): far_low = lax.ppermute(p_far[1:2], 'row', up)]
    ppermute x1, waiting for transfers between devices: 2.34 us -> 0.01 us  [per_device(): p_near = lax.ppermute(p_vals, 'col', near_way)]
    ppermute x3, starting transfers between devices: 1.93 us -> 0.28 us  [per_device(): from_low = lax.ppermute(high, 'row', up)]
    ppermute x3, starting transfers between devices: 3.45 us -> 5.1 us  [per_device(): from_high = lax.ppermute(low, 'row', down)]
    ppermute x1, starting transfers between devices: 1.76 us -> 0.19 us  [per_device(): p_far = lax.ppermute(p_near, 'col', on_way)]
    select_n x2 -> x0, other arithmetic: 1.46 us -> none  [the longest x1 1.36 us: per_device(): mirrored = jnp.where(odd == 1, info[:, :, ::-1], info)]
  transfers between devices with their start and end apart: 16 -> 14, of which waited for: 5 -> 7; matrix products, arithmetic and copies ran while one was open for 9% -> 0% of each run, Pallas kernels for 18% -> 17%
where the time goes in v4:
time: 74.7 us; the launch traced here: 74.4 us
  waiting for transfers between devices  37.8 us (51%)
  starting transfers between devices  19.8 us (27%)
  Pallas kernels  13.9 us (19%)
  local copies, waits for them, and re-layouts  2.73 us (4%)
    ppermute x3, waiting for transfers between devices, per_device(): from_low = lax.ppermute(high, 'row', up)  13.8 us
    ppermute x1, waiting for transfers between devices, per_device(): from_pair = lax.ppermute(joined, 'col', near_way)  12.1 us
    ppermute x1, waiting for transfers between devices, per_device(): moved = lax.ppermute(own_0, 'col', aside_way)  6.78 us
    ppermute x3, starting transfers between devices, per_device(): from_high = lax.ppermute(low, 'row', down)  5.1 us
    ppermute x1, starting transfers between devices, per_device(): a_far += [lax.ppermute(send, 'col', far_way) for send in later[1::2]]  4.15 us
    ppermute x1, starting transfers between devices, per_device(): moved = lax.ppermute(own_0, 'col', aside_way)  3.65 us
    ppermute x1, waiting for transfers between devices, per_device(): far_low = lax.ppermute(p_far[1:2], 'row', up)  2.99 us
    ppermute x1, starting transfers between devices, per_device(): p_near = lax.ppermute(p_vals, 'col', near_way)  2.94 us
  transfers between devices with their start and end apart: 14, of which 7 were waited for; matrix products, arithmetic and copies ran while one was open for 0% of the time, Pallas kernels for 17%

profile of v4, /device:TPU:0, one launch (start us, length us, event | category | flops | bytes accessed | tf_op | source)
XLA Modules:
  0.0 74.4 jit_solution(10433911431005841661)
XLA Ops:
  0.0 2.9 %collective-permute-start = (bf16[2,2,4,128,128]{4,3,2,1,0:T(8,128)(2,1)}, bf16[2,2,4,128,128]{4,3,2,1,0:T(8,128)(2,1)S(1)}, u32[]{:S(2)}, u32[]{:S(2)}) collective-permute-start(bf16[2,2,4,128,128]{4,3,2,1,0:T(8,128)(2,1)} %p_own.9), channel_id=1, source_target_pairs={{0,1},{1,0},{2,3},{3,2},{4,5},{5,4},{6,7},{7,6},{8,9},{9,8},{10,11... | collective-permute-start | bytes 1572872 | tf_op jit(solution)/shard_map/ppermute | solution.py:275
  2.9 0.0 copy-start
  2.9 1.3 %copy-done = bf16[2,2,2,5,128,128]{5,4,3,2,1,0:T(8,128)(2,1)S(1)} copy-done((bf16[2,2,2,5,128,128]{5,4,3,2,1,0:T(8,128)(2,1)S(1)}, bf16[2,2,2,5,128,128]{5,4,3,2,1,0:T(8,128)(2,1)}, u32[]{:S(2)}) %copy-start) | copy-done | bytes 1310744
  4.3 0.0 copy-start.3
  4.3 0.7 copy-done.3
  4.9 0.0 copy-start.4
  4.9 0.7 copy-done.4
  5.6 0.7 pack.1
  6.4 3.7 %collective-permute-start.1 = (bf16[1296,128]{1,0:T(8,128)(2,1)S(1)}, bf16[1296,128]{1,0:T(8,128)(2,1)S(1)}, u32[]{:S(2)}, u32[]{:S(2)}) collective-permute-start(bf16[1296,128]{1,0:T(8,128)(2,1)S(1)} %get-tuple-element.28.own_0), channel_id=1, source_target_pairs={{0,6},{1,3},{2,0},{3,5},{4,2},{5,7},{6,4},{7,1},{8,14},{9,11},{10,... | collective-permute-start | bytes 995336 | tf_op jit(solution)/shard_map/ppermute | solution.py:281
  10.0 6.8 %collective-permute-done.1.far = bf16[1296,128]{1,0:T(8,128)(2,1)S(1)} collective-permute-done((bf16[1296,128]{1,0:T(8,128)(2,1)S(1)}, bf16[1296,128]{1,0:T(8,128)(2,1)S(1)}, u32[]{:S(2)}, u32[]{:S(2)}) %collective-permute-start.1) | collective-permute-done | bytes 331808 | tf_op jit(solution)/shard_map/ppermute | solution.py:281
  16.8 0.0 copy-start.1
  16.8 0.0 collective-permute-done.near.p_near
  16.9 1.3 %collective-permute-start.3 = (bf16[2592,128]{1,0:T(8,128)(2,1)S(1)}, bf16[2592,128]{1,0:T(8,128)(2,1)S(1)}, u32[]{:S(2)}, u32[]{:S(2)}) collective-permute-start(bf16[2592,128]{1,0:T(8,128)(2,1)S(1)} %join.1), channel_id=1, source_target_pairs={{0,1},{1,0},{2,3},{3,2},{4,5},{5,4},{6,7},{7,6},{8,9},{9,8},{10,11... | collective-permute-start | bytes 1990664 | tf_op jit(solution)/shard_map/ppermute | solution.py:286
  18.2 0.2 collective-permute-start.2
  18.4 0.0 copy-done.2
  18.4 0.1 rows.1
  18.5 0.1 collective-permute-start.4
  18.5 1.7 %collective-permute-start.5 = (bf16[1,4,4,128,128]{4,3,2,1,0:T(8,128)(2,1)S(1)}, bf16[1,4,4,128,128]{4,3,2,1,0:T(8,128)(2,1)S(1)}, u32[]{:S(2)}, u32[]{:S(2)}) collective-permute-start(bf16[1,4,4,128,128]{4,3,2,1,0:T(8,128)(2,1)S(1)} %get-tuple-element.35), channel_id=1, source_target_pairs={{0,24},{8,0},{16,8},{24,16},{1,25},{9,1},{17,9},{25,17},{2,26},{10... | collective-permute-start | bytes 1572872 | tf_op jit(solution)/shard_map/ppermute | solution.py:291
  20.3 12.1 %collective-permute-done.3.joined.a_pair = bf16[2592,128]{1,0:T(8,128)(2,1)S(1)} collective-permute-done((bf16[2592,128]{1,0:T(8,128)(2,1)S(1)}, bf16[2592,128]{1,0:T(8,128)(2,1)S(1)}, u32[]{:S(2)}, u32[]{:S(2)}) %collective-permute-start.3) | collective-permute-done | bytes 663584 | tf_op jit(solution)/shard_map/ppermute | solution.py:286
  32.4 1.6 %collective-permute-start.10 = (bf16[2,1,5,128,128]{4,3,2,1,0:T(8,128)(2,1)S(1)}, bf16[2,1,5,128,128]{4,3,2,1,0:T(8,128)(2,1)S(1)}, u32[]{:S(2)}, u32[]{:S(2)}) collective-permute-start(bf16[2,1,5,128,128]{4,3,2,1,0:T(8,128)(2,1)S(1)} %get-tuple-element.42), channel_id=1, source_target_pairs={{0,1},{1,0},{2,3},{3,2},{4,5},{5,4},{6,7},{7,6},{8,9},{9,8},{10,11... | collective-permute-start | bytes 983048 | tf_op jit(solution)/shard_map/ppermute | solution.py:302
  34.0 4.1 %collective-permute-start.11 = (bf16[2,1,5,128,128]{4,3,2,1,0:T(8,128)(2,1)S(1)}, bf16[2,1,5,128,128]{4,3,2,1,0:T(8,128)(2,1)S(1)}, u32[]{:S(2)}, u32[]{:S(2)}) collective-permute-start(bf16[2,1,5,128,128]{4,3,2,1,0:T(8,128)(2,1)S(1)} %get-tuple-element.43), channel_id=1, source_target_pairs={{0,7},{1,2},{2,1},{3,4},{4,3},{5,6},{6,5},{7,0},{8,15},{9,10},{10,... | collective-permute-start | bytes 983048 | tf_op jit(solution)/shard_map/ppermute | solution.py:303
  38.1 0.0 collective-permute-done.2.p_far
  38.2 0.1 collective-permute-start.7
  38.2 0.0 collective-permute-done.4.low
  38.3 0.5 collective-permute-start.6
  38.7 0.1 table.1
  38.9 0.0 collective-permute-done.5.high
  38.9 0.0 copy-done.1
  38.9 2.2 %near_own.1 = (bf16[97,128,128]{2,1,0:T(8,128)(2,1)S(1)}, bf16[2,2,3,128,384]{4,3,2,1,0:T(8,128)(2,1)S(1)}) custom-call(s32[16,45]{1,0:T(8,128)S(1)} %table.1, s32[1]{0:T(128)} %bitcast.odd_ref, bf16[2,2,2,5,128,128]{5,4,3,2,1,0:T(8,128)(2,1)S(1)} %copy-done.1, bf16[2,2,4,128,128]{4,3,2,1,0:T(8,128)(2,1)S(1)} %copy-done.2, ...), custom_call_target="tpu_custom_call" | custom-call | flops 360 | bytes 1024 | tf_op jit(solution)/shard_map/near_own/pallas_call | solution.py:305
  41.0 1.4 %near.1.w_near = bf16[2,3,128,384]{3,2,1,0:T(8,128)(2,1)S(1)} custom-call(s32[16,45]{1,0:T(8,128)S(1)} %table.1, bf16[97,128,128]{2,1,0:T(8,128)(2,1)S(1)} %get-tuple-element.37.flat.held, bf16[2592,128]{1,0:T(8,128)(2,1)S(1)} %collective-permute-done.3.joined.a_pair), custom_call_target="tpu_custom_call" | custom-call | flops 90 | bytes 1024 | tf_op jit(solution)/shard_map/near/pallas_call | solution.py:316
  42.5 1.4 %collective-permute-done.7.far_high = bf16[1,2,4,128,128]{4,3,2,1,0:T(8,128)(2,1)S(1)} collective-permute-done((bf16[1,2,4,128,128]{4,3,2,1,0:T(8,128)(2,1)S(1)}, bf16[1,2,4,128,128]{4,3,2,1,0:T(8,128)(2,1)S(1)}, u32[]{:S(2)}, u32[]{:S(2)}) %collective-permute-start.7) | collective-permute-done | bytes 262176 | tf_op jit(solution)/shard_map/ppermute | solution.py:301
  43.9 3.0 %collective-permute-done.6.far_low = bf16[1,2,4,128,128]{4,3,2,1,0:T(8,128)(2,1)S(1)} collective-permute-done((bf16[1,2,4,128,128]{4,3,2,1,0:T(8,128)(2,1)S(1)}, bf16[1,2,4,128,128]{4,3,2,1,0:T(8,128)(2,1)S(1)}, u32[]{:S(2)}, u32[]{:S(2)}) %collective-permute-start.6) | collective-permute-done | bytes 262176 | tf_op jit(solution)/shard_map/ppermute | solution.py:300
  46.9 2.6 %far_first.1 = (bf16[3,5,128,128]{3,2,1,0:T(8,128)(2,1)S(1)}, bf16[3,5,128,128]{3,2,1,0:T(8,128)(2,1)S(1)}, bf16[97,128,128]{2,1,0:T(8,128)(2,1)S(1)}, bf16[2,3,...) custom-call(s32[16,45]{1,0:T(8,128)S(1)} %table.1, s32[1]{0:T(128)} %bitcast.odd_ref, ...), custom_call_target="tpu_custom_call", output_to_operand_aliasing={{2}: (11, {})} | custom-call | flops 300 | bytes 1024 | tf_op jit(solution)/shard_map/far_first/pallas_call | solution.py:319
  49.5 0.2 collective-permute-start.8
  49.7 1.6 %collective-permute-start.9 = (bf16[3,5,128,128]{3,2,1,0:T(8,128)(2,1)S(1)}, bf16[3,5,128,128]{3,2,1,0:T(8,128)(2,1)S(1)}, u32[]{:S(2)}, u32[]{:S(2)}) collective-permute-start(bf16[3,5,128,128]{3,2,1,0:T(8,128)(2,1)S(1)} %get-tuple-element.41), channel_id=1, source_target_pairs={{0,24},{8,0},{16,8},{24,16},{1,25},{9,1},{17,9},{25,17},{2,26},{10... | collective-permute-start | bytes 1474568 | tf_op jit(solution)/shard_map/ppermute | solution.py:339
  51.3 1.4 %own_0.1.w_own_0 = bf16[2,3,128,384]{3,2,1,0:T(8,128)(2,1)S(1)} custom-call(s32[16,45]{1,0:T(8,128)S(1)} %table.1, s32[1]{0:T(128)} %bitcast.odd_ref, bf16[2,2,2,5,128,128]{5,4,3,2,1,0:T(8,128)(2,1)S(1)} %copy-done.1, bf16[97,128,128]{2,1,0:T(8,128)(2,1)S(1)} %get-tuple-element.44.flat), custom_call_target="tpu_custom_call" | custom-call | flops 90 | bytes 1024 | tf_op jit(solution)/shard_map/own_0/pallas_call | solution.py:328
  52.8 0.0 collective-permute-done.10.a_near
  52.8 0.0 collective-permute-done.11.a_far
  52.8 2.6 %sides.1 = (bf16[3,5,128,128]{3,2,1,0:T(8,128)(2,1)S(1)}, bf16[3,5,128,128]{3,2,1,0:T(8,128)(2,1)S(1)}, bf16[2,3,128,384]{3,2,1,0:T(8,128)(2,1)S(1)}, bf16[2,3,128,384]{3,2,1,0:T(8,128)(2,1)S(1)}) custom-call(s32[16,45]{1,0:T(8,128)S(1)} %table.1, s32[1]{0:T(128)} %bitcast.odd_ref, bf16[2,1,5,128,128]{4,3,2,1,0:T(8,128)(2,1)S(1)} %collective-permute-done.10.a_near, ...), custom_call_target="tpu_custom_call" | custom-call | flops 200 | bytes 1024 | tf_op jit(solution)/shard_map/sides/pallas_call | solution.py:331
  55.4 0.1 collective-permute-start.12
  55.4 1.7 %collective-permute-start.13 = (bf16[3,5,128,128]{3,2,1,0:T(8,128)(2,1)S(1)}, bf16[3,5,128,128]{3,2,1,0:T(8,128)(2,1)S(1)}, u32[]{:S(2)}, u32[]{:S(2)}) collective-permute-start(bf16[3,5,128,128]{3,2,1,0:T(8,128)(2,1)S(1)} %get-tuple-element.48), channel_id=1, source_target_pairs={{0,24},{8,0},{16,8},{24,16},{1,25},{9,1},{17,9},{25,17},{2,26},{10... | collective-permute-start | bytes 1474568 | tf_op jit(solution)/shard_map/ppermute | solution.py:339
  57.2 0.6 centre.2.refs_0_
  57.8 0.6 centre.3.refs_3_
  58.4 3.9 %collective-permute-done.8.refs_1_ = bf16[3,5,128,128]{3,2,1,0:T(8,128)(2,1)S(1)} collective-permute-done((bf16[3,5,128,128]{3,2,1,0:T(8,128)(2,1)S(1)}, bf16[3,5,128,128]{3,2,1,0:T(8,128)(2,1)S(1)}, u32[]{:S(2)}, u32[]{:S(2)}) %collective-permute-start.8) | collective-permute-done | bytes 491552 | tf_op jit(solution)/shard_map/ppermute | solution.py:338
  62.3 0.7 collective-permute-done.9.refs_2_
  63.0 9.9 %collective-permute-done.12.refs_4_ = bf16[3,5,128,128]{3,2,1,0:T(8,128)(2,1)S(1)} collective-permute-done((bf16[3,5,128,128]{3,2,1,0:T(8,128)(2,1)S(1)}, bf16[3,5,128,128]{3,2,1,0:T(8,128)(2,1)S(1)}, u32[]{:S(2)}, u32[]{:S(2)}) %collective-permute-start.12) | collective-permute-done | bytes 491552 | tf_op jit(solution)/shard_map/ppermute | solution.py:338
  72.9 0.0 collective-permute-done.13.refs_5_
  72.9 1.5 %final.1 = bf16[2,1,1,25,128,128]{5,4,3,2,1,0:T(8,128)(2,1)} custom-call(s32[1]{0:T(128)} %bitcast.odd_ref, f32[3,5,128,128]{3,2,1,0:T(8,128)S(1)} %centre.2.refs_0_, bf16[3,5,128,128]{3,2,1,0:T(8,128)(2,1)S(1)} %collective-permute-done.8.refs_1_, bf16[3,5,128,128]{3,2,1,0:T(8,128)(2,1)S(1)} %collective-permute-done.9.refs_2_, ...), custom_call_target="tpu_custom_call" | custom-call | flops 1 | bytes 1024 | tf_op jit(solution)/shard_map/final/pallas_call | solution.py:348
  (3 shorter events, 0.1 us)
Async XLA Ops:
  0.0 16.8 %collective-permute-start = (bf16[2,2,4,128,128]{4,3,2,1,0:T(8,128)(2,1)}, bf16[2,2,4,128,128]{4,3,2,1,0:T(8,128)(2,1)S(1)}, u32[]{:S(2)}, u32[]{:S(2)}) collective-permute-start(bf16[2,2,4,128,128]{4,3,2,1,0:T(8,128)(2,1)} %p_own.9), channel_id=1, source_target_pairs={{0,1},{1,0},{2,3},{3,2},{4,5},{5,4},{6,7},{7,6},{8,9},{9,8},{10,11... | collective-permute-start | bytes 1572872 | tf_op jit(solution)/shard_map/ppermute | solution.py:275
  2.9 1.3 %copy-start = (bf16[2,2,2,5,128,128]{5,4,3,2,1,0:T(8,128)(2,1)S(1)}, bf16[2,2,2,5,128,128]{5,4,3,2,1,0:T(8,128)(2,1)}, u32[]{:S(2)}) copy-start(bf16[2,2,2,5,128,128]{5,4,3,2,1,0:T(8,128)(2,1)} %a_own.7) | copy-start | bytes 3932164
  4.3 0.7 copy-start.3
  4.9 0.7 copy-start.4
  5.6 12.8 %copy-start.2 = (bf16[2,2,4,128,128]{4,3,2,1,0:T(8,128)(2,1)S(1)}, bf16[2,2,4,128,128]{4,3,2,1,0:T(8,128)(2,1)}, u32[]{:S(2)}) copy-start(bf16[2,2,4,128,128]{4,3,2,1,0:T(8,128)(2,1)} %p_own.9) | copy-start | bytes 1572868
  6.4 10.4 %collective-permute-start.1 = (bf16[1296,128]{1,0:T(8,128)(2,1)S(1)}, bf16[1296,128]{1,0:T(8,128)(2,1)S(1)}, u32[]{:S(2)}, u32[]{:S(2)}) collective-permute-start(bf16[1296,128]{1,0:T(8,128)(2,1)S(1)} %get-tuple-element.28.own_0), channel_id=1, source_target_pairs={{0,6},{1,3},{2,0},{3,5},{4,2},{5,7},{6,4},{7,1},{8,14},{9,11},{10,... | collective-permute-start | bytes 995336 | tf_op jit(solution)/shard_map/ppermute | solution.py:281
  16.8 22.0 %copy-start.1 = (bf16[2,2,2,5,128,128]{5,4,3,2,1,0:T(8,128)(2,1)S(1)}, bf16[2,2,2,5,128,128]{5,4,3,2,1,0:T(8,128)(2,1)}, u32[]{:S(2)}) copy-start(bf16[2,2,2,5,128,128]{5,4,3,2,1,0:T(8,128)(2,1)} %a_own.7) | copy-start | bytes 3932164
  16.9 15.5 %collective-permute-start.3 = (bf16[2592,128]{1,0:T(8,128)(2,1)S(1)}, bf16[2592,128]{1,0:T(8,128)(2,1)S(1)}, u32[]{:S(2)}, u32[]{:S(2)}) collective-permute-start(bf16[2592,128]{1,0:T(8,128)(2,1)S(1)} %join.1), channel_id=1, source_target_pairs={{0,1},{1,0},{2,3},{3,2},{4,5},{5,4},{6,7},{7,6},{8,9},{9,8},{10,11... | collective-permute-start | bytes 1990664 | tf_op jit(solution)/shard_map/ppermute | solution.py:286
  18.2 19.9 %collective-permute-start.2 = (bf16[2,2,4,128,128]{4,3,2,1,0:T(8,128)(2,1)S(1)}, bf16[2,2,4,128,128]{4,3,2,1,0:T(8,128)(2,1)S(1)}, u32[]{:S(2)}, u32[]{:S(2)}) collective-permute-start(bf16[2,2,4,128,128]{4,3,2,1,0:T(8,128)(2,1)S(1)} %collective-permute-done.near.p_near), channel_id=1, source_target_pairs={{0,2},{1,7},{2,4},{3,1},{4,6},{5,3},{6,0},{7,5},{8,10},{9,15},{10,... | collective-permute-start | bytes 1572872 | tf_op jit(solution)/shard_map/ppermute | solution.py:285
  18.5 19.8 %collective-permute-start.4 = (bf16[1,4,4,128,128]{4,3,2,1,0:T(8,128)(2,1)S(1)}, bf16[1,4,4,128,128]{4,3,2,1,0:T(8,128)(2,1)S(1)}, u32[]{:S(2)}, u32[]{:S(2)}) collective-permute-start(bf16[1,4,4,128,128]{4,3,2,1,0:T(8,128)(2,1)S(1)} %get-tuple-element.34), channel_id=1, source_target_pairs={{0,8},{8,16},{16,24},{24,0},{1,9},{9,17},{17,25},{25,1},{2,10},{10... | collective-permute-start | bytes 1572872 | tf_op jit(solution)/shard_map/ppermute | solution.py:290
  18.5 20.3 %collective-permute-start.5 = (bf16[1,4,4,128,128]{4,3,2,1,0:T(8,128)(2,1)S(1)}, bf16[1,4,4,128,128]{4,3,2,1,0:T(8,128)(2,1)S(1)}, u32[]{:S(2)}, u32[]{:S(2)}) collective-permute-start(bf16[1,4,4,128,128]{4,3,2,1,0:T(8,128)(2,1)S(1)} %get-tuple-element.35), channel_id=1, source_target_pairs={{0,24},{8,0},{16,8},{24,16},{1,25},{9,1},{17,9},{25,17},{2,26},{10... | collective-permute-start | bytes 1572872 | tf_op jit(solution)/shard_map/ppermute | solution.py:291
  32.4 20.4 %collective-permute-start.10 = (bf16[2,1,5,128,128]{4,3,2,1,0:T(8,128)(2,1)S(1)}, bf16[2,1,5,128,128]{4,3,2,1,0:T(8,128)(2,1)S(1)}, u32[]{:S(2)}, u32[]{:S(2)}) collective-permute-start(bf16[2,1,5,128,128]{4,3,2,1,0:T(8,128)(2,1)S(1)} %get-tuple-element.42), channel_id=1, source_target_pairs={{0,1},{1,0},{2,3},{3,2},{4,5},{5,4},{6,7},{7,6},{8,9},{9,8},{10,11... | collective-permute-start | bytes 983048 | tf_op jit(solution)/shard_map/ppermute | solution.py:302
  34.0 18.8 %collective-permute-start.11 = (bf16[2,1,5,128,128]{4,3,2,1,0:T(8,128)(2,1)S(1)}, bf16[2,1,5,128,128]{4,3,2,1,0:T(8,128)(2,1)S(1)}, u32[]{:S(2)}, u32[]{:S(2)}) collective-permute-start(bf16[2,1,5,128,128]{4,3,2,1,0:T(8,128)(2,1)S(1)} %get-tuple-element.43), channel_id=1, source_target_pairs={{0,7},{1,2},{2,1},{3,4},{4,3},{5,6},{6,5},{7,0},{8,15},{9,10},{10,... | collective-permute-start | bytes 983048 | tf_op jit(solution)/shard_map/ppermute | solution.py:303
  38.2 5.7 %collective-permute-start.7 = (bf16[1,2,4,128,128]{4,3,2,1,0:T(8,128)(2,1)S(1)}, bf16[1,2,4,128,128]{4,3,2,1,0:T(8,128)(2,1)S(1)}, u32[]{:S(2)}, u32[]{:S(2)}) collective-permute-start(bf16[1,2,4,128,128]{4,3,2,1,0:T(8,128)(2,1)S(1)} %get-tuple-element.49), channel_id=1, source_target_pairs={{0,24},{8,0},{16,8},{24,16},{1,25},{9,1},{17,9},{25,17},{2,26},{10... | collective-permute-start | bytes 786440 | tf_op jit(solution)/shard_map/ppermute | solution.py:301
  38.3 8.7 %collective-permute-start.6 = (bf16[1,2,4,128,128]{4,3,2,1,0:T(8,128)(2,1)S(1)}, bf16[1,2,4,128,128]{4,3,2,1,0:T(8,128)(2,1)S(1)}, u32[]{:S(2)}, u32[]{:S(2)}) collective-permute-start(bf16[1,2,4,128,128]{4,3,2,1,0:T(8,128)(2,1)S(1)} %get-tuple-element.50), channel_id=1, source_target_pairs={{0,8},{8,16},{16,24},{24,0},{1,9},{9,17},{17,25},{25,1},{2,10},{10... | collective-permute-start | bytes 786440 | tf_op jit(solution)/shard_map/ppermute | solution.py:300
  49.5 12.8 %collective-permute-start.8 = (bf16[3,5,128,128]{3,2,1,0:T(8,128)(2,1)S(1)}, bf16[3,5,128,128]{3,2,1,0:T(8,128)(2,1)S(1)}, u32[]{:S(2)}, u32[]{:S(2)}) collective-permute-start(bf16[3,5,128,128]{3,2,1,0:T(8,128)(2,1)S(1)} %get-tuple-element.40), channel_id=1, source_target_pairs={{0,8},{8,16},{16,24},{24,0},{1,9},{9,17},{17,25},{25,1},{2,10},{10... | collective-permute-start | bytes 1474568 | tf_op jit(solution)/shard_map/ppermute | solution.py:338
  49.7 13.3 %collective-permute-start.9 = (bf16[3,5,128,128]{3,2,1,0:T(8,128)(2,1)S(1)}, bf16[3,5,128,128]{3,2,1,0:T(8,128)(2,1)S(1)}, u32[]{:S(2)}, u32[]{:S(2)}) collective-permute-start(bf16[3,5,128,128]{3,2,1,0:T(8,128)(2,1)S(1)} %get-tuple-element.41), channel_id=1, source_target_pairs={{0,24},{8,0},{16,8},{24,16},{1,25},{9,1},{17,9},{25,17},{2,26},{10... | collective-permute-start | bytes 1474568 | tf_op jit(solution)/shard_map/ppermute | solution.py:339
  55.4 17.5 %collective-permute-start.12 = (bf16[3,5,128,128]{3,2,1,0:T(8,128)(2,1)S(1)}, bf16[3,5,128,128]{3,2,1,0:T(8,128)(2,1)S(1)}, u32[]{:S(2)}, u32[]{:S(2)}) collective-permute-start(bf16[3,5,128,128]{3,2,1,0:T(8,128)(2,1)S(1)} %get-tuple-element.47), channel_id=1, source_target_pairs={{0,8},{8,16},{16,24},{24,0},{1,9},{9,17},{17,25},{25,1},{2,10},{10... | collective-permute-start | bytes 1474568 | tf_op jit(solution)/shard_map/ppermute | solution.py:338
  55.4 17.4 %collective-permute-start.13 = (bf16[3,5,128,128]{3,2,1,0:T(8,128)(2,1)S(1)}, bf16[3,5,128,128]{3,2,1,0:T(8,128)(2,1)S(1)}, u32[]{:S(2)}, u32[]{:S(2)}) collective-permute-start(bf16[3,5,128,128]{3,2,1,0:T(8,128)(2,1)S(1)} %get-tuple-element.48), channel_id=1, source_target_pairs={{0,24},{8,0},{16,8},{24,16},{1,25},{9,1},{17,9},{25,17},{2,26},{10... | collective-permute-start | bytes 1474568 | tf_op jit(solution)/shard_map/ppermute | solution.py:339

commit v5 on v4

v5 whole, which is shorter than its diff:
```python
import functools

import jax
import jax.numpy as jnp
from jax import lax
from jax.experimental import pallas as pl
from jax.experimental.pallas import tpu as pltpu
from jax.sharding import PartitionSpec as P

FAR, OWN_0, OWN_1, NEAR = range(4)
HALF = 32
ZERO = 3 * HALF
INFO = 16
LONG = 10**11
VMEM_LIMIT = 24 * 1024 * 1024


def pair(count):
    return [(i, i ^ 1) for i in range(count)]


def outward(count):
    return [(i, (i + (1 if i % 2 else -1)) % count) for i in range(count)]


def aside(count):
    return [(i, (i + (2 if i % 2 else -2)) % count) for i in range(count)]


def onward(count):
    return [(i, (i + (-2 if i % 2 else 2)) % count) for i in range(count)]


def table_kernel(operators, roles, turn, *refs):
    table = refs[-1]
    odd, flip = turns(turn)
    each = 2 * operators
    wide = table.shape[1] // 9 + 1
    parts = []
    for place in range(2):
        array = refs[min(place, len(refs) - 2)]
        last = array.shape[0] - (INFO if len(refs) == 2 and place == 0 else 0)
        parts.append(array[last - INFO : last, :].astype(jnp.float32)[:each, :wide])
    info = jnp.concatenate(parts, axis=0).astype(jnp.int32)
    slots = info.shape[1] - 1
    shape = table.shape
    row = lax.broadcasted_iota(jnp.int32, shape, 0)
    place = lax.broadcasted_iota(jnp.int32, shape, 1)
    slot = place // 9
    band = place - 9 * slot
    band_y = band // 3
    band_x = band - 3 * band_y
    fine_x = row & 1
    fine_y = jnp.where(row < each, roles[0], roles[1]) - 1
    off = jnp.zeros(shape, jnp.int32)
    for k in range(slots):
        off = off + jnp.where(slot == k, info[:, k : k + 1], 0)
    off_x = jnp.where(off >= 6, 2, jnp.where(off >= 3, 1, 0))
    near_x = fine_x + (off_x - 1) * (1 - 2 * flip)
    near_y = fine_y + (off - 3 * off_x - 1) * (1 - 2 * odd)
    place_x = band_x - (((near_x - 1) >> 1) - (fine_x >> 1) + 1)
    place_y = band_y - (((near_y - 1) >> 1) - (fine_y >> 1) + 1)
    corner_x = jnp.where((near_x & 1) == 1, place_x, 1 - place_x)
    corner_y = jnp.where((near_y & 1) == 1, place_y, 1 - place_y)
    good = (place_x >= 0) & (place_x < 2) & (place_y >= 0) & (place_y < 2)
    good = good & (slot < info[:, slots:])
    side = jnp.where(near_y < 0, 2 * HALF, jnp.where(near_y < 2, 0, HALF))
    index = side + (near_x + 1) * 8 + ((near_y & 1) ^ odd) * 4 + 2 * corner_x + corner_y
    table[...] = jnp.where(good, index, ZERO)


def table_row(operators, role, operator, x):
    return (operators if role in (OWN_1, FAR) else 0) * 2 + operator * 2 + x


def turns(turn):
    return turn[0] & 1, turn[0] >> 1


def fill(flat, first, rows):
    for x, piece, at in rows:
        for y in range(2):
            flat[pl.ds(first + 8 * (x + 1) + 4 * y, 4)] = piece[at, y]


def rows_kernel(turn, piece, *outs):
    flip = turns(turn)[1]
    for out, x in zip(outs, (1 - flip, flip)):
        out[0] = piece[x]


def pack_kernel(turn, off, count, a_own, *outs):
    operators, _, _, slots = off.shape
    block = a_own.shape[-1]
    odd, flip = turns(turn)
    row = lax.broadcasted_iota(jnp.int32, (INFO, block), 0)
    lane = lax.broadcasted_iota(jnp.int32, (INFO, block), 1)
    for out, y in zip(outs, (1 - odd, odd)):
        for x in range(2):
            for k in range(slots):
                out[pl.ds((x * slots + k) * block, block), :] = a_own[0, x ^ flip, y, k]
        line = jnp.zeros((INFO, block), jnp.int32)
        for s in range(operators):
            for x in range(2):
                here = row == 2 * s + x
                line = jnp.where(here & (lane == slots), count[s, x ^ flip, y], line)
                for k in range(slots):
                    line = jnp.where(here & (lane == k), off[s, x ^ flip, y, k], line)
        out[pl.ds(2 * slots * block, INFO), :] = line.astype(jnp.float32).astype(out.dtype)


def later_kernel(turn, a_own, after, *outs):
    odd, flip = turns(turn)
    for i, out in enumerate(outs):
        for x in range(2):
            out[x, 0] = a_own[i // 2 + 1, x ^ flip, odd if i % 2 else 1 - odd]


def join_kernel(near, far, out):
    count = near.shape[0] - INFO
    out[pl.ds(0, count), :] = near[pl.ds(0, count), :]
    out[pl.ds(count, count), :] = far[pl.ds(0, count), :]
    out[pl.ds(2 * count, INFO), :] = near[pl.ds(count, INFO), :]
    out[pl.ds(2 * count + INFO, INFO), :] = far[pl.ds(count, INFO), :]


def joined_row(joined, side, x):
    block = joined.shape[1]
    slots = joined.shape[0] // (4 * block)
    first = (side * 2 + x) * slots
    return [joined.at[pl.ds((first + k) * block, block), :] for k in range(slots)]


def row_of(array):
    return [array.at[k] for k in range(array.shape[0])]


def fine_row(table, number, flat, blocks, w_ref):
    slots = len(blocks)
    left = jnp.concatenate([ref[...] for ref in blocks], axis=1)
    for band_y in range(3):
        right = jnp.concatenate(
            [
                jnp.concatenate(
                    [flat[table[number, k * 9 + band_y * 3 + band_x]] for band_x in range(3)], axis=1
                )
                for k in range(slots)
            ],
            axis=0,
        )
        w_ref[band_y] = jnp.dot(left, right, preferred_element_type=jnp.float32).astype(w_ref.dtype)


def coarse_column(turn, pieces, w_refs, fine_rows, lag_y, corner_x):
    odd, flip = turns(turn)
    lefts, rights = [], []
    for fine_x in fine_rows:
        for role in range(4):
            fine_y = role - 1
            band_y = lag_y - (fine_y // 2 + 1)
            if 0 <= band_y < 3:
                corner_y = 1 if role in (FAR, NEAR) else 0
                lefts.append(pieces[role][fine_x ^ flip, (fine_y & 1) ^ odd, corner_x + corner_y])
                rights.append(w_refs[role][fine_x][band_y])
    left = jnp.concatenate(lefts, axis=0)
    right = jnp.concatenate(rights, axis=0)
    return lax.dot_general(left, right, (((0,), (0,)), ((), ())), preferred_element_type=jnp.float32)


def edge(turn, pieces, w_refs, fine_x, out):
    block = out.shape[-1]
    for lag_y in range(5):
        total = coarse_column(turn, pieces, w_refs, (fine_x,), lag_y, 2)
        for lag_x in range(3):
            out[lag_x, lag_y] = total[:, lag_x * block : (lag_x + 1) * block].astype(out.dtype)


def near_own_kernel(operators, table, turn, a_own, p_own, p_near, own_out, own_in, near_out, near_in, flat, w_ref):
    odd, flip = turns(turn)
    fill(flat, 0, ((-1, own_out, 0), (0, p_own, flip), (1, p_own, 1 - flip), (2, own_in, 0)))
    fill(flat, HALF, ((-1, near_out, 0), (0, p_near, flip), (1, p_near, 1 - flip), (2, near_in, 0)))
    flat[ZERO] = jnp.zeros(flat.shape[1:], flat.dtype)
    for s in range(operators):
        for x in range(2):
            fine_row(table, table_row(operators, OWN_1, s, x), flat, row_of(a_own.at[s, x ^ flip, 1 - odd]), w_ref.at[s, x])


def near_kernel(operators, table, flat, a_pair, w_ref):
    fine_row(table, table_row(operators, NEAR, 0, 0), flat, joined_row(a_pair, 0, 0), w_ref)


def first_outer_kernel(
    operators, own_table, table, turn, a_own, a_pair, w_own, w_near, p_own, p_near, p_far, far_out, held, out, flat, w_far, w_own_0
):
    odd, flip = turns(turn)
    fill(flat, 2 * HALF, ((-1, far_out, 0), (0, p_far, flip), (1, p_far, 1 - flip)))
    fine_row(table, table_row(operators, FAR, 0, 0), flat, joined_row(a_pair, 1, 0), w_far)
    fine_row(own_table, table_row(operators, OWN_0, 0, 0), flat, row_of(a_own.at[0, flip, odd]), w_own_0)
    edge(turn, (p_far, p_own, p_own, p_near), one_row(0, w_far, w_own_0, w_own.at[0, 0], w_near), 0, out)


def first_inner_kernel(
    operators, own_table, table, turn, a_own, a_pair, w_own, p_own, p_near, p_far, far_in, held, out, flat, w_far, w_own_0, w_near
):
    odd, flip = turns(turn)
    fill(flat, 2 * HALF, ((2, far_in, 0),))
    fine_row(table, table_row(operators, NEAR, 0, 1), flat, joined_row(a_pair, 0, 1), w_near)
    fine_row(table, table_row(operators, FAR, 0, 1), flat, joined_row(a_pair, 1, 1), w_far)
    fine_row(own_table, table_row(operators, OWN_0, 0, 1), flat, row_of(a_own.at[0, 1 - flip, odd]), w_own_0)
    edge(turn, (p_far, p_own, p_own, p_near), one_row(1, w_far, w_own_0, w_own.at[0, 1], w_near), 1, out)


def one_row(x, *w_refs):
    return [{x: ref} for ref in w_refs]


def own_0_kernel(operators, operator, table, turn, a_own, flat, *w_refs):
    odd, flip = turns(turn)
    for x in range(2):
        fine_row(table, table_row(operators, OWN_0, operator, x), flat, row_of(a_own.at[operator, x ^ flip, odd]), w_refs[x])


def sides_kernel(
    operators, operator, table, turn, a_near, a_far, flat, w_own, own_w_0, own_w_1, p_own, p_near, p_far, outer, inner, *w_refs
):
    for x, (out, w_own_0) in enumerate(((outer, own_w_0), (inner, own_w_1))):
        w_near, w_far = w_refs[2 * x : 2 * x + 2]
        fine_row(table, table_row(operators, NEAR, operator, x), flat, row_of(a_near.at[x, 0]), w_near)
        fine_row(table, table_row(operators, FAR, operator, x), flat, row_of(a_far.at[x, 0]), w_far)
        edge(turn, (p_far, p_own, p_own, p_near), one_row(x, w_far, w_own_0, w_own.at[operator, x], w_near), x, out)


def centre_kernel(operator, turn, p_own, p_near, p_far, w_own, *refs):
    out = refs[-1]
    block = out.shape[-1]
    w_refs = (refs[0:2], refs[2:4], (w_own.at[operator, 0], w_own.at[operator, 1]), refs[4:6])
    for lag_y in range(5):
        total = coarse_column(turn, (p_far, p_own, p_own, p_near), w_refs, (0, 1), lag_y, 0)
        for lag_x in range(3):
            out[lag_x, lag_y] = total[:, lag_x * block : (lag_x + 1) * block]


def final_kernel(turn, *refs):
    out = refs[-1]
    odd, flip = turns(turn)
    for operator in range(out.shape[0]):
        own, outer, inner = refs[3 * operator : 3 * operator + 3]
        for lag_x in range(5):
            for lag_y in range(5):
                total = None
                for part, at in ((outer, 2 - lag_x), (own, lag_x - 1), (inner, 4 - lag_x)):
                    if 0 <= at < 3:
                        term = part[at, lag_y].astype(jnp.float32)
                        total = term if total is None else total + term
                place = 5 * (lag_x + flip * (4 - 2 * lag_x)) + lag_y + odd * (4 - 2 * lag_y)
                out[operator, 0, 0, place] = total.astype(out.dtype)


def per_device(a_vals, a_off, a_count, p_vals):
    operators, _, _, slots, block, _ = a_vals.shape
    cols = lax.axis_size("col")
    rows = lax.axis_size("row")
    odd = (lax.axis_index("col") & 1).astype(jnp.int32)
    flip = (lax.axis_index("row") & 1).astype(jnp.int32)
    in_way, out_way = pair(rows), outward(rows)
    near_way, far_way, on_way, aside_way = pair(cols), outward(cols), onward(cols), aside(cols)

    smem = pl.BlockSpec(memory_space=pltpu.SMEM)
    any_spec = pl.BlockSpec(memory_space=pl.ANY)
    vmem = pl.BlockSpec(memory_space=pltpu.VMEM)
    bf16, f32 = jnp.bfloat16, jnp.float32
    turn = (odd + 2 * flip)[None]
    flat_shape = jax.ShapeDtypeStruct((ZERO + 1, block, block), bf16)
    w_shape = jax.ShapeDtypeStruct((3, block, 3 * block), bf16)
    part_shape = jax.ShapeDtypeStruct((3, 5, block, block), bf16)

    def call(kernel, in_specs, out_shape, products, name, scratch=(), aliases=None, limit=VMEM_LIMIT):
        single = not isinstance(out_shape, list)
        return pl.pallas_call(
            kernel,
            in_specs=in_specs,
            out_specs=vmem if single else [vmem] * len(out_shape),
            out_shape=out_shape,
            scratch_shapes=list(scratch),
            input_output_aliases=aliases or {},
            compiler_params=pltpu.CompilerParams(vmem_limit_bytes=limit),
            cost_estimate=pl.CostEstimate(flops=products, bytes_accessed=1024, transcendentals=0),
            name=name,
        )

    p_near = lax.ppermute(p_vals, "col", near_way)
    column = jax.ShapeDtypeStruct((2 * slots * block + INFO, block), bf16)
    own_1, own_0 = call(pack_kernel, [smem] * 3 + [vmem], [column] * 2, 1, "pack")(turn, a_off, a_count, a_vals)
    moved = lax.ppermute(own_0, "col", aside_way)
    table_shape = jax.ShapeDtypeStruct((operators * 4, slots * 9), jnp.int32)
    own_table = call(
        functools.partial(table_kernel, operators, (OWN_0, OWN_1)), [smem, vmem, vmem], table_shape, 1, "own_table"
    )(turn, own_0, own_1)
    joined = jax.ShapeDtypeStruct((4 * slots * block + 2 * INFO, block), bf16)
    joined = call(join_kernel, [vmem, vmem], joined, 1, "join")(own_1, moved)
    row_shape = jax.ShapeDtypeStruct((1, 2, 4, block, block), bf16)
    rows_of = call(rows_kernel, [smem, vmem], [row_shape] * 2, 1, "rows")
    own_in, own_out = rows_of(turn, p_vals)
    own_in = lax.ppermute(own_in, "row", in_way)
    own_out = lax.ppermute(own_out, "row", out_way)
    p_near, joined = lax.optimization_barrier((p_near, joined))
    p_far = lax.ppermute(p_near, "col", on_way)
    from_pair = lax.ppermute(joined, "col", near_way)
    p_rows, own_in, own_out = lax.optimization_barrier((p_near, own_in, own_out))
    near_in, near_out = rows_of(turn, p_rows)
    near_in = lax.ppermute(near_in, "row", in_way)
    near_out = lax.ppermute(near_out, "row", out_way)
    far_out = lax.ppermute(near_out, "col", on_way)
    flat, w_own = call(
        functools.partial(near_own_kernel, operators),
        [smem, smem] + [vmem] * 7,
        [flat_shape, jax.ShapeDtypeStruct((operators, 2) + w_shape.shape, bf16)],
        360,
        "near_own",
    )(own_table, turn, a_vals, p_vals, p_near, own_out, own_in, near_out, near_in)

    p_far, w_own = lax.optimization_barrier((p_far, w_own))
    far_in = call(rows_kernel, [smem, vmem], [row_shape], 1, "row")(turn, p_far)[0]
    later = call(
        later_kernel,
        [smem, vmem, any_spec],
        [jax.ShapeDtypeStruct((2, 1, slots, block, block), bf16)] * (2 * operators - 2),
        1,
        "later",
    )(turn, a_vals, near_in)
    far_in = lax.ppermute(far_in, "row", in_way)
    near_out, later_near = lax.optimization_barrier((near_out, later[0::2]))
    w_own, later_far = lax.optimization_barrier((w_own, later[1::2]))
    side_table = call(
        functools.partial(table_kernel, operators, (NEAR, FAR)), [smem, vmem], table_shape, 1, "side_table"
    )(turn, from_pair)

    near_w = call(functools.partial(near_kernel, operators), [smem, vmem, vmem], w_shape, 45, "near")(
        side_table, flat, from_pair
    )
    a_near, a_far = [None], [None]
    a_near += [lax.ppermute(send, "col", near_way) for send in later_near]
    a_far += [lax.ppermute(send, "col", far_way) for send in later_far]

    finals = []
    for s in range(operators):
        own_w, far_w, sums = [None, None], [None, None], [None, None]
        if s == 0:
            sums[0], flat, far_w[0], own_w[0] = call(
                functools.partial(first_outer_kernel, operators),
                [smem, smem, smem] + [vmem] * 9,
                [part_shape, flat_shape, w_shape, w_shape],
                150,
                "first_outer",
                aliases={11: 1},
            )(own_table, side_table, turn, a_vals, from_pair, w_own, near_w, p_vals, p_near, p_far, far_out, flat)
            sums[1], flat, far_w[1], own_w[1], inner_w = call(
                functools.partial(first_inner_kernel, operators),
                [smem, smem, smem] + [vmem] * 8,
                [part_shape, flat_shape, w_shape, w_shape, w_shape],
                LONG,
                "first_inner",
                aliases={10: 1},
            )(own_table, side_table, turn, a_vals, from_pair, w_own, p_vals, p_near, p_far, far_in, flat)
            near_w = [near_w, inner_w]
        else:
            near_w = [None, None]
            own_w = call(
                functools.partial(own_0_kernel, operators, s), [smem, smem, vmem, vmem], [w_shape] * 2, 90, "own_0"
            )(own_table, turn, a_vals, flat)
            *sums, near_w[0], far_w[0], near_w[1], far_w[1] = call(
                functools.partial(sides_kernel, operators, s),
                [smem, smem] + [vmem] * 9,
                [part_shape] * 2 + [w_shape] * 4,
                200,
                "sides",
            )(side_table, turn, a_near[s], a_far[s], flat, w_own, *own_w, p_vals, p_near, p_far)
        from_out = lax.ppermute(sums[0], "row", out_way)
        from_in = lax.ppermute(sums[1], "row", in_way)
        centre = call(
            functools.partial(centre_kernel, s),
            [smem] + [vmem] * 10,
            jax.ShapeDtypeStruct((3, 5, block, block), f32),
            144,
            "centre",
        )(turn, p_vals, p_near, p_far, w_own, *far_w, *own_w, *near_w)
        finals += [centre, from_out, from_in]
    return call(
        final_kernel,
        [smem] + [vmem] * len(finals),
        jax.ShapeDtypeStruct((operators, 1, 1, 25, block, block), bf16),
        1,
        "final",
    )(turn, *finals)


def solution(mesh):
    placed = (
        P(None, "row", "col", None, None, None),
        P(None, "row", "col", None),
        P(None, "row", "col"),
        P("row", "col", None, None, None),
    )
    return jax.shard_map(
        per_device,
        mesh=mesh,
        in_specs=placed,
        out_specs=P(None, "row", "col", None, None, None),
        check_vma=False,
    )
```

time: 74.7 us -> 68.1 us (0.912)
  waiting for transfers between devices: 37.8 us -> 30.4 us
  local copies, waits for them, and re-layouts: 2.73 us -> 3.73 us
  starting transfers between devices: 19.8 us -> 18.9 us
  Pallas kernels: 13.9 us -> 14.7 us
    ppermute x1, waiting for transfers between devices: 12.1 us -> 0.01 us  [per_device(): from_pair = lax.ppermute(joined, 'col', near_way)]
    ppermute x10 -> x12, waiting for transfers between devices: 18.9 us -> 25.1 us  [the longest x2 11.4 us: per_device(): from_out = lax.ppermute(sums[0], 'row', out_way)]
    ppermute x10 -> x12, starting transfers between devices: 11.7 us -> 9.28 us  [the longest x1 2.82 us: per_device(): a_near += [lax.ppermute(send, 'col', near_way) for send in later_near]]
    ppermute x1, waiting for transfers between devices: 6.78 us -> 4.59 us  [per_device(): moved = lax.ppermute(own_0, 'col', aside_way)]
    ppermute x1, starting transfers between devices: 1.34 us -> 2.92 us  [per_device(): from_pair = lax.ppermute(joined, 'col', near_way)]
    unnamed x10 -> x12, local copies, waits for them, and re-layouts: 2.69 us -> 3.73 us
    pallas_call x7 -> x12, Pallas kernels: 6.2 us -> 7.11 us  [the longest x1 1.99 us: per_device(): call(functools.partial(first_inner_kernel, operators), [smem, smem, smem]...]
  transfers between devices with their start and end apart: 14 -> 16, of which waited for: 7 -> 6; matrix products, arithmetic and copies ran while one was open for 0% -> 0% of each run, Pallas kernels for 17% -> 19%
where the time goes in v5:
time: 68.1 us; the launch traced here: 67.9 us
  waiting for transfers between devices  30.4 us (45%)
  starting transfers between devices  18.9 us (28%)
  Pallas kernels  14.7 us (22%)
  local copies, waits for them, and re-layouts  3.73 us (5%)
    ppermute x2, waiting for transfers between devices, per_device(): from_out = lax.ppermute(sums[0], 'row', out_way)  11.4 us
    ppermute x1, waiting for transfers between devices, per_device(): near_out = lax.ppermute(near_out, 'row', out_way)  6.79 us
    ppermute x1, waiting for transfers between devices, per_device(): a_near += [lax.ppermute(send, 'col', near_way) for send in later_near]  4.82 us
    ppermute x1, waiting for transfers between devices, per_device(): moved = lax.ppermute(own_0, 'col', aside_way)  4.59 us
    unnamed x12, local copies, waits for them, and re-layouts  3.73 us
    ppermute x1, starting transfers between devices, per_device(): moved = lax.ppermute(own_0, 'col', aside_way)  3.65 us
    ppermute x1, starting transfers between devices, per_device(): p_near = lax.ppermute(p_vals, 'col', near_way)  2.94 us
    ppermute x1, starting transfers between devices, per_device(): from_pair = lax.ppermute(joined, 'col', near_way)  2.92 us
  transfers between devices with their start and end apart: 16, of which 6 were waited for; matrix products, arithmetic and copies ran while one was open for 0% of the time, Pallas kernels for 19%

profile of v5, /device:TPU:0, one launch (start us, length us, event | category | flops | bytes accessed | tf_op | source)
XLA Modules:
  0.0 67.9 jit_solution(9768433303594356542)
XLA Ops:
  0.0 2.9 %collective-permute-start = (bf16[2,2,4,128,128]{4,3,2,1,0:T(8,128)(2,1)}, bf16[2,2,4,128,128]{4,3,2,1,0:T(8,128)(2,1)S(1)}, u32[]{:S(2)}, u32[]{:S(2)}) collective-permute-start(bf16[2,2,4,128,128]{4,3,2,1,0:T(8,128)(2,1)} %p_own.11), channel_id=1, source_target_pairs={{0,1},{1,0},{2,3},{3,2},{4,5},{5,4},{6,7},{7,6},{8,9},{9,8},{10,11... | collective-permute-start | bytes 1572872 | tf_op jit(solution)/shard_map/ppermute | solution.py:291
  2.9 1.3 %copy-done = bf16[2,2,2,5,128,128]{5,4,3,2,1,0:T(8,128)(2,1)S(1)} copy-done((bf16[2,2,2,5,128,128]{5,4,3,2,1,0:T(8,128)(2,1)S(1)}, bf16[2,2,2,5,128,128]{5,4,3,2,1,0:T(8,128)(2,1)}, u32[]{:S(2)}) %copy-start) | copy-done | bytes 1310744
  4.3 0.7 %copy-done.4 = s32[2,2,2,5]{3,2,1,0:T(2,128)S(1)} copy-done((s32[2,2,2,5]{3,2,1,0:T(2,128)S(1)}, s32[2,2,2,5]{3,2,1,0:T(2,128)}, u32[]{:S(2)}) %copy-start.4) | copy-done | bytes 184
  4.9 0.7 %copy-done.5 = s32[2,2,2]{2,1,0:T(2,128)S(1)} copy-done((s32[2,2,2]{2,1,0:T(2,128)S(1)}, s32[2,2,2]{2,1,0:T(2,128)}, u32[]{:S(2)}) %copy-start.5) | copy-done | bytes 56
  5.6 0.7 %pack.1 = (bf16[1296,128]{1,0:T(8,128)(2,1)S(1)}, bf16[1296,128]{1,0:T(8,128)(2,1)S(1)}) custom-call(s32[1]{0:T(128)} %bitcast.turn, s32[2,2,2,5]{3,2,1,0:T(2,128)S(1)} %copy-done.4, s32[2,2,2]{2,1,0:T(2,128)S(1)} %copy-done.5, bf16[2,2,2,5,128,128]{5,4,3,2,1,0:T(8,128)(2,1)S(1)} %copy-done), custom_call_target="tpu_custom_call" | custom-call | flops 1 | bytes 1024 | tf_op jit(solution)/shard_map/pack/pallas_call | solution.py:293
  6.3 3.7 %collective-permute-start.1 = (bf16[1296,128]{1,0:T(8,128)(2,1)S(1)}, bf16[1296,128]{1,0:T(8,128)(2,1)S(1)}, u32[]{:S(2)}, u32[]{:S(2)}) collective-permute-start(bf16[1296,128]{1,0:T(8,128)(2,1)S(1)} %get-tuple-element.43.refs_0_), channel_id=1, source_target_pairs={{0,6},{1,3},{2,0},{3,5},{4,2},{5,7},{6,4},{7,1},{8,14},{9,11},{10,... | collective-permute-start | bytes 995336 | tf_op jit(solution)/shard_map/ppermute | solution.py:294
  10.0 1.0 %copy-done.2 = bf16[2,2,4,128,128]{4,3,2,1,0:T(8,128)(2,1)S(1)} copy-done((bf16[2,2,4,128,128]{4,3,2,1,0:T(8,128)(2,1)S(1)}, bf16[2,2,4,128,128]{4,3,2,1,0:T(8,128)(2,1)}, u32[]{:S(2)}) %copy-start.2) | copy-done | bytes 524312
  11.1 0.1 collective-permute-start.3
  11.1 1.6 %collective-permute-start.4 = (bf16[1,2,4,128,128]{4,3,2,1,0:T(8,128)(2,1)S(1)}, bf16[1,2,4,128,128]{4,3,2,1,0:T(8,128)(2,1)S(1)}, u32[]{:S(2)}, u32[]{:S(2)}) collective-permute-start(bf16[1,2,4,128,128]{4,3,2,1,0:T(8,128)(2,1)S(1)} %get-tuple-element.46), channel_id=1, source_target_pairs={{0,24},{8,16},{16,8},{24,0},{1,25},{9,17},{17,9},{25,1},{2,26},{10... | collective-permute-start | bytes 786440 | tf_op jit(solution)/shard_map/ppermute | solution.py:305
  12.8 4.6 %collective-permute-done.1.far = bf16[1296,128]{1,0:T(8,128)(2,1)S(1)} collective-permute-done((bf16[1296,128]{1,0:T(8,128)(2,1)S(1)}, bf16[1296,128]{1,0:T(8,128)(2,1)S(1)}, u32[]{:S(2)}, u32[]{:S(2)}) %collective-permute-start.1) | collective-permute-done | bytes 331808 | tf_op jit(solution)/shard_map/ppermute | solution.py:294
  17.4 0.0 collective-permute-done.piece.p_near
  17.4 0.1 collective-permute-start.2
  17.5 2.9 %collective-permute-start.7 = (bf16[2592,128]{1,0:T(8,128)(2,1)S(1)}, bf16[2592,128]{1,0:T(8,128)(2,1)S(1)}, u32[]{:S(2)}, u32[]{:S(2)}) collective-permute-start(bf16[2592,128]{1,0:T(8,128)(2,1)S(1)} %join.1), channel_id=1, source_target_pairs={{0,1},{1,0},{2,3},{3,2},{4,5},{5,4},{6,7},{7,6},{8,9},{9,8},{10,11... | collective-permute-start | bytes 1990664 | tf_op jit(solution)/shard_map/ppermute | solution.py:308
  20.4 0.0 collective-permute-done.3.own_in
  20.4 0.0 collective-permute-done.4.own_out
  20.5 0.4 collective-permute-start.5
  20.9 1.3 %collective-permute-start.6 = (bf16[1,2,4,128,128]{4,3,2,1,0:T(8,128)(2,1)S(1)}, bf16[1,2,4,128,128]{4,3,2,1,0:T(8,128)(2,1)S(1)}, u32[]{:S(2)}, u32[]{:S(2)}) collective-permute-start(bf16[1,2,4,128,128]{4,3,2,1,0:T(8,128)(2,1)S(1)} %get-tuple-element.51), channel_id=1, source_target_pairs={{0,8},{8,0},{16,24},{24,16},{1,9},{9,1},{17,25},{25,17},{2,10},{10... | collective-permute-start | bytes 786440 | tf_op jit(solution)/shard_map/ppermute | solution.py:311
  22.2 0.1 own_table.1.table
  22.3 6.8 %collective-permute-done.5.near_out = bf16[1,2,4,128,128]{4,3,2,1,0:T(8,128)(2,1)S(1)} collective-permute-done((bf16[1,2,4,128,128]{4,3,2,1,0:T(8,128)(2,1)S(1)}, bf16[1,2,4,128,128]{4,3,2,1,0:T(8,128)(2,1)S(1)}, u32[]{:S(2)}, u32[]{:S(2)}) %collective-permute-start.5) | collective-permute-done | bytes 262176 | tf_op jit(solution)/shard_map/ppermute | solution.py:312
  29.1 0.0 collective-permute-start.8
  29.1 0.0 collective-permute-done.6.near_in.after
  29.1 2.1 %near_own.1 = (bf16[97,128,128]{2,1,0:T(8,128)(2,1)S(1)}, bf16[2,2,3,128,384]{4,3,2,1,0:T(8,128)(2,1)S(1)}) custom-call(s32[8,45]{1,0:T(8,128)S(1)} %own_table.1.table, s32[1]{0:T(128)} %bitcast.turn, bf16[2,2,2,5,128,128]{5,4,3,2,1,0:T(8,128)(2,1)S(1)} %copy-done.1, bf16[2,2,4,128,128]{4,3,2,1,0:T(8,128)(2,1)S(1)} %copy-done.3, ...), custom_call_target="tpu_custom_call" | custom-call | flops 360 | bytes 1024 | tf_op jit(solution)/shard_map/near_own/pallas_call | solution.py:314
  31.2 0.7 %collective-permute-done.2.p_far.piece = bf16[2,2,4,128,128]{4,3,2,1,0:T(8,128)(2,1)S(1)} collective-permute-done((bf16[2,2,4,128,128]{4,3,2,1,0:T(8,128)(2,1)S(1)}, bf16[2,2,4,128,128]{4,3,2,1,0:T(8,128)(2,1)S(1)}, u32[]{:S(2)}, u32[]{:S(2)}) %collective-permute-start.2) | collective-permute-done | bytes 524320 | tf_op jit(solution)/shard_map/ppermute | solution.py:307
  31.9 0.1 collective-permute-start.9
  32.0 0.1 later.1
  32.0 2.8 %collective-permute-start.12 = (bf16[2,1,5,128,128]{4,3,2,1,0:T(8,128)(2,1)S(1)}, bf16[2,1,5,128,128]{4,3,2,1,0:T(8,128)(2,1)S(1)}, u32[]{:S(2)}, u32[]{:S(2)}) collective-permute-start(bf16[2,1,5,128,128]{4,3,2,1,0:T(8,128)(2,1)S(1)} %get-tuple-element.68), channel_id=1, source_target_pairs={{0,1},{1,0},{2,3},{3,2},{4,5},{5,4},{6,7},{7,6},{8,9},{9,8},{10,11... | collective-permute-start | bytes 983048 | tf_op jit(solution)/shard_map/ppermute | solution.py:342
  34.9 1.8 %collective-permute-start.13 = (bf16[2,1,5,128,128]{4,3,2,1,0:T(8,128)(2,1)S(1)}, bf16[2,1,5,128,128]{4,3,2,1,0:T(8,128)(2,1)S(1)}, u32[]{:S(2)}, u32[]{:S(2)}) collective-permute-start(bf16[2,1,5,128,128]{4,3,2,1,0:T(8,128)(2,1)S(1)} %get-tuple-element.69), channel_id=1, source_target_pairs={{0,7},{1,2},{2,1},{3,4},{4,3},{5,6},{6,5},{7,0},{8,15},{9,10},{10,... | collective-permute-start | bytes 983048 | tf_op jit(solution)/shard_map/ppermute | solution.py:343
  36.7 0.0 collective-permute-done.7.refs_0_.a_pair
  36.7 0.1 side_table.1.table
  36.8 1.1 %near.1.w_near.refs_4_ = bf16[3,128,384]{2,1,0:T(8,128)(2,1)S(1)} custom-call(s32[8,45]{1,0:T(8,128)S(1)} %side_table.1.table, bf16[97,128,128]{2,1,0:T(8,128)(2,1)S(1)} %get-tuple-element.58.flat.held, bf16[2592,128]{1,0:T(8,128)(2,1)S(1)} %collective-permute-done.7.refs_0_.a_pair), custom_call_target="tpu_custom_call" | custom-call | flops 45 | bytes 1024 | tf_op jit(solution)/shard_map/near/pallas_call | solution.py:338
  37.9 2.1 %collective-permute-done.8.far_out = bf16[1,2,4,128,128]{4,3,2,1,0:T(8,128)(2,1)S(1)} collective-permute-done((bf16[1,2,4,128,128]{4,3,2,1,0:T(8,128)(2,1)S(1)}, bf16[1,2,4,128,128]{4,3,2,1,0:T(8,128)(2,1)S(1)}, u32[]{:S(2)}, u32[]{:S(2)}) %collective-permute-start.8) | collective-permute-done | bytes 262176 | tf_op jit(solution)/shard_map/ppermute | solution.py:313
  40.0 1.7 %first_outer.1 = (bf16[3,5,128,128]{3,2,1,0:T(8,128)(2,1)S(1)}, bf16[97,128,128]{2,1,0:T(8,128)(2,1)S(1)}, bf16[3,128,384]{2,1,0:T(8,128)(2,1)S(1)}, bf16[3,128,384]{2,1,0:T(8,128)(2,1)S(1)}) custom-call(s32[8,45]{1,0:T(8,128)S(1)} %own_table.1.table, s32[8,45]{1,0:T(8,128)S(1)} %side_table.1.table, s32[1]{0:T(128)} %bitcast.turn, ...), custom_call_target="tpu_custom_call", output_to_operand_aliasing={{1}: (11, {})} | custom-call | flops 150 | bytes 1024 | tf_op jit(solution)/shard_map/first_outer/pallas_call | solution.py:349
  41.7 0.1 collective-permute-start.10
  41.8 0.0 collective-permute-done.9.far_in
  41.8 2.0 %first_inner.1 = (bf16[3,5,128,128]{3,2,1,0:T(8,128)(2,1)S(1)}, bf16[97,128,128]{2,1,0:T(8,128)(2,1)S(1)}, bf16[3,128,384]{2,1,0:T(8,128)(2,1)S(1)}, bf16[3,128,...) custom-call(s32[8,45]{1,0:T(8,128)S(1)} %own_table.1.table, ...), custom_call_target="tpu_custom_call", output_to_operand_aliasing={{1}: (10, {})} | custom-call | flops 99999997952 | bytes 1024 | tf_op jit(solution)/shard_map/first_inner/pallas_call | solution.py:357
  43.8 0.2 collective-permute-start.11
  44.1 1.4 %own_0.1 = (bf16[3,128,384]{2,1,0:T(8,128)(2,1)S(1)}, bf16[3,128,384]{2,1,0:T(8,128)(2,1)S(1)}) custom-call(s32[8,45]{1,0:T(8,128)S(1)} %own_table.1.table, s32[1]{0:T(128)} %bitcast.turn, bf16[2,2,2,5,128,128]{5,4,3,2,1,0:T(8,128)(2,1)S(1)} %copy-done.1, bf16[97,128,128]{2,1,0:T(8,128)(2,1)S(1)} %get-tuple-element.70.flat), custom_call_target="tpu_custom_call" | custom-call | flops 90 | bytes 1024 | tf_op jit(solution)/shard_map/own_0/pallas_call | solution.py:368
  45.4 4.8 %collective-permute-done.12.a_near = bf16[2,1,5,128,128]{4,3,2,1,0:T(8,128)(2,1)S(1)} collective-permute-done((bf16[2,1,5,128,128]{4,3,2,1,0:T(8,128)(2,1)S(1)}, bf16[2,1,5,128,128]{4,3,2,1,0:T(8,128)(2,1)S(1)}, u32[]{:S(2)}, u32[]{:S(2)}) %collective-permute-start.12) | collective-permute-done | bytes 327712 | tf_op jit(solution)/shard_map/ppermute | solution.py:342
  50.3 2.6 %sides.1 = (bf16[3,5,128,128]{3,2,1,0:T(8,128)(2,1)S(1)}, bf16[3,5,128,128]{3,2,1,0:T(8,128)(2,1)S(1)}, bf16[3,128,384]{2,1,0:T(8,128)(2,1)S(1)}, bf16[3,128,384...) custom-call(s32[8,45]{1,0:T(8,128)S(1)} %side_table.1.table, s32[1]{0:T(128)} %bitcast.turn, ...), custom_call_target="tpu_custom_call" | custom-call | flops 200 | bytes 1024 | tf_op jit(solution)/shard_map/sides/pallas_call | solution.py:371
  52.9 0.1 collective-permute-start.14
  53.0 0.7 %collective-permute-start.15 = (bf16[3,5,128,128]{3,2,1,0:T(8,128)(2,1)S(1)}, bf16[3,5,128,128]{3,2,1,0:T(8,128)(2,1)S(1)}, u32[]{:S(2)}, u32[]{:S(2)}) collective-permute-start(bf16[3,5,128,128]{3,2,1,0:T(8,128)(2,1)S(1)} %get-tuple-element.78), channel_id=1, source_target_pairs={{0,8},{8,0},{16,24},{24,16},{1,9},{9,1},{17,25},{25,17},{2,10},{10... | collective-permute-start | bytes 1474568 | tf_op jit(solution)/shard_map/ppermute | solution.py:379
  53.7 0.6 centre.2.refs_0_
  54.3 0.6 centre.3.refs_3_
  55.0 0.0 collective-permute-done.10.refs_1_
  55.0 0.0 collective-permute-done.11.refs_2_
  55.0 11.4 %collective-permute-done.14.refs_4_ = bf16[3,5,128,128]{3,2,1,0:T(8,128)(2,1)S(1)} collective-permute-done((bf16[3,5,128,128]{3,2,1,0:T(8,128)(2,1)S(1)}, bf16[3,5,128,128]{3,2,1,0:T(8,128)(2,1)S(1)}, u32[]{:S(2)}, u32[]{:S(2)}) %collective-permute-start.14) | collective-permute-done | bytes 491552 | tf_op jit(solution)/shard_map/ppermute | solution.py:378
  66.4 0.0 collective-permute-done.15.refs_5_
  66.4 1.5 %final.1 = bf16[2,1,1,25,128,128]{5,4,3,2,1,0:T(8,128)(2,1)} custom-call(s32[1]{0:T(128)} %bitcast.turn, f32[3,5,128,128]{3,2,1,0:T(8,128)S(1)} %centre.2.refs_0_, bf16[3,5,128,128]{3,2,1,0:T(8,128)(2,1)S(1)} %collective-permute-done.10.refs_1_, bf16[3,5,128,128]{3,2,1,0:T(8,128)(2,1)S(1)} %collective-permute-done.11.refs_2_, ...), custom_call_target="tpu_custom_call" | custom-call | flops 1 | bytes 1024 | tf_op jit(solution)/shard_map/final/pallas_call | solution.py:388
  (13 shorter events, 0.1 us)
Async XLA Ops:
  0.0 17.4 %collective-permute-start = (bf16[2,2,4,128,128]{4,3,2,1,0:T(8,128)(2,1)}, bf16[2,2,4,128,128]{4,3,2,1,0:T(8,128)(2,1)S(1)}, u32[]{:S(2)}, u32[]{:S(2)}) collective-permute-start(bf16[2,2,4,128,128]{4,3,2,1,0:T(8,128)(2,1)} %p_own.11), channel_id=1, source_target_pairs={{0,1},{1,0},{2,3},{3,2},{4,5},{5,4},{6,7},{7,6},{8,9},{9,8},{10,11... | collective-permute-start | bytes 1572872 | tf_op jit(solution)/shard_map/ppermute | solution.py:291
  2.9 1.3 %copy-start = (bf16[2,2,2,5,128,128]{5,4,3,2,1,0:T(8,128)(2,1)S(1)}, bf16[2,2,2,5,128,128]{5,4,3,2,1,0:T(8,128)(2,1)}, u32[]{:S(2)}) copy-start(bf16[2,2,2,5,128,128]{5,4,3,2,1,0:T(8,128)(2,1)} %a_own.11) | copy-start | bytes 3932164
  4.3 0.7 %copy-start.4 = (s32[2,2,2,5]{3,2,1,0:T(2,128)S(1)}, s32[2,2,2,5]{3,2,1,0:T(2,128)}, u32[]{:S(2)}) copy-start(s32[2,2,2,5]{3,2,1,0:T(2,128)} %off.1) | copy-start | bytes 484
  4.9 0.7 %copy-start.5 = (s32[2,2,2]{2,1,0:T(2,128)S(1)}, s32[2,2,2]{2,1,0:T(2,128)}, u32[]{:S(2)}) copy-start(s32[2,2,2]{2,1,0:T(2,128)} %count.1) | copy-start | bytes 100
  5.6 23.4 %copy-start.1 = (bf16[2,2,2,5,128,128]{5,4,3,2,1,0:T(8,128)(2,1)S(1)}, bf16[2,2,2,5,128,128]{5,4,3,2,1,0:T(8,128)(2,1)}, u32[]{:S(2)}) copy-start(bf16[2,2,2,5,128,128]{5,4,3,2,1,0:T(8,128)(2,1)} %a_own.11) | copy-start | bytes 3932164
  6.3 11.0 %collective-permute-start.1 = (bf16[1296,128]{1,0:T(8,128)(2,1)S(1)}, bf16[1296,128]{1,0:T(8,128)(2,1)S(1)}, u32[]{:S(2)}, u32[]{:S(2)}) collective-permute-start(bf16[1296,128]{1,0:T(8,128)(2,1)S(1)} %get-tuple-element.43.refs_0_), channel_id=1, source_target_pairs={{0,6},{1,3},{2,0},{3,5},{4,2},{5,7},{6,4},{7,1},{8,14},{9,11},{10,... | collective-permute-start | bytes 995336 | tf_op jit(solution)/shard_map/ppermute | solution.py:294
  10.0 1.0 %copy-start.2 = (bf16[2,2,4,128,128]{4,3,2,1,0:T(8,128)(2,1)S(1)}, bf16[2,2,4,128,128]{4,3,2,1,0:T(8,128)(2,1)}, u32[]{:S(2)}) copy-start(bf16[2,2,4,128,128]{4,3,2,1,0:T(8,128)(2,1)} %p_own.11) | copy-start | bytes 1572868
  11.0 18.0 %copy-start.3 = (bf16[2,2,4,128,128]{4,3,2,1,0:T(8,128)(2,1)S(1)}, bf16[2,2,4,128,128]{4,3,2,1,0:T(8,128)(2,1)}, u32[]{:S(2)}) copy-start(bf16[2,2,4,128,128]{4,3,2,1,0:T(8,128)(2,1)} %p_own.11) | copy-start | bytes 1572868
  11.1 9.4 %collective-permute-start.3 = (bf16[1,2,4,128,128]{4,3,2,1,0:T(8,128)(2,1)S(1)}, bf16[1,2,4,128,128]{4,3,2,1,0:T(8,128)(2,1)S(1)}, u32[]{:S(2)}, u32[]{:S(2)}) collective-permute-start(bf16[1,2,4,128,128]{4,3,2,1,0:T(8,128)(2,1)S(1)} %get-tuple-element.45), channel_id=1, source_target_pairs={{0,8},{8,0},{16,24},{24,16},{1,9},{9,1},{17,25},{25,17},{2,10},{10... | collective-permute-start | bytes 786440 | tf_op jit(solution)/shard_map/ppermute | solution.py:304
  11.1 9.3 %collective-permute-start.4 = (bf16[1,2,4,128,128]{4,3,2,1,0:T(8,128)(2,1)S(1)}, bf16[1,2,4,128,128]{4,3,2,1,0:T(8,128)(2,1)S(1)}, u32[]{:S(2)}, u32[]{:S(2)}) collective-permute-start(bf16[1,2,4,128,128]{4,3,2,1,0:T(8,128)(2,1)S(1)} %get-tuple-element.46), channel_id=1, source_target_pairs={{0,24},{8,16},{16,8},{24,0},{1,25},{9,17},{17,9},{25,1},{2,26},{10... | collective-permute-start | bytes 786440 | tf_op jit(solution)/shard_map/ppermute | solution.py:305
  17.4 14.5 %collective-permute-start.2 = (bf16[2,2,4,128,128]{4,3,2,1,0:T(8,128)(2,1)S(1)}, bf16[2,2,4,128,128]{4,3,2,1,0:T(8,128)(2,1)S(1)}, u32[]{:S(2)}, u32[]{:S(2)}) collective-permute-start(bf16[2,2,4,128,128]{4,3,2,1,0:T(8,128)(2,1)S(1)} %collective-permute-done.piece.p_near), channel_id=1, source_target_pairs={{0,2},{1,7},{2,4},{3,1},{4,6},{5,3},{6,0},{7,5},{8,10},{9,15},{10,... | collective-permute-start | bytes 1572872 | tf_op jit(solution)/shard_map/ppermute | solution.py:307
  17.5 19.2 %collective-permute-start.7 = (bf16[2592,128]{1,0:T(8,128)(2,1)S(1)}, bf16[2592,128]{1,0:T(8,128)(2,1)S(1)}, u32[]{:S(2)}, u32[]{:S(2)}) collective-permute-start(bf16[2592,128]{1,0:T(8,128)(2,1)S(1)} %join.1), channel_id=1, source_target_pairs={{0,1},{1,0},{2,3},{3,2},{4,5},{5,4},{6,7},{7,6},{8,9},{9,8},{10,11... | collective-permute-start | bytes 1990664 | tf_op jit(solution)/shard_map/ppermute | solution.py:308
  20.5 8.6 %collective-permute-start.5 = (bf16[1,2,4,128,128]{4,3,2,1,0:T(8,128)(2,1)S(1)}, bf16[1,2,4,128,128]{4,3,2,1,0:T(8,128)(2,1)S(1)}, u32[]{:S(2)}, u32[]{:S(2)}) collective-permute-start(bf16[1,2,4,128,128]{4,3,2,1,0:T(8,128)(2,1)S(1)} %get-tuple-element.50), channel_id=1, source_target_pairs={{0,24},{8,16},{16,8},{24,0},{1,25},{9,17},{17,9},{25,1},{2,26},{10... | collective-permute-start | bytes 786440 | tf_op jit(solution)/shard_map/ppermute | solution.py:312
  20.9 8.2 %collective-permute-start.6 = (bf16[1,2,4,128,128]{4,3,2,1,0:T(8,128)(2,1)S(1)}, bf16[1,2,4,128,128]{4,3,2,1,0:T(8,128)(2,1)S(1)}, u32[]{:S(2)}, u32[]{:S(2)}) collective-permute-start(bf16[1,2,4,128,128]{4,3,2,1,0:T(8,128)(2,1)S(1)} %get-tuple-element.51), channel_id=1, source_target_pairs={{0,8},{8,0},{16,24},{24,16},{1,9},{9,1},{17,25},{25,17},{2,10},{10... | collective-permute-start | bytes 786440 | tf_op jit(solution)/shard_map/ppermute | solution.py:311
  29.1 10.9 %collective-permute-start.8 = (bf16[1,2,4,128,128]{4,3,2,1,0:T(8,128)(2,1)S(1)}, bf16[1,2,4,128,128]{4,3,2,1,0:T(8,128)(2,1)S(1)}, u32[]{:S(2)}, u32[]{:S(2)}) collective-permute-start(bf16[1,2,4,128,128]{4,3,2,1,0:T(8,128)(2,1)S(1)} %collective-permute-done.5.near_out), channel_id=1, source_target_pairs={{0,2},{1,7},{2,4},{3,1},{4,6},{5,3},{6,0},{7,5},{8,10},{9,15},{10,... | collective-permute-start | bytes 786440 | tf_op jit(solution)/shard_map/ppermute | solution.py:313
  31.9 9.9 %collective-permute-start.9 = (bf16[1,2,4,128,128]{4,3,2,1,0:T(8,128)(2,1)S(1)}, bf16[1,2,4,128,128]{4,3,2,1,0:T(8,128)(2,1)S(1)}, u32[]{:S(2)}, u32[]{:S(2)}) collective-permute-start(bf16[1,2,4,128,128]{4,3,2,1,0:T(8,128)(2,1)S(1)} %row.1), channel_id=1, source_target_pairs={{0,8},{8,0},{16,24},{24,16},{1,9},{9,1},{17,25},{25,17},{2,10},{10... | collective-permute-start | bytes 786440 | tf_op jit(solution)/shard_map/ppermute | solution.py:331
  32.0 18.2 %collective-permute-start.12 = (bf16[2,1,5,128,128]{4,3,2,1,0:T(8,128)(2,1)S(1)}, bf16[2,1,5,128,128]{4,3,2,1,0:T(8,128)(2,1)S(1)}, u32[]{:S(2)}, u32[]{:S(2)}) collective-permute-start(bf16[2,1,5,128,128]{4,3,2,1,0:T(8,128)(2,1)S(1)} %get-tuple-element.68), channel_id=1, source_target_pairs={{0,1},{1,0},{2,3},{3,2},{4,5},{5,4},{6,7},{7,6},{8,9},{9,8},{10,11... | collective-permute-start | bytes 983048 | tf_op jit(solution)/shard_map/ppermute | solution.py:342
  34.9 15.4 %collective-permute-start.13 = (bf16[2,1,5,128,128]{4,3,2,1,0:T(8,128)(2,1)S(1)}, bf16[2,1,5,128,128]{4,3,2,1,0:T(8,128)(2,1)S(1)}, u32[]{:S(2)}, u32[]{:S(2)}) collective-permute-start(bf16[2,1,5,128,128]{4,3,2,1,0:T(8,128)(2,1)S(1)} %get-tuple-element.69), channel_id=1, source_target_pairs={{0,7},{1,2},{2,1},{3,4},{4,3},{5,6},{6,5},{7,0},{8,15},{9,10},{10,... | collective-permute-start | bytes 983048 | tf_op jit(solution)/shard_map/ppermute | solution.py:343
  41.7 13.3 %collective-permute-start.10 = (bf16[3,5,128,128]{3,2,1,0:T(8,128)(2,1)S(1)}, bf16[3,5,128,128]{3,2,1,0:T(8,128)(2,1)S(1)}, u32[]{:S(2)}, u32[]{:S(2)}) collective-permute-start(bf16[3,5,128,128]{3,2,1,0:T(8,128)(2,1)S(1)} %get-tuple-element.65), channel_id=1, source_target_pairs={{0,24},{8,16},{16,8},{24,0},{1,25},{9,17},{17,9},{25,1},{2,26},{10... | collective-permute-start | bytes 1474568 | tf_op jit(solution)/shard_map/ppermute | solution.py:378
  43.8 11.2 %collective-permute-start.11 = (bf16[3,5,128,128]{3,2,1,0:T(8,128)(2,1)S(1)}, bf16[3,5,128,128]{3,2,1,0:T(8,128)(2,1)S(1)}, u32[]{:S(2)}, u32[]{:S(2)}) collective-permute-start(bf16[3,5,128,128]{3,2,1,0:T(8,128)(2,1)S(1)} %get-tuple-element.66), channel_id=1, source_target_pairs={{0,8},{8,0},{16,24},{24,16},{1,9},{9,1},{17,25},{25,17},{2,10},{10... | collective-permute-start | bytes 1474568 | tf_op jit(solution)/shard_map/ppermute | solution.py:379
  52.9 13.5 %collective-permute-start.14 = (bf16[3,5,128,128]{3,2,1,0:T(8,128)(2,1)S(1)}, bf16[3,5,128,128]{3,2,1,0:T(8,128)(2,1)S(1)}, u32[]{:S(2)}, u32[]{:S(2)}) collective-permute-start(bf16[3,5,128,128]{3,2,1,0:T(8,128)(2,1)S(1)} %get-tuple-element.77), channel_id=1, source_target_pairs={{0,24},{8,16},{16,8},{24,0},{1,25},{9,17},{17,9},{25,1},{2,26},{10... | collective-permute-start | bytes 1474568 | tf_op jit(solution)/shard_map/ppermute | solution.py:378
  53.0 13.4 %collective-permute-start.15 = (bf16[3,5,128,128]{3,2,1,0:T(8,128)(2,1)S(1)}, bf16[3,5,128,128]{3,2,1,0:T(8,128)(2,1)S(1)}, u32[]{:S(2)}, u32[]{:S(2)}) collective-permute-start(bf16[3,5,128,128]{3,2,1,0:T(8,128)(2,1)S(1)} %get-tuple-element.78), channel_id=1, source_target_pairs={{0,8},{8,0},{16,24},{24,16},{1,9},{9,1},{17,25},{25,17},{2,10},{10... | collective-permute-start | bytes 1474568 | tf_op jit(solution)/shard_map/ppermute | solution.py:379

commit v6 on v5

--- a/solution.py
+++ b/solution.py
@@ -112,8 +112,7 @@
 def later_kernel(turn, a_own, after, *outs):
     odd, flip = turns(turn)
     for i, out in enumerate(outs):
-        for x in range(2):
-            out[x, 0] = a_own[i // 2 + 1, x ^ flip, odd if i % 2 else 1 - odd]
+        out[...] = a_own[i // 4 + 1, (i // 2 & 1) ^ flip, odd if i % 2 else 1 - odd]
 
 
 def join_kernel(near, far, out):
@@ -175,14 +174,21 @@
             out[lag_x, lag_y] = total[:, lag_x * block : (lag_x + 1) * block].astype(out.dtype)
 
 
-def near_own_kernel(operators, table, turn, a_own, p_own, p_near, own_out, own_in, near_out, near_in, flat, w_ref):
-    odd, flip = turns(turn)
-    fill(flat, 0, ((-1, own_out, 0), (0, p_own, flip), (1, p_own, 1 - flip), (2, own_in, 0)))
-    fill(flat, HALF, ((-1, near_out, 0), (0, p_near, flip), (1, p_near, 1 - flip), (2, near_in, 0)))
+def near_own_inner_kernel(operators, table, turn, a_own, p_own, p_near, own_in, near_in, flat, *w_refs):
+    odd, flip = turns(turn)
+    fill(flat, 0, ((0, p_own, flip), (1, p_own, 1 - flip), (2, own_in, 0)))
+    fill(flat, HALF, ((0, p_near, flip), (1, p_near, 1 - flip), (2, near_in, 0)))
     flat[ZERO] = jnp.zeros(flat.shape[1:], flat.dtype)
-    for s in range(operators):
-        for x in range(2):
-            fine_row(table, table_row(operators, OWN_1, s, x), flat, row_of(a_own.at[s, x ^ flip, 1 - odd]), w_ref.at[s, x])
+    for s, w_ref in enumerate(w_refs):
+        fine_row(table, table_row(operators, OWN_1, s, 1), flat, row_of(a_own.at[s, 1 - flip, 1 - odd]), w_ref)
+
+
+def near_own_outer_kernel(operators, table, turn, a_own, own_out, near_out, held, flat, *w_refs):
+    odd, flip = turns(turn)
+    fill(flat, 0, ((-1, own_out, 0),))
+    fill(flat, HALF, ((-1, near_out, 0),))
+    for s, w_ref in enumerate(w_refs):
+        fine_row(table, table_row(operators, OWN_1, s, 0), flat, row_of(a_own.at[s, flip, 1 - odd]), w_ref)
 
 
 def near_kernel(operators, table, flat, a_pair, w_ref):
@@ -196,7 +202,7 @@
     fill(flat, 2 * HALF, ((-1, far_out, 0), (0, p_far, flip), (1, p_far, 1 - flip)))
     fine_row(table, table_row(operators, FAR, 0, 0), flat, joined_row(a_pair, 1, 0), w_far)
     fine_row(own_table, table_row(operators, OWN_0, 0, 0), flat, row_of(a_own.at[0, flip, odd]), w_own_0)
-    edge(turn, (p_far, p_own, p_own, p_near), one_row(0, w_far, w_own_0, w_own.at[0, 0], w_near), 0, out)
+    edge(turn, (p_far, p_own, p_own, p_near), one_row(0, w_far, w_own_0, w_own, w_near), 0, out)
 
 
 def first_inner_kernel(
@@ -207,53 +213,50 @@
     fine_row(table, table_row(operators, NEAR, 0, 1), flat, joined_row(a_pair, 0, 1), w_near)
     fine_row(table, table_row(operators, FAR, 0, 1), flat, joined_row(a_pair, 1, 1), w_far)
     fine_row(own_table, table_row(operators, OWN_0, 0, 1), flat, row_of(a_own.at[0, 1 - flip, odd]), w_own_0)
-    edge(turn, (p_far, p_own, p_own, p_near), one_row(1, w_far, w_own_0, w_own.at[0, 1], w_near), 1, out)
+    edge(turn, (p_far, p_own, p_own, p_near), one_row(1, w_far, w_own_0, w_own, w_near), 1, out)
 
 
 def one_row(x, *w_refs):
     return [{x: ref} for ref in w_refs]
 
 
-def own_0_kernel(operators, operator, table, turn, a_own, flat, *w_refs):
-    odd, flip = turns(turn)
-    for x in range(2):
-        fine_row(table, table_row(operators, OWN_0, operator, x), flat, row_of(a_own.at[operator, x ^ flip, odd]), w_refs[x])
-
-
 def sides_kernel(
-    operators, operator, table, turn, a_near, a_far, flat, w_own, own_w_0, own_w_1, p_own, p_near, p_far, outer, inner, *w_refs
+    operators, operator, x, own_table, table, turn, a_own, a_near, a_far, flat, w_own, p_own, p_near, p_far, out, w_near, w_far, w_own_0
 ):
-    for x, (out, w_own_0) in enumerate(((outer, own_w_0), (inner, own_w_1))):
-        w_near, w_far = w_refs[2 * x : 2 * x + 2]
-        fine_row(table, table_row(operators, NEAR, operator, x), flat, row_of(a_near.at[x, 0]), w_near)
-        fine_row(table, table_row(operators, FAR, operator, x), flat, row_of(a_far.at[x, 0]), w_far)
-        edge(turn, (p_far, p_own, p_own, p_near), one_row(x, w_far, w_own_0, w_own.at[operator, x], w_near), x, out)
-
-
-def centre_kernel(operator, turn, p_own, p_near, p_far, w_own, *refs):
+    odd, flip = turns(turn)
+    fine_row(own_table, table_row(operators, OWN_0, operator, x), flat, row_of(a_own.at[operator, x ^ flip, odd]), w_own_0)
+    fine_row(table, table_row(operators, NEAR, operator, x), flat, row_of(a_near), w_near)
+    fine_row(table, table_row(operators, FAR, operator, x), flat, row_of(a_far), w_far)
+    edge(turn, (p_far, p_own, p_own, p_near), one_row(x, w_far, w_own_0, w_own, w_near), x, out)
+
+
+def centre_kernel(turn, p_own, p_near, p_far, *refs):
     out = refs[-1]
     block = out.shape[-1]
-    w_refs = (refs[0:2], refs[2:4], (w_own.at[operator, 0], w_own.at[operator, 1]), refs[4:6])
+    w_refs = (refs[0:2], refs[2:4], refs[4:6], refs[6:8])
     for lag_y in range(5):
         total = coarse_column(turn, (p_far, p_own, p_own, p_near), w_refs, (0, 1), lag_y, 0)
         for lag_x in range(3):
             out[lag_x, lag_y] = total[:, lag_x * block : (lag_x + 1) * block]
 
 
-def final_kernel(turn, *refs):
-    out = refs[-1]
-    odd, flip = turns(turn)
-    for operator in range(out.shape[0]):
-        own, outer, inner = refs[3 * operator : 3 * operator + 3]
-        for lag_x in range(5):
-            for lag_y in range(5):
-                total = None
-                for part, at in ((outer, 2 - lag_x), (own, lag_x - 1), (inner, 4 - lag_x)):
-                    if 0 <= at < 3:
-                        term = part[at, lag_y].astype(jnp.float32)
-                        total = term if total is None else total + term
-                place = 5 * (lag_x + flip * (4 - 2 * lag_x)) + lag_y + odd * (4 - 2 * lag_y)
-                out[operator, 0, 0, place] = total.astype(out.dtype)
+def final_kernel(operator, turn, own, outer, inner, *refs):
+    out, total, sems = refs[-3:]
+    odd, flip = turns(turn)
+    copies = []
+    for lag_x in range(5):
+        for lag_y in range(5):
+            block = None
+            for part, at in ((outer, 2 - lag_x), (own, lag_x - 1), (inner, 4 - lag_x)):
+                if 0 <= at < 3:
+                    term = part[at, lag_y].astype(jnp.float32)
+                    block = term if block is None else block + term
+            total[lag_x, lag_y + odd * (4 - 2 * lag_y)] = block.astype(out.dtype)
+        place = pl.ds(5 * (lag_x + flip * (4 - 2 * lag_x)), 5)
+        copies.append(pltpu.make_async_copy(total.at[lag_x], out.at[operator, 0, 0, place], sems.at[lag_x]))
+        copies[-1].start()
+    for copy in copies:
+        copy.wait()
 
 
 def per_device(a_vals, a_off, a_count, p_vals):
@@ -274,12 +277,12 @@
     w_shape = jax.ShapeDtypeStruct((3, block, 3 * block), bf16)
     part_shape = jax.ShapeDtypeStruct((3, 5, block, block), bf16)
 
-    def call(kernel, in_specs, out_shape, products, name, scratch=(), aliases=None, limit=VMEM_LIMIT):
+    def call(kernel, in_specs, out_shape, products, name, scratch=(), aliases=None, limit=VMEM_LIMIT, out_spec=None):
         single = not isinstance(out_shape, list)
         return pl.pallas_call(
             kernel,
             in_specs=in_specs,
-            out_specs=vmem if single else [vmem] * len(out_shape),
+            out_specs=(out_spec or vmem) if single else [vmem] * len(out_shape),
             out_shape=out_shape,
             scratch_shapes=list(scratch),
             input_output_aliases=aliases or {},
@@ -311,26 +314,31 @@
     near_in = lax.ppermute(near_in, "row", in_way)
     near_out = lax.ppermute(near_out, "row", out_way)
     far_out = lax.ppermute(near_out, "col", on_way)
-    flat, w_own = call(
-        functools.partial(near_own_kernel, operators),
-        [smem, smem] + [vmem] * 7,
-        [flat_shape, jax.ShapeDtypeStruct((operators, 2) + w_shape.shape, bf16)],
-        360,
-        "near_own",
-    )(own_table, turn, a_vals, p_vals, p_near, own_out, own_in, near_out, near_in)
-
-    p_far, w_own = lax.optimization_barrier((p_far, w_own))
-    far_in = call(rows_kernel, [smem, vmem], [row_shape], 1, "row")(turn, p_far)[0]
+    flat, *w_inner = call(
+        functools.partial(near_own_inner_kernel, operators),
+        [smem, smem] + [vmem] * 5,
+        [flat_shape] + [w_shape] * operators,
+        180,
+        "near_own_inner",
+    )(own_table, turn, a_vals, p_vals, p_near, own_in, near_in)
+    near_out, flat = lax.optimization_barrier((near_out, flat))
+    flat, *w_outer = call(
+        functools.partial(near_own_outer_kernel, operators),
+        [smem, smem] + [vmem] * 4,
+        [flat_shape] + [w_shape] * operators,
+        180,
+        "near_own_outer",
+        aliases={5: 0},
+    )(own_table, turn, a_vals, own_out, near_out, flat)
+    w_own = [w_outer, w_inner]
+
     later = call(
         later_kernel,
         [smem, vmem, any_spec],
-        [jax.ShapeDtypeStruct((2, 1, slots, block, block), bf16)] * (2 * operators - 2),
+        [jax.ShapeDtypeStruct((slots, block, block), bf16)] * (4 * operators - 4),
         1,
         "later",
-    )(turn, a_vals, near_in)
-    far_in = lax.ppermute(far_in, "row", in_way)
-    near_out, later_near = lax.optimization_barrier((near_out, later[0::2]))
-    w_own, later_far = lax.optimization_barrier((w_own, later[1::2]))
+    )(turn, a_vals, own_in)
     side_table = call(
         functools.partial(table_kernel, operators, (NEAR, FAR)), [smem, vmem], table_shape, 1, "side_table"
     )(turn, from_pair)
@@ -338,11 +346,22 @@
     near_w = call(functools.partial(near_kernel, operators), [smem, vmem, vmem], w_shape, 45, "near")(
         side_table, flat, from_pair
     )
-    a_near, a_far = [None], [None]
-    a_near += [lax.ppermute(send, "col", near_way) for send in later_near]
-    a_far += [lax.ppermute(send, "col", far_way) for send in later_far]
-
-    finals = []
+
+    near_w, p_far = lax.optimization_barrier((near_w, p_far))
+    far_in = call(rows_kernel, [smem, vmem], [row_shape], 1, "row")(turn, p_far)[0]
+    far_in = lax.ppermute(far_in, "row", in_way)
+
+    def send_row(x):
+        rows_sent = []
+        for s in range(1, operators):
+            near, far = later[4 * s - 4 + 2 * x : 4 * s - 2 + 2 * x]
+            rows_sent.append((lax.ppermute(near, "col", near_way), lax.ppermute(far, "col", far_way)))
+        return rows_sent
+
+    w_own, later = lax.optimization_barrier((w_own, later))
+    outer_a = send_row(0)
+
+    result = None
     for s in range(operators):
         own_w, far_w, sums = [None, None], [None, None], [None, None]
         if s == 0:
@@ -350,10 +369,10 @@
                 functools.partial(first_outer_kernel, operators),
                 [smem, smem, smem] + [vmem] * 9,
                 [part_shape, flat_shape, w_shape, w_shape],
-                150,
+                LONG,
                 "first_outer",
                 aliases={11: 1},
-            )(own_table, side_table, turn, a_vals, from_pair, w_own, near_w, p_vals, p_near, p_far, far_out, flat)
+            )(own_table, side_table, turn, a_vals, from_pair, w_own[0][0], near_w, p_vals, p_near, p_far, far_out, flat)
             sums[1], flat, far_w[1], own_w[1], inner_w = call(
                 functools.partial(first_inner_kernel, operators),
                 [smem, smem, smem] + [vmem] * 8,
@@ -361,37 +380,42 @@
                 LONG,
                 "first_inner",
                 aliases={10: 1},
-            )(own_table, side_table, turn, a_vals, from_pair, w_own, p_vals, p_near, p_far, far_in, flat)
+            )(own_table, side_table, turn, a_vals, from_pair, w_own[1][0], p_vals, p_near, p_far, far_in, flat)
             near_w = [near_w, inner_w]
+            inner_w, later = lax.optimization_barrier((inner_w, later))
+            a_sides = [None] + list(zip(outer_a, send_row(1)))
         else:
             near_w = [None, None]
-            own_w = call(
-                functools.partial(own_0_kernel, operators, s), [smem, smem, vmem, vmem], [w_shape] * 2, 90, "own_0"
-            )(own_table, turn, a_vals, flat)
-            *sums, near_w[0], far_w[0], near_w[1], far_w[1] = call(
-                functools.partial(sides_kernel, operators, s),
-                [smem, smem] + [vmem] * 9,
-                [part_shape] * 2 + [w_shape] * 4,
-                200,
-                "sides",
-            )(side_table, turn, a_near[s], a_far[s], flat, w_own, *own_w, p_vals, p_near, p_far)
+            for x in range(2):
+                if x == 1:
+                    from_out, w_own = lax.optimization_barrier((from_out, w_own))
+                sums[x], near_w[x], far_w[x], own_w[x] = call(
+                    functools.partial(sides_kernel, operators, s, x),
+                    [smem, smem, smem] + [vmem] * 8,
+                    [part_shape, w_shape, w_shape, w_shape],
+                    100,
+                    "sides",
+                )(own_table, side_table, turn, a_vals, *a_sides[s][x], flat, w_own[x][s], p_vals, p_near, p_far)
         from_out = lax.ppermute(sums[0], "row", out_way)
         from_in = lax.ppermute(sums[1], "row", in_way)
         centre = call(
-            functools.partial(centre_kernel, s),
-            [smem] + [vmem] * 10,
+            centre_kernel,
+            [smem] + [vmem] * 11,
             jax.ShapeDtypeStruct((3, 5, block, block), f32),
             144,
             "centre",
-        )(turn, p_vals, p_near, p_far, w_own, *far_w, *own_w, *near_w)
-        finals += [centre, from_out, from_in]
-    return call(
-        final_kernel,
-        [smem] + [vmem] * len(finals),
-        jax.ShapeDtypeStruct((operators, 1, 1, 25, block, block), bf16),
-        1,
-        "final",
-    )(turn, *finals)
+        )(turn, p_vals, p_near, p_far, *far_w, *own_w, w_own[0][s], w_own[1][s], *near_w)
+        result = call(
+            functools.partial(final_kernel, s),
+            [smem] + [vmem] * 3 + ([any_spec] if s else []),
+            jax.ShapeDtypeStruct((operators, 1, 1, 25, block, block), bf16),
+            1,
+            "final",
+            [pltpu.VMEM((5, 5, block, block), bf16), pltpu.SemaphoreType.DMA((5,))],
+            aliases={4: 0} if s else None,
+            out_spec=any_spec,
+        )(turn, centre, from_out, from_in, *([result] if s else []))
+    return result
 
 
 def solution(mesh):

time: 68.1 us -> 65.9 us (0.968)
  waiting for transfers between devices: 30.4 us -> 20.2 us
  starting transfers between devices: 18.9 us -> 24.5 us
  Pallas kernels: 14.7 us -> 17 us
    ppermute x2 -> x4, waiting for transfers between devices: 4.82 us -> 0.84 us  [the longest x2 0.83 us: send_row(): lax.ppermute(far, 'col', far_way)]
    ppermute x2, waiting for transfers between devices: 11.4 us -> 7.81 us  [per_device(): from_out = lax.ppermute(sums[0], 'row', out_way)]
    ppermute x2 -> x4, starting transfers between devices: 4.66 us -> 7.3 us  [the longest x2 5.02 us: send_row(): lax.ppermute(near, 'col', near_way)]
    pallas_call x7 -> x9, Pallas kernels: 8.92 us -> 11.2 us  [the longest x2 4.43 us: per_device(): call(functools.partial(sides_kernel, operators, s, x), [smem, smem, smem]...]
    ppermute x1, waiting for transfers between devices: 2.11 us -> 0.2 us  [per_device(): far_out = lax.ppermute(near_out, 'col', on_way)]
    ppermute x2, starting transfers between devices: 0.19 us -> 1.86 us  [per_device(): from_out = lax.ppermute(sums[0], 'row', out_way)]
    ppermute x2, starting transfers between devices: 0.96 us -> 2.56 us  [per_device(): from_in = lax.ppermute(sums[1], 'row', in_way)]
    ppermute x1, starting transfers between devices: 2.92 us -> 1.34 us  [per_device(): from_pair = lax.ppermute(joined, 'col', near_way)]
  transfers between devices with their start and end apart: 16 -> 18, of which waited for: 6 -> 7; matrix products, arithmetic and copies ran while one was open for 0% -> 0% of each run, Pallas kernels for 19% -> 24%
where the time goes in v6:
time: 65.9 us; the launch traced here: 65.6 us
  starting transfers between devices  24.5 us (37%)
  waiting for transfers between devices  20.2 us (31%)
  Pallas kernels  17 us (26%)
  local copies, waits for them, and re-layouts  3.73 us (6%)
    ppermute x2, waiting for transfers between devices, per_device(): from_out = lax.ppermute(sums[0], 'row', out_way)  7.81 us
    ppermute x1, waiting for transfers between devices, per_device(): near_out = lax.ppermute(near_out, 'row', out_way)  6.49 us
    ppermute x2, starting transfers between devices, send_row(): lax.ppermute(near, 'col', near_way)  5.02 us
    pallas_call x2, Pallas kernels, per_device(): call(functools.partial(sides_kernel, operators, s, x), [smem, smem, smem]...  4.43 us
    ppermute x1, waiting for transfers between devices, per_device(): moved = lax.ppermute(own_0, 'col', aside_way)  3.98 us
    unnamed x12, local copies, waits for them, and re-layouts  3.73 us
    ppermute x1, starting transfers between devices, per_device(): moved = lax.ppermute(own_0, 'col', aside_way)  3.65 us
    ppermute x1, starting transfers between devices, per_device(): p_near = lax.ppermute(p_vals, 'col', near_way)  2.94 us
  transfers between devices with their start and end apart: 18, of which 7 were waited for; matrix products, arithmetic and copies ran while one was open for 0% of the time, Pallas kernels for 24%

profile of v6, /device:TPU:0, one launch (start us, length us, event | category | flops | bytes accessed | tf_op | source)
XLA Modules:
  0.0 65.6 jit_solution(15461411325828141439)
XLA Ops:
  0.0 2.9 %collective-permute-start = (bf16[2,2,4,128,128]{4,3,2,1,0:T(8,128)(2,1)}, bf16[2,2,4,128,128]{4,3,2,1,0:T(8,128)(2,1)S(1)}, u32[]{:S(2)}, u32[]{:S(2)}) collective-permute-start(bf16[2,2,4,128,128]{4,3,2,1,0:T(8,128)(2,1)} %p_own.13), channel_id=1, source_target_pairs={{0,1},{1,0},{2,3},{3,2},{4,5},{5,4},{6,7},{7,6},{8,9},{9,8},{10,11... | collective-permute-start | bytes 1572872 | tf_op jit(solution)/shard_map/ppermute | solution.py:294
  2.9 1.3 %copy-done = bf16[2,2,2,5,128,128]{5,4,3,2,1,0:T(8,128)(2,1)S(1)} copy-done((bf16[2,2,2,5,128,128]{5,4,3,2,1,0:T(8,128)(2,1)S(1)}, bf16[2,2,2,5,128,128]{5,4,3,2,1,0:T(8,128)(2,1)}, u32[]{:S(2)}) %copy-start) | copy-done | bytes 1310744
  4.3 0.7 %copy-done.4 = s32[2,2,2,5]{3,2,1,0:T(2,128)S(1)} copy-done((s32[2,2,2,5]{3,2,1,0:T(2,128)S(1)}, s32[2,2,2,5]{3,2,1,0:T(2,128)}, u32[]{:S(2)}) %copy-start.4) | copy-done | bytes 184
  4.9 0.7 %copy-done.5 = s32[2,2,2]{2,1,0:T(2,128)S(1)} copy-done((s32[2,2,2]{2,1,0:T(2,128)S(1)}, s32[2,2,2]{2,1,0:T(2,128)}, u32[]{:S(2)}) %copy-start.5) | copy-done | bytes 56
  5.6 0.7 %pack.1 = (bf16[1296,128]{1,0:T(8,128)(2,1)S(1)}, bf16[1296,128]{1,0:T(8,128)(2,1)S(1)}) custom-call(s32[1]{0:T(128)} %bitcast.turn, s32[2,2,2,5]{3,2,1,0:T(2,128)S(1)} %copy-done.4, s32[2,2,2]{2,1,0:T(2,128)S(1)} %copy-done.5, bf16[2,2,2,5,128,128]{5,4,3,2,1,0:T(8,128)(2,1)S(1)} %copy-done), custom_call_target="tpu_custom_call" | custom-call | flops 1 | bytes 1024 | tf_op jit(solution)/shard_map/pack/pallas_call | solution.py:296
  6.3 3.7 %collective-permute-start.1 = (bf16[1296,128]{1,0:T(8,128)(2,1)S(1)}, bf16[1296,128]{1,0:T(8,128)(2,1)S(1)}, u32[]{:S(2)}, u32[]{:S(2)}) collective-permute-start(bf16[1296,128]{1,0:T(8,128)(2,1)S(1)} %get-tuple-element.60.refs_0_), channel_id=1, source_target_pairs={{0,6},{1,3},{2,0},{3,5},{4,2},{5,7},{6,4},{7,1},{8,14},{9,11},{10,... | collective-permute-start | bytes 995336 | tf_op jit(solution)/shard_map/ppermute | solution.py:297
  10.0 1.0 %copy-done.2 = bf16[2,2,4,128,128]{4,3,2,1,0:T(8,128)(2,1)S(1)} copy-done((bf16[2,2,4,128,128]{4,3,2,1,0:T(8,128)(2,1)S(1)}, bf16[2,2,4,128,128]{4,3,2,1,0:T(8,128)(2,1)}, u32[]{:S(2)}) %copy-start.2) | copy-done | bytes 524312
  11.1 0.1 collective-permute-start.3
  11.1 1.6 %collective-permute-start.4 = (bf16[1,2,4,128,128]{4,3,2,1,0:T(8,128)(2,1)S(1)}, bf16[1,2,4,128,128]{4,3,2,1,0:T(8,128)(2,1)S(1)}, u32[]{:S(2)}, u32[]{:S(2)}) collective-permute-start(bf16[1,2,4,128,128]{4,3,2,1,0:T(8,128)(2,1)S(1)} %get-tuple-element.64), channel_id=1, source_target_pairs={{0,24},{8,16},{16,8},{24,0},{1,25},{9,17},{17,9},{25,1},{2,26},{10... | collective-permute-start | bytes 786440 | tf_op jit(solution)/shard_map/ppermute | solution.py:308
  12.8 4.0 %collective-permute-done.1.far = bf16[1296,128]{1,0:T(8,128)(2,1)S(1)} collective-permute-done((bf16[1296,128]{1,0:T(8,128)(2,1)S(1)}, bf16[1296,128]{1,0:T(8,128)(2,1)S(1)}, u32[]{:S(2)}, u32[]{:S(2)}) %collective-permute-start.1) | collective-permute-done | bytes 331808 | tf_op jit(solution)/shard_map/ppermute | solution.py:297
  16.8 1.3 %collective-permute-start.2 = (bf16[2592,128]{1,0:T(8,128)(2,1)S(1)}, bf16[2592,128]{1,0:T(8,128)(2,1)S(1)}, u32[]{:S(2)}, u32[]{:S(2)}) collective-permute-start(bf16[2592,128]{1,0:T(8,128)(2,1)S(1)} %join.1), channel_id=1, source_target_pairs={{0,1},{1,0},{2,3},{3,2},{4,5},{5,4},{6,7},{7,6},{8,9},{9,8},{10,11... | collective-permute-start | bytes 1990664 | tf_op jit(solution)/shard_map/ppermute | solution.py:311
  18.2 0.2 collective-permute-start.7
  18.4 0.0 collective-permute-done.3.own_in.after
  18.4 0.9 %collective-permute-done.4.own_out = bf16[1,2,4,128,128]{4,3,2,1,0:T(8,128)(2,1)S(1)} collective-permute-done((bf16[1,2,4,128,128]{4,3,2,1,0:T(8,128)(2,1)S(1)}, bf16[1,2,4,128,128]{4,3,2,1,0:T(8,128)(2,1)S(1)}, u32[]{:S(2)}, u32[]{:S(2)}) %collective-permute-start.4) | collective-permute-done | bytes 262176 | tf_op jit(solution)/shard_map/ppermute | solution.py:308
  19.3 1.6 %collective-permute-start.5 = (bf16[1,2,4,128,128]{4,3,2,1,0:T(8,128)(2,1)S(1)}, bf16[1,2,4,128,128]{4,3,2,1,0:T(8,128)(2,1)S(1)}, u32[]{:S(2)}, u32[]{:S(2)}) collective-permute-start(bf16[1,2,4,128,128]{4,3,2,1,0:T(8,128)(2,1)S(1)} %get-tuple-element.67), channel_id=1, source_target_pairs={{0,24},{8,16},{16,8},{24,0},{1,25},{9,17},{17,9},{25,1},{2,26},{10... | collective-permute-start | bytes 786440 | tf_op jit(solution)/shard_map/ppermute | solution.py:315
  20.9 0.1 collective-permute-start.6
  21.0 6.5 %collective-permute-done.5.near_out = bf16[1,2,4,128,128]{4,3,2,1,0:T(8,128)(2,1)S(1)} collective-permute-done((bf16[1,2,4,128,128]{4,3,2,1,0:T(8,128)(2,1)S(1)}, bf16[1,2,4,128,128]{4,3,2,1,0:T(8,128)(2,1)S(1)}, u32[]{:S(2)}, u32[]{:S(2)}) %collective-permute-start.5) | collective-permute-done | bytes 262176 | tf_op jit(solution)/shard_map/ppermute | solution.py:315
  27.5 1.1 %collective-permute-start.11 = (bf16[1,2,4,128,128]{4,3,2,1,0:T(8,128)(2,1)S(1)}, bf16[1,2,4,128,128]{4,3,2,1,0:T(8,128)(2,1)S(1)}, u32[]{:S(2)}, u32[]{:S(2)}) collective-permute-start(bf16[1,2,4,128,128]{4,3,2,1,0:T(8,128)(2,1)S(1)} %collective-permute-done.5.near_out), channel_id=1, source_target_pairs={{0,2},{1,7},{2,4},{3,1},{4,6},{5,3},{6,0},{7,5},{8,10},{9,15},{10,... | collective-permute-start | bytes 786440 | tf_op jit(solution)/shard_map/ppermute | solution.py:316
  28.6 0.1 own_table.1.table
  28.7 0.8 %later.1 = (bf16[5,128,128]{2,1,0:T(8,128)(2,1)}, bf16[5,128,128]{2,1,0:T(8,128)(2,1)}, bf16[5,128,128]{2,1,0:T(8,128)(2,1)S(1)}, bf16[5,128,128]{2,1,0:T(8,128)(2,1)S(1)}) custom-call(s32[1]{0:T(128)} %bitcast.turn, bf16[2,2,2,5,128,128]{5,4,3,2,1,0:T(8,128)(2,1)S(1)} %copy-done.1, bf16[1,2,4,128,128]{4,3,2,1,0:T(8,128)(2,1)S(1)} %collective-permute-done.3.own_in.after), custom_call_target="tpu_custom_call" | custom-call | flops 1 | bytes 1024 | tf_op jit(solution)/shard_map/later/pallas_call | solution.py:335
  29.5 0.0 collective-permute-done.6.near_in
  29.5 1.5 %near_own_inner.1 = (bf16[97,128,128]{2,1,0:T(8,128)(2,1)S(1)}, bf16[3,128,384]{2,1,0:T(8,128)(2,1)S(1)}, bf16[3,128,384]{2,1,0:T(8,128)(2,1)S(1)}) custom-call(s32[8,45]{1,0:T(8,128)S(1)} %own_table.1.table, s32[1]{0:T(128)} %bitcast.turn, bf16[2,2,2,5,128,128]{5,4,3,2,1,0:T(8,128)(2,1)S(1)} %copy-done.1, bf16[2,2,4,128,128]{4,3,2,1,0:T(8,128)(2,1)S(1)} %copy-done.3, ...), custom_call_target="tpu_custom_call" | custom-call | flops 180 | bytes 1024 | tf_op jit(solution)/shard_map/near_own_inner/pallas_call | solution.py:317
  31.0 1.4 %near_own_outer.1 = (bf16[97,128,128]{2,1,0:T(8,128)(2,1)S(1)}, bf16[3,128,384]{2,1,0:T(8,128)(2,1)S(1)}, bf16[3,128,384]{2,1,0:T(8,128)(2,1)S(1)}) custom-call(s32[8,45]{1,0:T(8,128)S(1)} %own_table.1.table, s32[1]{0:T(128)} %bitcast.turn, bf16[2,2,2,5,128,128]{5,4,3,2,1,0:T(8,128)(2,1)S(1)} %copy-done.1, ...), custom_call_target="tpu_custom_call", output_to_operand_aliasing={{0}: (5, {})} | custom-call | flops 180 | bytes 1024 | tf_op jit(solution)/shard_map/near_own_outer/pallas_call | solution.py:325
  32.3 3.3 %collective-permute-start.8 = (bf16[5,128,128]{2,1,0:T(8,128)(2,1)}, bf16[5,128,128]{2,1,0:T(8,128)(2,1)}, u32[]{:S(2)}, u32[]{:S(2)}) collective-permute-start(bf16[5,128,128]{2,1,0:T(8,128)(2,1)} %get-tuple-element.83), channel_id=1, source_target_pairs={{0,1},{1,0},{2,3},{3,2},{4,5},{5,4},{6,7},{7,6},{8,9},{9,8},{10,11... | collective-permute-start | bytes 491528 | tf_op jit(solution)/shard_map/ppermute | solution.py:358
  35.6 1.0 %collective-permute-start.9 = (bf16[5,128,128]{2,1,0:T(8,128)(2,1)}, bf16[5,128,128]{2,1,0:T(8,128)(2,1)}, u32[]{:S(2)}, u32[]{:S(2)}) collective-permute-start(bf16[5,128,128]{2,1,0:T(8,128)(2,1)} %get-tuple-element.84), channel_id=1, source_target_pairs={{0,7},{1,2},{2,1},{3,4},{4,3},{5,6},{6,5},{7,0},{8,15},{9,10},{10,... | collective-permute-start | bytes 491528 | tf_op jit(solution)/shard_map/ppermute | solution.py:358
  36.6 0.0 collective-permute-done.2.refs_0_.a_pair
  36.6 0.1 side_table.1.table
  36.7 1.1 %near.1.w_near.refs_6_ = bf16[3,128,384]{2,1,0:T(8,128)(2,1)S(1)} custom-call(s32[8,45]{1,0:T(8,128)S(1)} %side_table.1.table, bf16[97,128,128]{2,1,0:T(8,128)(2,1)S(1)} %get-tuple-element.73.flat.held, bf16[2592,128]{1,0:T(8,128)(2,1)S(1)} %collective-permute-done.2.refs_0_.a_pair), custom_call_target="tpu_custom_call" | custom-call | flops 45 | bytes 1024 | tf_op jit(solution)/shard_map/near/pallas_call | solution.py:346
  37.8 0.1 collective-permute-start.10
  37.9 0.2 collective-permute-done.11.far_out
  38.1 1.7 %first_outer.1 = (bf16[3,5,128,128]{3,2,1,0:T(8,128)(2,1)S(1)}, bf16[97,128,128]{2,1,0:T(8,128)(2,1)S(1)}, bf16[3,128,384]{2,1,0:T(8,128)(2,1)S(1)}, bf16[3,128,384]{2,1,0:T(8,128)(2,1)S(1)}) custom-call(s32[8,45]{1,0:T(8,128)S(1)} %own_table.1.table, s32[8,45]{1,0:T(8,128)S(1)} %side_table.1.table, s32[1]{0:T(128)} %bitcast.turn, ...), custom_call_target="tpu_custom_call", output_to_operand_aliasing={{1}: (11, {})} | custom-call | flops 99999997952 | bytes 1024 | tf_op jit(solution)/shard_map/first_outer/pallas_call | solution.py:368
  39.8 1.5 %collective-permute-start.14 = (bf16[3,5,128,128]{3,2,1,0:T(8,128)(2,1)S(1)}, bf16[3,5,128,128]{3,2,1,0:T(8,128)(2,1)S(1)}, u32[]{:S(2)}, u32[]{:S(2)}) collective-permute-start(bf16[3,5,128,128]{3,2,1,0:T(8,128)(2,1)S(1)} %get-tuple-element.97), channel_id=1, source_target_pairs={{0,24},{8,16},{16,8},{24,0},{1,25},{9,17},{17,9},{25,1},{2,26},{10... | collective-permute-start | bytes 1474568 | tf_op jit(solution)/shard_map/ppermute | solution.py:399
  41.3 2.0 %first_inner.1 = (bf16[3,5,128,128]{3,2,1,0:T(8,128)(2,1)S(1)}, bf16[97,128,128]{2,1,0:T(8,128)(2,1)S(1)}, bf16[3,128,384]{2,1,0:T(8,128)(2,1)S(1)}, bf16[3,128,...) custom-call(s32[8,45]{1,0:T(8,128)S(1)} %own_table.1.table, ...), custom_call_target="tpu_custom_call", output_to_operand_aliasing={{1}: (10, {})} | custom-call | flops 99999997952 | bytes 1024 | tf_op jit(solution)/shard_map/first_inner/pallas_call | solution.py:376
  43.3 1.7 %collective-permute-start.12 = (bf16[5,128,128]{2,1,0:T(8,128)(2,1)S(1)}, bf16[5,128,128]{2,1,0:T(8,128)(2,1)S(1)}, u32[]{:S(2)}, u32[]{:S(2)}) collective-permute-start(bf16[5,128,128]{2,1,0:T(8,128)(2,1)S(1)} %get-tuple-element.95), channel_id=1, source_target_pairs={{0,1},{1,0},{2,3},{3,2},{4,5},{5,4},{6,7},{7,6},{8,9},{9,8},{10,11... | collective-permute-start | bytes 491528 | tf_op jit(solution)/shard_map/ppermute | solution.py:358
  45.0 1.3 %collective-permute-start.13 = (bf16[5,128,128]{2,1,0:T(8,128)(2,1)S(1)}, bf16[5,128,128]{2,1,0:T(8,128)(2,1)S(1)}, u32[]{:S(2)}, u32[]{:S(2)}) collective-permute-start(bf16[5,128,128]{2,1,0:T(8,128)(2,1)S(1)} %get-tuple-element.96), channel_id=1, source_target_pairs={{0,7},{1,2},{2,1},{3,4},{4,3},{5,6},{6,5},{7,0},{8,15},{9,10},{10,... | collective-permute-start | bytes 491528 | tf_op jit(solution)/shard_map/ppermute | solution.py:358
  46.4 2.5 %collective-permute-start.17 = (bf16[3,5,128,128]{3,2,1,0:T(8,128)(2,1)S(1)}, bf16[3,5,128,128]{3,2,1,0:T(8,128)(2,1)S(1)}, u32[]{:S(2)}, u32[]{:S(2)}) collective-permute-start(bf16[3,5,128,128]{3,2,1,0:T(8,128)(2,1)S(1)} %get-tuple-element.112), channel_id=1, source_target_pairs={{0,8},{8,0},{16,24},{24,16},{1,9},{9,1},{17,25},{25,17},{2,10},{10... | collective-permute-start | bytes 1474568 | tf_op jit(solution)/shard_map/ppermute | solution.py:400
  48.9 0.0 collective-permute-done.9.a_far
  48.9 2.4 %sides.2 = (bf16[3,5,128,128]{3,2,1,0:T(8,128)(2,1)S(1)}, bf16[3,128,384]{2,1,0:T(8,128)(2,1)S(1)}, bf16[3,128,384]{2,1,0:T(8,128)(2,1)S(1)}, bf16[3,128,384]{2,1,0:T(8,128)(2,1)S(1)}) custom-call(s32[8,45]{1,0:T(8,128)S(1)} %own_table.1.table, s32[8,45]{1,0:T(8,128)S(1)} %side_table.1.table, s32[1]{0:T(128)} %bitcast.turn, ...), custom_call_target="tpu_custom_call" | custom-call | flops 100 | bytes 1024 | tf_op jit(solution)/shard_map/sides/pallas_call | solution.py:392
  51.3 0.4 collective-permute-start.15
  51.6 1.4 %collective-permute-done.14.outer = bf16[3,5,128,128]{3,2,1,0:T(8,128)(2,1)S(1)} collective-permute-done((bf16[3,5,128,128]{3,2,1,0:T(8,128)(2,1)S(1)}, bf16[3,5,128,128]{3,2,1,0:T(8,128)(2,1)S(1)}, u32[]{:S(2)}, u32[]{:S(2)}) %collective-permute-start.14) | collective-permute-done | bytes 491552 | tf_op jit(solution)/shard_map/ppermute | solution.py:399
  53.0 0.8 %collective-permute-done.13.a_far = bf16[5,128,128]{2,1,0:T(8,128)(2,1)S(1)} collective-permute-done((bf16[5,128,128]{2,1,0:T(8,128)(2,1)S(1)}, bf16[5,128,128]{2,1,0:T(8,128)(2,1)S(1)}, u32[]{:S(2)}, u32[]{:S(2)}) %collective-permute-start.13) | collective-permute-done | bytes 163872 | tf_op jit(solution)/shard_map/ppermute | solution.py:358
  53.9 2.0 %sides.3 = (bf16[3,5,128,128]{3,2,1,0:T(8,128)(2,1)S(1)}, bf16[3,128,384]{2,1,0:T(8,128)(2,1)S(1)}, bf16[3,128,384]{2,1,0:T(8,128)(2,1)S(1)}, bf16[3,128,384]{2,1,0:T(8,128)(2,1)S(1)}) custom-call(s32[8,45]{1,0:T(8,128)S(1)} %own_table.1.table, s32[8,45]{1,0:T(8,128)S(1)} %side_table.1.table, s32[1]{0:T(128)} %bitcast.turn, ...), custom_call_target="tpu_custom_call" | custom-call | flops 100 | bytes 1024 | tf_op jit(solution)/shard_map/sides/pallas_call | solution.py:392
  55.9 0.1 collective-permute-start.16
  56.0 0.6 centre.3.own
  56.6 0.6 centre.2.own
  57.3 1.0 %final.2.refs_0_ = bf16[2,1,1,25,128,128]{5,4,3,2,1,0:T(8,128)(2,1)} custom-call(s32[1]{0:T(128)} %bitcast.turn, f32[3,5,128,128]{3,2,1,0:T(8,128)S(1)} %centre.3.own, bf16[3,5,128,128]{3,2,1,0:T(8,128)(2,1)S(1)} %collective-permute-done.14.outer, bf16[3,5,128,128]{3,2,1,0:T(8,128)(2,1)S(1)} %collective-permute-done.17.inner), custom_call_target="tpu_custom_call" | custom-call | flops 1 | bytes 1024 | tf_op jit(solution)/shard_map/final/pallas_call | solution.py:408
  58.2 6.4 %collective-permute-done.15.outer = bf16[3,5,128,128]{3,2,1,0:T(8,128)(2,1)S(1)} collective-permute-done((bf16[3,5,128,128]{3,2,1,0:T(8,128)(2,1)S(1)}, bf16[3,5,128,128]{3,2,1,0:T(8,128)(2,1)S(1)}, u32[]{:S(2)}, u32[]{:S(2)}) %collective-permute-start.15) | collective-permute-done | bytes 491552 | tf_op jit(solution)/shard_map/ppermute | solution.py:399
  64.7 1.0 %final.3 = bf16[2,1,1,25,128,128]{5,4,3,2,1,0:T(8,128)(2,1)} custom-call(s32[1]{0:T(128)} %bitcast.turn, f32[3,5,128,128]{3,2,1,0:T(8,128)S(1)} %centre.2.own, bf16[3,5,128,128]{3,2,1,0:T(8,128)(2,1)S(1)} %collective-permute-done.15.outer, bf16[3,5,128,128]{3,2,1,0:T(8,128)(2,1)S(1)} %collective-permute-done.16.inner, ...), custom_call_target="tpu_custom_call", output_to_operand_aliasing={{}: (4, {})} | custom-call | flops 1 | bytes 1024 | tf_op jit(solution)/shard_map/final/pallas_call | solution.py:408
  (19 shorter events, 0.2 us)
Async XLA Ops:
  0.0 16.8 %collective-permute-start = (bf16[2,2,4,128,128]{4,3,2,1,0:T(8,128)(2,1)}, bf16[2,2,4,128,128]{4,3,2,1,0:T(8,128)(2,1)S(1)}, u32[]{:S(2)}, u32[]{:S(2)}) collective-permute-start(bf16[2,2,4,128,128]{4,3,2,1,0:T(8,128)(2,1)} %p_own.13), channel_id=1, source_target_pairs={{0,1},{1,0},{2,3},{3,2},{4,5},{5,4},{6,7},{7,6},{8,9},{9,8},{10,11... | collective-permute-start | bytes 1572872 | tf_op jit(solution)/shard_map/ppermute | solution.py:294
  2.9 1.3 %copy-start = (bf16[2,2,2,5,128,128]{5,4,3,2,1,0:T(8,128)(2,1)S(1)}, bf16[2,2,2,5,128,128]{5,4,3,2,1,0:T(8,128)(2,1)}, u32[]{:S(2)}) copy-start(bf16[2,2,2,5,128,128]{5,4,3,2,1,0:T(8,128)(2,1)} %a_own.15) | copy-start | bytes 3932164
  4.3 0.7 %copy-start.4 = (s32[2,2,2,5]{3,2,1,0:T(2,128)S(1)}, s32[2,2,2,5]{3,2,1,0:T(2,128)}, u32[]{:S(2)}) copy-start(s32[2,2,2,5]{3,2,1,0:T(2,128)} %off.1) | copy-start | bytes 484
  4.9 0.7 %copy-start.5 = (s32[2,2,2]{2,1,0:T(2,128)S(1)}, s32[2,2,2]{2,1,0:T(2,128)}, u32[]{:S(2)}) copy-start(s32[2,2,2]{2,1,0:T(2,128)} %count.1) | copy-start | bytes 100
  5.6 23.1 %copy-start.1 = (bf16[2,2,2,5,128,128]{5,4,3,2,1,0:T(8,128)(2,1)S(1)}, bf16[2,2,2,5,128,128]{5,4,3,2,1,0:T(8,128)(2,1)}, u32[]{:S(2)}) copy-start(bf16[2,2,2,5,128,128]{5,4,3,2,1,0:T(8,128)(2,1)} %a_own.15) | copy-start | bytes 3932164
  6.3 10.4 %collective-permute-start.1 = (bf16[1296,128]{1,0:T(8,128)(2,1)S(1)}, bf16[1296,128]{1,0:T(8,128)(2,1)S(1)}, u32[]{:S(2)}, u32[]{:S(2)}) collective-permute-start(bf16[1296,128]{1,0:T(8,128)(2,1)S(1)} %get-tuple-element.60.refs_0_), channel_id=1, source_target_pairs={{0,6},{1,3},{2,0},{3,5},{4,2},{5,7},{6,4},{7,1},{8,14},{9,11},{10,... | collective-permute-start | bytes 995336 | tf_op jit(solution)/shard_map/ppermute | solution.py:297
  10.0 1.0 %copy-start.2 = (bf16[2,2,4,128,128]{4,3,2,1,0:T(8,128)(2,1)S(1)}, bf16[2,2,4,128,128]{4,3,2,1,0:T(8,128)(2,1)}, u32[]{:S(2)}) copy-start(bf16[2,2,4,128,128]{4,3,2,1,0:T(8,128)(2,1)} %p_own.13) | copy-start | bytes 1572868
  11.0 18.5 %copy-start.3 = (bf16[2,2,4,128,128]{4,3,2,1,0:T(8,128)(2,1)S(1)}, bf16[2,2,4,128,128]{4,3,2,1,0:T(8,128)(2,1)}, u32[]{:S(2)}) copy-start(bf16[2,2,4,128,128]{4,3,2,1,0:T(8,128)(2,1)} %p_own.13) | copy-start | bytes 1572868
  11.1 7.3 %collective-permute-start.3 = (bf16[1,2,4,128,128]{4,3,2,1,0:T(8,128)(2,1)S(1)}, bf16[1,2,4,128,128]{4,3,2,1,0:T(8,128)(2,1)S(1)}, u32[]{:S(2)}, u32[]{:S(2)}) collective-permute-start(bf16[1,2,4,128,128]{4,3,2,1,0:T(8,128)(2,1)S(1)} %get-tuple-element.63), channel_id=1, source_target_pairs={{0,8},{8,0},{16,24},{24,16},{1,9},{9,1},{17,25},{25,17},{2,10},{10... | collective-permute-start | bytes 786440 | tf_op jit(solution)/shard_map/ppermute | solution.py:307
  11.1 8.1 %collective-permute-start.4 = (bf16[1,2,4,128,128]{4,3,2,1,0:T(8,128)(2,1)S(1)}, bf16[1,2,4,128,128]{4,3,2,1,0:T(8,128)(2,1)S(1)}, u32[]{:S(2)}, u32[]{:S(2)}) collective-permute-start(bf16[1,2,4,128,128]{4,3,2,1,0:T(8,128)(2,1)S(1)} %get-tuple-element.64), channel_id=1, source_target_pairs={{0,24},{8,16},{16,8},{24,0},{1,25},{9,17},{17,9},{25,1},{2,26},{10... | collective-permute-start | bytes 786440 | tf_op jit(solution)/shard_map/ppermute | solution.py:308
  16.8 19.8 %collective-permute-start.2 = (bf16[2592,128]{1,0:T(8,128)(2,1)S(1)}, bf16[2592,128]{1,0:T(8,128)(2,1)S(1)}, u32[]{:S(2)}, u32[]{:S(2)}) collective-permute-start(bf16[2592,128]{1,0:T(8,128)(2,1)S(1)} %join.1), channel_id=1, source_target_pairs={{0,1},{1,0},{2,3},{3,2},{4,5},{5,4},{6,7},{7,6},{8,9},{9,8},{10,11... | collective-permute-start | bytes 1990664 | tf_op jit(solution)/shard_map/ppermute | solution.py:311
  18.2 19.6 %collective-permute-start.7 = (bf16[2,2,4,128,128]{4,3,2,1,0:T(8,128)(2,1)S(1)}, bf16[2,2,4,128,128]{4,3,2,1,0:T(8,128)(2,1)S(1)}, u32[]{:S(2)}, u32[]{:S(2)}) collective-permute-start(bf16[2,2,4,128,128]{4,3,2,1,0:T(8,128)(2,1)S(1)} %collective-permute-done.piece.p_near), channel_id=1, source_target_pairs={{0,2},{1,7},{2,4},{3,1},{4,6},{5,3},{6,0},{7,5},{8,10},{9,15},{10,... | collective-permute-start | bytes 1572872 | tf_op jit(solution)/shard_map/ppermute | solution.py:310
  19.3 8.2 %collective-permute-start.5 = (bf16[1,2,4,128,128]{4,3,2,1,0:T(8,128)(2,1)S(1)}, bf16[1,2,4,128,128]{4,3,2,1,0:T(8,128)(2,1)S(1)}, u32[]{:S(2)}, u32[]{:S(2)}) collective-permute-start(bf16[1,2,4,128,128]{4,3,2,1,0:T(8,128)(2,1)S(1)} %get-tuple-element.67), channel_id=1, source_target_pairs={{0,24},{8,16},{16,8},{24,0},{1,25},{9,17},{17,9},{25,1},{2,26},{10... | collective-permute-start | bytes 786440 | tf_op jit(solution)/shard_map/ppermute | solution.py:315
  20.9 8.6 %collective-permute-start.6 = (bf16[1,2,4,128,128]{4,3,2,1,0:T(8,128)(2,1)S(1)}, bf16[1,2,4,128,128]{4,3,2,1,0:T(8,128)(2,1)S(1)}, u32[]{:S(2)}, u32[]{:S(2)}) collective-permute-start(bf16[1,2,4,128,128]{4,3,2,1,0:T(8,128)(2,1)S(1)} %get-tuple-element.69), channel_id=1, source_target_pairs={{0,8},{8,0},{16,24},{24,16},{1,9},{9,1},{17,25},{25,17},{2,10},{10... | collective-permute-start | bytes 786440 | tf_op jit(solution)/shard_map/ppermute | solution.py:314
  27.5 10.6 %collective-permute-start.11 = (bf16[1,2,4,128,128]{4,3,2,1,0:T(8,128)(2,1)S(1)}, bf16[1,2,4,128,128]{4,3,2,1,0:T(8,128)(2,1)S(1)}, u32[]{:S(2)}, u32[]{:S(2)}) collective-permute-start(bf16[1,2,4,128,128]{4,3,2,1,0:T(8,128)(2,1)S(1)} %collective-permute-done.5.near_out), channel_id=1, source_target_pairs={{0,2},{1,7},{2,4},{3,1},{4,6},{5,3},{6,0},{7,5},{8,10},{9,15},{10,... | collective-permute-start | bytes 786440 | tf_op jit(solution)/shard_map/ppermute | solution.py:316
  32.3 14.0 %collective-permute-start.8 = (bf16[5,128,128]{2,1,0:T(8,128)(2,1)}, bf16[5,128,128]{2,1,0:T(8,128)(2,1)}, u32[]{:S(2)}, u32[]{:S(2)}) collective-permute-start(bf16[5,128,128]{2,1,0:T(8,128)(2,1)} %get-tuple-element.83), channel_id=1, source_target_pairs={{0,1},{1,0},{2,3},{3,2},{4,5},{5,4},{6,7},{7,6},{8,9},{9,8},{10,11... | collective-permute-start | bytes 491528 | tf_op jit(solution)/shard_map/ppermute | solution.py:358
  35.6 13.2 %collective-permute-start.9 = (bf16[5,128,128]{2,1,0:T(8,128)(2,1)}, bf16[5,128,128]{2,1,0:T(8,128)(2,1)}, u32[]{:S(2)}, u32[]{:S(2)}) collective-permute-start(bf16[5,128,128]{2,1,0:T(8,128)(2,1)} %get-tuple-element.84), channel_id=1, source_target_pairs={{0,7},{1,2},{2,1},{3,4},{4,3},{5,6},{6,5},{7,0},{8,15},{9,10},{10,... | collective-permute-start | bytes 491528 | tf_op jit(solution)/shard_map/ppermute | solution.py:358
  37.8 3.5 %collective-permute-start.10 = (bf16[1,2,4,128,128]{4,3,2,1,0:T(8,128)(2,1)S(1)}, bf16[1,2,4,128,128]{4,3,2,1,0:T(8,128)(2,1)S(1)}, u32[]{:S(2)}, u32[]{:S(2)}) collective-permute-start(bf16[1,2,4,128,128]{4,3,2,1,0:T(8,128)(2,1)S(1)} %row.1), channel_id=1, source_target_pairs={{0,8},{8,0},{16,24},{24,16},{1,9},{9,1},{17,25},{25,17},{2,10},{10... | collective-permute-start | bytes 786440 | tf_op jit(solution)/shard_map/ppermute | solution.py:352
  39.8 13.2 %collective-permute-start.14 = (bf16[3,5,128,128]{3,2,1,0:T(8,128)(2,1)S(1)}, bf16[3,5,128,128]{3,2,1,0:T(8,128)(2,1)S(1)}, u32[]{:S(2)}, u32[]{:S(2)}) collective-permute-start(bf16[3,5,128,128]{3,2,1,0:T(8,128)(2,1)S(1)} %get-tuple-element.97), channel_id=1, source_target_pairs={{0,24},{8,16},{16,8},{24,0},{1,25},{9,17},{17,9},{25,1},{2,26},{10... | collective-permute-start | bytes 1474568 | tf_op jit(solution)/shard_map/ppermute | solution.py:399
  43.3 9.7 %collective-permute-start.12 = (bf16[5,128,128]{2,1,0:T(8,128)(2,1)S(1)}, bf16[5,128,128]{2,1,0:T(8,128)(2,1)S(1)}, u32[]{:S(2)}, u32[]{:S(2)}) collective-permute-start(bf16[5,128,128]{2,1,0:T(8,128)(2,1)S(1)} %get-tuple-element.95), channel_id=1, source_target_pairs={{0,1},{1,0},{2,3},{3,2},{4,5},{5,4},{6,7},{7,6},{8,9},{9,8},{10,11... | collective-permute-start | bytes 491528 | tf_op jit(solution)/shard_map/ppermute | solution.py:358
  45.0 8.8 %collective-permute-start.13 = (bf16[5,128,128]{2,1,0:T(8,128)(2,1)S(1)}, bf16[5,128,128]{2,1,0:T(8,128)(2,1)S(1)}, u32[]{:S(2)}, u32[]{:S(2)}) collective-permute-start(bf16[5,128,128]{2,1,0:T(8,128)(2,1)S(1)} %get-tuple-element.96), channel_id=1, source_target_pairs={{0,7},{1,2},{2,1},{3,4},{4,3},{5,6},{6,5},{7,0},{8,15},{9,10},{10,... | collective-permute-start | bytes 491528 | tf_op jit(solution)/shard_map/ppermute | solution.py:358
  46.4 10.9 %collective-permute-start.17 = (bf16[3,5,128,128]{3,2,1,0:T(8,128)(2,1)S(1)}, bf16[3,5,128,128]{3,2,1,0:T(8,128)(2,1)S(1)}, u32[]{:S(2)}, u32[]{:S(2)}) collective-permute-start(bf16[3,5,128,128]{3,2,1,0:T(8,128)(2,1)S(1)} %get-tuple-element.112), channel_id=1, source_target_pairs={{0,8},{8,0},{16,24},{24,16},{1,9},{9,1},{17,25},{25,17},{2,10},{10... | collective-permute-start | bytes 1474568 | tf_op jit(solution)/shard_map/ppermute | solution.py:400
  51.3 13.4 %collective-permute-start.15 = (bf16[3,5,128,128]{3,2,1,0:T(8,128)(2,1)S(1)}, bf16[3,5,128,128]{3,2,1,0:T(8,128)(2,1)S(1)}, u32[]{:S(2)}, u32[]{:S(2)}) collective-permute-start(bf16[3,5,128,128]{3,2,1,0:T(8,128)(2,1)S(1)} %get-tuple-element.106), channel_id=1, source_target_pairs={{0,24},{8,16},{16,8},{24,0},{1,25},{9,17},{17,9},{25,1},{2,26},{10... | collective-permute-start | bytes 1474568 | tf_op jit(solution)/shard_map/ppermute | solution.py:399
  55.9 8.8 %collective-permute-start.16 = (bf16[3,5,128,128]{3,2,1,0:T(8,128)(2,1)S(1)}, bf16[3,5,128,128]{3,2,1,0:T(8,128)(2,1)S(1)}, u32[]{:S(2)}, u32[]{:S(2)}) collective-permute-start(bf16[3,5,128,128]{3,2,1,0:T(8,128)(2,1)S(1)} %get-tuple-element.107), channel_id=1, source_target_pairs={{0,8},{8,0},{16,24},{24,16},{1,9},{9,1},{17,25},{25,17},{2,10},{10... | collective-permute-start | bytes 1474568 | tf_op jit(solution)/shard_map/ppermute | solution.py:400

commit v7 on v6

--- a/solution.py
+++ b/solution.py
@@ -89,30 +89,37 @@
         out[0] = piece[x]
 
 
-def pack_kernel(turn, off, count, a_own, *outs):
+def pack_column(turn, off, count, a_own, y, out):
     operators, _, _, slots = off.shape
     block = a_own.shape[-1]
-    odd, flip = turns(turn)
+    flip = turns(turn)[1]
     row = lax.broadcasted_iota(jnp.int32, (INFO, block), 0)
     lane = lax.broadcasted_iota(jnp.int32, (INFO, block), 1)
-    for out, y in zip(outs, (1 - odd, odd)):
+    for x in range(2):
+        for k in range(slots):
+            out[pl.ds((x * slots + k) * block, block), :] = a_own[0, x ^ flip, y, k]
+    line = jnp.zeros((INFO, block), jnp.int32)
+    for s in range(operators):
         for x in range(2):
+            here = row == 2 * s + x
+            line = jnp.where(here & (lane == slots), count[s, x ^ flip, y], line)
             for k in range(slots):
-                out[pl.ds((x * slots + k) * block, block), :] = a_own[0, x ^ flip, y, k]
-        line = jnp.zeros((INFO, block), jnp.int32)
-        for s in range(operators):
-            for x in range(2):
-                here = row == 2 * s + x
-                line = jnp.where(here & (lane == slots), count[s, x ^ flip, y], line)
-                for k in range(slots):
-                    line = jnp.where(here & (lane == k), off[s, x ^ flip, y, k], line)
-        out[pl.ds(2 * slots * block, INFO), :] = line.astype(jnp.float32).astype(out.dtype)
-
-
-def later_kernel(turn, a_own, after, *outs):
-    odd, flip = turns(turn)
-    for i, out in enumerate(outs):
-        out[...] = a_own[i // 4 + 1, (i // 2 & 1) ^ flip, odd if i % 2 else 1 - odd]
+                line = jnp.where(here & (lane == k), off[s, x ^ flip, y, k], line)
+    out[pl.ds(2 * slots * block, INFO), :] = line.astype(jnp.float32).astype(out.dtype)
+
+
+def pack_far_kernel(turn, off, count, a_own, out):
+    pack_column(turn, off, count, a_own, turns(turn)[0], out)
+
+
+def pack_kernel(turn, off, count, a_own, after, own_1, *later):
+    odd, flip = turns(turn)
+    for s in range(1, a_own.shape[0]):
+        far_0, far_1, near = later[3 * s - 3 : 3 * s]
+        for x, far in enumerate((far_0, far_1)):
+            far[...] = a_own[s, x ^ flip, odd]
+            near[x] = a_own[s, x ^ flip, 1 - odd]
+    pack_column(turn, off, count, a_own, 1 - odd, own_1)
 
 
 def join_kernel(near, far, out):
@@ -174,21 +181,16 @@
             out[lag_x, lag_y] = total[:, lag_x * block : (lag_x + 1) * block].astype(out.dtype)
 
 
-def near_own_inner_kernel(operators, table, turn, a_own, p_own, p_near, own_in, near_in, flat, *w_refs):
-    odd, flip = turns(turn)
-    fill(flat, 0, ((0, p_own, flip), (1, p_own, 1 - flip), (2, own_in, 0)))
-    fill(flat, HALF, ((0, p_near, flip), (1, p_near, 1 - flip), (2, near_in, 0)))
+def near_own_kernel(operators, table, turn, a_own, p_own, p_near, own_out, own_in, near_out, near_in, flat, *w_refs):
+    odd, flip = turns(turn)
+    fill(flat, 0, ((-1, own_out, 0), (0, p_own, flip), (1, p_own, 1 - flip), (2, own_in, 0)))
+    fill(flat, HALF, ((-1, near_out, 0), (0, p_near, flip), (1, p_near, 1 - flip), (2, near_in, 0)))
     flat[ZERO] = jnp.zeros(flat.shape[1:], flat.dtype)
-    for s, w_ref in enumerate(w_refs):
-        fine_row(table, table_row(operators, OWN_1, s, 1), flat, row_of(a_own.at[s, 1 - flip, 1 - odd]), w_ref)
-
-
-def near_own_outer_kernel(operators, table, turn, a_own, own_out, near_out, held, flat, *w_refs):
-    odd, flip = turns(turn)
-    fill(flat, 0, ((-1, own_out, 0),))
-    fill(flat, HALF, ((-1, near_out, 0),))
-    for s, w_ref in enumerate(w_refs):
-        fine_row(table, table_row(operators, OWN_1, s, 0), flat, row_of(a_own.at[s, flip, 1 - odd]), w_ref)
+    for s in range(operators):
+        for x in range(2):
+            fine_row(
+                table, table_row(operators, OWN_1, s, x), flat, row_of(a_own.at[s, x ^ flip, 1 - odd]), w_refs[2 * s + x]
+            )
 
 
 def near_kernel(operators, table, flat, a_pair, w_ref):
@@ -225,7 +227,7 @@
 ):
     odd, flip = turns(turn)
     fine_row(own_table, table_row(operators, OWN_0, operator, x), flat, row_of(a_own.at[operator, x ^ flip, odd]), w_own_0)
-    fine_row(table, table_row(operators, NEAR, operator, x), flat, row_of(a_near), w_near)
+    fine_row(table, table_row(operators, NEAR, operator, x), flat, row_of(a_near.at[x]), w_near)
     fine_row(table, table_row(operators, FAR, operator, x), flat, row_of(a_far), w_far)
     edge(turn, (p_far, p_own, p_own, p_near), one_row(x, w_far, w_own_0, w_own, w_near), x, out)
 
@@ -293,7 +295,14 @@
 
     p_near = lax.ppermute(p_vals, "col", near_way)
     column = jax.ShapeDtypeStruct((2 * slots * block + INFO, block), bf16)
-    own_1, own_0 = call(pack_kernel, [smem] * 3 + [vmem], [column] * 2, 1, "pack")(turn, a_off, a_count, a_vals)
+    slots_shape = jax.ShapeDtypeStruct((slots, block, block), bf16)
+    two_slots = jax.ShapeDtypeStruct((2, slots, block, block), bf16)
+    own_0 = call(pack_far_kernel, [smem] * 3 + [vmem], column, 1, "pack_far", limit=60 << 20)(
+        turn, a_off, a_count, a_vals
+    )
+    own_1, *later = call(
+        pack_kernel, [smem] * 3 + [vmem, any_spec], [column] + [slots_shape, slots_shape, two_slots] * (operators - 1), 1, "pack"
+    )(turn, a_off, a_count, a_vals, own_0)
     moved = lax.ppermute(own_0, "col", aside_way)
     table_shape = jax.ShapeDtypeStruct((operators * 4, slots * 9), jnp.int32)
     own_table = call(
@@ -314,31 +323,15 @@
     near_in = lax.ppermute(near_in, "row", in_way)
     near_out = lax.ppermute(near_out, "row", out_way)
     far_out = lax.ppermute(near_out, "col", on_way)
-    flat, *w_inner = call(
-        functools.partial(near_own_inner_kernel, operators),
-        [smem, smem] + [vmem] * 5,
-        [flat_shape] + [w_shape] * operators,
-        180,
-        "near_own_inner",
-    )(own_table, turn, a_vals, p_vals, p_near, own_in, near_in)
-    near_out, flat = lax.optimization_barrier((near_out, flat))
-    flat, *w_outer = call(
-        functools.partial(near_own_outer_kernel, operators),
-        [smem, smem] + [vmem] * 4,
-        [flat_shape] + [w_shape] * operators,
-        180,
-        "near_own_outer",
-        aliases={5: 0},
-    )(own_table, turn, a_vals, own_out, near_out, flat)
-    w_own = [w_outer, w_inner]
-
-    later = call(
-        later_kernel,
-        [smem, vmem, any_spec],
-        [jax.ShapeDtypeStruct((slots, block, block), bf16)] * (4 * operators - 4),
-        1,
-        "later",
-    )(turn, a_vals, own_in)
+    flat, *w_own = call(
+        functools.partial(near_own_kernel, operators),
+        [smem, smem] + [vmem] * 7,
+        [flat_shape] + [w_shape] * (2 * operators),
+        360,
+        "near_own",
+    )(own_table, turn, a_vals, p_vals, p_near, own_out, own_in, near_out, near_in)
+    w_own = [w_own[0::2], w_own[1::2]]
+
     side_table = call(
         functools.partial(table_kernel, operators, (NEAR, FAR)), [smem, vmem], table_shape, 1, "side_table"
     )(turn, from_pair)
@@ -351,15 +344,12 @@
     far_in = call(rows_kernel, [smem, vmem], [row_shape], 1, "row")(turn, p_far)[0]
     far_in = lax.ppermute(far_in, "row", in_way)
 
-    def send_row(x):
-        rows_sent = []
-        for s in range(1, operators):
-            near, far = later[4 * s - 4 + 2 * x : 4 * s - 2 + 2 * x]
-            rows_sent.append((lax.ppermute(near, "col", near_way), lax.ppermute(far, "col", far_way)))
-        return rows_sent
+    def send(place, way):
+        return [lax.ppermute(later[3 * s - 3 + place], "col", way) for s in range(1, operators)]
 
     w_own, later = lax.optimization_barrier((w_own, later))
-    outer_a = send_row(0)
+    far_a = [send(0, far_way)]
+    near_a = send(2, near_way)
 
     result = None
     for s in range(operators):
@@ -383,7 +373,8 @@
             )(own_table, side_table, turn, a_vals, from_pair, w_own[1][0], p_vals, p_near, p_far, far_in, flat)
             near_w = [near_w, inner_w]
             inner_w, later = lax.optimization_barrier((inner_w, later))
-            a_sides = [None] + list(zip(outer_a, send_row(1)))
+            far_a.append(send(1, far_way))
+            a_sides = [None] + [[(near_a[s], far_a[x][s]) for x in range(2)] for s in range(operators - 1)]
         else:
             near_w = [None, None]
             for x in range(2):

time: 65.9 us -> 65.4 us (level)
  Pallas kernels: 17 us -> 18.9 us
  waiting for transfers between devices: 20.2 us -> 18.3 us
  starting transfers between devices: 24.5 us -> 22.9 us
  local copies, waits for them, and re-layouts: 3.73 us -> 4.71 us
    ppermute x1, waiting for transfers between devices: 3.98 us -> 0.01 us  [per_device(): moved = lax.ppermute(own_0, 'col', aside_way)]
    ppermute x1, waiting for transfers between devices: 0.2 us -> 3.21 us  [per_device(): far_out = lax.ppermute(near_out, 'col', on_way)]
    pallas_call x4 -> x3, Pallas kernels: 4.29 us -> 5.8 us  [the longest x1 2.19 us: per_device(): call(pack_far_kernel, [smem] * 3 + [vmem], column, 1, 'pack_far', limit=6...]
    ppermute x2, starting transfers between devices: 1.86 us -> 0.44 us  [per_device(): from_out = lax.ppermute(sums[0], 'row', out_way)]
    ppermute x1, starting transfers between devices: 0.23 us -> 1.27 us  [per_device(): p_far = lax.ppermute(p_near, 'col', on_way)]
    unnamed x12 -> x16, local copies, waits for them, and re-layouts: 3.73 us -> 4.71 us
    ppermute x4 -> x3, starting transfers between devices: 7.3 us -> 6.34 us  [send(): lax.ppermute(later[3 * s - 3 + place], 'col', way)]
    ppermute x1, starting transfers between devices: 1.34 us -> 0.38 us  [per_device(): from_pair = lax.ppermute(joined, 'col', near_way)]
  transfers between devices with their start and end apart: 18 -> 17, of which waited for: 7 -> 4; matrix products, arithmetic and copies ran while one was open for 0% -> 0% of each run, Pallas kernels for 24% -> 28%
where the time goes in v7:
time: 65.4 us; the launch traced here: 65 us
  starting transfers between devices  22.9 us (35%)
  Pallas kernels  18.9 us (29%)
  waiting for transfers between devices  18.3 us (28%)
  local copies, waits for them, and re-layouts  4.71 us (7%)
    ppermute x2, waiting for transfers between devices, per_device(): from_out = lax.ppermute(sums[0], 'row', out_way)  8.27 us
    ppermute x1, waiting for transfers between devices, per_device(): near_out = lax.ppermute(near_out, 'row', out_way)  6.8 us
    ppermute x3, starting transfers between devices, send(): lax.ppermute(later[3 * s - 3 + place], 'col', way)  6.34 us
    pallas_call x2, Pallas kernels, per_device(): call(functools.partial(sides_kernel, operators, s, x), [smem, smem, smem]...  4.81 us
    unnamed x16, local copies, waits for them, and re-layouts  4.71 us
    ppermute x1, starting transfers between devices, per_device(): moved = lax.ppermute(own_0, 'col', aside_way)  3.6 us
    ppermute x1, waiting for transfers between devices, per_device(): far_out = lax.ppermute(near_out, 'col', on_way)  3.21 us
    ppermute x1, starting transfers between devices, per_device(): p_near = lax.ppermute(p_vals, 'col', near_way)  2.94 us
  transfers between devices with their start and end apart: 17, of which 4 were waited for; matrix products, arithmetic and copies ran while one was open for 0% of the time, Pallas kernels for 28%

profile of v7, /device:TPU:0, one launch (start us, length us, event | category | flops | bytes accessed | tf_op | source)
XLA Modules:
  0.0 65.0 jit_solution(7822135969852239371)
XLA Ops:
  0.0 2.9 %collective-permute-start = (bf16[2,2,4,128,128]{4,3,2,1,0:T(8,128)(2,1)}, bf16[2,2,4,128,128]{4,3,2,1,0:T(8,128)(2,1)S(1)}, u32[]{:S(2)}, u32[]{:S(2)}) collective-permute-start(bf16[2,2,4,128,128]{4,3,2,1,0:T(8,128)(2,1)} %p_own.13), channel_id=1, source_target_pairs={{0,1},{1,0},{2,3},{3,2},{4,5},{5,4},{6,7},{7,6},{8,9},{9,8},{10,11... | collective-permute-start | bytes 1572872 | tf_op jit(solution)/shard_map/ppermute | solution.py:296
  2.9 2.2 %pack_far.1.after.refs_0_ = bf16[1296,128]{1,0:T(8,128)(2,1)} custom-call(s32[1]{0:T(128)} %bitcast.turn, s32[2,2,2,5]{3,2,1,0:T(2,128)} %off.3, s32[2,2,2]{2,1,0:T(2,128)} %count.3, bf16[2,2,2,5,128,128]{5,4,3,2,1,0:T(8,128)(2,1)} %a_own.13), custom_call_target="tpu_custom_call" | custom-call | flops 1 | bytes 1024 | tf_op jit(solution)/shard_map/pack_far/pallas_call | solution.py:300
  5.1 3.6 %collective-permute-start.1 = (bf16[1296,128]{1,0:T(8,128)(2,1)}, bf16[1296,128]{1,0:T(8,128)(2,1)S(1)}, u32[]{:S(2)}, u32[]{:S(2)}) collective-permute-start(bf16[1296,128]{1,0:T(8,128)(2,1)} %pack_far.1.after.refs_0_), channel_id=1, source_target_pairs={{0,6},{1,3},{2,0},{3,5},{4,2},{5,7},{6,4},{7,1},{8,14},{9,11},{10,... | collective-permute-start | bytes 995336 | tf_op jit(solution)/shard_map/ppermute | solution.py:306
  8.7 1.0 %copy-done.2 = bf16[2,2,4,128,128]{4,3,2,1,0:T(8,128)(2,1)S(1)} copy-done((bf16[2,2,4,128,128]{4,3,2,1,0:T(8,128)(2,1)S(1)}, bf16[2,2,4,128,128]{4,3,2,1,0:T(8,128)(2,1)}, u32[]{:S(2)}) %copy-start.2) | copy-done | bytes 524312
  9.8 0.1 collective-permute-start.3
  9.9 1.6 %collective-permute-start.4 = (bf16[1,2,4,128,128]{4,3,2,1,0:T(8,128)(2,1)S(1)}, bf16[1,2,4,128,128]{4,3,2,1,0:T(8,128)(2,1)S(1)}, u32[]{:S(2)}, u32[]{:S(2)}) collective-permute-start(bf16[1,2,4,128,128]{4,3,2,1,0:T(8,128)(2,1)S(1)} %get-tuple-element.56), channel_id=1, source_target_pairs={{0,24},{8,16},{16,8},{24,0},{1,25},{9,17},{17,9},{25,1},{2,26},{10... | collective-permute-start | bytes 786440 | tf_op jit(solution)/shard_map/ppermute | solution.py:317
  11.5 1.3 %copy-done = bf16[2,2,2,5,128,128]{5,4,3,2,1,0:T(8,128)(2,1)S(1)} copy-done((bf16[2,2,2,5,128,128]{5,4,3,2,1,0:T(8,128)(2,1)S(1)}, bf16[2,2,2,5,128,128]{5,4,3,2,1,0:T(8,128)(2,1)}, u32[]{:S(2)}) %copy-start) | copy-done | bytes 1310744
  12.9 1.0 %copy-done.4 = bf16[1296,128]{1,0:T(8,128)(2,1)S(1)} copy-done((bf16[1296,128]{1,0:T(8,128)(2,1)S(1)}, bf16[1296,128]{1,0:T(8,128)(2,1)}, u32[]{:S(2)}) %copy-start.4) | copy-done | bytes 331800
  13.8 0.7 %copy-done.6 = s32[2,2,2,5]{3,2,1,0:T(2,128)S(1)} copy-done((s32[2,2,2,5]{3,2,1,0:T(2,128)S(1)}, s32[2,2,2,5]{3,2,1,0:T(2,128)}, u32[]{:S(2)}) %copy-start.6) | copy-done | bytes 184
  14.5 0.7 %copy-done.7 = s32[2,2,2]{2,1,0:T(2,128)S(1)} copy-done((s32[2,2,2]{2,1,0:T(2,128)S(1)}, s32[2,2,2]{2,1,0:T(2,128)}, u32[]{:S(2)}) %copy-start.7) | copy-done | bytes 56
  15.2 1.5 %pack.1 = (bf16[1296,128]{1,0:T(8,128)(2,1)S(1)}, bf16[5,128,128]{2,1,0:T(8,128)(2,1)}, bf16[5,128,128]{2,1,0:T(8,128)(2,1)S(1)}, bf16[2,5,128,128]{3,2,1,0:T(8,128)(2,1)}) custom-call(s32[1]{0:T(128)} %bitcast.turn, s32[2,2,2,5]{3,2,1,0:T(2,128)S(1)} %copy-done.6, s32[2,2,2]{2,1,0:T(2,128)S(1)} %copy-done.7, bf16[2,2,2,5,128,128]{5,4,3,2,1,0:T(8,128)(2,1)S(1)} %copy-done, ...), custom_call_target="tpu_custom_call" | custom-call | flops 1 | bytes 1024 | tf_op jit(solution)/shard_map/pack/pallas_call | solution.py:303
  16.7 0.0 collective-permute-done.1.far
  16.7 0.4 collective-permute-start.2
  17.1 1.3 %collective-permute-start.7 = (bf16[2,2,4,128,128]{4,3,2,1,0:T(8,128)(2,1)S(1)}, bf16[2,2,4,128,128]{4,3,2,1,0:T(8,128)(2,1)S(1)}, u32[]{:S(2)}, u32[]{:S(2)}) collective-permute-start(bf16[2,2,4,128,128]{4,3,2,1,0:T(8,128)(2,1)S(1)} %collective-permute-done.piece.p_near), channel_id=1, source_target_pairs={{0,2},{1,7},{2,4},{3,1},{4,6},{5,3},{6,0},{7,5},{8,10},{9,15},{10,... | collective-permute-start | bytes 1572872 | tf_op jit(solution)/shard_map/ppermute | solution.py:319
  18.4 0.0 collective-permute-done.3.own_in
  18.4 0.0 collective-permute-done.4.own_out
  18.4 1.2 %collective-permute-start.5 = (bf16[1,2,4,128,128]{4,3,2,1,0:T(8,128)(2,1)S(1)}, bf16[1,2,4,128,128]{4,3,2,1,0:T(8,128)(2,1)S(1)}, u32[]{:S(2)}, u32[]{:S(2)}) collective-permute-start(bf16[1,2,4,128,128]{4,3,2,1,0:T(8,128)(2,1)S(1)} %get-tuple-element.60), channel_id=1, source_target_pairs={{0,24},{8,16},{16,8},{24,0},{1,25},{9,17},{17,9},{25,1},{2,26},{10... | collective-permute-start | bytes 786440 | tf_op jit(solution)/shard_map/ppermute | solution.py:324
  19.6 0.5 collective-permute-start.6
  20.1 6.8 %collective-permute-done.5.near_out = bf16[1,2,4,128,128]{4,3,2,1,0:T(8,128)(2,1)S(1)} collective-permute-done((bf16[1,2,4,128,128]{4,3,2,1,0:T(8,128)(2,1)S(1)}, bf16[1,2,4,128,128]{4,3,2,1,0:T(8,128)(2,1)S(1)}, u32[]{:S(2)}, u32[]{:S(2)}) %collective-permute-start.5) | collective-permute-done | bytes 262176 | tf_op jit(solution)/shard_map/ppermute | solution.py:324
  26.9 1.7 %collective-permute-start.11 = (bf16[1,2,4,128,128]{4,3,2,1,0:T(8,128)(2,1)S(1)}, bf16[1,2,4,128,128]{4,3,2,1,0:T(8,128)(2,1)S(1)}, u32[]{:S(2)}, u32[]{:S(2)}) collective-permute-start(bf16[1,2,4,128,128]{4,3,2,1,0:T(8,128)(2,1)S(1)} %collective-permute-done.5.near_out), channel_id=1, source_target_pairs={{0,2},{1,7},{2,4},{3,1},{4,6},{5,3},{6,0},{7,5},{8,10},{9,15},{10,... | collective-permute-start | bytes 786440 | tf_op jit(solution)/shard_map/ppermute | solution.py:325
  28.6 0.1 own_table.1.table
  28.7 0.0 collective-permute-done.6.near_in
  28.7 2.1 %near_own.1 = (bf16[97,128,128]{2,1,0:T(8,128)(2,1)S(1)}, bf16[3,128,384]{2,1,0:T(8,128)(2,1)S(1)}, bf16[3,128,384]{2,1,0:T(8,128)(2,1)S(1)}, bf16[3,128,384]{2,1,0:T(8,128)(2,1)S(1)}, bf16[3,128,384]{2,1,0:T(8,128)(2,1)S(1)}) custom-call(s32[8,45]{1,0:T(8,128)S(1)} %own_table.1.table, s32[1]{0:T(128)} %bitcast.turn, ...), custom_call_target="tpu_custom_call" | custom-call | flops 360 | bytes 1024 | tf_op jit(solution)/shard_map/near_own/pallas_call | solution.py:326
  30.9 2.3 %collective-permute-start.8 = (bf16[2,5,128,128]{3,2,1,0:T(8,128)(2,1)}, bf16[2,5,128,128]{3,2,1,0:T(8,128)(2,1)}, u32[]{:S(2)}, u32[]{:S(2)}) collective-permute-start(bf16[2,5,128,128]{3,2,1,0:T(8,128)(2,1)} %get-tuple-element.71), channel_id=1, source_target_pairs={{0,1},{1,0},{2,3},{3,2},{4,5},{5,4},{6,7},{7,6},{8,9},{9,8},{10,11... | collective-permute-start | bytes 983048 | tf_op jit(solution)/shard_map/ppermute | solution.py:348
  33.1 1.4 %collective-permute-start.9 = (bf16[5,128,128]{2,1,0:T(8,128)(2,1)}, bf16[5,128,128]{2,1,0:T(8,128)(2,1)}, u32[]{:S(2)}, u32[]{:S(2)}) collective-permute-start(bf16[5,128,128]{2,1,0:T(8,128)(2,1)} %get-tuple-element.72), channel_id=1, source_target_pairs={{0,7},{1,2},{2,1},{3,4},{4,3},{5,6},{6,5},{7,0},{8,15},{9,10},{10,... | collective-permute-start | bytes 491528 | tf_op jit(solution)/shard_map/ppermute | solution.py:348
  34.6 0.0 collective-permute-done.2.refs_0_.a_pair
  34.6 0.1 side_table.1.table
  34.7 1.1 %near.1.w_near.refs_6_ = bf16[3,128,384]{2,1,0:T(8,128)(2,1)S(1)} custom-call(s32[8,45]{1,0:T(8,128)S(1)} %side_table.1.table, bf16[97,128,128]{2,1,0:T(8,128)(2,1)S(1)} %get-tuple-element.62.flat.held, bf16[2592,128]{1,0:T(8,128)(2,1)S(1)} %collective-permute-done.2.refs_0_.a_pair), custom_call_target="tpu_custom_call" | custom-call | flops 45 | bytes 1024 | tf_op jit(solution)/shard_map/near/pallas_call | solution.py:339
  35.7 0.0 collective-permute-done.7.piece.p_far
  35.8 0.1 collective-permute-start.10
  35.9 3.2 %collective-permute-done.11.far_out = bf16[1,2,4,128,128]{4,3,2,1,0:T(8,128)(2,1)S(1)} collective-permute-done((bf16[1,2,4,128,128]{4,3,2,1,0:T(8,128)(2,1)S(1)}, bf16[1,2,4,128,128]{4,3,2,1,0:T(8,128)(2,1)S(1)}, u32[]{:S(2)}, u32[]{:S(2)}) %collective-permute-start.11) | collective-permute-done | bytes 262176 | tf_op jit(solution)/shard_map/ppermute | solution.py:325
  39.1 1.7 %first_outer.1 = (bf16[3,5,128,128]{3,2,1,0:T(8,128)(2,1)S(1)}, bf16[97,128,128]{2,1,0:T(8,128)(2,1)S(1)}, bf16[3,128,384]{2,1,0:T(8,128)(2,1)S(1)}, bf16[3,128,384]{2,1,0:T(8,128)(2,1)S(1)}) custom-call(s32[8,45]{1,0:T(8,128)S(1)} %own_table.1.table, s32[8,45]{1,0:T(8,128)S(1)} %side_table.1.table, s32[1]{0:T(128)} %bitcast.turn, ...), custom_call_target="tpu_custom_call", output_to_operand_aliasing={{1}: (11, {})} | custom-call | flops 99999997952 | bytes 1024 | tf_op jit(solution)/shard_map/first_outer/pallas_call | solution.py:358
  40.8 0.1 collective-permute-start.13
  40.9 0.0 collective-permute-done.10.far_in
  40.9 2.0 %first_inner.1 = (bf16[3,5,128,128]{3,2,1,0:T(8,128)(2,1)S(1)}, bf16[97,128,128]{2,1,0:T(8,128)(2,1)S(1)}, bf16[3,128,384]{2,1,0:T(8,128)(2,1)S(1)}, bf16[3,128,...) custom-call(s32[8,45]{1,0:T(8,128)S(1)} %own_table.1.table, ...), custom_call_target="tpu_custom_call", output_to_operand_aliasing={{1}: (10, {})} | custom-call | flops 99999997952 | bytes 1024 | tf_op jit(solution)/shard_map/first_inner/pallas_call | solution.py:366
  42.9 2.7 %collective-permute-start.12 = (bf16[5,128,128]{2,1,0:T(8,128)(2,1)S(1)}, bf16[5,128,128]{2,1,0:T(8,128)(2,1)S(1)}, u32[]{:S(2)}, u32[]{:S(2)}) collective-permute-start(bf16[5,128,128]{2,1,0:T(8,128)(2,1)S(1)} %get-tuple-element.82), channel_id=1, source_target_pairs={{0,7},{1,2},{2,1},{3,4},{4,3},{5,6},{6,5},{7,0},{8,15},{9,10},{10,... | collective-permute-start | bytes 491528 | tf_op jit(solution)/shard_map/ppermute | solution.py:348
  45.5 2.7 %collective-permute-start.16 = (bf16[3,5,128,128]{3,2,1,0:T(8,128)(2,1)S(1)}, bf16[3,5,128,128]{3,2,1,0:T(8,128)(2,1)S(1)}, u32[]{:S(2)}, u32[]{:S(2)}) collective-permute-start(bf16[3,5,128,128]{3,2,1,0:T(8,128)(2,1)S(1)} %get-tuple-element.98), channel_id=1, source_target_pairs={{0,8},{8,0},{16,24},{24,16},{1,9},{9,1},{17,25},{25,17},{2,10},{10... | collective-permute-start | bytes 1474568 | tf_op jit(solution)/shard_map/ppermute | solution.py:391
  48.2 0.0 collective-permute-done.9.a_far
  48.2 2.4 %sides.2 = (bf16[3,5,128,128]{3,2,1,0:T(8,128)(2,1)S(1)}, bf16[3,128,384]{2,1,0:T(8,128)(2,1)S(1)}, bf16[3,128,384]{2,1,0:T(8,128)(2,1)S(1)}, bf16[3,128,384]{2,1,0:T(8,128)(2,1)S(1)}) custom-call(s32[8,45]{1,0:T(8,128)S(1)} %own_table.1.table, s32[8,45]{1,0:T(8,128)S(1)} %side_table.1.table, s32[1]{0:T(128)} %bitcast.turn, ...), custom_call_target="tpu_custom_call" | custom-call | flops 100 | bytes 1024 | tf_op jit(solution)/shard_map/sides/pallas_call | solution.py:383
  50.7 0.4 collective-permute-start.14
  51.0 2.3 %collective-permute-done.13.outer = bf16[3,5,128,128]{3,2,1,0:T(8,128)(2,1)S(1)} collective-permute-done((bf16[3,5,128,128]{3,2,1,0:T(8,128)(2,1)S(1)}, bf16[3,5,128,128]{3,2,1,0:T(8,128)(2,1)S(1)}, u32[]{:S(2)}, u32[]{:S(2)}) %collective-permute-start.13) | collective-permute-done | bytes 491552 | tf_op jit(solution)/shard_map/ppermute | solution.py:390
  53.3 2.4 %sides.3 = (bf16[3,5,128,128]{3,2,1,0:T(8,128)(2,1)S(1)}, bf16[3,128,384]{2,1,0:T(8,128)(2,1)S(1)}, bf16[3,128,384]{2,1,0:T(8,128)(2,1)S(1)}, bf16[3,128,384]{2,1,0:T(8,128)(2,1)S(1)}) custom-call(s32[8,45]{1,0:T(8,128)S(1)} %own_table.1.table, s32[8,45]{1,0:T(8,128)S(1)} %side_table.1.table, s32[1]{0:T(128)} %bitcast.turn, ...), custom_call_target="tpu_custom_call" | custom-call | flops 100 | bytes 1024 | tf_op jit(solution)/shard_map/sides/pallas_call | solution.py:383
  55.7 0.1 collective-permute-start.15
  55.8 0.7 %centre.3.own = f32[3,5,128,128]{3,2,1,0:T(8,128)S(1)} custom-call(s32[1]{0:T(128)} %bitcast.turn, bf16[2,2,4,128,128]{4,3,2,1,0:T(8,128)(2,1)S(1)} %copy-done.3, bf16[2,2,4,128,128]{4,3,2,1,0:T(8,128)(2,1)S(1)} %collective-permute-done.piece.p_near, bf16[2,2,4,128,128]{4,3,2,1,0:T(8,128)(2,1)S(1)} %collective-permute-done.7.piece.p_far, ...), custom_call_target="tpu_custom_call" | custom-call | flops 144 | bytes 1024 | tf_op jit(solution)/shard_map/centre/pallas_call | solution.py:392
  56.4 0.6 centre.2.own
  57.1 1.0 %final.2.refs_0_ = bf16[2,1,1,25,128,128]{5,4,3,2,1,0:T(8,128)(2,1)} custom-call(s32[1]{0:T(128)} %bitcast.turn, f32[3,5,128,128]{3,2,1,0:T(8,128)S(1)} %centre.3.own, bf16[3,5,128,128]{3,2,1,0:T(8,128)(2,1)S(1)} %collective-permute-done.13.outer, bf16[3,5,128,128]{3,2,1,0:T(8,128)(2,1)S(1)} %collective-permute-done.16.inner), custom_call_target="tpu_custom_call" | custom-call | flops 1 | bytes 1024 | tf_op jit(solution)/shard_map/final/pallas_call | solution.py:399
  58.0 6.0 %collective-permute-done.14.outer = bf16[3,5,128,128]{3,2,1,0:T(8,128)(2,1)S(1)} collective-permute-done((bf16[3,5,128,128]{3,2,1,0:T(8,128)(2,1)S(1)}, bf16[3,5,128,128]{3,2,1,0:T(8,128)(2,1)S(1)}, u32[]{:S(2)}, u32[]{:S(2)}) %collective-permute-start.14) | collective-permute-done | bytes 491552 | tf_op jit(solution)/shard_map/ppermute | solution.py:390
  64.1 1.0 %final.3 = bf16[2,1,1,25,128,128]{5,4,3,2,1,0:T(8,128)(2,1)} custom-call(s32[1]{0:T(128)} %bitcast.turn, f32[3,5,128,128]{3,2,1,0:T(8,128)S(1)} %centre.2.own, bf16[3,5,128,128]{3,2,1,0:T(8,128)(2,1)S(1)} %collective-permute-done.14.outer, bf16[3,5,128,128]{3,2,1,0:T(8,128)(2,1)S(1)} %collective-permute-done.15.inner, ...), custom_call_target="tpu_custom_call", output_to_operand_aliasing={{}: (4, {})} | custom-call | flops 1 | bytes 1024 | tf_op jit(solution)/shard_map/final/pallas_call | solution.py:399
  (20 shorter events, 0.2 us)
Async XLA Ops:
  0.0 16.7 %collective-permute-start = (bf16[2,2,4,128,128]{4,3,2,1,0:T(8,128)(2,1)}, bf16[2,2,4,128,128]{4,3,2,1,0:T(8,128)(2,1)S(1)}, u32[]{:S(2)}, u32[]{:S(2)}) collective-permute-start(bf16[2,2,4,128,128]{4,3,2,1,0:T(8,128)(2,1)} %p_own.13), channel_id=1, source_target_pairs={{0,1},{1,0},{2,3},{3,2},{4,5},{5,4},{6,7},{7,6},{8,9},{9,8},{10,11... | collective-permute-start | bytes 1572872 | tf_op jit(solution)/shard_map/ppermute | solution.py:296
  2.9 25.8 %copy-start.1 = (bf16[2,2,2,5,128,128]{5,4,3,2,1,0:T(8,128)(2,1)S(1)}, bf16[2,2,2,5,128,128]{5,4,3,2,1,0:T(8,128)(2,1)}, u32[]{:S(2)}) copy-start(bf16[2,2,2,5,128,128]{5,4,3,2,1,0:T(8,128)(2,1)} %a_own.13) | copy-start | bytes 3932164
  5.1 11.5 %collective-permute-start.1 = (bf16[1296,128]{1,0:T(8,128)(2,1)}, bf16[1296,128]{1,0:T(8,128)(2,1)S(1)}, u32[]{:S(2)}, u32[]{:S(2)}) collective-permute-start(bf16[1296,128]{1,0:T(8,128)(2,1)} %pack_far.1.after.refs_0_), channel_id=1, source_target_pairs={{0,6},{1,3},{2,0},{3,5},{4,2},{5,7},{6,4},{7,1},{8,14},{9,11},{10,... | collective-permute-start | bytes 995336 | tf_op jit(solution)/shard_map/ppermute | solution.py:306
  8.7 1.0 %copy-start.2 = (bf16[2,2,4,128,128]{4,3,2,1,0:T(8,128)(2,1)S(1)}, bf16[2,2,4,128,128]{4,3,2,1,0:T(8,128)(2,1)}, u32[]{:S(2)}) copy-start(bf16[2,2,4,128,128]{4,3,2,1,0:T(8,128)(2,1)} %p_own.13) | copy-start | bytes 1572868
  9.8 19.0 %copy-start.3 = (bf16[2,2,4,128,128]{4,3,2,1,0:T(8,128)(2,1)S(1)}, bf16[2,2,4,128,128]{4,3,2,1,0:T(8,128)(2,1)}, u32[]{:S(2)}) copy-start(bf16[2,2,4,128,128]{4,3,2,1,0:T(8,128)(2,1)} %p_own.13) | copy-start | bytes 1572868
  9.8 8.6 %collective-permute-start.3 = (bf16[1,2,4,128,128]{4,3,2,1,0:T(8,128)(2,1)S(1)}, bf16[1,2,4,128,128]{4,3,2,1,0:T(8,128)(2,1)S(1)}, u32[]{:S(2)}, u32[]{:S(2)}) collective-permute-start(bf16[1,2,4,128,128]{4,3,2,1,0:T(8,128)(2,1)S(1)} %get-tuple-element.55), channel_id=1, source_target_pairs={{0,8},{8,0},{16,24},{24,16},{1,9},{9,1},{17,25},{25,17},{2,10},{10... | collective-permute-start | bytes 786440 | tf_op jit(solution)/shard_map/ppermute | solution.py:316
  9.9 8.5 %collective-permute-start.4 = (bf16[1,2,4,128,128]{4,3,2,1,0:T(8,128)(2,1)S(1)}, bf16[1,2,4,128,128]{4,3,2,1,0:T(8,128)(2,1)S(1)}, u32[]{:S(2)}, u32[]{:S(2)}) collective-permute-start(bf16[1,2,4,128,128]{4,3,2,1,0:T(8,128)(2,1)S(1)} %get-tuple-element.56), channel_id=1, source_target_pairs={{0,24},{8,16},{16,8},{24,0},{1,25},{9,17},{17,9},{25,1},{2,26},{10... | collective-permute-start | bytes 786440 | tf_op jit(solution)/shard_map/ppermute | solution.py:317
  11.5 1.3 %copy-start = (bf16[2,2,2,5,128,128]{5,4,3,2,1,0:T(8,128)(2,1)S(1)}, bf16[2,2,2,5,128,128]{5,4,3,2,1,0:T(8,128)(2,1)}, u32[]{:S(2)}) copy-start(bf16[2,2,2,5,128,128]{5,4,3,2,1,0:T(8,128)(2,1)} %a_own.13) | copy-start | bytes 3932164
  12.8 1.0 %copy-start.4 = (bf16[1296,128]{1,0:T(8,128)(2,1)S(1)}, bf16[1296,128]{1,0:T(8,128)(2,1)}, u32[]{:S(2)}) copy-start(bf16[1296,128]{1,0:T(8,128)(2,1)} %pack_far.1.after.refs_0_) | copy-start | bytes 995332
  13.8 0.7 %copy-start.6 = (s32[2,2,2,5]{3,2,1,0:T(2,128)S(1)}, s32[2,2,2,5]{3,2,1,0:T(2,128)}, u32[]{:S(2)}) copy-start(s32[2,2,2,5]{3,2,1,0:T(2,128)} %off.3) | copy-start | bytes 484
  14.5 0.7 %copy-start.7 = (s32[2,2,2]{2,1,0:T(2,128)S(1)}, s32[2,2,2]{2,1,0:T(2,128)}, u32[]{:S(2)}) copy-start(s32[2,2,2]{2,1,0:T(2,128)} %count.3) | copy-start | bytes 100
  15.2 13.4 %copy-start.5 = (bf16[1296,128]{1,0:T(8,128)(2,1)S(1)}, bf16[1296,128]{1,0:T(8,128)(2,1)}, u32[]{:S(2)}) copy-start(bf16[1296,128]{1,0:T(8,128)(2,1)} %pack_far.1.after.refs_0_) | copy-start | bytes 995332
  16.7 17.8 %collective-permute-start.2 = (bf16[2592,128]{1,0:T(8,128)(2,1)S(1)}, bf16[2592,128]{1,0:T(8,128)(2,1)S(1)}, u32[]{:S(2)}, u32[]{:S(2)}) collective-permute-start(bf16[2592,128]{1,0:T(8,128)(2,1)S(1)} %join.1), channel_id=1, source_target_pairs={{0,1},{1,0},{2,3},{3,2},{4,5},{5,4},{6,7},{7,6},{8,9},{9,8},{10,11... | collective-permute-start | bytes 1990664 | tf_op jit(solution)/shard_map/ppermute | solution.py:320
  17.1 18.6 %collective-permute-start.7 = (bf16[2,2,4,128,128]{4,3,2,1,0:T(8,128)(2,1)S(1)}, bf16[2,2,4,128,128]{4,3,2,1,0:T(8,128)(2,1)S(1)}, u32[]{:S(2)}, u32[]{:S(2)}) collective-permute-start(bf16[2,2,4,128,128]{4,3,2,1,0:T(8,128)(2,1)S(1)} %collective-permute-done.piece.p_near), channel_id=1, source_target_pairs={{0,2},{1,7},{2,4},{3,1},{4,6},{5,3},{6,0},{7,5},{8,10},{9,15},{10,... | collective-permute-start | bytes 1572872 | tf_op jit(solution)/shard_map/ppermute | solution.py:319
  18.4 8.5 %collective-permute-start.5 = (bf16[1,2,4,128,128]{4,3,2,1,0:T(8,128)(2,1)S(1)}, bf16[1,2,4,128,128]{4,3,2,1,0:T(8,128)(2,1)S(1)}, u32[]{:S(2)}, u32[]{:S(2)}) collective-permute-start(bf16[1,2,4,128,128]{4,3,2,1,0:T(8,128)(2,1)S(1)} %get-tuple-element.60), channel_id=1, source_target_pairs={{0,24},{8,16},{16,8},{24,0},{1,25},{9,17},{17,9},{25,1},{2,26},{10... | collective-permute-start | bytes 786440 | tf_op jit(solution)/shard_map/ppermute | solution.py:324
  19.6 9.1 %collective-permute-start.6 = (bf16[1,2,4,128,128]{4,3,2,1,0:T(8,128)(2,1)S(1)}, bf16[1,2,4,128,128]{4,3,2,1,0:T(8,128)(2,1)S(1)}, u32[]{:S(2)}, u32[]{:S(2)}) collective-permute-start(bf16[1,2,4,128,128]{4,3,2,1,0:T(8,128)(2,1)S(1)} %get-tuple-element.61), channel_id=1, source_target_pairs={{0,8},{8,0},{16,24},{24,16},{1,9},{9,1},{17,25},{25,17},{2,10},{10... | collective-permute-start | bytes 786440 | tf_op jit(solution)/shard_map/ppermute | solution.py:323
  26.9 12.1 %collective-permute-start.11 = (bf16[1,2,4,128,128]{4,3,2,1,0:T(8,128)(2,1)S(1)}, bf16[1,2,4,128,128]{4,3,2,1,0:T(8,128)(2,1)S(1)}, u32[]{:S(2)}, u32[]{:S(2)}) collective-permute-start(bf16[1,2,4,128,128]{4,3,2,1,0:T(8,128)(2,1)S(1)} %collective-permute-done.5.near_out), channel_id=1, source_target_pairs={{0,2},{1,7},{2,4},{3,1},{4,6},{5,3},{6,0},{7,5},{8,10},{9,15},{10,... | collective-permute-start | bytes 786440 | tf_op jit(solution)/shard_map/ppermute | solution.py:325
  30.9 17.3 %collective-permute-start.8 = (bf16[2,5,128,128]{3,2,1,0:T(8,128)(2,1)}, bf16[2,5,128,128]{3,2,1,0:T(8,128)(2,1)}, u32[]{:S(2)}, u32[]{:S(2)}) collective-permute-start(bf16[2,5,128,128]{3,2,1,0:T(8,128)(2,1)} %get-tuple-element.71), channel_id=1, source_target_pairs={{0,1},{1,0},{2,3},{3,2},{4,5},{5,4},{6,7},{7,6},{8,9},{9,8},{10,11... | collective-permute-start | bytes 983048 | tf_op jit(solution)/shard_map/ppermute | solution.py:348
  33.1 15.1 %collective-permute-start.9 = (bf16[5,128,128]{2,1,0:T(8,128)(2,1)}, bf16[5,128,128]{2,1,0:T(8,128)(2,1)}, u32[]{:S(2)}, u32[]{:S(2)}) collective-permute-start(bf16[5,128,128]{2,1,0:T(8,128)(2,1)} %get-tuple-element.72), channel_id=1, source_target_pairs={{0,7},{1,2},{2,1},{3,4},{4,3},{5,6},{6,5},{7,0},{8,15},{9,10},{10,... | collective-permute-start | bytes 491528 | tf_op jit(solution)/shard_map/ppermute | solution.py:348
  35.8 5.1 %collective-permute-start.10 = (bf16[1,2,4,128,128]{4,3,2,1,0:T(8,128)(2,1)S(1)}, bf16[1,2,4,128,128]{4,3,2,1,0:T(8,128)(2,1)S(1)}, u32[]{:S(2)}, u32[]{:S(2)}) collective-permute-start(bf16[1,2,4,128,128]{4,3,2,1,0:T(8,128)(2,1)S(1)} %row.1), channel_id=1, source_target_pairs={{0,8},{8,0},{16,24},{24,16},{1,9},{9,1},{17,25},{25,17},{2,10},{10... | collective-permute-start | bytes 786440 | tf_op jit(solution)/shard_map/ppermute | solution.py:345
  40.8 12.5 %collective-permute-start.13 = (bf16[3,5,128,128]{3,2,1,0:T(8,128)(2,1)S(1)}, bf16[3,5,128,128]{3,2,1,0:T(8,128)(2,1)S(1)}, u32[]{:S(2)}, u32[]{:S(2)}) collective-permute-start(bf16[3,5,128,128]{3,2,1,0:T(8,128)(2,1)S(1)} %get-tuple-element.83), channel_id=1, source_target_pairs={{0,24},{8,16},{16,8},{24,0},{1,25},{9,17},{17,9},{25,1},{2,26},{10... | collective-permute-start | bytes 1474568 | tf_op jit(solution)/shard_map/ppermute | solution.py:390
  42.9 10.4 %collective-permute-start.12 = (bf16[5,128,128]{2,1,0:T(8,128)(2,1)S(1)}, bf16[5,128,128]{2,1,0:T(8,128)(2,1)S(1)}, u32[]{:S(2)}, u32[]{:S(2)}) collective-permute-start(bf16[5,128,128]{2,1,0:T(8,128)(2,1)S(1)} %get-tuple-element.82), channel_id=1, source_target_pairs={{0,7},{1,2},{2,1},{3,4},{4,3},{5,6},{6,5},{7,0},{8,15},{9,10},{10,... | collective-permute-start | bytes 491528 | tf_op jit(solution)/shard_map/ppermute | solution.py:348
  45.5 11.5 %collective-permute-start.16 = (bf16[3,5,128,128]{3,2,1,0:T(8,128)(2,1)S(1)}, bf16[3,5,128,128]{3,2,1,0:T(8,128)(2,1)S(1)}, u32[]{:S(2)}, u32[]{:S(2)}) collective-permute-start(bf16[3,5,128,128]{3,2,1,0:T(8,128)(2,1)S(1)} %get-tuple-element.98), channel_id=1, source_target_pairs={{0,8},{8,0},{16,24},{24,16},{1,9},{9,1},{17,25},{25,17},{2,10},{10... | collective-permute-start | bytes 1474568 | tf_op jit(solution)/shard_map/ppermute | solution.py:391
  50.7 13.4 %collective-permute-start.14 = (bf16[3,5,128,128]{3,2,1,0:T(8,128)(2,1)S(1)}, bf16[3,5,128,128]{3,2,1,0:T(8,128)(2,1)S(1)}, u32[]{:S(2)}, u32[]{:S(2)}) collective-permute-start(bf16[3,5,128,128]{3,2,1,0:T(8,128)(2,1)S(1)} %get-tuple-element.92), channel_id=1, source_target_pairs={{0,24},{8,16},{16,8},{24,0},{1,25},{9,17},{17,9},{25,1},{2,26},{10... | collective-permute-start | bytes 1474568 | tf_op jit(solution)/shard_map/ppermute | solution.py:390
  55.7 8.4 %collective-permute-start.15 = (bf16[3,5,128,128]{3,2,1,0:T(8,128)(2,1)S(1)}, bf16[3,5,128,128]{3,2,1,0:T(8,128)(2,1)S(1)}, u32[]{:S(2)}, u32[]{:S(2)}) collective-permute-start(bf16[3,5,128,128]{3,2,1,0:T(8,128)(2,1)S(1)} %get-tuple-element.93), channel_id=1, source_target_pairs={{0,8},{8,0},{16,24},{24,16},{1,9},{9,1},{17,25},{25,17},{2,10},{10... | collective-permute-start | bytes 1474568 | tf_op jit(solution)/shard_map/ppermute | solution.py:391

commit v8 on v7

--- a/solution.py
+++ b/solution.py
@@ -315,8 +315,8 @@
     own_in, own_out = rows_of(turn, p_vals)
     own_in = lax.ppermute(own_in, "row", in_way)
     own_out = lax.ppermute(own_out, "row", out_way)
+    p_far = lax.ppermute(p_near, "col", on_way)
     p_near, joined = lax.optimization_barrier((p_near, joined))
-    p_far = lax.ppermute(p_near, "col", on_way)
     from_pair = lax.ppermute(joined, "col", near_way)
     p_rows, own_in, own_out = lax.optimization_barrier((p_near, own_in, own_out))
     near_in, near_out = rows_of(turn, p_rows)

time: 65.4 us -> 65.4 us (level)
  no operation moved by 1% of the time
where the time goes in v8:
time: 65.4 us; the launch traced here: 65 us
  starting transfers between devices  22.9 us (35%)
  Pallas kernels  18.9 us (29%)
  waiting for transfers between devices  18.3 us (28%)
  local copies, waits for them, and re-layouts  4.71 us (7%)
    ppermute x2, waiting for transfers between devices, per_device(): from_out = lax.ppermute(sums[0], 'row', out_way)  8.27 us
    ppermute x1, waiting for transfers between devices, per_device(): near_out = lax.ppermute(near_out, 'row', out_way)  6.8 us
    ppermute x3, starting transfers between devices, send(): lax.ppermute(later[3 * s - 3 + place], 'col', way)  6.34 us
    pallas_call x2, Pallas kernels, per_device(): call(functools.partial(sides_kernel, operators, s, x), [smem, smem, smem]...  4.81 us
    unnamed x16, local copies, waits for them, and re-layouts  4.71 us
    ppermute x1, starting transfers between devices, per_device(): moved = lax.ppermute(own_0, 'col', aside_way)  3.6 us
    ppermute x1, waiting for transfers between devices, per_device(): far_out = lax.ppermute(near_out, 'col', on_way)  3.21 us
    ppermute x1, starting transfers between devices, per_device(): p_near = lax.ppermute(p_vals, 'col', near_way)  2.94 us
  transfers between devices with their start and end apart: 17, of which 4 were waited for; matrix products, arithmetic and copies ran while one was open for 0% of the time, Pallas kernels for 28%

profile of v8, /device:TPU:0, one launch (start us, length us, event | category | flops | bytes accessed | tf_op | source)
XLA Modules:
  0.0 65.0 jit_solution(7822135969852239371)
XLA Ops:
  0.0 2.9 %collective-permute-start = (bf16[2,2,4,128,128]{4,3,2,1,0:T(8,128)(2,1)}, bf16[2,2,4,128,128]{4,3,2,1,0:T(8,128)(2,1)S(1)}, u32[]{:S(2)}, u32[]{:S(2)}) collective-permute-start(bf16[2,2,4,128,128]{4,3,2,1,0:T(8,128)(2,1)} %p_own.13), channel_id=1, source_target_pairs={{0,1},{1,0},{2,3},{3,2},{4,5},{5,4},{6,7},{7,6},{8,9},{9,8},{10,11... | collective-permute-start | bytes 1572872 | tf_op jit(solution)/shard_map/ppermute | solution.py:296
  2.9 2.2 %pack_far.1.after.refs_0_ = bf16[1296,128]{1,0:T(8,128)(2,1)} custom-call(s32[1]{0:T(128)} %bitcast.turn, s32[2,2,2,5]{3,2,1,0:T(2,128)} %off.3, s32[2,2,2]{2,1,0:T(2,128)} %count.3, bf16[2,2,2,5,128,128]{5,4,3,2,1,0:T(8,128)(2,1)} %a_own.13), custom_call_target="tpu_custom_call" | custom-call | flops 1 | bytes 1024 | tf_op jit(solution)/shard_map/pack_far/pallas_call | solution.py:300
  5.1 3.6 %collective-permute-start.1 = (bf16[1296,128]{1,0:T(8,128)(2,1)}, bf16[1296,128]{1,0:T(8,128)(2,1)S(1)}, u32[]{:S(2)}, u32[]{:S(2)}) collective-permute-start(bf16[1296,128]{1,0:T(8,128)(2,1)} %pack_far.1.after.refs_0_), channel_id=1, source_target_pairs={{0,6},{1,3},{2,0},{3,5},{4,2},{5,7},{6,4},{7,1},{8,14},{9,11},{10,... | collective-permute-start | bytes 995336 | tf_op jit(solution)/shard_map/ppermute | solution.py:306
  8.7 1.0 %copy-done.2 = bf16[2,2,4,128,128]{4,3,2,1,0:T(8,128)(2,1)S(1)} copy-done((bf16[2,2,4,128,128]{4,3,2,1,0:T(8,128)(2,1)S(1)}, bf16[2,2,4,128,128]{4,3,2,1,0:T(8,128)(2,1)}, u32[]{:S(2)}) %copy-start.2) | copy-done | bytes 524312
  9.8 0.1 collective-permute-start.3
  9.9 1.6 %collective-permute-start.4 = (bf16[1,2,4,128,128]{4,3,2,1,0:T(8,128)(2,1)S(1)}, bf16[1,2,4,128,128]{4,3,2,1,0:T(8,128)(2,1)S(1)}, u32[]{:S(2)}, u32[]{:S(2)}) collective-permute-start(bf16[1,2,4,128,128]{4,3,2,1,0:T(8,128)(2,1)S(1)} %get-tuple-element.56), channel_id=1, source_target_pairs={{0,24},{8,16},{16,8},{24,0},{1,25},{9,17},{17,9},{25,1},{2,26},{10... | collective-permute-start | bytes 786440 | tf_op jit(solution)/shard_map/ppermute | solution.py:317
  11.5 1.3 %copy-done = bf16[2,2,2,5,128,128]{5,4,3,2,1,0:T(8,128)(2,1)S(1)} copy-done((bf16[2,2,2,5,128,128]{5,4,3,2,1,0:T(8,128)(2,1)S(1)}, bf16[2,2,2,5,128,128]{5,4,3,2,1,0:T(8,128)(2,1)}, u32[]{:S(2)}) %copy-start) | copy-done | bytes 1310744
  12.9 1.0 %copy-done.4 = bf16[1296,128]{1,0:T(8,128)(2,1)S(1)} copy-done((bf16[1296,128]{1,0:T(8,128)(2,1)S(1)}, bf16[1296,128]{1,0:T(8,128)(2,1)}, u32[]{:S(2)}) %copy-start.4) | copy-done | bytes 331800
  13.8 0.7 %copy-done.6 = s32[2,2,2,5]{3,2,1,0:T(2,128)S(1)} copy-done((s32[2,2,2,5]{3,2,1,0:T(2,128)S(1)}, s32[2,2,2,5]{3,2,1,0:T(2,128)}, u32[]{:S(2)}) %copy-start.6) | copy-done | bytes 184
  14.5 0.7 %copy-done.7 = s32[2,2,2]{2,1,0:T(2,128)S(1)} copy-done((s32[2,2,2]{2,1,0:T(2,128)S(1)}, s32[2,2,2]{2,1,0:T(2,128)}, u32[]{:S(2)}) %copy-start.7) | copy-done | bytes 56
  15.2 1.5 %pack.1 = (bf16[1296,128]{1,0:T(8,128)(2,1)S(1)}, bf16[5,128,128]{2,1,0:T(8,128)(2,1)}, bf16[5,128,128]{2,1,0:T(8,128)(2,1)S(1)}, bf16[2,5,128,128]{3,2,1,0:T(8,128)(2,1)}) custom-call(s32[1]{0:T(128)} %bitcast.turn, s32[2,2,2,5]{3,2,1,0:T(2,128)S(1)} %copy-done.6, s32[2,2,2]{2,1,0:T(2,128)S(1)} %copy-done.7, bf16[2,2,2,5,128,128]{5,4,3,2,1,0:T(8,128)(2,1)S(1)} %copy-done, ...), custom_call_target="tpu_custom_call" | custom-call | flops 1 | bytes 1024 | tf_op jit(solution)/shard_map/pack/pallas_call | solution.py:303
  16.7 0.0 collective-permute-done.1.far
  16.7 0.4 collective-permute-start.2
  17.1 1.3 %collective-permute-start.7 = (bf16[2,2,4,128,128]{4,3,2,1,0:T(8,128)(2,1)S(1)}, bf16[2,2,4,128,128]{4,3,2,1,0:T(8,128)(2,1)S(1)}, u32[]{:S(2)}, u32[]{:S(2)}) collective-permute-start(bf16[2,2,4,128,128]{4,3,2,1,0:T(8,128)(2,1)S(1)} %collective-permute-done.piece.p_near), channel_id=1, source_target_pairs={{0,2},{1,7},{2,4},{3,1},{4,6},{5,3},{6,0},{7,5},{8,10},{9,15},{10,... | collective-permute-start | bytes 1572872 | tf_op jit(solution)/shard_map/ppermute | solution.py:318
  18.4 0.0 collective-permute-done.3.own_in
  18.4 0.0 collective-permute-done.4.own_out
  18.4 1.2 %collective-permute-start.5 = (bf16[1,2,4,128,128]{4,3,2,1,0:T(8,128)(2,1)S(1)}, bf16[1,2,4,128,128]{4,3,2,1,0:T(8,128)(2,1)S(1)}, u32[]{:S(2)}, u32[]{:S(2)}) collective-permute-start(bf16[1,2,4,128,128]{4,3,2,1,0:T(8,128)(2,1)S(1)} %get-tuple-element.60), channel_id=1, source_target_pairs={{0,24},{8,16},{16,8},{24,0},{1,25},{9,17},{17,9},{25,1},{2,26},{10... | collective-permute-start | bytes 786440 | tf_op jit(solution)/shard_map/ppermute | solution.py:324
  19.6 0.5 collective-permute-start.6
  20.1 6.8 %collective-permute-done.5.near_out = bf16[1,2,4,128,128]{4,3,2,1,0:T(8,128)(2,1)S(1)} collective-permute-done((bf16[1,2,4,128,128]{4,3,2,1,0:T(8,128)(2,1)S(1)}, bf16[1,2,4,128,128]{4,3,2,1,0:T(8,128)(2,1)S(1)}, u32[]{:S(2)}, u32[]{:S(2)}) %collective-permute-start.5) | collective-permute-done | bytes 262176 | tf_op jit(solution)/shard_map/ppermute | solution.py:324
  26.9 1.7 %collective-permute-start.11 = (bf16[1,2,4,128,128]{4,3,2,1,0:T(8,128)(2,1)S(1)}, bf16[1,2,4,128,128]{4,3,2,1,0:T(8,128)(2,1)S(1)}, u32[]{:S(2)}, u32[]{:S(2)}) collective-permute-start(bf16[1,2,4,128,128]{4,3,2,1,0:T(8,128)(2,1)S(1)} %collective-permute-done.5.near_out), channel_id=1, source_target_pairs={{0,2},{1,7},{2,4},{3,1},{4,6},{5,3},{6,0},{7,5},{8,10},{9,15},{10,... | collective-permute-start | bytes 786440 | tf_op jit(solution)/shard_map/ppermute | solution.py:325
  28.6 0.1 own_table.1.table
  28.7 0.0 collective-permute-done.6.near_in
  28.7 2.1 %near_own.1 = (bf16[97,128,128]{2,1,0:T(8,128)(2,1)S(1)}, bf16[3,128,384]{2,1,0:T(8,128)(2,1)S(1)}, bf16[3,128,384]{2,1,0:T(8,128)(2,1)S(1)}, bf16[3,128,384]{2,1,0:T(8,128)(2,1)S(1)}, bf16[3,128,384]{2,1,0:T(8,128)(2,1)S(1)}) custom-call(s32[8,45]{1,0:T(8,128)S(1)} %own_table.1.table, s32[1]{0:T(128)} %bitcast.turn, ...), custom_call_target="tpu_custom_call" | custom-call | flops 360 | bytes 1024 | tf_op jit(solution)/shard_map/near_own/pallas_call | solution.py:326
  30.9 2.3 %collective-permute-start.8 = (bf16[2,5,128,128]{3,2,1,0:T(8,128)(2,1)}, bf16[2,5,128,128]{3,2,1,0:T(8,128)(2,1)}, u32[]{:S(2)}, u32[]{:S(2)}) collective-permute-start(bf16[2,5,128,128]{3,2,1,0:T(8,128)(2,1)} %get-tuple-element.71), channel_id=1, source_target_pairs={{0,1},{1,0},{2,3},{3,2},{4,5},{5,4},{6,7},{7,6},{8,9},{9,8},{10,11... | collective-permute-start | bytes 983048 | tf_op jit(solution)/shard_map/ppermute | solution.py:348
  33.1 1.4 %collective-permute-start.9 = (bf16[5,128,128]{2,1,0:T(8,128)(2,1)}, bf16[5,128,128]{2,1,0:T(8,128)(2,1)}, u32[]{:S(2)}, u32[]{:S(2)}) collective-permute-start(bf16[5,128,128]{2,1,0:T(8,128)(2,1)} %get-tuple-element.72), channel_id=1, source_target_pairs={{0,7},{1,2},{2,1},{3,4},{4,3},{5,6},{6,5},{7,0},{8,15},{9,10},{10,... | collective-permute-start | bytes 491528 | tf_op jit(solution)/shard_map/ppermute | solution.py:348
  34.6 0.0 collective-permute-done.2.refs_0_.a_pair
  34.6 0.1 side_table.1.table
  34.7 1.1 %near.1.w_near.refs_6_ = bf16[3,128,384]{2,1,0:T(8,128)(2,1)S(1)} custom-call(s32[8,45]{1,0:T(8,128)S(1)} %side_table.1.table, bf16[97,128,128]{2,1,0:T(8,128)(2,1)S(1)} %get-tuple-element.62.flat.held, bf16[2592,128]{1,0:T(8,128)(2,1)S(1)} %collective-permute-done.2.refs_0_.a_pair), custom_call_target="tpu_custom_call" | custom-call | flops 45 | bytes 1024 | tf_op jit(solution)/shard_map/near/pallas_call | solution.py:339
  35.7 0.0 collective-permute-done.7.piece.p_far
  35.8 0.1 collective-permute-start.10
  35.9 3.2 %collective-permute-done.11.far_out = bf16[1,2,4,128,128]{4,3,2,1,0:T(8,128)(2,1)S(1)} collective-permute-done((bf16[1,2,4,128,128]{4,3,2,1,0:T(8,128)(2,1)S(1)}, bf16[1,2,4,128,128]{4,3,2,1,0:T(8,128)(2,1)S(1)}, u32[]{:S(2)}, u32[]{:S(2)}) %collective-permute-start.11) | collective-permute-done | bytes 262176 | tf_op jit(solution)/shard_map/ppermute | solution.py:325
  39.1 1.7 %first_outer.1 = (bf16[3,5,128,128]{3,2,1,0:T(8,128)(2,1)S(1)}, bf16[97,128,128]{2,1,0:T(8,128)(2,1)S(1)}, bf16[3,128,384]{2,1,0:T(8,128)(2,1)S(1)}, bf16[3,128,384]{2,1,0:T(8,128)(2,1)S(1)}) custom-call(s32[8,45]{1,0:T(8,128)S(1)} %own_table.1.table, s32[8,45]{1,0:T(8,128)S(1)} %side_table.1.table, s32[1]{0:T(128)} %bitcast.turn, ...), custom_call_target="tpu_custom_call", output_to_operand_aliasing={{1}: (11, {})} | custom-call | flops 99999997952 | bytes 1024 | tf_op jit(solution)/shard_map/first_outer/pallas_call | solution.py:358
  40.8 0.1 collective-permute-start.13
  40.9 0.0 collective-permute-done.10.far_in
  40.9 2.0 %first_inner.1 = (bf16[3,5,128,128]{3,2,1,0:T(8,128)(2,1)S(1)}, bf16[97,128,128]{2,1,0:T(8,128)(2,1)S(1)}, bf16[3,128,384]{2,1,0:T(8,128)(2,1)S(1)}, bf16[3,128,...) custom-call(s32[8,45]{1,0:T(8,128)S(1)} %own_table.1.table, ...), custom_call_target="tpu_custom_call", output_to_operand_aliasing={{1}: (10, {})} | custom-call | flops 99999997952 | bytes 1024 | tf_op jit(solution)/shard_map/first_inner/pallas_call | solution.py:366
  42.9 2.7 %collective-permute-start.12 = (bf16[5,128,128]{2,1,0:T(8,128)(2,1)S(1)}, bf16[5,128,128]{2,1,0:T(8,128)(2,1)S(1)}, u32[]{:S(2)}, u32[]{:S(2)}) collective-permute-start(bf16[5,128,128]{2,1,0:T(8,128)(2,1)S(1)} %get-tuple-element.82), channel_id=1, source_target_pairs={{0,7},{1,2},{2,1},{3,4},{4,3},{5,6},{6,5},{7,0},{8,15},{9,10},{10,... | collective-permute-start | bytes 491528 | tf_op jit(solution)/shard_map/ppermute | solution.py:348
  45.5 2.7 %collective-permute-start.16 = (bf16[3,5,128,128]{3,2,1,0:T(8,128)(2,1)S(1)}, bf16[3,5,128,128]{3,2,1,0:T(8,128)(2,1)S(1)}, u32[]{:S(2)}, u32[]{:S(2)}) collective-permute-start(bf16[3,5,128,128]{3,2,1,0:T(8,128)(2,1)S(1)} %get-tuple-element.98), channel_id=1, source_target_pairs={{0,8},{8,0},{16,24},{24,16},{1,9},{9,1},{17,25},{25,17},{2,10},{10... | collective-permute-start | bytes 1474568 | tf_op jit(solution)/shard_map/ppermute | solution.py:391
  48.2 0.0 collective-permute-done.9.a_far
  48.2 2.4 %sides.2 = (bf16[3,5,128,128]{3,2,1,0:T(8,128)(2,1)S(1)}, bf16[3,128,384]{2,1,0:T(8,128)(2,1)S(1)}, bf16[3,128,384]{2,1,0:T(8,128)(2,1)S(1)}, bf16[3,128,384]{2,1,0:T(8,128)(2,1)S(1)}) custom-call(s32[8,45]{1,0:T(8,128)S(1)} %own_table.1.table, s32[8,45]{1,0:T(8,128)S(1)} %side_table.1.table, s32[1]{0:T(128)} %bitcast.turn, ...), custom_call_target="tpu_custom_call" | custom-call | flops 100 | bytes 1024 | tf_op jit(solution)/shard_map/sides/pallas_call | solution.py:383
  50.7 0.4 collective-permute-start.14
  51.0 2.3 %collective-permute-done.13.outer = bf16[3,5,128,128]{3,2,1,0:T(8,128)(2,1)S(1)} collective-permute-done((bf16[3,5,128,128]{3,2,1,0:T(8,128)(2,1)S(1)}, bf16[3,5,128,128]{3,2,1,0:T(8,128)(2,1)S(1)}, u32[]{:S(2)}, u32[]{:S(2)}) %collective-permute-start.13) | collective-permute-done | bytes 491552 | tf_op jit(solution)/shard_map/ppermute | solution.py:390
  53.3 2.4 %sides.3 = (bf16[3,5,128,128]{3,2,1,0:T(8,128)(2,1)S(1)}, bf16[3,128,384]{2,1,0:T(8,128)(2,1)S(1)}, bf16[3,128,384]{2,1,0:T(8,128)(2,1)S(1)}, bf16[3,128,384]{2,1,0:T(8,128)(2,1)S(1)}) custom-call(s32[8,45]{1,0:T(8,128)S(1)} %own_table.1.table, s32[8,45]{1,0:T(8,128)S(1)} %side_table.1.table, s32[1]{0:T(128)} %bitcast.turn, ...), custom_call_target="tpu_custom_call" | custom-call | flops 100 | bytes 1024 | tf_op jit(solution)/shard_map/sides/pallas_call | solution.py:383
  55.7 0.1 collective-permute-start.15
  55.8 0.7 %centre.3.own = f32[3,5,128,128]{3,2,1,0:T(8,128)S(1)} custom-call(s32[1]{0:T(128)} %bitcast.turn, bf16[2,2,4,128,128]{4,3,2,1,0:T(8,128)(2,1)S(1)} %copy-done.3, bf16[2,2,4,128,128]{4,3,2,1,0:T(8,128)(2,1)S(1)} %collective-permute-done.piece.p_near, bf16[2,2,4,128,128]{4,3,2,1,0:T(8,128)(2,1)S(1)} %collective-permute-done.7.piece.p_far, ...), custom_call_target="tpu_custom_call" | custom-call | flops 144 | bytes 1024 | tf_op jit(solution)/shard_map/centre/pallas_call | solution.py:392
  56.4 0.6 centre.2.own
  57.1 1.0 %final.2.refs_0_ = bf16[2,1,1,25,128,128]{5,4,3,2,1,0:T(8,128)(2,1)} custom-call(s32[1]{0:T(128)} %bitcast.turn, f32[3,5,128,128]{3,2,1,0:T(8,128)S(1)} %centre.3.own, bf16[3,5,128,128]{3,2,1,0:T(8,128)(2,1)S(1)} %collective-permute-done.13.outer, bf16[3,5,128,128]{3,2,1,0:T(8,128)(2,1)S(1)} %collective-permute-done.16.inner), custom_call_target="tpu_custom_call" | custom-call | flops 1 | bytes 1024 | tf_op jit(solution)/shard_map/final/pallas_call | solution.py:399
  58.0 6.0 %collective-permute-done.14.outer = bf16[3,5,128,128]{3,2,1,0:T(8,128)(2,1)S(1)} collective-permute-done((bf16[3,5,128,128]{3,2,1,0:T(8,128)(2,1)S(1)}, bf16[3,5,128,128]{3,2,1,0:T(8,128)(2,1)S(1)}, u32[]{:S(2)}, u32[]{:S(2)}) %collective-permute-start.14) | collective-permute-done | bytes 491552 | tf_op jit(solution)/shard_map/ppermute | solution.py:390
  64.1 1.0 %final.3 = bf16[2,1,1,25,128,128]{5,4,3,2,1,0:T(8,128)(2,1)} custom-call(s32[1]{0:T(128)} %bitcast.turn, f32[3,5,128,128]{3,2,1,0:T(8,128)S(1)} %centre.2.own, bf16[3,5,128,128]{3,2,1,0:T(8,128)(2,1)S(1)} %collective-permute-done.14.outer, bf16[3,5,128,128]{3,2,1,0:T(8,128)(2,1)S(1)} %collective-permute-done.15.inner, ...), custom_call_target="tpu_custom_call", output_to_operand_aliasing={{}: (4, {})} | custom-call | flops 1 | bytes 1024 | tf_op jit(solution)/shard_map/final/pallas_call | solution.py:399
  (20 shorter events, 0.2 us)
Async XLA Ops:
  0.0 16.7 %collective-permute-start = (bf16[2,2,4,128,128]{4,3,2,1,0:T(8,128)(2,1)}, bf16[2,2,4,128,128]{4,3,2,1,0:T(8,128)(2,1)S(1)}, u32[]{:S(2)}, u32[]{:S(2)}) collective-permute-start(bf16[2,2,4,128,128]{4,3,2,1,0:T(8,128)(2,1)} %p_own.13), channel_id=1, source_target_pairs={{0,1},{1,0},{2,3},{3,2},{4,5},{5,4},{6,7},{7,6},{8,9},{9,8},{10,11... | collective-permute-start | bytes 1572872 | tf_op jit(solution)/shard_map/ppermute | solution.py:296
  2.9 25.8 %copy-start.1 = (bf16[2,2,2,5,128,128]{5,4,3,2,1,0:T(8,128)(2,1)S(1)}, bf16[2,2,2,5,128,128]{5,4,3,2,1,0:T(8,128)(2,1)}, u32[]{:S(2)}) copy-start(bf16[2,2,2,5,128,128]{5,4,3,2,1,0:T(8,128)(2,1)} %a_own.13) | copy-start | bytes 3932164
  5.1 11.5 %collective-permute-start.1 = (bf16[1296,128]{1,0:T(8,128)(2,1)}, bf16[1296,128]{1,0:T(8,128)(2,1)S(1)}, u32[]{:S(2)}, u32[]{:S(2)}) collective-permute-start(bf16[1296,128]{1,0:T(8,128)(2,1)} %pack_far.1.after.refs_0_), channel_id=1, source_target_pairs={{0,6},{1,3},{2,0},{3,5},{4,2},{5,7},{6,4},{7,1},{8,14},{9,11},{10,... | collective-permute-start | bytes 995336 | tf_op jit(solution)/shard_map/ppermute | solution.py:306
  8.7 1.0 %copy-start.2 = (bf16[2,2,4,128,128]{4,3,2,1,0:T(8,128)(2,1)S(1)}, bf16[2,2,4,128,128]{4,3,2,1,0:T(8,128)(2,1)}, u32[]{:S(2)}) copy-start(bf16[2,2,4,128,128]{4,3,2,1,0:T(8,128)(2,1)} %p_own.13) | copy-start | bytes 1572868
  9.8 19.0 %copy-start.3 = (bf16[2,2,4,128,128]{4,3,2,1,0:T(8,128)(2,1)S(1)}, bf16[2,2,4,128,128]{4,3,2,1,0:T(8,128)(2,1)}, u32[]{:S(2)}) copy-start(bf16[2,2,4,128,128]{4,3,2,1,0:T(8,128)(2,1)} %p_own.13) | copy-start | bytes 1572868
  9.8 8.6 %collective-permute-start.3 = (bf16[1,2,4,128,128]{4,3,2,1,0:T(8,128)(2,1)S(1)}, bf16[1,2,4,128,128]{4,3,2,1,0:T(8,128)(2,1)S(1)}, u32[]{:S(2)}, u32[]{:S(2)}) collective-permute-start(bf16[1,2,4,128,128]{4,3,2,1,0:T(8,128)(2,1)S(1)} %get-tuple-element.55), channel_id=1, source_target_pairs={{0,8},{8,0},{16,24},{24,16},{1,9},{9,1},{17,25},{25,17},{2,10},{10... | collective-permute-start | bytes 786440 | tf_op jit(solution)/shard_map/ppermute | solution.py:316
  9.9 8.5 %collective-permute-start.4 = (bf16[1,2,4,128,128]{4,3,2,1,0:T(8,128)(2,1)S(1)}, bf16[1,2,4,128,128]{4,3,2,1,0:T(8,128)(2,1)S(1)}, u32[]{:S(2)}, u32[]{:S(2)}) collective-permute-start(bf16[1,2,4,128,128]{4,3,2,1,0:T(8,128)(2,1)S(1)} %get-tuple-element.56), channel_id=1, source_target_pairs={{0,24},{8,16},{16,8},{24,0},{1,25},{9,17},{17,9},{25,1},{2,26},{10... | collective-permute-start | bytes 786440 | tf_op jit(solution)/shard_map/ppermute | solution.py:317
  11.5 1.3 %copy-start = (bf16[2,2,2,5,128,128]{5,4,3,2,1,0:T(8,128)(2,1)S(1)}, bf16[2,2,2,5,128,128]{5,4,3,2,1,0:T(8,128)(2,1)}, u32[]{:S(2)}) copy-start(bf16[2,2,2,5,128,128]{5,4,3,2,1,0:T(8,128)(2,1)} %a_own.13) | copy-start | bytes 3932164
  12.8 1.0 %copy-start.4 = (bf16[1296,128]{1,0:T(8,128)(2,1)S(1)}, bf16[1296,128]{1,0:T(8,128)(2,1)}, u32[]{:S(2)}) copy-start(bf16[1296,128]{1,0:T(8,128)(2,1)} %pack_far.1.after.refs_0_) | copy-start | bytes 995332
  13.8 0.7 %copy-start.6 = (s32[2,2,2,5]{3,2,1,0:T(2,128)S(1)}, s32[2,2,2,5]{3,2,1,0:T(2,128)}, u32[]{:S(2)}) copy-start(s32[2,2,2,5]{3,2,1,0:T(2,128)} %off.3) | copy-start | bytes 484
  14.5 0.7 %copy-start.7 = (s32[2,2,2]{2,1,0:T(2,128)S(1)}, s32[2,2,2]{2,1,0:T(2,128)}, u32[]{:S(2)}) copy-start(s32[2,2,2]{2,1,0:T(2,128)} %count.3) | copy-start | bytes 100
  15.2 13.4 %copy-start.5 = (bf16[1296,128]{1,0:T(8,128)(2,1)S(1)}, bf16[1296,128]{1,0:T(8,128)(2,1)}, u32[]{:S(2)}) copy-start(bf16[1296,128]{1,0:T(8,128)(2,1)} %pack_far.1.after.refs_0_) | copy-start | bytes 995332
  16.7 17.8 %collective-permute-start.2 = (bf16[2592,128]{1,0:T(8,128)(2,1)S(1)}, bf16[2592,128]{1,0:T(8,128)(2,1)S(1)}, u32[]{:S(2)}, u32[]{:S(2)}) collective-permute-start(bf16[2592,128]{1,0:T(8,128)(2,1)S(1)} %join.1), channel_id=1, source_target_pairs={{0,1},{1,0},{2,3},{3,2},{4,5},{5,4},{6,7},{7,6},{8,9},{9,8},{10,11... | collective-permute-start | bytes 1990664 | tf_op jit(solution)/shard_map/ppermute | solution.py:320
  17.1 18.6 %collective-permute-start.7 = (bf16[2,2,4,128,128]{4,3,2,1,0:T(8,128)(2,1)S(1)}, bf16[2,2,4,128,128]{4,3,2,1,0:T(8,128)(2,1)S(1)}, u32[]{:S(2)}, u32[]{:S(2)}) collective-permute-start(bf16[2,2,4,128,128]{4,3,2,1,0:T(8,128)(2,1)S(1)} %collective-permute-done.piece.p_near), channel_id=1, source_target_pairs={{0,2},{1,7},{2,4},{3,1},{4,6},{5,3},{6,0},{7,5},{8,10},{9,15},{10,... | collective-permute-start | bytes 1572872 | tf_op jit(solution)/shard_map/ppermute | solution.py:318
  18.4 8.5 %collective-permute-start.5 = (bf16[1,2,4,128,128]{4,3,2,1,0:T(8,128)(2,1)S(1)}, bf16[1,2,4,128,128]{4,3,2,1,0:T(8,128)(2,1)S(1)}, u32[]{:S(2)}, u32[]{:S(2)}) collective-permute-start(bf16[1,2,4,128,128]{4,3,2,1,0:T(8,128)(2,1)S(1)} %get-tuple-element.60), channel_id=1, source_target_pairs={{0,24},{8,16},{16,8},{24,0},{1,25},{9,17},{17,9},{25,1},{2,26},{10... | collective-permute-start | bytes 786440 | tf_op jit(solution)/shard_map/ppermute | solution.py:324
  19.6 9.1 %collective-permute-start.6 = (bf16[1,2,4,128,128]{4,3,2,1,0:T(8,128)(2,1)S(1)}, bf16[1,2,4,128,128]{4,3,2,1,0:T(8,128)(2,1)S(1)}, u32[]{:S(2)}, u32[]{:S(2)}) collective-permute-start(bf16[1,2,4,128,128]{4,3,2,1,0:T(8,128)(2,1)S(1)} %get-tuple-element.61), channel_id=1, source_target_pairs={{0,8},{8,0},{16,24},{24,16},{1,9},{9,1},{17,25},{25,17},{2,10},{10... | collective-permute-start | bytes 786440 | tf_op jit(solution)/shard_map/ppermute | solution.py:323
  26.9 12.1 %collective-permute-start.11 = (bf16[1,2,4,128,128]{4,3,2,1,0:T(8,128)(2,1)S(1)}, bf16[1,2,4,128,128]{4,3,2,1,0:T(8,128)(2,1)S(1)}, u32[]{:S(2)}, u32[]{:S(2)}) collective-permute-start(bf16[1,2,4,128,128]{4,3,2,1,0:T(8,128)(2,1)S(1)} %collective-permute-done.5.near_out), channel_id=1, source_target_pairs={{0,2},{1,7},{2,4},{3,1},{4,6},{5,3},{6,0},{7,5},{8,10},{9,15},{10,... | collective-permute-start | bytes 786440 | tf_op jit(solution)/shard_map/ppermute | solution.py:325
  30.9 17.3 %collective-permute-start.8 = (bf16[2,5,128,128]{3,2,1,0:T(8,128)(2,1)}, bf16[2,5,128,128]{3,2,1,0:T(8,128)(2,1)}, u32[]{:S(2)}, u32[]{:S(2)}) collective-permute-start(bf16[2,5,128,128]{3,2,1,0:T(8,128)(2,1)} %get-tuple-element.71), channel_id=1, source_target_pairs={{0,1},{1,0},{2,3},{3,2},{4,5},{5,4},{6,7},{7,6},{8,9},{9,8},{10,11... | collective-permute-start | bytes 983048 | tf_op jit(solution)/shard_map/ppermute | solution.py:348
  33.1 15.1 %collective-permute-start.9 = (bf16[5,128,128]{2,1,0:T(8,128)(2,1)}, bf16[5,128,128]{2,1,0:T(8,128)(2,1)}, u32[]{:S(2)}, u32[]{:S(2)}) collective-permute-start(bf16[5,128,128]{2,1,0:T(8,128)(2,1)} %get-tuple-element.72), channel_id=1, source_target_pairs={{0,7},{1,2},{2,1},{3,4},{4,3},{5,6},{6,5},{7,0},{8,15},{9,10},{10,... | collective-permute-start | bytes 491528 | tf_op jit(solution)/shard_map/ppermute | solution.py:348
  35.8 5.1 %collective-permute-start.10 = (bf16[1,2,4,128,128]{4,3,2,1,0:T(8,128)(2,1)S(1)}, bf16[1,2,4,128,128]{4,3,2,1,0:T(8,128)(2,1)S(1)}, u32[]{:S(2)}, u32[]{:S(2)}) collective-permute-start(bf16[1,2,4,128,128]{4,3,2,1,0:T(8,128)(2,1)S(1)} %row.1), channel_id=1, source_target_pairs={{0,8},{8,0},{16,24},{24,16},{1,9},{9,1},{17,25},{25,17},{2,10},{10... | collective-permute-start | bytes 786440 | tf_op jit(solution)/shard_map/ppermute | solution.py:345
  40.8 12.5 %collective-permute-start.13 = (bf16[3,5,128,128]{3,2,1,0:T(8,128)(2,1)S(1)}, bf16[3,5,128,128]{3,2,1,0:T(8,128)(2,1)S(1)}, u32[]{:S(2)}, u32[]{:S(2)}) collective-permute-start(bf16[3,5,128,128]{3,2,1,0:T(8,128)(2,1)S(1)} %get-tuple-element.83), channel_id=1, source_target_pairs={{0,24},{8,16},{16,8},{24,0},{1,25},{9,17},{17,9},{25,1},{2,26},{10... | collective-permute-start | bytes 1474568 | tf_op jit(solution)/shard_map/ppermute | solution.py:390
  42.9 10.4 %collective-permute-start.12 = (bf16[5,128,128]{2,1,0:T(8,128)(2,1)S(1)}, bf16[5,128,128]{2,1,0:T(8,128)(2,1)S(1)}, u32[]{:S(2)}, u32[]{:S(2)}) collective-permute-start(bf16[5,128,128]{2,1,0:T(8,128)(2,1)S(1)} %get-tuple-element.82), channel_id=1, source_target_pairs={{0,7},{1,2},{2,1},{3,4},{4,3},{5,6},{6,5},{7,0},{8,15},{9,10},{10,... | collective-permute-start | bytes 491528 | tf_op jit(solution)/shard_map/ppermute | solution.py:348
  45.5 11.5 %collective-permute-start.16 = (bf16[3,5,128,128]{3,2,1,0:T(8,128)(2,1)S(1)}, bf16[3,5,128,128]{3,2,1,0:T(8,128)(2,1)S(1)}, u32[]{:S(2)}, u32[]{:S(2)}) collective-permute-start(bf16[3,5,128,128]{3,2,1,0:T(8,128)(2,1)S(1)} %get-tuple-element.98), channel_id=1, source_target_pairs={{0,8},{8,0},{16,24},{24,16},{1,9},{9,1},{17,25},{25,17},{2,10},{10... | collective-permute-start | bytes 1474568 | tf_op jit(solution)/shard_map/ppermute | solution.py:391
  50.7 13.4 %collective-permute-start.14 = (bf16[3,5,128,128]{3,2,1,0:T(8,128)(2,1)S(1)}, bf16[3,5,128,128]{3,2,1,0:T(8,128)(2,1)S(1)}, u32[]{:S(2)}, u32[]{:S(2)}) collective-permute-start(bf16[3,5,128,128]{3,2,1,0:T(8,128)(2,1)S(1)} %get-tuple-element.92), channel_id=1, source_target_pairs={{0,24},{8,16},{16,8},{24,0},{1,25},{9,17},{17,9},{25,1},{2,26},{10... | collective-permute-start | bytes 1474568 | tf_op jit(solution)/shard_map/ppermute | solution.py:390
  55.7 8.4 %collective-permute-start.15 = (bf16[3,5,128,128]{3,2,1,0:T(8,128)(2,1)S(1)}, bf16[3,5,128,128]{3,2,1,0:T(8,128)(2,1)S(1)}, u32[]{:S(2)}, u32[]{:S(2)}) collective-permute-start(bf16[3,5,128,128]{3,2,1,0:T(8,128)(2,1)S(1)} %get-tuple-element.93), channel_id=1, source_target_pairs={{0,8},{8,0},{16,24},{24,16},{1,9},{9,1},{17,25},{25,17},{2,10},{10... | collective-permute-start | bytes 1474568 | tf_op jit(solution)/shard_map/ppermute | solution.py:391

commit v9 on v8

--- a/solution.py
+++ b/solution.py
@@ -372,21 +372,20 @@
                 aliases={10: 1},
             )(own_table, side_table, turn, a_vals, from_pair, w_own[1][0], p_vals, p_near, p_far, far_in, flat)
             near_w = [near_w, inner_w]
-            inner_w, later = lax.optimization_barrier((inner_w, later))
-            far_a.append(send(1, far_way))
-            a_sides = [None] + [[(near_a[s], far_a[x][s]) for x in range(2)] for s in range(operators - 1)]
         else:
             near_w = [None, None]
             for x in range(2):
                 if x == 1:
                     from_out, w_own = lax.optimization_barrier((from_out, w_own))
+                    sums[0], later = lax.optimization_barrier((sums[0], later))
+                    far_a.append(send(1, far_way))
                 sums[x], near_w[x], far_w[x], own_w[x] = call(
                     functools.partial(sides_kernel, operators, s, x),
                     [smem, smem, smem] + [vmem] * 8,
                     [part_shape, w_shape, w_shape, w_shape],
                     100,
                     "sides",
-                )(own_table, side_table, turn, a_vals, *a_sides[s][x], flat, w_own[x][s], p_vals, p_near, p_far)
+                )(own_table, side_table, turn, a_vals, near_a[s - 1], far_a[x][s - 1], flat, w_own[x][s], p_vals, p_near, p_far)
         from_out = lax.ppermute(sums[0], "row", out_way)
         from_in = lax.ppermute(sums[1], "row", in_way)
         centre = call(

time: 65.4 us -> 65.3 us (level)
  starting transfers between devices: 22.9 us -> 20.7 us
  waiting for transfers between devices: 18.3 us -> 20.5 us
    ppermute x3, waiting for transfers between devices: 0.01 us -> 4.86 us  [send(): lax.ppermute(later[3 * s - 3 + place], 'col', way)]
    ppermute x2, waiting for transfers between devices: 8.27 us -> 5.57 us  [per_device(): from_out = lax.ppermute(sums[0], 'row', out_way)]
    ppermute x3, starting transfers between devices: 6.34 us -> 4.98 us  [send(): lax.ppermute(later[3 * s - 3 + place], 'col', way)]
    ppermute x2, starting transfers between devices: 2.75 us -> 1.98 us  [per_device(): from_in = lax.ppermute(sums[1], 'row', in_way)]
  transfers between devices with their start and end apart: 17 -> 17, of which waited for: 4 -> 6; matrix products, arithmetic and copies ran while one was open for 0% -> 0% of each run, Pallas kernels for 28% -> 28%
where the time goes in v9:
time: 65.3 us; the launch traced here: 65 us
  starting transfers between devices  20.7 us (32%)
  waiting for transfers between devices  20.5 us (31%)
  Pallas kernels  18.9 us (29%)
  local copies, waits for them, and re-layouts  4.71 us (7%)
    ppermute x1, waiting for transfers between devices, per_device(): near_out = lax.ppermute(near_out, 'row', out_way)  6.8 us
    ppermute x2, waiting for transfers between devices, per_device(): from_out = lax.ppermute(sums[0], 'row', out_way)  5.57 us
    ppermute x3, starting transfers between devices, send(): lax.ppermute(later[3 * s - 3 + place], 'col', way)  4.98 us
    ppermute x3, waiting for transfers between devices, send(): lax.ppermute(later[3 * s - 3 + place], 'col', way)  4.86 us
    pallas_call x2, Pallas kernels, per_device(): call(functools.partial(sides_kernel, operators, s, x), [smem, smem, smem]...  4.81 us
    unnamed x16, local copies, waits for them, and re-layouts  4.71 us
    ppermute x1, starting transfers between devices, per_device(): moved = lax.ppermute(own_0, 'col', aside_way)  3.6 us
    ppermute x1, waiting for transfers between devices, per_device(): far_out = lax.ppermute(near_out, 'col', on_way)  3.21 us
  transfers between devices with their start and end apart: 17, of which 6 were waited for; matrix products, arithmetic and copies ran while one was open for 0% of the time, Pallas kernels for 28%

profile of v9, /device:TPU:0, one launch (start us, length us, event | category | flops | bytes accessed | tf_op | source)
XLA Modules:
  0.0 65.0 jit_solution(5148775468122254254)
XLA Ops:
  0.0 2.9 %collective-permute-start = (bf16[2,2,4,128,128]{4,3,2,1,0:T(8,128)(2,1)}, bf16[2,2,4,128,128]{4,3,2,1,0:T(8,128)(2,1)S(1)}, u32[]{:S(2)}, u32[]{:S(2)}) collective-permute-start(bf16[2,2,4,128,128]{4,3,2,1,0:T(8,128)(2,1)} %p_own.13), channel_id=1, source_target_pairs={{0,1},{1,0},{2,3},{3,2},{4,5},{5,4},{6,7},{7,6},{8,9},{9,8},{10,11... | collective-permute-start | bytes 1572872 | tf_op jit(solution)/shard_map/ppermute | solution.py:296
  2.9 2.2 %pack_far.1.after.refs_0_ = bf16[1296,128]{1,0:T(8,128)(2,1)} custom-call(s32[1]{0:T(128)} %bitcast.turn, s32[2,2,2,5]{3,2,1,0:T(2,128)} %off.3, s32[2,2,2]{2,1,0:T(2,128)} %count.3, bf16[2,2,2,5,128,128]{5,4,3,2,1,0:T(8,128)(2,1)} %a_own.13), custom_call_target="tpu_custom_call" | custom-call | flops 1 | bytes 1024 | tf_op jit(solution)/shard_map/pack_far/pallas_call | solution.py:300
  5.1 3.6 %collective-permute-start.1 = (bf16[1296,128]{1,0:T(8,128)(2,1)}, bf16[1296,128]{1,0:T(8,128)(2,1)S(1)}, u32[]{:S(2)}, u32[]{:S(2)}) collective-permute-start(bf16[1296,128]{1,0:T(8,128)(2,1)} %pack_far.1.after.refs_0_), channel_id=1, source_target_pairs={{0,6},{1,3},{2,0},{3,5},{4,2},{5,7},{6,4},{7,1},{8,14},{9,11},{10,... | collective-permute-start | bytes 995336 | tf_op jit(solution)/shard_map/ppermute | solution.py:306
  8.7 1.0 %copy-done.2 = bf16[2,2,4,128,128]{4,3,2,1,0:T(8,128)(2,1)S(1)} copy-done((bf16[2,2,4,128,128]{4,3,2,1,0:T(8,128)(2,1)S(1)}, bf16[2,2,4,128,128]{4,3,2,1,0:T(8,128)(2,1)}, u32[]{:S(2)}) %copy-start.2) | copy-done | bytes 524312
  9.8 0.1 collective-permute-start.3
  9.9 1.6 %collective-permute-start.4 = (bf16[1,2,4,128,128]{4,3,2,1,0:T(8,128)(2,1)S(1)}, bf16[1,2,4,128,128]{4,3,2,1,0:T(8,128)(2,1)S(1)}, u32[]{:S(2)}, u32[]{:S(2)}) collective-permute-start(bf16[1,2,4,128,128]{4,3,2,1,0:T(8,128)(2,1)S(1)} %get-tuple-element.57), channel_id=1, source_target_pairs={{0,24},{8,16},{16,8},{24,0},{1,25},{9,17},{17,9},{25,1},{2,26},{10... | collective-permute-start | bytes 786440 | tf_op jit(solution)/shard_map/ppermute | solution.py:317
  11.5 1.3 %copy-done = bf16[2,2,2,5,128,128]{5,4,3,2,1,0:T(8,128)(2,1)S(1)} copy-done((bf16[2,2,2,5,128,128]{5,4,3,2,1,0:T(8,128)(2,1)S(1)}, bf16[2,2,2,5,128,128]{5,4,3,2,1,0:T(8,128)(2,1)}, u32[]{:S(2)}) %copy-start) | copy-done | bytes 1310744
  12.9 1.0 %copy-done.4 = bf16[1296,128]{1,0:T(8,128)(2,1)S(1)} copy-done((bf16[1296,128]{1,0:T(8,128)(2,1)S(1)}, bf16[1296,128]{1,0:T(8,128)(2,1)}, u32[]{:S(2)}) %copy-start.4) | copy-done | bytes 331800
  13.8 0.7 %copy-done.6 = s32[2,2,2,5]{3,2,1,0:T(2,128)S(1)} copy-done((s32[2,2,2,5]{3,2,1,0:T(2,128)S(1)}, s32[2,2,2,5]{3,2,1,0:T(2,128)}, u32[]{:S(2)}) %copy-start.6) | copy-done | bytes 184
  14.5 0.7 %copy-done.7 = s32[2,2,2]{2,1,0:T(2,128)S(1)} copy-done((s32[2,2,2]{2,1,0:T(2,128)S(1)}, s32[2,2,2]{2,1,0:T(2,128)}, u32[]{:S(2)}) %copy-start.7) | copy-done | bytes 56
  15.2 1.5 %pack.1 = (bf16[1296,128]{1,0:T(8,128)(2,1)S(1)}, bf16[5,128,128]{2,1,0:T(8,128)(2,1)}, bf16[5,128,128]{2,1,0:T(8,128)(2,1)S(1)}, bf16[2,5,128,128]{3,2,1,0:T(8,128)(2,1)}) custom-call(s32[1]{0:T(128)} %bitcast.turn, s32[2,2,2,5]{3,2,1,0:T(2,128)S(1)} %copy-done.6, s32[2,2,2]{2,1,0:T(2,128)S(1)} %copy-done.7, bf16[2,2,2,5,128,128]{5,4,3,2,1,0:T(8,128)(2,1)S(1)} %copy-done, ...), custom_call_target="tpu_custom_call" | custom-call | flops 1 | bytes 1024 | tf_op jit(solution)/shard_map/pack/pallas_call | solution.py:303
  16.7 0.0 collective-permute-done.1.far
  16.7 0.0 collective-permute-done.piece.p_near
  16.7 0.4 collective-permute-start.2
  17.1 1.3 %collective-permute-start.7 = (bf16[2,2,4,128,128]{4,3,2,1,0:T(8,128)(2,1)S(1)}, bf16[2,2,4,128,128]{4,3,2,1,0:T(8,128)(2,1)S(1)}, u32[]{:S(2)}, u32[]{:S(2)}) collective-permute-start(bf16[2,2,4,128,128]{4,3,2,1,0:T(8,128)(2,1)S(1)} %collective-permute-done.piece.p_near), channel_id=1, source_target_pairs={{0,2},{1,7},{2,4},{3,1},{4,6},{5,3},{6,0},{7,5},{8,10},{9,15},{10,... | collective-permute-start | bytes 1572872 | tf_op jit(solution)/shard_map/ppermute | solution.py:318
  18.4 0.0 collective-permute-done.3.own_in
  18.4 1.2 %collective-permute-start.5 = (bf16[1,2,4,128,128]{4,3,2,1,0:T(8,128)(2,1)S(1)}, bf16[1,2,4,128,128]{4,3,2,1,0:T(8,128)(2,1)S(1)}, u32[]{:S(2)}, u32[]{:S(2)}) collective-permute-start(bf16[1,2,4,128,128]{4,3,2,1,0:T(8,128)(2,1)S(1)} %get-tuple-element.61), channel_id=1, source_target_pairs={{0,24},{8,16},{16,8},{24,0},{1,25},{9,17},{17,9},{25,1},{2,26},{10... | collective-permute-start | bytes 786440 | tf_op jit(solution)/shard_map/ppermute | solution.py:324
  19.6 0.5 collective-permute-start.6
  20.1 6.8 %collective-permute-done.5.near_out = bf16[1,2,4,128,128]{4,3,2,1,0:T(8,128)(2,1)S(1)} collective-permute-done((bf16[1,2,4,128,128]{4,3,2,1,0:T(8,128)(2,1)S(1)}, bf16[1,2,4,128,128]{4,3,2,1,0:T(8,128)(2,1)S(1)}, u32[]{:S(2)}, u32[]{:S(2)}) %collective-permute-start.5) | collective-permute-done | bytes 262176 | tf_op jit(solution)/shard_map/ppermute | solution.py:324
  26.9 1.7 %collective-permute-start.11 = (bf16[1,2,4,128,128]{4,3,2,1,0:T(8,128)(2,1)S(1)}, bf16[1,2,4,128,128]{4,3,2,1,0:T(8,128)(2,1)S(1)}, u32[]{:S(2)}, u32[]{:S(2)}) collective-permute-start(bf16[1,2,4,128,128]{4,3,2,1,0:T(8,128)(2,1)S(1)} %collective-permute-done.5.near_out), channel_id=1, source_target_pairs={{0,2},{1,7},{2,4},{3,1},{4,6},{5,3},{6,0},{7,5},{8,10},{9,15},{10,... | collective-permute-start | bytes 786440 | tf_op jit(solution)/shard_map/ppermute | solution.py:325
  28.6 0.1 own_table.1.table
  28.7 0.0 collective-permute-done.6.near_in
  28.7 2.1 %near_own.1 = (bf16[97,128,128]{2,1,0:T(8,128)(2,1)S(1)}, bf16[3,128,384]{2,1,0:T(8,128)(2,1)S(1)}, bf16[3,128,384]{2,1,0:T(8,128)(2,1)S(1)}, bf16[3,128,384]{2,1,0:T(8,128)(2,1)S(1)}, bf16[3,128,384]{2,1,0:T(8,128)(2,1)S(1)}) custom-call(s32[8,45]{1,0:T(8,128)S(1)} %own_table.1.table, s32[1]{0:T(128)} %bitcast.turn, ...), custom_call_target="tpu_custom_call" | custom-call | flops 360 | bytes 1024 | tf_op jit(solution)/shard_map/near_own/pallas_call | solution.py:326
  30.9 2.3 %collective-permute-start.8 = (bf16[2,5,128,128]{3,2,1,0:T(8,128)(2,1)}, bf16[2,5,128,128]{3,2,1,0:T(8,128)(2,1)}, u32[]{:S(2)}, u32[]{:S(2)}) collective-permute-start(bf16[2,5,128,128]{3,2,1,0:T(8,128)(2,1)} %get-tuple-element.72), channel_id=1, source_target_pairs={{0,1},{1,0},{2,3},{3,2},{4,5},{5,4},{6,7},{7,6},{8,9},{9,8},{10,11... | collective-permute-start | bytes 983048 | tf_op jit(solution)/shard_map/ppermute | solution.py:348
  33.1 1.4 %collective-permute-start.9 = (bf16[5,128,128]{2,1,0:T(8,128)(2,1)}, bf16[5,128,128]{2,1,0:T(8,128)(2,1)}, u32[]{:S(2)}, u32[]{:S(2)}) collective-permute-start(bf16[5,128,128]{2,1,0:T(8,128)(2,1)} %get-tuple-element.73), channel_id=1, source_target_pairs={{0,7},{1,2},{2,1},{3,4},{4,3},{5,6},{6,5},{7,0},{8,15},{9,10},{10,... | collective-permute-start | bytes 491528 | tf_op jit(solution)/shard_map/ppermute | solution.py:348
  34.6 0.1 side_table.1.table
  34.7 1.1 %near.1.w_near.refs_6_ = bf16[3,128,384]{2,1,0:T(8,128)(2,1)S(1)} custom-call(s32[8,45]{1,0:T(8,128)S(1)} %side_table.1.table, bf16[97,128,128]{2,1,0:T(8,128)(2,1)S(1)} %get-tuple-element.63.flat.held, bf16[2592,128]{1,0:T(8,128)(2,1)S(1)} %collective-permute-done.2.refs_0_.a_pair), custom_call_target="tpu_custom_call" | custom-call | flops 45 | bytes 1024 | tf_op jit(solution)/shard_map/near/pallas_call | solution.py:339
  35.7 0.0 collective-permute-done.7.piece.p_far
  35.8 0.1 collective-permute-start.10
  35.9 3.2 %collective-permute-done.11.far_out = bf16[1,2,4,128,128]{4,3,2,1,0:T(8,128)(2,1)S(1)} collective-permute-done((bf16[1,2,4,128,128]{4,3,2,1,0:T(8,128)(2,1)S(1)}, bf16[1,2,4,128,128]{4,3,2,1,0:T(8,128)(2,1)S(1)}, u32[]{:S(2)}, u32[]{:S(2)}) %collective-permute-start.11) | collective-permute-done | bytes 262176 | tf_op jit(solution)/shard_map/ppermute | solution.py:325
  39.1 1.7 %first_outer.1 = (bf16[3,5,128,128]{3,2,1,0:T(8,128)(2,1)S(1)}, bf16[97,128,128]{2,1,0:T(8,128)(2,1)S(1)}, bf16[3,128,384]{2,1,0:T(8,128)(2,1)S(1)}, bf16[3,128,384]{2,1,0:T(8,128)(2,1)S(1)}) custom-call(s32[8,45]{1,0:T(8,128)S(1)} %own_table.1.table, s32[8,45]{1,0:T(8,128)S(1)} %side_table.1.table, s32[1]{0:T(128)} %bitcast.turn, ...), custom_call_target="tpu_custom_call", output_to_operand_aliasing={{1}: (11, {})} | custom-call | flops 99999997952 | bytes 1024 | tf_op jit(solution)/shard_map/first_outer/pallas_call | solution.py:358
  40.8 0.1 collective-permute-start.13
  40.9 0.0 collective-permute-done.10.far_in
  40.9 2.0 %first_inner.1 = (bf16[3,5,128,128]{3,2,1,0:T(8,128)(2,1)S(1)}, bf16[97,128,128]{2,1,0:T(8,128)(2,1)S(1)}, bf16[3,128,384]{2,1,0:T(8,128)(2,1)S(1)}, bf16[3,128,...) custom-call(s32[8,45]{1,0:T(8,128)S(1)} %own_table.1.table, ...), custom_call_target="tpu_custom_call", output_to_operand_aliasing={{1}: (10, {})} | custom-call | flops 99999997952 | bytes 1024 | tf_op jit(solution)/shard_map/first_inner/pallas_call | solution.py:366
  42.9 2.1 %collective-permute-done.8.a_near = bf16[2,5,128,128]{3,2,1,0:T(8,128)(2,1)} collective-permute-done((bf16[2,5,128,128]{3,2,1,0:T(8,128)(2,1)}, bf16[2,5,128,128]{3,2,1,0:T(8,128)(2,1)}, u32[]{:S(2)}, u32[]{:S(2)}) %collective-permute-start.8) | collective-permute-done | bytes 327712 | tf_op jit(solution)/shard_map/ppermute | solution.py:348
  45.0 2.4 %sides.2 = (bf16[3,5,128,128]{3,2,1,0:T(8,128)(2,1)S(1)}, bf16[3,128,384]{2,1,0:T(8,128)(2,1)S(1)}, bf16[3,128,384]{2,1,0:T(8,128)(2,1)S(1)}, bf16[3,128,384]{2,1,0:T(8,128)(2,1)S(1)}) custom-call(s32[8,45]{1,0:T(8,128)S(1)} %own_table.1.table, s32[8,45]{1,0:T(8,128)S(1)} %side_table.1.table, s32[1]{0:T(128)} %bitcast.turn, ...), custom_call_target="tpu_custom_call" | custom-call | flops 100 | bytes 1024 | tf_op jit(solution)/shard_map/sides/pallas_call | solution.py:382
  47.5 1.3 %collective-permute-start.12 = (bf16[5,128,128]{2,1,0:T(8,128)(2,1)S(1)}, bf16[5,128,128]{2,1,0:T(8,128)(2,1)S(1)}, u32[]{:S(2)}, u32[]{:S(2)}) collective-permute-start(bf16[5,128,128]{2,1,0:T(8,128)(2,1)S(1)} %get-tuple-element.83), channel_id=1, source_target_pairs={{0,7},{1,2},{2,1},{3,4},{4,3},{5,6},{6,5},{7,0},{8,15},{9,10},{10,... | collective-permute-start | bytes 491528 | tf_op jit(solution)/shard_map/ppermute | solution.py:348
  48.8 1.9 %collective-permute-start.16 = (bf16[3,5,128,128]{3,2,1,0:T(8,128)(2,1)S(1)}, bf16[3,5,128,128]{3,2,1,0:T(8,128)(2,1)S(1)}, u32[]{:S(2)}, u32[]{:S(2)}) collective-permute-start(bf16[3,5,128,128]{3,2,1,0:T(8,128)(2,1)S(1)} %get-tuple-element.100), channel_id=1, source_target_pairs={{0,8},{8,0},{16,24},{24,16},{1,9},{9,1},{17,25},{25,17},{2,10},{10... | collective-permute-start | bytes 1474568 | tf_op jit(solution)/shard_map/ppermute | solution.py:390
  50.7 0.3 collective-permute-start.14
  51.0 2.3 %collective-permute-done.13.outer = bf16[3,5,128,128]{3,2,1,0:T(8,128)(2,1)S(1)} collective-permute-done((bf16[3,5,128,128]{3,2,1,0:T(8,128)(2,1)S(1)}, bf16[3,5,128,128]{3,2,1,0:T(8,128)(2,1)S(1)}, u32[]{:S(2)}, u32[]{:S(2)}) %collective-permute-start.13) | collective-permute-done | bytes 491552 | tf_op jit(solution)/shard_map/ppermute | solution.py:389
  53.3 2.7 %collective-permute-done.12.a_far = bf16[5,128,128]{2,1,0:T(8,128)(2,1)S(1)} collective-permute-done((bf16[5,128,128]{2,1,0:T(8,128)(2,1)S(1)}, bf16[5,128,128]{2,1,0:T(8,128)(2,1)S(1)}, u32[]{:S(2)}, u32[]{:S(2)}) %collective-permute-start.12) | collective-permute-done | bytes 163872 | tf_op jit(solution)/shard_map/ppermute | solution.py:348
  56.0 2.4 %sides.3 = (bf16[3,5,128,128]{3,2,1,0:T(8,128)(2,1)S(1)}, bf16[3,128,384]{2,1,0:T(8,128)(2,1)S(1)}, bf16[3,128,384]{2,1,0:T(8,128)(2,1)S(1)}, bf16[3,128,384]{2,1,0:T(8,128)(2,1)S(1)}) custom-call(s32[8,45]{1,0:T(8,128)S(1)} %own_table.1.table, s32[8,45]{1,0:T(8,128)S(1)} %side_table.1.table, s32[1]{0:T(128)} %bitcast.turn, ...), custom_call_target="tpu_custom_call" | custom-call | flops 100 | bytes 1024 | tf_op jit(solution)/shard_map/sides/pallas_call | solution.py:382
  58.4 0.1 collective-permute-start.15
  58.5 0.7 %centre.3.own = f32[3,5,128,128]{3,2,1,0:T(8,128)S(1)} custom-call(s32[1]{0:T(128)} %bitcast.turn, bf16[2,2,4,128,128]{4,3,2,1,0:T(8,128)(2,1)S(1)} %copy-done.3, bf16[2,2,4,128,128]{4,3,2,1,0:T(8,128)(2,1)S(1)} %collective-permute-done.piece.p_near, bf16[2,2,4,128,128]{4,3,2,1,0:T(8,128)(2,1)S(1)} %collective-permute-done.7.piece.p_far, ...), custom_call_target="tpu_custom_call" | custom-call | flops 144 | bytes 1024 | tf_op jit(solution)/shard_map/centre/pallas_call | solution.py:391
  59.1 0.6 centre.2.own
  59.8 1.0 %final.2.refs_0_ = bf16[2,1,1,25,128,128]{5,4,3,2,1,0:T(8,128)(2,1)} custom-call(s32[1]{0:T(128)} %bitcast.turn, f32[3,5,128,128]{3,2,1,0:T(8,128)S(1)} %centre.3.own, bf16[3,5,128,128]{3,2,1,0:T(8,128)(2,1)S(1)} %collective-permute-done.13.outer, bf16[3,5,128,128]{3,2,1,0:T(8,128)(2,1)S(1)} %collective-permute-done.16.inner), custom_call_target="tpu_custom_call" | custom-call | flops 1 | bytes 1024 | tf_op jit(solution)/shard_map/final/pallas_call | solution.py:398
  60.8 3.3 %collective-permute-done.14.outer = bf16[3,5,128,128]{3,2,1,0:T(8,128)(2,1)S(1)} collective-permute-done((bf16[3,5,128,128]{3,2,1,0:T(8,128)(2,1)S(1)}, bf16[3,5,128,128]{3,2,1,0:T(8,128)(2,1)S(1)}, u32[]{:S(2)}, u32[]{:S(2)}) %collective-permute-start.14) | collective-permute-done | bytes 491552 | tf_op jit(solution)/shard_map/ppermute | solution.py:389
  64.0 1.0 %final.3 = bf16[2,1,1,25,128,128]{5,4,3,2,1,0:T(8,128)(2,1)} custom-call(s32[1]{0:T(128)} %bitcast.turn, f32[3,5,128,128]{3,2,1,0:T(8,128)S(1)} %centre.2.own, bf16[3,5,128,128]{3,2,1,0:T(8,128)(2,1)S(1)} %collective-permute-done.14.outer, bf16[3,5,128,128]{3,2,1,0:T(8,128)(2,1)S(1)} %collective-permute-done.15.inner, ...), custom_call_target="tpu_custom_call", output_to_operand_aliasing={{}: (4, {})} | custom-call | flops 1 | bytes 1024 | tf_op jit(solution)/shard_map/final/pallas_call | solution.py:398
  (20 shorter events, 0.2 us)
Async XLA Ops:
  0.0 16.7 %collective-permute-start = (bf16[2,2,4,128,128]{4,3,2,1,0:T(8,128)(2,1)}, bf16[2,2,4,128,128]{4,3,2,1,0:T(8,128)(2,1)S(1)}, u32[]{:S(2)}, u32[]{:S(2)}) collective-permute-start(bf16[2,2,4,128,128]{4,3,2,1,0:T(8,128)(2,1)} %p_own.13), channel_id=1, source_target_pairs={{0,1},{1,0},{2,3},{3,2},{4,5},{5,4},{6,7},{7,6},{8,9},{9,8},{10,11... | collective-permute-start | bytes 1572872 | tf_op jit(solution)/shard_map/ppermute | solution.py:296
  2.9 25.8 %copy-start.1 = (bf16[2,2,2,5,128,128]{5,4,3,2,1,0:T(8,128)(2,1)S(1)}, bf16[2,2,2,5,128,128]{5,4,3,2,1,0:T(8,128)(2,1)}, u32[]{:S(2)}) copy-start(bf16[2,2,2,5,128,128]{5,4,3,2,1,0:T(8,128)(2,1)} %a_own.13) | copy-start | bytes 3932164
  5.1 11.5 %collective-permute-start.1 = (bf16[1296,128]{1,0:T(8,128)(2,1)}, bf16[1296,128]{1,0:T(8,128)(2,1)S(1)}, u32[]{:S(2)}, u32[]{:S(2)}) collective-permute-start(bf16[1296,128]{1,0:T(8,128)(2,1)} %pack_far.1.after.refs_0_), channel_id=1, source_target_pairs={{0,6},{1,3},{2,0},{3,5},{4,2},{5,7},{6,4},{7,1},{8,14},{9,11},{10,... | collective-permute-start | bytes 995336 | tf_op jit(solution)/shard_map/ppermute | solution.py:306
  8.7 1.0 %copy-start.2 = (bf16[2,2,4,128,128]{4,3,2,1,0:T(8,128)(2,1)S(1)}, bf16[2,2,4,128,128]{4,3,2,1,0:T(8,128)(2,1)}, u32[]{:S(2)}) copy-start(bf16[2,2,4,128,128]{4,3,2,1,0:T(8,128)(2,1)} %p_own.13) | copy-start | bytes 1572868
  9.8 19.0 %copy-start.3 = (bf16[2,2,4,128,128]{4,3,2,1,0:T(8,128)(2,1)S(1)}, bf16[2,2,4,128,128]{4,3,2,1,0:T(8,128)(2,1)}, u32[]{:S(2)}) copy-start(bf16[2,2,4,128,128]{4,3,2,1,0:T(8,128)(2,1)} %p_own.13) | copy-start | bytes 1572868
  9.8 8.6 %collective-permute-start.3 = (bf16[1,2,4,128,128]{4,3,2,1,0:T(8,128)(2,1)S(1)}, bf16[1,2,4,128,128]{4,3,2,1,0:T(8,128)(2,1)S(1)}, u32[]{:S(2)}, u32[]{:S(2)}) collective-permute-start(bf16[1,2,4,128,128]{4,3,2,1,0:T(8,128)(2,1)S(1)} %get-tuple-element.56), channel_id=1, source_target_pairs={{0,8},{8,0},{16,24},{24,16},{1,9},{9,1},{17,25},{25,17},{2,10},{10... | collective-permute-start | bytes 786440 | tf_op jit(solution)/shard_map/ppermute | solution.py:316
  9.9 8.5 %collective-permute-start.4 = (bf16[1,2,4,128,128]{4,3,2,1,0:T(8,128)(2,1)S(1)}, bf16[1,2,4,128,128]{4,3,2,1,0:T(8,128)(2,1)S(1)}, u32[]{:S(2)}, u32[]{:S(2)}) collective-permute-start(bf16[1,2,4,128,128]{4,3,2,1,0:T(8,128)(2,1)S(1)} %get-tuple-element.57), channel_id=1, source_target_pairs={{0,24},{8,16},{16,8},{24,0},{1,25},{9,17},{17,9},{25,1},{2,26},{10... | collective-permute-start | bytes 786440 | tf_op jit(solution)/shard_map/ppermute | solution.py:317
  11.5 1.3 %copy-start = (bf16[2,2,2,5,128,128]{5,4,3,2,1,0:T(8,128)(2,1)S(1)}, bf16[2,2,2,5,128,128]{5,4,3,2,1,0:T(8,128)(2,1)}, u32[]{:S(2)}) copy-start(bf16[2,2,2,5,128,128]{5,4,3,2,1,0:T(8,128)(2,1)} %a_own.13) | copy-start | bytes 3932164
  12.8 1.0 %copy-start.4 = (bf16[1296,128]{1,0:T(8,128)(2,1)S(1)}, bf16[1296,128]{1,0:T(8,128)(2,1)}, u32[]{:S(2)}) copy-start(bf16[1296,128]{1,0:T(8,128)(2,1)} %pack_far.1.after.refs_0_) | copy-start | bytes 995332
  13.8 0.7 %copy-start.6 = (s32[2,2,2,5]{3,2,1,0:T(2,128)S(1)}, s32[2,2,2,5]{3,2,1,0:T(2,128)}, u32[]{:S(2)}) copy-start(s32[2,2,2,5]{3,2,1,0:T(2,128)} %off.3) | copy-start | bytes 484
  14.5 0.7 %copy-start.7 = (s32[2,2,2]{2,1,0:T(2,128)S(1)}, s32[2,2,2]{2,1,0:T(2,128)}, u32[]{:S(2)}) copy-start(s32[2,2,2]{2,1,0:T(2,128)} %count.3) | copy-start | bytes 100
  15.2 13.4 %copy-start.5 = (bf16[1296,128]{1,0:T(8,128)(2,1)S(1)}, bf16[1296,128]{1,0:T(8,128)(2,1)}, u32[]{:S(2)}) copy-start(bf16[1296,128]{1,0:T(8,128)(2,1)} %pack_far.1.after.refs_0_) | copy-start | bytes 995332
  16.7 17.8 %collective-permute-start.2 = (bf16[2592,128]{1,0:T(8,128)(2,1)S(1)}, bf16[2592,128]{1,0:T(8,128)(2,1)S(1)}, u32[]{:S(2)}, u32[]{:S(2)}) collective-permute-start(bf16[2592,128]{1,0:T(8,128)(2,1)S(1)} %join.1), channel_id=1, source_target_pairs={{0,1},{1,0},{2,3},{3,2},{4,5},{5,4},{6,7},{7,6},{8,9},{9,8},{10,11... | collective-permute-start | bytes 1990664 | tf_op jit(solution)/shard_map/ppermute | solution.py:320
  17.1 18.6 %collective-permute-start.7 = (bf16[2,2,4,128,128]{4,3,2,1,0:T(8,128)(2,1)S(1)}, bf16[2,2,4,128,128]{4,3,2,1,0:T(8,128)(2,1)S(1)}, u32[]{:S(2)}, u32[]{:S(2)}) collective-permute-start(bf16[2,2,4,128,128]{4,3,2,1,0:T(8,128)(2,1)S(1)} %collective-permute-done.piece.p_near), channel_id=1, source_target_pairs={{0,2},{1,7},{2,4},{3,1},{4,6},{5,3},{6,0},{7,5},{8,10},{9,15},{10,... | collective-permute-start | bytes 1572872 | tf_op jit(solution)/shard_map/ppermute | solution.py:318
  18.4 8.5 %collective-permute-start.5 = (bf16[1,2,4,128,128]{4,3,2,1,0:T(8,128)(2,1)S(1)}, bf16[1,2,4,128,128]{4,3,2,1,0:T(8,128)(2,1)S(1)}, u32[]{:S(2)}, u32[]{:S(2)}) collective-permute-start(bf16[1,2,4,128,128]{4,3,2,1,0:T(8,128)(2,1)S(1)} %get-tuple-element.61), channel_id=1, source_target_pairs={{0,24},{8,16},{16,8},{24,0},{1,25},{9,17},{17,9},{25,1},{2,26},{10... | collective-permute-start | bytes 786440 | tf_op jit(solution)/shard_map/ppermute | solution.py:324
  19.6 9.1 %collective-permute-start.6 = (bf16[1,2,4,128,128]{4,3,2,1,0:T(8,128)(2,1)S(1)}, bf16[1,2,4,128,128]{4,3,2,1,0:T(8,128)(2,1)S(1)}, u32[]{:S(2)}, u32[]{:S(2)}) collective-permute-start(bf16[1,2,4,128,128]{4,3,2,1,0:T(8,128)(2,1)S(1)} %get-tuple-element.62), channel_id=1, source_target_pairs={{0,8},{8,0},{16,24},{24,16},{1,9},{9,1},{17,25},{25,17},{2,10},{10... | collective-permute-start | bytes 786440 | tf_op jit(solution)/shard_map/ppermute | solution.py:323
  26.9 12.1 %collective-permute-start.11 = (bf16[1,2,4,128,128]{4,3,2,1,0:T(8,128)(2,1)S(1)}, bf16[1,2,4,128,128]{4,3,2,1,0:T(8,128)(2,1)S(1)}, u32[]{:S(2)}, u32[]{:S(2)}) collective-permute-start(bf16[1,2,4,128,128]{4,3,2,1,0:T(8,128)(2,1)S(1)} %collective-permute-done.5.near_out), channel_id=1, source_target_pairs={{0,2},{1,7},{2,4},{3,1},{4,6},{5,3},{6,0},{7,5},{8,10},{9,15},{10,... | collective-permute-start | bytes 786440 | tf_op jit(solution)/shard_map/ppermute | solution.py:325
  30.9 14.1 %collective-permute-start.8 = (bf16[2,5,128,128]{3,2,1,0:T(8,128)(2,1)}, bf16[2,5,128,128]{3,2,1,0:T(8,128)(2,1)}, u32[]{:S(2)}, u32[]{:S(2)}) collective-permute-start(bf16[2,5,128,128]{3,2,1,0:T(8,128)(2,1)} %get-tuple-element.72), channel_id=1, source_target_pairs={{0,1},{1,0},{2,3},{3,2},{4,5},{5,4},{6,7},{7,6},{8,9},{9,8},{10,11... | collective-permute-start | bytes 983048 | tf_op jit(solution)/shard_map/ppermute | solution.py:348
  33.1 9.7 %collective-permute-start.9 = (bf16[5,128,128]{2,1,0:T(8,128)(2,1)}, bf16[5,128,128]{2,1,0:T(8,128)(2,1)}, u32[]{:S(2)}, u32[]{:S(2)}) collective-permute-start(bf16[5,128,128]{2,1,0:T(8,128)(2,1)} %get-tuple-element.73), channel_id=1, source_target_pairs={{0,7},{1,2},{2,1},{3,4},{4,3},{5,6},{6,5},{7,0},{8,15},{9,10},{10,... | collective-permute-start | bytes 491528 | tf_op jit(solution)/shard_map/ppermute | solution.py:348
  35.8 5.1 %collective-permute-start.10 = (bf16[1,2,4,128,128]{4,3,2,1,0:T(8,128)(2,1)S(1)}, bf16[1,2,4,128,128]{4,3,2,1,0:T(8,128)(2,1)S(1)}, u32[]{:S(2)}, u32[]{:S(2)}) collective-permute-start(bf16[1,2,4,128,128]{4,3,2,1,0:T(8,128)(2,1)S(1)} %row.1), channel_id=1, source_target_pairs={{0,8},{8,0},{16,24},{24,16},{1,9},{9,1},{17,25},{25,17},{2,10},{10... | collective-permute-start | bytes 786440 | tf_op jit(solution)/shard_map/ppermute | solution.py:345
  40.8 12.5 %collective-permute-start.13 = (bf16[3,5,128,128]{3,2,1,0:T(8,128)(2,1)S(1)}, bf16[3,5,128,128]{3,2,1,0:T(8,128)(2,1)S(1)}, u32[]{:S(2)}, u32[]{:S(2)}) collective-permute-start(bf16[3,5,128,128]{3,2,1,0:T(8,128)(2,1)S(1)} %get-tuple-element.84), channel_id=1, source_target_pairs={{0,24},{8,16},{16,8},{24,0},{1,25},{9,17},{17,9},{25,1},{2,26},{10... | collective-permute-start | bytes 1474568 | tf_op jit(solution)/shard_map/ppermute | solution.py:389
  47.5 8.5 %collective-permute-start.12 = (bf16[5,128,128]{2,1,0:T(8,128)(2,1)S(1)}, bf16[5,128,128]{2,1,0:T(8,128)(2,1)S(1)}, u32[]{:S(2)}, u32[]{:S(2)}) collective-permute-start(bf16[5,128,128]{2,1,0:T(8,128)(2,1)S(1)} %get-tuple-element.83), channel_id=1, source_target_pairs={{0,7},{1,2},{2,1},{3,4},{4,3},{5,6},{6,5},{7,0},{8,15},{9,10},{10,... | collective-permute-start | bytes 491528 | tf_op jit(solution)/shard_map/ppermute | solution.py:348
  48.8 11.0 %collective-permute-start.16 = (bf16[3,5,128,128]{3,2,1,0:T(8,128)(2,1)S(1)}, bf16[3,5,128,128]{3,2,1,0:T(8,128)(2,1)S(1)}, u32[]{:S(2)}, u32[]{:S(2)}) collective-permute-start(bf16[3,5,128,128]{3,2,1,0:T(8,128)(2,1)S(1)} %get-tuple-element.100), channel_id=1, source_target_pairs={{0,8},{8,0},{16,24},{24,16},{1,9},{9,1},{17,25},{25,17},{2,10},{10... | collective-permute-start | bytes 1474568 | tf_op jit(solution)/shard_map/ppermute | solution.py:390
  50.7 13.3 %collective-permute-start.14 = (bf16[3,5,128,128]{3,2,1,0:T(8,128)(2,1)S(1)}, bf16[3,5,128,128]{3,2,1,0:T(8,128)(2,1)S(1)}, u32[]{:S(2)}, u32[]{:S(2)}) collective-permute-start(bf16[3,5,128,128]{3,2,1,0:T(8,128)(2,1)S(1)} %get-tuple-element.93), channel_id=1, source_target_pairs={{0,24},{8,16},{16,8},{24,0},{1,25},{9,17},{17,9},{25,1},{2,26},{10... | collective-permute-start | bytes 1474568 | tf_op jit(solution)/shard_map/ppermute | solution.py:389
  58.4 5.6 %collective-permute-start.15 = (bf16[3,5,128,128]{3,2,1,0:T(8,128)(2,1)S(1)}, bf16[3,5,128,128]{3,2,1,0:T(8,128)(2,1)S(1)}, u32[]{:S(2)}, u32[]{:S(2)}) collective-permute-start(bf16[3,5,128,128]{3,2,1,0:T(8,128)(2,1)S(1)} %get-tuple-element.94), channel_id=1, source_target_pairs={{0,8},{8,0},{16,24},{24,16},{1,9},{9,1},{17,25},{25,17},{2,10},{10... | collective-permute-start | bytes 1474568 | tf_op jit(solution)/shard_map/ppermute | solution.py:390

commit v10 on v8

--- a/solution.py
+++ b/solution.py
@@ -12,7 +12,7 @@
 ZERO = 3 * HALF
 INFO = 16
 LONG = 10**11
-VMEM_LIMIT = 24 * 1024 * 1024
+VMEM_LIMIT = 16 * 1024 * 1024
 
 
 def pair(count):

time: 65.4 us -> 65.4 us (level)
  no operation moved by 1% of the time
where the time goes in v10:
time: 65.4 us; the launch traced here: 65 us
  starting transfers between devices  22.9 us (35%)
  Pallas kernels  18.9 us (29%)
  waiting for transfers between devices  18.3 us (28%)
  local copies, waits for them, and re-layouts  4.71 us (7%)
    ppermute x2, waiting for transfers between devices, per_device(): from_out = lax.ppermute(sums[0], 'row', out_way)  8.27 us
    ppermute x1, waiting for transfers between devices, per_device(): near_out = lax.ppermute(near_out, 'row', out_way)  6.8 us
    ppermute x3, starting transfers between devices, send(): lax.ppermute(later[3 * s - 3 + place], 'col', way)  6.34 us
    pallas_call x2, Pallas kernels, per_device(): call(functools.partial(sides_kernel, operators, s, x), [smem, smem, smem]...  4.81 us
    unnamed x16, local copies, waits for them, and re-layouts  4.71 us
    ppermute x1, starting transfers between devices, per_device(): moved = lax.ppermute(own_0, 'col', aside_way)  3.6 us
    ppermute x1, waiting for transfers between devices, per_device(): far_out = lax.ppermute(near_out, 'col', on_way)  3.21 us
    ppermute x1, starting transfers between devices, per_device(): p_near = lax.ppermute(p_vals, 'col', near_way)  2.94 us
  transfers between devices with their start and end apart: 17, of which 4 were waited for; matrix products, arithmetic and copies ran while one was open for 0% of the time, Pallas kernels for 28%

profile of v10, /device:TPU:0, one launch (start us, length us, event | category | flops | bytes accessed | tf_op | source)
XLA Modules:
  0.0 65.0 jit_solution(7017969497321362509)
XLA Ops:
  0.0 2.9 %collective-permute-start = (bf16[2,2,4,128,128]{4,3,2,1,0:T(8,128)(2,1)}, bf16[2,2,4,128,128]{4,3,2,1,0:T(8,128)(2,1)S(1)}, u32[]{:S(2)}, u32[]{:S(2)}) collective-permute-start(bf16[2,2,4,128,128]{4,3,2,1,0:T(8,128)(2,1)} %p_own.13), channel_id=1, source_target_pairs={{0,1},{1,0},{2,3},{3,2},{4,5},{5,4},{6,7},{7,6},{8,9},{9,8},{10,11... | collective-permute-start | bytes 1572872 | tf_op jit(solution)/shard_map/ppermute | solution.py:296
  2.9 2.2 %pack_far.1.after.refs_0_ = bf16[1296,128]{1,0:T(8,128)(2,1)} custom-call(s32[1]{0:T(128)} %bitcast.turn, s32[2,2,2,5]{3,2,1,0:T(2,128)} %off.3, s32[2,2,2]{2,1,0:T(2,128)} %count.3, bf16[2,2,2,5,128,128]{5,4,3,2,1,0:T(8,128)(2,1)} %a_own.13), custom_call_target="tpu_custom_call" | custom-call | flops 1 | bytes 1024 | tf_op jit(solution)/shard_map/pack_far/pallas_call | solution.py:300
  5.1 3.6 %collective-permute-start.1 = (bf16[1296,128]{1,0:T(8,128)(2,1)}, bf16[1296,128]{1,0:T(8,128)(2,1)S(1)}, u32[]{:S(2)}, u32[]{:S(2)}) collective-permute-start(bf16[1296,128]{1,0:T(8,128)(2,1)} %pack_far.1.after.refs_0_), channel_id=1, source_target_pairs={{0,6},{1,3},{2,0},{3,5},{4,2},{5,7},{6,4},{7,1},{8,14},{9,11},{10,... | collective-permute-start | bytes 995336 | tf_op jit(solution)/shard_map/ppermute | solution.py:306
  8.7 1.0 %copy-done.2 = bf16[2,2,4,128,128]{4,3,2,1,0:T(8,128)(2,1)S(1)} copy-done((bf16[2,2,4,128,128]{4,3,2,1,0:T(8,128)(2,1)S(1)}, bf16[2,2,4,128,128]{4,3,2,1,0:T(8,128)(2,1)}, u32[]{:S(2)}) %copy-start.2) | copy-done | bytes 524312
  9.8 0.1 collective-permute-start.3
  9.9 1.6 %collective-permute-start.4 = (bf16[1,2,4,128,128]{4,3,2,1,0:T(8,128)(2,1)S(1)}, bf16[1,2,4,128,128]{4,3,2,1,0:T(8,128)(2,1)S(1)}, u32[]{:S(2)}, u32[]{:S(2)}) collective-permute-start(bf16[1,2,4,128,128]{4,3,2,1,0:T(8,128)(2,1)S(1)} %get-tuple-element.56), channel_id=1, source_target_pairs={{0,24},{8,16},{16,8},{24,0},{1,25},{9,17},{17,9},{25,1},{2,26},{10... | collective-permute-start | bytes 786440 | tf_op jit(solution)/shard_map/ppermute | solution.py:317
  11.5 1.3 %copy-done = bf16[2,2,2,5,128,128]{5,4,3,2,1,0:T(8,128)(2,1)S(1)} copy-done((bf16[2,2,2,5,128,128]{5,4,3,2,1,0:T(8,128)(2,1)S(1)}, bf16[2,2,2,5,128,128]{5,4,3,2,1,0:T(8,128)(2,1)}, u32[]{:S(2)}) %copy-start) | copy-done | bytes 1310744
  12.9 1.0 %copy-done.4 = bf16[1296,128]{1,0:T(8,128)(2,1)S(1)} copy-done((bf16[1296,128]{1,0:T(8,128)(2,1)S(1)}, bf16[1296,128]{1,0:T(8,128)(2,1)}, u32[]{:S(2)}) %copy-start.4) | copy-done | bytes 331800
  13.8 0.7 %copy-done.6 = s32[2,2,2,5]{3,2,1,0:T(2,128)S(1)} copy-done((s32[2,2,2,5]{3,2,1,0:T(2,128)S(1)}, s32[2,2,2,5]{3,2,1,0:T(2,128)}, u32[]{:S(2)}) %copy-start.6) | copy-done | bytes 184
  14.5 0.7 %copy-done.7 = s32[2,2,2]{2,1,0:T(2,128)S(1)} copy-done((s32[2,2,2]{2,1,0:T(2,128)S(1)}, s32[2,2,2]{2,1,0:T(2,128)}, u32[]{:S(2)}) %copy-start.7) | copy-done | bytes 56
  15.2 1.5 %pack.1 = (bf16[1296,128]{1,0:T(8,128)(2,1)S(1)}, bf16[5,128,128]{2,1,0:T(8,128)(2,1)}, bf16[5,128,128]{2,1,0:T(8,128)(2,1)S(1)}, bf16[2,5,128,128]{3,2,1,0:T(8,128)(2,1)}) custom-call(s32[1]{0:T(128)} %bitcast.turn, s32[2,2,2,5]{3,2,1,0:T(2,128)S(1)} %copy-done.6, s32[2,2,2]{2,1,0:T(2,128)S(1)} %copy-done.7, bf16[2,2,2,5,128,128]{5,4,3,2,1,0:T(8,128)(2,1)S(1)} %copy-done, ...), custom_call_target="tpu_custom_call" | custom-call | flops 1 | bytes 1024 | tf_op jit(solution)/shard_map/pack/pallas_call | solution.py:303
  16.7 0.0 collective-permute-done.1.far
  16.7 0.4 collective-permute-start.2
  17.1 1.3 %collective-permute-start.7 = (bf16[2,2,4,128,128]{4,3,2,1,0:T(8,128)(2,1)S(1)}, bf16[2,2,4,128,128]{4,3,2,1,0:T(8,128)(2,1)S(1)}, u32[]{:S(2)}, u32[]{:S(2)}) collective-permute-start(bf16[2,2,4,128,128]{4,3,2,1,0:T(8,128)(2,1)S(1)} %collective-permute-done.piece.p_near), channel_id=1, source_target_pairs={{0,2},{1,7},{2,4},{3,1},{4,6},{5,3},{6,0},{7,5},{8,10},{9,15},{10,... | collective-permute-start | bytes 1572872 | tf_op jit(solution)/shard_map/ppermute | solution.py:318
  18.4 0.0 collective-permute-done.3.own_in
  18.4 0.0 collective-permute-done.4.own_out
  18.4 1.2 %collective-permute-start.5 = (bf16[1,2,4,128,128]{4,3,2,1,0:T(8,128)(2,1)S(1)}, bf16[1,2,4,128,128]{4,3,2,1,0:T(8,128)(2,1)S(1)}, u32[]{:S(2)}, u32[]{:S(2)}) collective-permute-start(bf16[1,2,4,128,128]{4,3,2,1,0:T(8,128)(2,1)S(1)} %get-tuple-element.60), channel_id=1, source_target_pairs={{0,24},{8,16},{16,8},{24,0},{1,25},{9,17},{17,9},{25,1},{2,26},{10... | collective-permute-start | bytes 786440 | tf_op jit(solution)/shard_map/ppermute | solution.py:324
  19.6 0.5 collective-permute-start.6
  20.1 6.8 %collective-permute-done.5.near_out = bf16[1,2,4,128,128]{4,3,2,1,0:T(8,128)(2,1)S(1)} collective-permute-done((bf16[1,2,4,128,128]{4,3,2,1,0:T(8,128)(2,1)S(1)}, bf16[1,2,4,128,128]{4,3,2,1,0:T(8,128)(2,1)S(1)}, u32[]{:S(2)}, u32[]{:S(2)}) %collective-permute-start.5) | collective-permute-done | bytes 262176 | tf_op jit(solution)/shard_map/ppermute | solution.py:324
  26.9 1.7 %collective-permute-start.11 = (bf16[1,2,4,128,128]{4,3,2,1,0:T(8,128)(2,1)S(1)}, bf16[1,2,4,128,128]{4,3,2,1,0:T(8,128)(2,1)S(1)}, u32[]{:S(2)}, u32[]{:S(2)}) collective-permute-start(bf16[1,2,4,128,128]{4,3,2,1,0:T(8,128)(2,1)S(1)} %collective-permute-done.5.near_out), channel_id=1, source_target_pairs={{0,2},{1,7},{2,4},{3,1},{4,6},{5,3},{6,0},{7,5},{8,10},{9,15},{10,... | collective-permute-start | bytes 786440 | tf_op jit(solution)/shard_map/ppermute | solution.py:325
  28.6 0.1 own_table.1.table
  28.7 0.0 collective-permute-done.6.near_in
  28.7 2.1 %near_own.1 = (bf16[97,128,128]{2,1,0:T(8,128)(2,1)S(1)}, bf16[3,128,384]{2,1,0:T(8,128)(2,1)S(1)}, bf16[3,128,384]{2,1,0:T(8,128)(2,1)S(1)}, bf16[3,128,384]{2,1,0:T(8,128)(2,1)S(1)}, bf16[3,128,384]{2,1,0:T(8,128)(2,1)S(1)}) custom-call(s32[8,45]{1,0:T(8,128)S(1)} %own_table.1.table, s32[1]{0:T(128)} %bitcast.turn, ...), custom_call_target="tpu_custom_call" | custom-call | flops 360 | bytes 1024 | tf_op jit(solution)/shard_map/near_own/pallas_call | solution.py:326
  30.9 2.3 %collective-permute-start.8 = (bf16[2,5,128,128]{3,2,1,0:T(8,128)(2,1)}, bf16[2,5,128,128]{3,2,1,0:T(8,128)(2,1)}, u32[]{:S(2)}, u32[]{:S(2)}) collective-permute-start(bf16[2,5,128,128]{3,2,1,0:T(8,128)(2,1)} %get-tuple-element.71), channel_id=1, source_target_pairs={{0,1},{1,0},{2,3},{3,2},{4,5},{5,4},{6,7},{7,6},{8,9},{9,8},{10,11... | collective-permute-start | bytes 983048 | tf_op jit(solution)/shard_map/ppermute | solution.py:348
  33.1 1.4 %collective-permute-start.9 = (bf16[5,128,128]{2,1,0:T(8,128)(2,1)}, bf16[5,128,128]{2,1,0:T(8,128)(2,1)}, u32[]{:S(2)}, u32[]{:S(2)}) collective-permute-start(bf16[5,128,128]{2,1,0:T(8,128)(2,1)} %get-tuple-element.72), channel_id=1, source_target_pairs={{0,7},{1,2},{2,1},{3,4},{4,3},{5,6},{6,5},{7,0},{8,15},{9,10},{10,... | collective-permute-start | bytes 491528 | tf_op jit(solution)/shard_map/ppermute | solution.py:348
  34.6 0.0 collective-permute-done.2.refs_0_.a_pair
  34.6 0.1 side_table.1.table
  34.7 1.1 %near.1.w_near.refs_6_ = bf16[3,128,384]{2,1,0:T(8,128)(2,1)S(1)} custom-call(s32[8,45]{1,0:T(8,128)S(1)} %side_table.1.table, bf16[97,128,128]{2,1,0:T(8,128)(2,1)S(1)} %get-tuple-element.62.flat.held, bf16[2592,128]{1,0:T(8,128)(2,1)S(1)} %collective-permute-done.2.refs_0_.a_pair), custom_call_target="tpu_custom_call" | custom-call | flops 45 | bytes 1024 | tf_op jit(solution)/shard_map/near/pallas_call | solution.py:339
  35.7 0.0 collective-permute-done.7.piece.p_far
  35.8 0.1 collective-permute-start.10
  35.9 3.2 %collective-permute-done.11.far_out = bf16[1,2,4,128,128]{4,3,2,1,0:T(8,128)(2,1)S(1)} collective-permute-done((bf16[1,2,4,128,128]{4,3,2,1,0:T(8,128)(2,1)S(1)}, bf16[1,2,4,128,128]{4,3,2,1,0:T(8,128)(2,1)S(1)}, u32[]{:S(2)}, u32[]{:S(2)}) %collective-permute-start.11) | collective-permute-done | bytes 262176 | tf_op jit(solution)/shard_map/ppermute | solution.py:325
  39.1 1.7 %first_outer.1 = (bf16[3,5,128,128]{3,2,1,0:T(8,128)(2,1)S(1)}, bf16[97,128,128]{2,1,0:T(8,128)(2,1)S(1)}, bf16[3,128,384]{2,1,0:T(8,128)(2,1)S(1)}, bf16[3,128,384]{2,1,0:T(8,128)(2,1)S(1)}) custom-call(s32[8,45]{1,0:T(8,128)S(1)} %own_table.1.table, s32[8,45]{1,0:T(8,128)S(1)} %side_table.1.table, s32[1]{0:T(128)} %bitcast.turn, ...), custom_call_target="tpu_custom_call", output_to_operand_aliasing={{1}: (11, {})} | custom-call | flops 99999997952 | bytes 1024 | tf_op jit(solution)/shard_map/first_outer/pallas_call | solution.py:358
  40.8 0.1 collective-permute-start.13
  40.9 0.0 collective-permute-done.10.far_in
  40.9 2.0 %first_inner.1 = (bf16[3,5,128,128]{3,2,1,0:T(8,128)(2,1)S(1)}, bf16[97,128,128]{2,1,0:T(8,128)(2,1)S(1)}, bf16[3,128,384]{2,1,0:T(8,128)(2,1)S(1)}, bf16[3,128,...) custom-call(s32[8,45]{1,0:T(8,128)S(1)} %own_table.1.table, ...), custom_call_target="tpu_custom_call", output_to_operand_aliasing={{1}: (10, {})} | custom-call | flops 99999997952 | bytes 1024 | tf_op jit(solution)/shard_map/first_inner/pallas_call | solution.py:366
  42.9 2.7 %collective-permute-start.12 = (bf16[5,128,128]{2,1,0:T(8,128)(2,1)S(1)}, bf16[5,128,128]{2,1,0:T(8,128)(2,1)S(1)}, u32[]{:S(2)}, u32[]{:S(2)}) collective-permute-start(bf16[5,128,128]{2,1,0:T(8,128)(2,1)S(1)} %get-tuple-element.82), channel_id=1, source_target_pairs={{0,7},{1,2},{2,1},{3,4},{4,3},{5,6},{6,5},{7,0},{8,15},{9,10},{10,... | collective-permute-start | bytes 491528 | tf_op jit(solution)/shard_map/ppermute | solution.py:348
  45.5 2.7 %collective-permute-start.16 = (bf16[3,5,128,128]{3,2,1,0:T(8,128)(2,1)S(1)}, bf16[3,5,128,128]{3,2,1,0:T(8,128)(2,1)S(1)}, u32[]{:S(2)}, u32[]{:S(2)}) collective-permute-start(bf16[3,5,128,128]{3,2,1,0:T(8,128)(2,1)S(1)} %get-tuple-element.98), channel_id=1, source_target_pairs={{0,8},{8,0},{16,24},{24,16},{1,9},{9,1},{17,25},{25,17},{2,10},{10... | collective-permute-start | bytes 1474568 | tf_op jit(solution)/shard_map/ppermute | solution.py:391
  48.2 0.0 collective-permute-done.9.a_far
  48.2 2.4 %sides.2 = (bf16[3,5,128,128]{3,2,1,0:T(8,128)(2,1)S(1)}, bf16[3,128,384]{2,1,0:T(8,128)(2,1)S(1)}, bf16[3,128,384]{2,1,0:T(8,128)(2,1)S(1)}, bf16[3,128,384]{2,1,0:T(8,128)(2,1)S(1)}) custom-call(s32[8,45]{1,0:T(8,128)S(1)} %own_table.1.table, s32[8,45]{1,0:T(8,128)S(1)} %side_table.1.table, s32[1]{0:T(128)} %bitcast.turn, ...), custom_call_target="tpu_custom_call" | custom-call | flops 100 | bytes 1024 | tf_op jit(solution)/shard_map/sides/pallas_call | solution.py:383
  50.7 0.4 collective-permute-start.14
  51.0 2.3 %collective-permute-done.13.outer = bf16[3,5,128,128]{3,2,1,0:T(8,128)(2,1)S(1)} collective-permute-done((bf16[3,5,128,128]{3,2,1,0:T(8,128)(2,1)S(1)}, bf16[3,5,128,128]{3,2,1,0:T(8,128)(2,1)S(1)}, u32[]{:S(2)}, u32[]{:S(2)}) %collective-permute-start.13) | collective-permute-done | bytes 491552 | tf_op jit(solution)/shard_map/ppermute | solution.py:390
  53.3 2.4 %sides.3 = (bf16[3,5,128,128]{3,2,1,0:T(8,128)(2,1)S(1)}, bf16[3,128,384]{2,1,0:T(8,128)(2,1)S(1)}, bf16[3,128,384]{2,1,0:T(8,128)(2,1)S(1)}, bf16[3,128,384]{2,1,0:T(8,128)(2,1)S(1)}) custom-call(s32[8,45]{1,0:T(8,128)S(1)} %own_table.1.table, s32[8,45]{1,0:T(8,128)S(1)} %side_table.1.table, s32[1]{0:T(128)} %bitcast.turn, ...), custom_call_target="tpu_custom_call" | custom-call | flops 100 | bytes 1024 | tf_op jit(solution)/shard_map/sides/pallas_call | solution.py:383
  55.7 0.1 collective-permute-start.15
  55.8 0.7 %centre.3.own = f32[3,5,128,128]{3,2,1,0:T(8,128)S(1)} custom-call(s32[1]{0:T(128)} %bitcast.turn, bf16[2,2,4,128,128]{4,3,2,1,0:T(8,128)(2,1)S(1)} %copy-done.3, bf16[2,2,4,128,128]{4,3,2,1,0:T(8,128)(2,1)S(1)} %collective-permute-done.piece.p_near, bf16[2,2,4,128,128]{4,3,2,1,0:T(8,128)(2,1)S(1)} %collective-permute-done.7.piece.p_far, ...), custom_call_target="tpu_custom_call" | custom-call | flops 144 | bytes 1024 | tf_op jit(solution)/shard_map/centre/pallas_call | solution.py:392
  56.4 0.6 centre.2.own
  57.1 1.0 %final.2.refs_0_ = bf16[2,1,1,25,128,128]{5,4,3,2,1,0:T(8,128)(2,1)} custom-call(s32[1]{0:T(128)} %bitcast.turn, f32[3,5,128,128]{3,2,1,0:T(8,128)S(1)} %centre.3.own, bf16[3,5,128,128]{3,2,1,0:T(8,128)(2,1)S(1)} %collective-permute-done.13.outer, bf16[3,5,128,128]{3,2,1,0:T(8,128)(2,1)S(1)} %collective-permute-done.16.inner), custom_call_target="tpu_custom_call" | custom-call | flops 1 | bytes 1024 | tf_op jit(solution)/shard_map/final/pallas_call | solution.py:399
  58.0 6.0 %collective-permute-done.14.outer = bf16[3,5,128,128]{3,2,1,0:T(8,128)(2,1)S(1)} collective-permute-done((bf16[3,5,128,128]{3,2,1,0:T(8,128)(2,1)S(1)}, bf16[3,5,128,128]{3,2,1,0:T(8,128)(2,1)S(1)}, u32[]{:S(2)}, u32[]{:S(2)}) %collective-permute-start.14) | collective-permute-done | bytes 491552 | tf_op jit(solution)/shard_map/ppermute | solution.py:390
  64.1 1.0 %final.3 = bf16[2,1,1,25,128,128]{5,4,3,2,1,0:T(8,128)(2,1)} custom-call(s32[1]{0:T(128)} %bitcast.turn, f32[3,5,128,128]{3,2,1,0:T(8,128)S(1)} %centre.2.own, bf16[3,5,128,128]{3,2,1,0:T(8,128)(2,1)S(1)} %collective-permute-done.14.outer, bf16[3,5,128,128]{3,2,1,0:T(8,128)(2,1)S(1)} %collective-permute-done.15.inner, ...), custom_call_target="tpu_custom_call", output_to_operand_aliasing={{}: (4, {})} | custom-call | flops 1 | bytes 1024 | tf_op jit(solution)/shard_map/final/pallas_call | solution.py:399
  (20 shorter events, 0.2 us)
Async XLA Ops:
  0.0 16.7 %collective-permute-start = (bf16[2,2,4,128,128]{4,3,2,1,0:T(8,128)(2,1)}, bf16[2,2,4,128,128]{4,3,2,1,0:T(8,128)(2,1)S(1)}, u32[]{:S(2)}, u32[]{:S(2)}) collective-permute-start(bf16[2,2,4,128,128]{4,3,2,1,0:T(8,128)(2,1)} %p_own.13), channel_id=1, source_target_pairs={{0,1},{1,0},{2,3},{3,2},{4,5},{5,4},{6,7},{7,6},{8,9},{9,8},{10,11... | collective-permute-start | bytes 1572872 | tf_op jit(solution)/shard_map/ppermute | solution.py:296
  2.9 25.8 %copy-start.1 = (bf16[2,2,2,5,128,128]{5,4,3,2,1,0:T(8,128)(2,1)S(1)}, bf16[2,2,2,5,128,128]{5,4,3,2,1,0:T(8,128)(2,1)}, u32[]{:S(2)}) copy-start(bf16[2,2,2,5,128,128]{5,4,3,2,1,0:T(8,128)(2,1)} %a_own.13) | copy-start | bytes 3932164
  5.1 11.5 %collective-permute-start.1 = (bf16[1296,128]{1,0:T(8,128)(2,1)}, bf16[1296,128]{1,0:T(8,128)(2,1)S(1)}, u32[]{:S(2)}, u32[]{:S(2)}) collective-permute-start(bf16[1296,128]{1,0:T(8,128)(2,1)} %pack_far.1.after.refs_0_), channel_id=1, source_target_pairs={{0,6},{1,3},{2,0},{3,5},{4,2},{5,7},{6,4},{7,1},{8,14},{9,11},{10,... | collective-permute-start | bytes 995336 | tf_op jit(solution)/shard_map/ppermute | solution.py:306
  8.7 1.0 %copy-start.2 = (bf16[2,2,4,128,128]{4,3,2,1,0:T(8,128)(2,1)S(1)}, bf16[2,2,4,128,128]{4,3,2,1,0:T(8,128)(2,1)}, u32[]{:S(2)}) copy-start(bf16[2,2,4,128,128]{4,3,2,1,0:T(8,128)(2,1)} %p_own.13) | copy-start | bytes 1572868
  9.8 19.0 %copy-start.3 = (bf16[2,2,4,128,128]{4,3,2,1,0:T(8,128)(2,1)S(1)}, bf16[2,2,4,128,128]{4,3,2,1,0:T(8,128)(2,1)}, u32[]{:S(2)}) copy-start(bf16[2,2,4,128,128]{4,3,2,1,0:T(8,128)(2,1)} %p_own.13) | copy-start | bytes 1572868
  9.8 8.6 %collective-permute-start.3 = (bf16[1,2,4,128,128]{4,3,2,1,0:T(8,128)(2,1)S(1)}, bf16[1,2,4,128,128]{4,3,2,1,0:T(8,128)(2,1)S(1)}, u32[]{:S(2)}, u32[]{:S(2)}) collective-permute-start(bf16[1,2,4,128,128]{4,3,2,1,0:T(8,128)(2,1)S(1)} %get-tuple-element.55), channel_id=1, source_target_pairs={{0,8},{8,0},{16,24},{24,16},{1,9},{9,1},{17,25},{25,17},{2,10},{10... | collective-permute-start | bytes 786440 | tf_op jit(solution)/shard_map/ppermute | solution.py:316
  9.9 8.5 %collective-permute-start.4 = (bf16[1,2,4,128,128]{4,3,2,1,0:T(8,128)(2,1)S(1)}, bf16[1,2,4,128,128]{4,3,2,1,0:T(8,128)(2,1)S(1)}, u32[]{:S(2)}, u32[]{:S(2)}) collective-permute-start(bf16[1,2,4,128,128]{4,3,2,1,0:T(8,128)(2,1)S(1)} %get-tuple-element.56), channel_id=1, source_target_pairs={{0,24},{8,16},{16,8},{24,0},{1,25},{9,17},{17,9},{25,1},{2,26},{10... | collective-permute-start | bytes 786440 | tf_op jit(solution)/shard_map/ppermute | solution.py:317
  11.5 1.3 %copy-start = (bf16[2,2,2,5,128,128]{5,4,3,2,1,0:T(8,128)(2,1)S(1)}, bf16[2,2,2,5,128,128]{5,4,3,2,1,0:T(8,128)(2,1)}, u32[]{:S(2)}) copy-start(bf16[2,2,2,5,128,128]{5,4,3,2,1,0:T(8,128)(2,1)} %a_own.13) | copy-start | bytes 3932164
  12.8 1.0 %copy-start.4 = (bf16[1296,128]{1,0:T(8,128)(2,1)S(1)}, bf16[1296,128]{1,0:T(8,128)(2,1)}, u32[]{:S(2)}) copy-start(bf16[1296,128]{1,0:T(8,128)(2,1)} %pack_far.1.after.refs_0_) | copy-start | bytes 995332
  13.8 0.7 %copy-start.6 = (s32[2,2,2,5]{3,2,1,0:T(2,128)S(1)}, s32[2,2,2,5]{3,2,1,0:T(2,128)}, u32[]{:S(2)}) copy-start(s32[2,2,2,5]{3,2,1,0:T(2,128)} %off.3) | copy-start | bytes 484
  14.5 0.7 %copy-start.7 = (s32[2,2,2]{2,1,0:T(2,128)S(1)}, s32[2,2,2]{2,1,0:T(2,128)}, u32[]{:S(2)}) copy-start(s32[2,2,2]{2,1,0:T(2,128)} %count.3) | copy-start | bytes 100
  15.2 13.4 %copy-start.5 = (bf16[1296,128]{1,0:T(8,128)(2,1)S(1)}, bf16[1296,128]{1,0:T(8,128)(2,1)}, u32[]{:S(2)}) copy-start(bf16[1296,128]{1,0:T(8,128)(2,1)} %pack_far.1.after.refs_0_) | copy-start | bytes 995332
  16.7 17.8 %collective-permute-start.2 = (bf16[2592,128]{1,0:T(8,128)(2,1)S(1)}, bf16[2592,128]{1,0:T(8,128)(2,1)S(1)}, u32[]{:S(2)}, u32[]{:S(2)}) collective-permute-start(bf16[2592,128]{1,0:T(8,128)(2,1)S(1)} %join.1), channel_id=1, source_target_pairs={{0,1},{1,0},{2,3},{3,2},{4,5},{5,4},{6,7},{7,6},{8,9},{9,8},{10,11... | collective-permute-start | bytes 1990664 | tf_op jit(solution)/shard_map/ppermute | solution.py:320
  17.1 18.6 %collective-permute-start.7 = (bf16[2,2,4,128,128]{4,3,2,1,0:T(8,128)(2,1)S(1)}, bf16[2,2,4,128,128]{4,3,2,1,0:T(8,128)(2,1)S(1)}, u32[]{:S(2)}, u32[]{:S(2)}) collective-permute-start(bf16[2,2,4,128,128]{4,3,2,1,0:T(8,128)(2,1)S(1)} %collective-permute-done.piece.p_near), channel_id=1, source_target_pairs={{0,2},{1,7},{2,4},{3,1},{4,6},{5,3},{6,0},{7,5},{8,10},{9,15},{10,... | collective-permute-start | bytes 1572872 | tf_op jit(solution)/shard_map/ppermute | solution.py:318
  18.4 8.5 %collective-permute-start.5 = (bf16[1,2,4,128,128]{4,3,2,1,0:T(8,128)(2,1)S(1)}, bf16[1,2,4,128,128]{4,3,2,1,0:T(8,128)(2,1)S(1)}, u32[]{:S(2)}, u32[]{:S(2)}) collective-permute-start(bf16[1,2,4,128,128]{4,3,2,1,0:T(8,128)(2,1)S(1)} %get-tuple-element.60), channel_id=1, source_target_pairs={{0,24},{8,16},{16,8},{24,0},{1,25},{9,17},{17,9},{25,1},{2,26},{10... | collective-permute-start | bytes 786440 | tf_op jit(solution)/shard_map/ppermute | solution.py:324
  19.6 9.1 %collective-permute-start.6 = (bf16[1,2,4,128,128]{4,3,2,1,0:T(8,128)(2,1)S(1)}, bf16[1,2,4,128,128]{4,3,2,1,0:T(8,128)(2,1)S(1)}, u32[]{:S(2)}, u32[]{:S(2)}) collective-permute-start(bf16[1,2,4,128,128]{4,3,2,1,0:T(8,128)(2,1)S(1)} %get-tuple-element.61), channel_id=1, source_target_pairs={{0,8},{8,0},{16,24},{24,16},{1,9},{9,1},{17,25},{25,17},{2,10},{10... | collective-permute-start | bytes 786440 | tf_op jit(solution)/shard_map/ppermute | solution.py:323
  26.9 12.1 %collective-permute-start.11 = (bf16[1,2,4,128,128]{4,3,2,1,0:T(8,128)(2,1)S(1)}, bf16[1,2,4,128,128]{4,3,2,1,0:T(8,128)(2,1)S(1)}, u32[]{:S(2)}, u32[]{:S(2)}) collective-permute-start(bf16[1,2,4,128,128]{4,3,2,1,0:T(8,128)(2,1)S(1)} %collective-permute-done.5.near_out), channel_id=1, source_target_pairs={{0,2},{1,7},{2,4},{3,1},{4,6},{5,3},{6,0},{7,5},{8,10},{9,15},{10,... | collective-permute-start | bytes 786440 | tf_op jit(solution)/shard_map/ppermute | solution.py:325
  30.9 17.3 %collective-permute-start.8 = (bf16[2,5,128,128]{3,2,1,0:T(8,128)(2,1)}, bf16[2,5,128,128]{3,2,1,0:T(8,128)(2,1)}, u32[]{:S(2)}, u32[]{:S(2)}) collective-permute-start(bf16[2,5,128,128]{3,2,1,0:T(8,128)(2,1)} %get-tuple-element.71), channel_id=1, source_target_pairs={{0,1},{1,0},{2,3},{3,2},{4,5},{5,4},{6,7},{7,6},{8,9},{9,8},{10,11... | collective-permute-start | bytes 983048 | tf_op jit(solution)/shard_map/ppermute | solution.py:348
  33.1 15.1 %collective-permute-start.9 = (bf16[5,128,128]{2,1,0:T(8,128)(2,1)}, bf16[5,128,128]{2,1,0:T(8,128)(2,1)}, u32[]{:S(2)}, u32[]{:S(2)}) collective-permute-start(bf16[5,128,128]{2,1,0:T(8,128)(2,1)} %get-tuple-element.72), channel_id=1, source_target_pairs={{0,7},{1,2},{2,1},{3,4},{4,3},{5,6},{6,5},{7,0},{8,15},{9,10},{10,... | collective-permute-start | bytes 491528 | tf_op jit(solution)/shard_map/ppermute | solution.py:348
  35.8 5.1 %collective-permute-start.10 = (bf16[1,2,4,128,128]{4,3,2,1,0:T(8,128)(2,1)S(1)}, bf16[1,2,4,128,128]{4,3,2,1,0:T(8,128)(2,1)S(1)}, u32[]{:S(2)}, u32[]{:S(2)}) collective-permute-start(bf16[1,2,4,128,128]{4,3,2,1,0:T(8,128)(2,1)S(1)} %row.1), channel_id=1, source_target_pairs={{0,8},{8,0},{16,24},{24,16},{1,9},{9,1},{17,25},{25,17},{2,10},{10... | collective-permute-start | bytes 786440 | tf_op jit(solution)/shard_map/ppermute | solution.py:345
  40.8 12.5 %collective-permute-start.13 = (bf16[3,5,128,128]{3,2,1,0:T(8,128)(2,1)S(1)}, bf16[3,5,128,128]{3,2,1,0:T(8,128)(2,1)S(1)}, u32[]{:S(2)}, u32[]{:S(2)}) collective-permute-start(bf16[3,5,128,128]{3,2,1,0:T(8,128)(2,1)S(1)} %get-tuple-element.83), channel_id=1, source_target_pairs={{0,24},{8,16},{16,8},{24,0},{1,25},{9,17},{17,9},{25,1},{2,26},{10... | collective-permute-start | bytes 1474568 | tf_op jit(solution)/shard_map/ppermute | solution.py:390
  42.9 10.4 %collective-permute-start.12 = (bf16[5,128,128]{2,1,0:T(8,128)(2,1)S(1)}, bf16[5,128,128]{2,1,0:T(8,128)(2,1)S(1)}, u32[]{:S(2)}, u32[]{:S(2)}) collective-permute-start(bf16[5,128,128]{2,1,0:T(8,128)(2,1)S(1)} %get-tuple-element.82), channel_id=1, source_target_pairs={{0,7},{1,2},{2,1},{3,4},{4,3},{5,6},{6,5},{7,0},{8,15},{9,10},{10,... | collective-permute-start | bytes 491528 | tf_op jit(solution)/shard_map/ppermute | solution.py:348
  45.5 11.5 %collective-permute-start.16 = (bf16[3,5,128,128]{3,2,1,0:T(8,128)(2,1)S(1)}, bf16[3,5,128,128]{3,2,1,0:T(8,128)(2,1)S(1)}, u32[]{:S(2)}, u32[]{:S(2)}) collective-permute-start(bf16[3,5,128,128]{3,2,1,0:T(8,128)(2,1)S(1)} %get-tuple-element.98), channel_id=1, source_target_pairs={{0,8},{8,0},{16,24},{24,16},{1,9},{9,1},{17,25},{25,17},{2,10},{10... | collective-permute-start | bytes 1474568 | tf_op jit(solution)/shard_map/ppermute | solution.py:391
  50.7 13.4 %collective-permute-start.14 = (bf16[3,5,128,128]{3,2,1,0:T(8,128)(2,1)S(1)}, bf16[3,5,128,128]{3,2,1,0:T(8,128)(2,1)S(1)}, u32[]{:S(2)}, u32[]{:S(2)}) collective-permute-start(bf16[3,5,128,128]{3,2,1,0:T(8,128)(2,1)S(1)} %get-tuple-element.92), channel_id=1, source_target_pairs={{0,24},{8,16},{16,8},{24,0},{1,25},{9,17},{17,9},{25,1},{2,26},{10... | collective-permute-start | bytes 1474568 | tf_op jit(solution)/shard_map/ppermute | solution.py:390
  55.7 8.4 %collective-permute-start.15 = (bf16[3,5,128,128]{3,2,1,0:T(8,128)(2,1)S(1)}, bf16[3,5,128,128]{3,2,1,0:T(8,128)(2,1)S(1)}, u32[]{:S(2)}, u32[]{:S(2)}) collective-permute-start(bf16[3,5,128,128]{3,2,1,0:T(8,128)(2,1)S(1)} %get-tuple-element.93), channel_id=1, source_target_pairs={{0,8},{8,0},{16,24},{24,16},{1,9},{9,1},{17,25},{25,17},{2,10},{10... | collective-permute-start | bytes 1474568 | tf_op jit(solution)/shard_map/ppermute | solution.py:391
